TPU v7x, 32 devices: a whole 2x2x4 slice. The times are simulated.
32 devices in a mesh: groups: 2 (over y), sec: 4 (over z), col: 2 (over x), rep: 2 (over core).
Axes of the slice: x: 2, y: 2, z: 4, core: 2. Of those that a mesh axis runs over, the one named last changes fastest.
Arguments:
- h_core: bfloat16 [10240, 5120], P(('groups', 'sec'), ('col', 'rep')), parts along dimension 0, may hold values from -2 to 2
- centers: float32 [3, 10240], P(None, 'groups'), parts along dimension 1, may hold values from 7 to 13
- mm_coords: float32 [3, 16384], P(None, ('groups', 'sec', 'col', 'rep')), parts along dimension 1, may hold values from 0 to 20
- mm_charges: float32 [16384], P(('groups', 'sec', 'col', 'rep')), parts along dimension 0, may hold values from -0.53033006 to 0.53033006
Outputs:
- density: float32 [10240, 5120], P(('groups', 'sec'), ('col', 'rep')), parts along dimension 0
- forces: float32 [3, 16384], P(None, ('groups', 'sec', 'col', 'rep')), parts along dimension 1
There are 2 independent parts, one for each index of `groups`. A program takes and returns all parts, laid end to end along the dimension named above; each array names one. Nothing has to cross between parts.
All inputs are finite; a program needn't handle non-finite values.
Results may differ from a plain program's by a relative error of at most 0.0054.
Values may be sent and summed in bfloat16 or wider, within the bound.
No kernel may reach another device: no remote copies, remote signals or barrier semaphores. Data moves between devices by JAX's collectives and lax.ppermute only.
A program may use at most 128 MiB of HBM per device.

v0:
```python
import jax
import jax.numpy as jnp
from jax import lax
from jax.sharding import PartitionSpec as P


def potential_terms(centers, mm_coords, mm_charges):
    total = centers.shape[1]
    width = min(512, total)

    def potential_one_block(index):
        spots = lax.dynamic_slice_in_dim(centers, index * width, width, 1)
        dist = jnp.sum((spots[:, :, None] - mm_coords[:, None, :]) ** 2, 0) + 1.0
        return jnp.sum(mm_charges[None, :] * lax.rsqrt(dist), 1)

    values = lax.map(potential_one_block, jnp.arange(total // width, dtype=jnp.int32))
    return values.reshape(total)


def force_terms(centers, occupation, mm_coords, mm_charges):
    total = centers.shape[1]
    width = min(512, total)

    def force_one_block(index, accum):
        spots = lax.dynamic_slice_in_dim(centers, index * width, width, 1)
        occ = lax.dynamic_slice_in_dim(occupation, index * width, width, 0)
        diff = mm_coords[:, None, :] - spots[:, :, None]
        dist = jnp.sum(diff * diff, 0) + 1.0
        weight = occ[:, None] * lax.rsqrt(dist) / dist
        return accum + jnp.sum(diff * weight[None], 1)

    summed = lax.fori_loop(
        0, total // width, force_one_block, jnp.zeros(mm_coords.shape, jnp.float32)
    )
    return -mm_charges[None, :] * summed


def fold_with(left, piece):
    return jnp.dot(left, piece, preferred_element_type=jnp.float32)


def shards(h_core, centers, mm_coords, mm_charges):
    row_count, col_count = h_core.shape
    total = centers.shape[1]
    row_start = lax.axis_index("sec") * row_count
    col_start = lax.axis_index(("col", "rep")) * col_count
    partial_value = potential_terms(centers, mm_coords, mm_charges)
    whole_pot = lax.psum(partial_value, ("sec", "col", "rep"))
    rows_pot = lax.dynamic_slice_in_dim(whole_pot, row_start, row_count, 0)
    rows_glob = row_start + lax.broadcasted_iota(jnp.int32, (row_count, col_count), 0)
    cols_glob = col_start + lax.broadcasted_iota(jnp.int32, (row_count, col_count), 1)
    on_diag = rows_glob == cols_glob
    ham = h_core.astype(jnp.float32) + jnp.where(on_diag, rows_pot[:, None], 0.0)
    off_part = jnp.sum(jnp.where(on_diag, 0.0, ham * ham), 1)
    diag_part = jnp.sum(jnp.where(on_diag, ham, 0.0), 1)
    off_rows, diag_vals = lax.psum((off_part, diag_part), ("col", "rep"))
    trace_val, off_total = lax.psum((jnp.sum(diag_vals), jnp.sum(off_rows)), "sec")
    mean_level = trace_val / total
    dev_total = lax.psum(jnp.sum((diag_vals - mean_level) ** 2), "sec")
    spread = jnp.sqrt((off_total + dev_total) / total + 1e-05)
    scale = 2.0 / (3.0 * spread)
    eye_local = on_diag.astype(jnp.float32)
    start_x = (0.5 * scale * (mean_level * eye_local - ham) + 0.5 * eye_local).astype(jnp.bfloat16)
    row_panel = lax.all_gather(start_x, ("col", "rep"), axis=1, tiled=True)
    square = fold_with(row_panel, lax.all_gather(start_x, "sec", axis=0, tiled=True))
    square_b = square.astype(jnp.bfloat16)
    square_panel = lax.all_gather(square_b, ("col", "rep"), axis=1, tiled=True)
    cube = fold_with(square_panel, lax.all_gather(start_x, "sec", axis=0, tiled=True))
    density = 3.0 * square - 2.0 * cube
    diag_local = jnp.sum(jnp.where(on_diag, density, 0.0), 1)
    occ_rows = lax.psum(diag_local, ("col", "rep"))
    occupation = lax.all_gather(occ_rows, "sec", axis=0, tiled=True)
    forces = force_terms(centers, occupation, mm_coords, mm_charges)
    return (density, forces)


def solution(mesh):
    in_specs = (
        P(("groups", "sec"), ("col", "rep")),
        P(None, "groups"),
        P(None, ("groups", "sec", "col", "rep")),
        P(("groups", "sec", "col", "rep")),
    )
    out_specs = (P(("groups", "sec"), ("col", "rep")), P(None, ("groups", "sec", "col", "rep")))
    return jax.shard_map(shards, mesh=mesh, in_specs=in_specs, out_specs=out_specs, check_vma=False)
```

profile of v0, /device:TPU:0, one launch (start us, length us, event | category | flops | bytes accessed | tf_op | source)
XLA Modules:
  0.0 654.4 jit_solution(15897886073996384153)
XLA Ops:
  7.2 40.9 %while.24 = (s32[]{:T(128)}, f32[10,512]{1,0:T(8,128)S(1)}, f32[512]{0:T(512)}, s32[10]{0:T(128)S(1)}, f32[3,5120]{1,0:T(4,128)}, /*index=5*/f32[3,512]{1,0:T(4,128)}, s32[]{:T(128)}, s32[1]{0:T(128)}, s32[]{:T(128)}, s32[]{:T(128)}) while((s32[]{:T(128)}, f32[10,512]{1,0:T(8,128)S(1)}, f32[512]{0:T(512)}, s32[10]{0:T(128)S(1)}, ...), condition=%wide.region_3.4_spmd, body=%wide.region_0.3_spmd.sunk | while | flops 2883078 | bytes 2130087 | solution.py:16
  7.2 0.6 dynamic_slice.34
  8.5 0.7 constant_dynamic-slice_fusion.4
  9.2 1.1 multiply_reduce_fusion.5
  10.4 0.9 multiply_reduce_fusion.6
  11.3 0.6 dynamic_slice.34
  12.6 0.7 constant_dynamic-slice_fusion.4
  13.3 1.1 multiply_reduce_fusion.5
  14.4 0.9 multiply_reduce_fusion.6
  16.7 0.7 constant_dynamic-slice_fusion.4
  17.4 1.1 multiply_reduce_fusion.5
  18.5 0.9 multiply_reduce_fusion.6
  20.8 0.7 constant_dynamic-slice_fusion.4
  21.5 1.1 multiply_reduce_fusion.5
  22.6 0.9 multiply_reduce_fusion.6
  24.9 0.7 constant_dynamic-slice_fusion.4
  25.6 1.1 multiply_reduce_fusion.5
  26.7 0.9 multiply_reduce_fusion.6
  29.0 0.7 constant_dynamic-slice_fusion.4
  29.7 1.1 multiply_reduce_fusion.5
  30.8 0.9 multiply_reduce_fusion.6
  33.0 0.7 constant_dynamic-slice_fusion.4
  33.8 1.1 multiply_reduce_fusion.5
  34.9 0.9 multiply_reduce_fusion.6
  37.1 0.7 constant_dynamic-slice_fusion.4
  37.8 1.1 multiply_reduce_fusion.5
  39.0 0.9 multiply_reduce_fusion.6
  41.2 0.7 constant_dynamic-slice_fusion.4
  41.9 1.1 multiply_reduce_fusion.5
  43.1 0.9 multiply_reduce_fusion.6
  45.3 0.7 constant_dynamic-slice_fusion.4
  46.0 1.1 multiply_reduce_fusion.5
  47.2 0.9 multiply_reduce_fusion.6
  48.2 62.9 %psum.49 = f32[5120]{0:T(1024)S(1)} all-reduce(f32[5120]{0:T(1024)S(1)} %reshape.36), channel_id=1, replica_groups=mesh['groups'=2,'sec'=4,'col'=2,'rep'=2] {'sec','col','rep'}, use_global_device_ids=true, to_apply=%region_4.5 | all-reduce | flops 5120 | bytes 40960 | tf_op jit(solution)/shard_map/psum | solution.py:48
  111.1 4.0 copy.10
  115.2 2.3 fusion.4
  117.6 10.1 %all-reduce = (f32[1280]{0:T(1024)S(1)}, f32[1280]{0:T(1024)S(1)}) all-reduce(f32[1280]{0:T(1024)S(1)} %get-tuple-element.155, f32[1280]{0:T(1024)S(1)} %get-tuple-element.154), channel_id=1, replica_groups=mesh['groups'=2,'sec'=4,'col'=2,'rep'=2] {'col','rep'}, use_global_device_ids=true, to_apply=%region_10.11 | all-reduce | flops 2560 | bytes 20480 | tf_op jit(solution)/shard_map/psum | solution.py:56
  127.7 0.6 reduce_sum.101
  128.3 9.0 %psum.53 = f32[]{:T(128)} all-reduce(f32[]{:T(128)} %reduce_sum.101), channel_id=1, replica_groups=mesh['groups'=2,'sec'=4,'col'=2,'rep'=2] {'sec'}, use_global_device_ids=true, to_apply=%region_12.13 | all-reduce | flops 1 | bytes 8 | tf_op jit(solution)/shard_map/psum | solution.py:57
  137.9 0.6 multiply_reduce_fusion.2
  138.6 0.6 reduce_sum.99
  140.5 10.9 %psum.56 = f32[]{:T(128)} all-reduce(f32[]{:T(128)S(6)} %add.104), channel_id=1, replica_groups=mesh['groups'=2,'sec'=4,'col'=2,'rep'=2] {'sec'}, use_global_device_ids=true, to_apply=%region_8.9 | all-reduce | flops 1 | bytes 8 | tf_op jit(solution)/shard_map/psum | solution.py:57
  152.1 3.6 fusion.9
  155.7 0.7 all-gather.7.cloned.1.call-update
  156.7 81.5 %all-gather.5.cloned.1.call-done = bf16[1280,5120]{0,1:T(8,128)(2,1)} async-done(((bf16[1280,1280]{0,1:T(8,128)(2,1)}), bf16[1280,5120]{0,1:T(8,128)(2,1)}) %all-gather.5.cloned.1.call-update) | async-done | bytes 13107216 | tf_op jit(solution)/shard_map/all_gather | solution.py:64
  238.2 229.0 %all-gather.7.cloned.1.call-done = bf16[5120,1280]{0,1:T(8,128)(2,1)} async-done(((bf16[1280,1280]{0,1:T(8,128)(2,1)}), bf16[5120,1280]{0,1:T(8,128)(2,1)}) %all-gather.7.cloned.1.call-update) | async-done | bytes 13107216 | tf_op jit(solution)/shard_map/all_gather | solution.py:65
  467.2 24.8 %fusion.11 = (bf16[1280,1280]{0,1:T(8,128)(2,1)}, f32[1280,1280]{0,1:T(8,128)}) fusion(bf16[5120,1280]{0,1:T(8,128)(2,1)} %all-gather.7.cloned.1.call-done, bf16[1280,5120]{0,1:T(8,128)(2,1)} %all-gather.5.cloned.1.call-done), kind=kOutput, calls=%fused_computation.30 | convolution fusion | flops 16778854400 | bytes 36044800 | tf_op jit(solution)/shard_map/dot_general | solution.py:39
  492.0 83.4 %all-gather.9.cloned.1.call-done = bf16[1280,5120]{0,1:T(8,128)(2,1)} async-done(((bf16[1280,1280]{0,1:T(8,128)(2,1)}), bf16[1280,5120]{0,1:T(8,128)(2,1)}) %all-gather.9.cloned.1.call-update) | async-done | bytes 13107216 | tf_op jit(solution)/shard_map/all_gather | solution.py:67
  575.4 25.3 %fusion.10 = (f32[1280]{0:T(1024)S(1)}, f32[1280,1280]{0,1:T(8,128)}) fusion(s32[1280]{0:T(1024)S(1)} %get-tuple-element.185, s32[1280]{0:T(1024)S(1)} %get-tuple-element.184, bf16[5120,1280]{0,1:T(8,128)(2,1)} %all-gather.7.cloned.1.call-done, bf16[1280,5120]{0,1:T(8,128)(2,1)} %all-gather.9.cloned.1.call-done, f32[1280,1280]{0,1:T(8,128)} %get-tuple-element.181), kind=kOutput, calls=%fused_computation.25 | convolution fusion | flops 16787045376 | bytes 39336960 | tf_op jit(solution)/shard_map/dot_general | solution.py:39
  600.7 8.1 %copy.11 = f32[1280,1280]{1,0:T(8,128)} copy(f32[1280,1280]{0,1:T(8,128)} %get-tuple-element.183) | data formatting | bytes 13107200
  608.8 6.0 psum.55
  614.8 13.3 %all-gather = f32[4,1,1280]{2,1,0:T(1,128)S(1)} all-gather(f32[1,1,1280]{2,1,0:T(1,128)S(1)} %reshape.37), channel_id=1, replica_groups=mesh['groups'=2,'sec'=4,'col'=2,'rep'=2] {'sec'}, dimensions={0}, use_global_device_ids=true | all-gather | bytes 25600 | tf_op jit(solution)/shard_map/all_gather | solution.py:72
  628.2 19.1 %while.25 = (s32[]{:T(128)}, f32[3,512]{1,0:T(4,128)S(1)}, f32[3,512]{1,0:T(4,128)S(1)}, f32[3,5120]{1,0:T(4,128)}, f32[5120]{0:T(1024)S(1)}, /*index=5*/s32[]{:T(128)}, s32[]{:T(128)}, s32[]{:T(128)}, s32[]{:T(128)}) while((s32[]{:T(128)}, f32[3,512]{1,0:T(4,128)S(1)}, f32[3,512]{1,0:T(4,128)S(1)}, f32[3,5120]{1,0:T(4,128)}, ...), condition=%wide.region_20.21_spmd.clone, body=%wide.region_17.20_spmd.clone.sunk | while | flops 5244423 | bytes 4262045 | solution.py:32
  628.2 0.7 constant_dynamic-slice_fusion.5
  630.1 0.7 constant_dynamic-slice_fusion.5
  632.0 0.7 constant_dynamic-slice_fusion.5
  633.9 0.7 constant_dynamic-slice_fusion.5
  635.8 0.7 constant_dynamic-slice_fusion.5
  637.7 0.7 constant_dynamic-slice_fusion.5
  639.6 0.7 constant_dynamic-slice_fusion.5
  641.6 0.7 constant_dynamic-slice_fusion.5
  643.5 0.7 constant_dynamic-slice_fusion.5
  645.4 0.7 constant_dynamic-slice_fusion.5
  647.3 0.6 broadcast_multiply_fusion
  (85 shorter events, 17.3 us)
Async XLA Ops:
  7.2 231.0 %all-gather.5.cloned.1.call-start = ((), (), s32[]{:S(2)}) async-start(), calls=%async_computation | async-start | bytes 16384000 | tf_op jit(solution)/shard_map/all_gather | solution.py:64
  155.7 311.5 %all-gather.7.cloned.1.call-start = ((), (), s32[]{:S(2)}) async-start(), calls=%async_computation.1 | async-start | bytes 16384000 | tf_op jit(solution)/shard_map/all_gather | solution.py:65
  156.4 335.5 %copy-start.1 = (f32[512]{0:T(512)S(1)}, f32[512]{0:T(512)}, u32[]{:S(2)}) copy-start(f32[512]{0:T(512)} %get-tuple-element.322) | copy-start | bytes 6148
  156.4 418.9 %all-gather.9.cloned.1.call-start = ((), (), s32[]{:S(2)}) async-start(), calls=%async_computation.2 | async-start | bytes 16384000 | tf_op jit(solution)/shard_map/all_gather | solution.py:67
  600.7 27.5 %copy-start = (f32[3,512]{1,0:T(4,128)S(1)}, f32[3,512]{1,0:T(4,128)}, u32[]{:S(2)}) copy-start(f32[3,512]{1,0:T(4,128)} %get-tuple-element.320) | copy-start | bytes 18436
Sparse Core Ops, SparseCore 0:
  155.8 82.3 all-gather.4
  240.3 226.7 all-gather.6
  492.1 83.2 all-gather.8
where the time goes:
time: 657 us; the launch traced here: 654 us
  waiting for transfers between devices  395 us (60%)
  blocking collectives  112 us (17%)
  matrix products  50.1 us (8%)
  other arithmetic  39.7 us (6%)
  local copies, waits for them, and re-layouts  33.6 us (5%)
  between operations  16.5 us (3%)
  loops' own time  7.32 us (1%)
    all_gather x1, waiting for transfers between devices, shards(): lax.all_gather(start_x, 'sec', axis=0, tiled=True)  229 us
    all_gather x1, waiting for transfers between devices, shards(): square_panel = lax.all_gather(square_b, ('col', 'rep'), axis=1, tiled=True)  83.4 us
    all_gather x1, waiting for transfers between devices, shards(): row_panel = lax.all_gather(start_x, ('col', 'rep'), axis=1, tiled=True)  81.5 us
    psum x1, blocking collectives, shards(): whole_pot = lax.psum(partial_value, ('sec', 'col', 'rep'))  62.9 us
    dot_general x2, matrix products, fold_with(): return jnp.dot(left, piece, preferred_element_type=jnp.float32)  50.1 us
    psum x2, blocking collectives, shards(): lax.psum((jnp.sum(diag_vals), jnp.sum(off_rows)), 'sec')  19.9 us
    all_gather x1, blocking collectives, shards(): occupation = lax.all_gather(occ_rows, 'sec', axis=0, tiled=True)  13.3 us
  transfers between devices with their start and end apart: 3, of which 3 were waited for; matrix products, arithmetic and copies ran while one was open for 0% of the time, Pallas kernels for 0%

commit v1 on v0

v1 whole, which is shorter than its diff:
```python
import functools

import jax
import jax.numpy as jnp
from jax import lax
from jax.experimental import pallas as pl
from jax.experimental.pallas import tpu as pltpu
from jax.sharding import PartitionSpec as P

PART = ("sec", "col", "rep")


def potential_kernel(spots_ref, points_ref, out_ref):
    count = points_ref.shape[0]
    width = spots_ref.shape[1]
    sx, sy, sz = (spots_ref[k : k + 1, :] for k in range(3))

    def step(index, accum):
        rows = points_ref[pl.ds(pl.multiple_of(index * 8, 8), 8), :]
        dx = sx - rows[:, 0:1]
        dy = sy - rows[:, 1:2]
        dz = sz - rows[:, 2:3]
        dist = dx * dx + dy * dy + dz * dz + 1.0
        return accum + rows[:, 3:4] * lax.rsqrt(dist)

    total = lax.fori_loop(0, count // 8, step, jnp.zeros((8, width), jnp.float32), unroll=4)
    out_ref[...] = jnp.sum(total, 0, keepdims=True)


def potential_terms(centers, mm_coords, mm_charges):
    total = centers.shape[1]
    count = mm_coords.shape[1]
    width = 1024 if total % 1024 == 0 else total
    points = jnp.concatenate([mm_coords, mm_charges[None]], 0).T
    return pl.pallas_call(
        potential_kernel,
        grid=(total // width,),
        out_shape=jax.ShapeDtypeStruct((1, total), jnp.float32),
        in_specs=[
            pl.BlockSpec((3, width), lambda i: (0, i)),
            pl.BlockSpec((count, 4), lambda i: (0, 0)),
        ],
        out_specs=pl.BlockSpec((1, width), lambda i: (0, i)),
        name="potential",
    )(centers, points)


def force_kernel(spots_ref, occ_ref, points_ref, out_ref):
    total = spots_ref.shape[1]
    rows = points_ref[...]
    px, py, pz, charge = (rows[:, k : k + 1] for k in range(4))
    count = rows.shape[0]

    def step(index, accum):
        lanes = pl.ds(pl.multiple_of(index * 128, 128), 128)
        dx = px - spots_ref[0:1, lanes]
        dy = py - spots_ref[1:2, lanes]
        dz = pz - spots_ref[2:3, lanes]
        inv = lax.rsqrt(dx * dx + dy * dy + dz * dz + 1.0)
        weight = occ_ref[:, lanes] * inv * (inv * inv)
        return (accum[0] + dx * weight, accum[1] + dy * weight, accum[2] + dz * weight)

    zero = jnp.zeros((count, 128), jnp.float32)
    sums = lax.fori_loop(0, total // 128, step, (zero, zero, zero), unroll=4)
    for k in range(3):
        out_ref[:, k : k + 1] = -charge * jnp.sum(sums[k], 1, keepdims=True)


def force_terms(centers, occupation, mm_coords, mm_charges):
    total = centers.shape[1]
    count = mm_coords.shape[1]
    width = 32
    points = jnp.concatenate([mm_coords, mm_charges[None]], 0).T
    summed = pl.pallas_call(
        force_kernel,
        grid=(count // width,),
        out_shape=jax.ShapeDtypeStruct((count, 4), jnp.float32),
        in_specs=[
            pl.BlockSpec((3, total), lambda i: (0, 0)),
            pl.BlockSpec((1, total), lambda i: (0, 0)),
            pl.BlockSpec((width, 4), lambda i: (i, 0)),
        ],
        out_specs=pl.BlockSpec((width, 4), lambda i: (i, 0)),
        name="forces",
    )(centers, occupation, points)
    return summed[:, :3].T


def butterfly_sum(value, sizes):
    for axis in ("rep", "col", "sec"):
        size = sizes[axis]
        if size & (size - 1):
            value = lax.psum(value, axis)
            continue
        hop = 1
        while hop < size:
            value = value + lax.ppermute(value, axis, [(i, i ^ hop) for i in range(size)])
            hop *= 2
    return value


def fold_with(left, piece):
    return jnp.dot(left, piece, preferred_element_type=jnp.float32)


def shards(sizes, h_core, centers, mm_coords, mm_charges):
    row_count, col_count = h_core.shape
    total = centers.shape[1]
    row_start = lax.axis_index("sec") * row_count
    col_start = lax.axis_index(("col", "rep")) * col_count
    rows_glob = row_start + lax.broadcasted_iota(jnp.int32, (row_count, col_count), 0)
    cols_glob = col_start + lax.broadcasted_iota(jnp.int32, (row_count, col_count), 1)
    on_diag = rows_glob == cols_glob
    off = jnp.where(on_diag, jnp.zeros((), h_core.dtype), h_core)
    row_panel = lax.all_gather(off, ("col", "rep"), axis=1, tiled=True)
    col_panel = lax.all_gather(off, "sec", axis=0, tiled=True)

    wide = h_core.astype(jnp.float32)
    own_diag = jnp.sum(jnp.where(on_diag, wide, 0.0), 0)
    own_off = jnp.sum(jnp.where(on_diag, 0.0, wide * wide))
    terms = potential_terms(centers, mm_coords, mm_charges)[0]
    own_cols = lax.dynamic_slice_in_dim(terms, col_start, col_count, 0) + own_diag
    terms = lax.dynamic_update_slice_in_dim(terms, own_cols, col_start, 0)
    sums = butterfly_sum(jnp.concatenate([terms, jnp.full((128,), own_off)]), sizes)
    diag_vals, off_total = sums[:total], sums[total]
    mean_level = jnp.sum(diag_vals) / total
    level = diag_vals - mean_level
    spread = jnp.sqrt((off_total + jnp.sum(level * level)) / total + 1e-05)
    gain = 1.0 / (3.0 * spread)

    level_rows = lax.dynamic_slice_in_dim(level, row_start, row_count, 0)[:, None]
    level_cols = lax.dynamic_slice_in_dim(level, col_start, col_count, 0)[None, :]
    off_wide = off.astype(jnp.float32)
    square = fold_with(row_panel, col_panel)
    square = square + off_wide * (level_rows + level_cols) + jnp.where(on_diag, level_rows * level_rows, 0.0)
    shifted = off_wide + jnp.where(on_diag, level_rows, 0.0)
    square_b = square.astype(jnp.bfloat16)
    square_panel = lax.all_gather(square_b, ("col", "rep"), axis=1, tiled=True)
    own_cube = jnp.sum(square * shifted, 0)
    cube_diag = lax.dynamic_update_slice_in_dim(jnp.zeros((total,), jnp.float32), own_cube, col_start, 0)
    cube_diag = butterfly_sum(cube_diag, sizes)
    occupation = 0.5 - 1.5 * gain * level + 2.0 * gain**3 * cube_diag
    forces = force_terms(centers, occupation[None], mm_coords, mm_charges)

    cube = fold_with(square_panel, col_panel) + square_b.astype(jnp.float32) * level_cols
    density = jnp.where(on_diag, 0.5, 0.0) - 1.5 * gain * shifted + 2.0 * gain**3 * cube
    return (density, forces)


def solution(mesh):
    in_specs = (
        P(("groups", "sec"), ("col", "rep")),
        P(None, "groups"),
        P(None, ("groups", "sec", "col", "rep")),
        P(("groups", "sec", "col", "rep")),
    )
    out_specs = (P(("groups", "sec"), ("col", "rep")), P(None, ("groups", "sec", "col", "rep")))
    body = functools.partial(shards, dict(mesh.shape))
    return jax.shard_map(body, mesh=mesh, in_specs=in_specs, out_specs=out_specs, check_vma=False)
```

time: 657 us -> 471 us (0.72)
  blocking collectives: 112 us -> 0 us
  waiting for transfers between devices: 395 us -> 335 us
  Pallas kernels: 0 us -> 39.7 us
  local copies, waits for them, and re-layouts: 33.6 us -> 5.52 us
  other arithmetic: 39.7 us -> 13.3 us
  starting transfers between devices: 0.3 us -> 10.1 us
  loops' own time: 7.32 us -> 0 us
    psum x5 -> x0, blocking collectives: 98.9 us -> none  [the longest x1 62.9 us: shards(): whole_pot = lax.psum(partial_value, ('sec', 'col', 'rep'))]
    all_gather x2, waiting for transfers between devices: 310 us -> 267 us  [the longest x1 182 us: shards(): col_panel = lax.all_gather(off, 'sec', axis=0, tiled=True)]
    all_gather x1, waiting for transfers between devices: 83.4 us -> 40.6 us  [shards(): square_panel = lax.all_gather(square_b, ('col', 'rep'), axis=1, tiled=True)]
    pallas_call x0 -> x2, Pallas kernels: none -> 39.7 us  [the longest x1 28.3 us: force_terms(): pl.pallas_call(force_kernel, grid=(count // width,), out_shape=jax.ShapeD...]
    reduce_sum x44 -> x3, other arithmetic: 32.4 us -> 5.07 us  [the longest x1 3.86 us: shards(): own_off = jnp.sum(jnp.where(on_diag, 0.0, wide * wide))]
    ppermute x0 -> x8, waiting for transfers between devices: none -> 26.5 us  [butterfly_sum(): lax.ppermute(value, axis, [(i, i ^ hop) for i in range(size)])]
    dynamic_slice x41 -> x1, local copies, waits for them, and re-layouts: 20.8 us -> 0.71 us  [shards(): lax.dynamic_slice_in_dim(terms, col_start, col_count, 0) + own_diag]
    all_gather x1 -> x0, blocking collectives: 13.3 us -> none  [shards(): occupation = lax.all_gather(occ_rows, 'sec', axis=0, tiled=True)]
  transfers between devices with their start and end apart: 3 -> 11, of which waited for: 3 -> 11; matrix products, arithmetic and copies ran while one was open for 0% -> 3% of each run, Pallas kernels for 0% -> 8%
where the time goes in v1:
time: 471 us
  waiting for transfers between devices  335 us (71%)
  matrix products  50.7 us (11%)
  Pallas kernels  39.7 us (8%)
  between operations  15.9 us (3%)
  other arithmetic  13.3 us (3%)
  starting transfers between devices  10.1 us (2%)
  local copies, waits for them, and re-layouts  5.52 us (1%)
    all_gather x1, waiting for transfers between devices, shards(): col_panel = lax.all_gather(off, 'sec', axis=0, tiled=True)  182 us
    all_gather x1, waiting for transfers between devices, shards(): row_panel = lax.all_gather(off, ('col', 'rep'), axis=1, tiled=True)  85.4 us
    dot_general x2, matrix products, fold_with(): return jnp.dot(left, piece, preferred_element_type=jnp.float32)  50.7 us
    all_gather x1, waiting for transfers between devices, shards(): square_panel = lax.all_gather(square_b, ('col', 'rep'), axis=1, tiled=True)  40.6 us
    pallas_call x1, Pallas kernels, force_terms(): pl.pallas_call(force_kernel, grid=(count // width,), out_shape=jax.ShapeD...  28.3 us
    ppermute x8, waiting for transfers between devices, butterfly_sum(): lax.ppermute(value, axis, [(i, i ^ hop) for i in range(size)])  26.5 us
    pallas_call x1, Pallas kernels, potential_terms(): pl.pallas_call(potential_kernel, grid=(total // width,), out_shape=jax.Sh...  11.5 us
    ppermute x8, starting transfers between devices, butterfly_sum(): lax.ppermute(value, axis, [(i, i ^ hop) for i in range(size)])  9.98 us
  transfers between devices with their start and end apart: 11, of which 11 were waited for; matrix products, arithmetic and copies ran while one was open for 3% of the time, Pallas kernels for 8%

profile of v1, /device:TPU:0, one launch (start us, length us, event | category | flops | bytes accessed | tf_op | source)
XLA Modules:
  0.0 470.6 jit_solution(11126058425190730306)
XLA Ops:
  7.2 0.0 all-gather.6.cloned.1.call-start
  7.2 0.0 copy-start.1
  7.2 0.0 copy-start.4
  7.3 0.0 copy-start
  7.3 4.6 compare_select_fusion.2
  11.9 0.0 all-gather.6.cloned.1.call-update
  11.9 0.0 all-gather.4.cloned.1.call-start
  11.9 0.7 all-gather.4.cloned.1.call-update
  12.6 0.0 all-gather.8.cloned.1.call-start
  12.7 0.0 copy-done.1
  12.7 0.0 copy-done.4
  12.7 0.9 copy.11
  13.6 11.5 %potential.1 = f32[1,5120]{1,0:T(1,128)} custom-call(f32[3,5120]{1,0:T(4,128)} %spots_ref.3, f32[512,4]{1,0:T(8,128)} %bitcast.11), custom_call_target="tpu_custom_call" | custom-call | tf_op jit(solution)/shard_map/potential/pallas_call | solution.py:35
  25.1 0.7 dynamic-slice_reduce_fusion
  25.8 0.0 copy-done
  25.8 3.9 fusion.5
  29.7 1.4 add_dynamic-update-slice_fusion.1
  31.1 1.4 concatenate.8
  32.4 0.5 collective-permute-start
  32.9 0.8 collective-permute-done
  33.7 1.4 pad_add_fusion
  35.1 2.8 collective-permute-start.1
  38.0 1.8 collective-permute-done.1
  39.8 2.1 collective-permute-start.2
  41.9 7.5 %collective-permute-done.2 = f32[5248]{0:T(1024)S(1)} collective-permute-done((f32[5248]{0:T(1024)S(1)}, f32[5248]{0:T(1024)S(1)}, u32[]{:S(2)}, u32[]{:S(2)}) %collective-permute-start.2) | collective-permute-done | bytes 21024 | tf_op jit(solution)/shard_map/ppermute | solution.py:97
  49.3 0.0 collective-permute-start.3
  49.4 9.3 %collective-permute-done.3 = f32[5248]{0:T(1024)S(1)} collective-permute-done((f32[5248]{0:T(1024)S(1)}, f32[5248]{0:T(1024)S(1)}, u32[]{:S(2)}, u32[]{:S(2)}) %collective-permute-start.3) | collective-permute-done | bytes 21024 | tf_op jit(solution)/shard_map/ppermute | solution.py:97
  58.7 0.6 slice_reduce_fusion
  60.0 0.6 multiply_reduce_fusion
  60.6 0.1 fusion.9
  60.6 0.0 copy-start.2
  60.6 0.0 copy-start.3
  60.6 181.9 %all-gather.6.cloned.1.call-done = bf16[5120,1280]{1,0:T(8,128)(2,1)} async-done(((bf16[1280,1280]{1,0:T(8,128)(2,1)}), bf16[5120,1280]{1,0:T(8,128)(2,1)}) %all-gather.6.cloned.1.call-update) | async-done | bytes 13107216 | tf_op jit(solution)/shard_map/all_gather | solution.py:116
  242.6 85.4 %all-gather.4.cloned.1.call-done = bf16[1280,5120]{1,0:T(8,128)(2,1)} async-done(((bf16[1280,1280]{1,0:T(8,128)(2,1)}), bf16[1280,5120]{1,0:T(8,128)(2,1)}) %all-gather.4.cloned.1.call-update) | async-done | bytes 13107216 | tf_op jit(solution)/shard_map/all_gather | solution.py:115
  328.0 25.1 %fusion.8 = (f32[1280]{0:T(1024)S(1)}, bf16[1280,1280]{1,0:T(8,128)(2,1)}) fusion(f32[1280]{0:T(1024)S(1)} %get-tuple-element.13, s32[1280]{0:T(1024)S(1)} %get-tuple-element.18, s32[1280]{0:T(1024)S(1)} %get-tuple-element.19, bf16[1280,1280]{1,0:T(8,128)(2,1)S(1)} %copy-done, f32[1280]{0:T(1024)S(1)} %get-tuple-element.12, ...), kind=kOutput, calls=%fused_computation.19 | convolution fusion | flops 16798514176 | bytes 32798720 | tf_op jit(solution)/shard_map/dot_general | solution.py:103
  353.1 0.0 copy-done.2
  353.1 0.0 copy-done.3
  353.1 0.0 all-gather.8.cloned.1.call-update
  353.1 0.3 dynamic_update_slice.9
  353.5 0.3 collective-permute-start.4
  353.8 0.9 collective-permute-done.4
  354.7 0.2 add_dynamic-update-slice_fusion
  354.9 0.4 collective-permute-start.5
  355.2 3.5 collective-permute-done.5
  358.7 1.5 collective-permute-start.6
  360.2 2.3 collective-permute-done.6
  362.5 2.4 collective-permute-start.7
  364.9 0.5 slice.12
  366.8 0.3 collective-permute-done.7
  367.2 0.6 multiply_add_fusion
  367.8 28.3 %forces.1 = f32[512,4]{1,0:T(8,128)} custom-call(f32[3,5120]{1,0:T(4,128)} %spots_ref.3, f32[1,5120]{1,0:T(1,128)} %bitcast.14, f32[512,4]{1,0:T(8,128)} %bitcast.12), custom_call_target="tpu_custom_call" | custom-call | tf_op jit(solution)/shard_map/forces/pallas_call | solution.py:74
  396.0 1.0 slice_bitcast_fusion
  397.0 0.7 copy.12
  397.7 40.6 %all-gather.8.cloned.1.call-done = bf16[1280,5120]{1,0:T(8,128)(2,1)} async-done(((bf16[1280,1280]{1,0:T(8,128)(2,1)}), bf16[1280,5120]{1,0:T(8,128)(2,1)}) %all-gather.8.cloned.1.call-update) | async-done | bytes 13107216 | tf_op jit(solution)/shard_map/all_gather | solution.py:138
  438.4 25.7 %fusion.1 = f32[1280,1280]{1,0:T(8,128)} fusion(bf16[1280,5120]{1,0:T(8,128)(2,1)} %all-gather.8.cloned.1.call-done, bf16[5120,1280]{1,0:T(8,128)(2,1)} %all-gather.6.cloned.1.call-done, bf16[1280,1280]{1,0:T(8,128)(2,1)} %get-tuple-element.15, f32[1280]{0:T(1024)} %copy-done.3, f32[]{:T(128)S(6)} %mul.71, f32[1280]{0:T(1024)} %copy-done.2, f32[]{:T(128)S(6)} %mul.68, ...), kind=kOutput, calls=%fused_computation.8 | convolution fusion | flops 16798515200 | bytes 39342088 | tf_op jit(solution)/shard_map/dot_general | solution.py:103
  (8 shorter events, 0.0 us)
Async XLA Ops:
  7.2 235.4 %all-gather.6.cloned.1.call-start = ((), (), s32[]{:S(2)}) async-start(), calls=%async_computation.1 | async-start | bytes 16384000 | tf_op jit(solution)/shard_map/all_gather | solution.py:116
  7.2 5.5 %copy-start.1 = (f32[3,512]{1,0:T(4,128)S(1)}, f32[3,512]{1,0:T(4,128)}, u32[]{:S(2)}) copy-start(f32[3,512]{1,0:T(4,128)} %param.6) | copy-start | bytes 18436
  7.2 5.5 %copy-start.4 = (f32[512]{0:T(512)S(1)}, f32[512]{0:T(512)}, u32[]{:S(2)}) copy-start(f32[512]{0:T(512)} %param.7) | copy-start | bytes 6148
  7.3 18.5 %copy-start = (bf16[1280,1280]{1,0:T(8,128)(2,1)S(1)}, bf16[1280,1280]{1,0:T(8,128)(2,1)}, u32[]{:S(2)}) copy-start(bf16[1280,1280]{1,0:T(8,128)(2,1)} %param.4) | copy-start | bytes 9830404
  11.9 316.1 %all-gather.4.cloned.1.call-start = ((), (), s32[]{:S(2)}) async-start(), calls=%async_computation | async-start | bytes 16384000 | tf_op jit(solution)/shard_map/all_gather | solution.py:115
  12.6 425.7 %all-gather.8.cloned.1.call-start = ((), (), s32[]{:S(2)}) async-start(), calls=%async_computation.2 | async-start | bytes 16384000 | tf_op jit(solution)/shard_map/all_gather | solution.py:138
  32.4 1.3 collective-permute-start
  35.1 4.6 collective-permute-start.1
  39.8 9.6 %collective-permute-start.2 = (f32[5248]{0:T(1024)S(1)}, f32[5248]{0:T(1024)S(1)}, u32[]{:S(2)}, u32[]{:S(2)}) collective-permute-start(f32[5248]{0:T(1024)S(1)} %add.99), channel_id=1, source_target_pairs={{0,4},{4,0},{8,12},{12,8},{1,5},{5,1},{9,13},{13,9},{2,6},{6,2},{1... | collective-permute-start | bytes 62984 | tf_op jit(solution)/shard_map/ppermute | solution.py:97
  49.3 9.3 %collective-permute-start.3 = (f32[5248]{0:T(1024)S(1)}, f32[5248]{0:T(1024)S(1)}, u32[]{:S(2)}, u32[]{:S(2)}) collective-permute-start(f32[5248]{0:T(1024)S(1)} %add.100), channel_id=1, source_target_pairs={{0,8},{4,12},{8,0},{12,4},{1,9},{5,13},{9,1},{13,5},{2,10},{6,14},... | collective-permute-start | bytes 62984 | tf_op jit(solution)/shard_map/ppermute | solution.py:97
  60.6 292.4 %copy-start.2 = (f32[1280]{0:T(1024)}, f32[1280]{0:T(1024)S(1)}, u32[]{:S(2)}) copy-start(f32[1280]{0:T(1024)S(1)} %get-tuple-element.13) | copy-start | bytes 15364
  60.6 292.4 %copy-start.3 = (f32[1280]{0:T(1024)}, f32[1280]{0:T(1024)S(1)}, u32[]{:S(2)}) copy-start(f32[1280]{0:T(1024)S(1)} %get-tuple-element.16) | copy-start | bytes 15364
  353.5 1.2 collective-permute-start.4
  354.9 3.8 collective-permute-start.5
  358.7 3.8 collective-permute-start.6
  362.5 4.7 collective-permute-start.7
Sparse Core Ops, SparseCore 0:
  12.0 230.5 all-gather.5
  244.7 83.2 all-gather.3
  353.2 85.0 all-gather.7

commit v2 on v1

--- a/solution.py
+++ b/solution.py
@@ -86,8 +86,8 @@
     return summed[:, :3].T
 
 
-def butterfly_sum(value, sizes):
-    for axis in ("rep", "col", "sec"):
+def butterfly_sum(value, sizes, axes=("rep", "col", "sec")):
+    for axis in axes:
         size = sizes[axis]
         if size & (size - 1):
             value = lax.psum(value, axis)
@@ -103,7 +103,7 @@
     return jnp.dot(left, piece, preferred_element_type=jnp.float32)
 
 
-def shards(sizes, h_core, centers, mm_coords, mm_charges):
+def gather_shards(sizes, h_core, centers, mm_coords, mm_charges):
     row_count, col_count = h_core.shape
     total = centers.shape[1]
     row_start = lax.axis_index("sec") * row_count
@@ -147,6 +147,767 @@
     return (density, forces)
 
 
+ROUND = ((0, 1), (1, 2), (2, 3), (3, 0))
+BACK = ((0, 3), (3, 2), (2, 1), (1, 0))
+Z_MOVES = ((ROUND, BACK), (BACK, ROUND), (ROUND, BACK), (ROUND, BACK))
+OWN0, OWN1, X1, Z1, X2, Z2, X3, Z3, X4, Z4 = range(10)
+X_SENDS = ((OWN1, OWN0, OWN1, OWN0), (OWN0, OWN1, OWN0, OWN1), (Z2,) * 4, (Z3, Z1, Z1, Z3))
+Z_SENDS = ((OWN0, OWN1, OWN0, OWN1), (OWN1, X1, X1, OWN0), (X2,) * 4, (Z3, Z1, Z1, Z3))
+SLOT_STAGE = (0, 0, 0, 0, 1, 1, 2, 2, 3, 3)
+LEFT_SLOTS = (OWN0, OWN1, X1, X2)
+LEFT_STAGE = (0, 0, 0, 1)
+FIELDS = 8
+NOTHING, MULTIPLY, FINISH, LEVEL = range(4)
+BLOCK_BIT, LEFT_BIT, TOTAL_BIT = 0, 8, 16
+
+
+def block_places():
+    chips = [(z, x) for z in range(4) for x in range(2)]
+    held = {(z, x): [(z, 2 * x), (z, 2 * x + 1)] for z, x in chips}
+    for step in range(4):
+        arrived = {}
+        for z, x in chips:
+            before = next(start for start, to in Z_MOVES[step][x] if to == z)
+            arrived[(z, x)] = [held[(z, 1 - x)][X_SENDS[step][z]], held[(before, x)][Z_SENDS[step][before]]]
+        for chip in chips:
+            held[chip] = held[chip] + arrived[chip]
+    return [held[chip] for chip in chips]
+
+
+def rows_of(products, length):
+    seen, rows = set(), []
+    for kind, left, block, flip, total, column in products:
+        bits = [LEFT_BIT + left, TOTAL_BIT + total]
+        if kind == MULTIPLY:
+            bits.append(BLOCK_BIT + block)
+        waits = sum(1 << bit for bit in bits if bit not in seen)
+        seen.update(bits)
+        rows.append([kind, left, block, flip, total, waits, column, 0])
+    rows += [[NOTHING] + [0] * (FIELDS - 1)] * (length - len(rows))
+    rest = sum(1 << bit for bit in range(24) if bit not in seen)
+    return rows + [[NOTHING, 0, 0, 0, 0, rest, 0, 0]]
+
+
+def device_lists():
+    devices = []
+    for chip, slots in enumerate(block_places()):
+        assert len({tuple(sorted(place)) for place in slots}) == 10
+        row, col = divmod(chip, 2)
+        assert all(slots[s][0] == row for s in LEFT_SLOTS)
+        lefts = [slots[s][1] for s in LEFT_SLOTS]
+        stages = [[], [], [], []]
+        for slot, (first, second) in enumerate(slots):
+            for inner, outer, flip in [(first, second, 0), (second, first, 1)][: 1 if first == second else 2]:
+                left = lefts.index(inner)
+                stage = max(LEFT_STAGE[left], SLOT_STAGE[slot])
+                base = (0, 0, X3, X4)[stage]
+                key = max(slot, LEFT_SLOTS[left])
+                stages[stage].append((key, (MULTIPLY, left, slot - base, flip, outer, 0)))
+        stages = [[product for _, product in sorted(stage)] for stage in stages]
+        open_columns = sorted({product[4] for product in stages[3]})
+        done_columns = [column for column in range(4) if column not in open_columns]
+        assert len(open_columns) == 2
+
+        def find(inner, outer):
+            if (inner, outer) in slots:
+                return slots.index((inner, outer)), 0
+            return slots.index((outer, inner)), 1
+
+        for core in range(2):
+            early, early_slots = [], []
+            for k, column in enumerate(done_columns):
+                early.append((FINISH, 4 + k, lefts.index(column), int(column == row), column, column))
+            for k, column in enumerate(done_columns):
+                for which in range(2):
+                    slot, flip = find(column, 2 * col + which)
+                    early.append((MULTIPLY, 4 + k, 2 + len(early_slots), flip, 4 + which, 0))
+                    early_slots.append(slot)
+                    if column == 2 * col + which:
+                        early.append((LEVEL, 4 + k, 0, 0, 4 + which, column))
+            tails = []
+            for which in (1 - core, core):
+                tail, tail_slots = [], []
+                last = which == core
+                for k, column in enumerate(open_columns):
+                    slot, flip = find(column, 2 * col + which)
+                    position, left = (k, k) if last else (2 + k, 4 + k)
+                    tail.append((MULTIPLY, left, position, flip, 0 if last else 2, 0))
+                    tail_slots.append(slot)
+                    if column == 2 * col + which:
+                        tail.append((LEVEL, left, 0, 0, 0 if last else 2, column))
+                tails.append((tail, tail_slots))
+            late = [product[:4] + (open_columns.index(product[4]), 0) for product in stages[3]]
+            late += [
+                (FINISH, 4 + k, lefts.index(column), int(column == row), k, column)
+                for k, column in enumerate(open_columns)
+            ]
+            devices.append(
+                dict(
+                    kernels=[stages[0], stages[1], stages[2], early, late, tails[0][0], tails[1][0]],
+                    slots=[early_slots, tails[0][1], tails[1][1]],
+                    open=open_columns,
+                )
+            )
+    return devices
+
+
+def device_tables():
+    devices = device_lists()
+    steps, rows = [], [[] for _ in devices]
+    for kernel in range(7):
+        length = max(len(device["kernels"][kernel]) for device in devices)
+        steps.append((len(rows[0]), length))
+        for row, device in zip(rows, devices):
+            for fields in rows_of(device["kernels"][kernel], length):
+                row += fields
+    slots = []
+    for kernel in range(3):
+        slots.append(len(rows[0]))
+        for row, device in zip(rows, devices):
+            row += device["slots"][kernel]
+    opened = len(rows[0])
+    for row, device in zip(rows, devices):
+        row += device["open"]
+    return rows, steps, slots, opened
+
+
+def bit_set(mask, bit):
+    return lax.rem(lax.div(mask, jnp.int32(1 << bit)), jnp.int32(2)) == 1
+
+
+class Worker:
+    def __init__(self, table_ref, core, half, block_ref, block_sem, left_ref, left_sem, total_ref, total_sem):
+        self.table_ref, self.core, self.half = table_ref, core, half
+        self.block_ref, self.block_sem = block_ref, block_sem
+        self.left_ref, self.left_sem = left_ref, left_sem
+        self.total_ref, self.total_sem = total_ref, total_sem
+        self.near = pl.ds(pl.multiple_of(core * half, half), half)
+        self.far = pl.ds(pl.multiple_of((1 - core) * half, half), half)
+        self.blocks, self.lefts, self.totals = [], [], []
+        self.levels = None
+
+    def load_halves(self, position, near_ref, far_ref):
+        pltpu.make_async_copy(near_ref, self.block_ref.at[position, self.near], self.block_sem.at[position, 0]).start()
+        pltpu.make_async_copy(far_ref, self.block_ref.at[position, self.far], self.block_sem.at[position, 1]).start()
+
+    def load_block(self, position, slot, sources):
+        self.blocks.append(position)
+        whole_ref, got_ref, other_ref = sources["own"] if "own" in sources else (None, None, None)
+        fixed = isinstance(slot, int)
+        if whole_ref is not None and (not fixed or slot <= OWN1):
+            @pl.when(slot == self.core)
+            def _():
+                self.load_halves(position, whole_ref.at[self.near], whole_ref.at[self.far])
+
+            @pl.when(slot == 1 - self.core)
+            def _():
+                self.load_halves(position, got_ref, other_ref)
+
+        if not fixed:
+            for number, halves in sources.items():
+                if number != "own":
+                    pl.when(slot == number)(functools.partial(self.load_halves, position, *halves))
+        if fixed and slot > OWN1:
+            self.load_halves(position, *sources[slot])
+
+    def load_left(self, index, ref, to=None):
+        self.lefts.append(index)
+        to = index if to is None else to
+        pltpu.make_async_copy(ref, self.left_ref.at[to], self.left_sem.at[to]).start()
+
+    def load_rows(self, refs):
+        self.load_left(0, refs[0], self.core)
+        self.load_left(1, refs[1], 1 - self.core)
+        for k in range(2, len(refs)):
+            self.load_left(k, refs[k])
+
+    def load_total(self, index, ref):
+        self.totals.append(index)
+        pltpu.make_async_copy(ref, self.total_ref.at[index], self.total_sem.at[index]).start()
+
+    def wait(self, mask):
+        half_block = self.block_ref.at[0, pl.ds(0, self.half)]
+        for position in self.blocks:
+            @pl.when(bit_set(mask, BLOCK_BIT + position))
+            def _():
+                for part in range(2):
+                    pltpu.make_async_copy(half_block, half_block, self.block_sem.at[position, part]).wait()
+        for index in self.lefts:
+            @pl.when(bit_set(mask, LEFT_BIT + index))
+            def _():
+                pltpu.make_async_copy(self.left_ref.at[0], self.left_ref.at[0], self.left_sem.at[index]).wait()
+        for index in self.totals:
+            @pl.when(bit_set(mask, TOTAL_BIT + index))
+            def _():
+                pltpu.make_async_copy(self.total_ref.at[0], self.total_ref.at[0], self.total_sem.at[index]).wait()
+
+    def multiply(self, field):
+        total, left, block = self.total_ref.at[field[4]], self.left_ref.at[field[1]], self.block_ref.at[field[2]]
+
+        @pl.when(field[3] == 0)
+        def _():
+            total[...] += jnp.dot(left[...], block[...], preferred_element_type=jnp.float32)
+
+        @pl.when(field[3] == 1)
+        def _():
+            total[...] += lax.dot_general(
+                left[...], block[...], (((1,), (1,)), ((), ())), preferred_element_type=jnp.float32
+            )
+
+    def finish(self, field):
+        rows_ref, cols_ref, diag_ref = self.levels
+        half, width = self.half, self.block_ref.shape[2]
+        total, left, made = self.total_ref.at[field[4]], self.left_ref.at[field[2]], self.left_ref.at[field[1]]
+        cols = cols_ref[:, pl.ds(pl.multiple_of(field[6] * width, width), width)]
+        chunk = 16
+
+        def pass_rows(with_diag):
+            def one(index, carry):
+                rows = pl.ds(pl.multiple_of(index * chunk, chunk), chunk)
+                level = rows_ref[rows, :]
+                shifted = left[rows, :].astype(jnp.float32)
+                square = total[rows, :] + shifted * (level + cols)
+                if with_diag:
+                    in_block = lax.broadcasted_iota(jnp.int32, (chunk, width), 1)
+                    own = lax.broadcasted_iota(jnp.int32, (chunk, width), 0) + (self.core * half + index * chunk)
+                    on_diag = in_block == own
+                    square = square + jnp.where(on_diag, level * level, 0.0)
+                    shifted = shifted + jnp.where(on_diag, level, 0.0)
+                made[rows, :] = square.astype(jnp.bfloat16)
+                diag_ref[rows, :] += jnp.sum(square * shifted, 1, keepdims=True)
+                return carry
+
+            lax.fori_loop(0, half // chunk, one, 0, unroll=2)
+
+        @pl.when(field[3] == 0)
+        def _():
+            pass_rows(False)
+
+        @pl.when(field[3] == 1)
+        def _():
+            pass_rows(True)
+
+    def add_level(self, field):
+        _, cols_ref, _ = self.levels
+        width = self.block_ref.shape[2]
+        total, left = self.total_ref.at[field[4]], self.left_ref.at[field[1]]
+        cols = cols_ref[:, pl.ds(pl.multiple_of(field[6] * width, width), width)]
+        chunk = 16
+
+        def one(index, carry):
+            rows = pl.ds(pl.multiple_of(index * chunk, chunk), chunk)
+            total[rows, :] += left[rows, :].astype(jnp.float32) * cols
+            return carry
+
+        lax.fori_loop(0, self.half // chunk, one, 0, unroll=2)
+
+    def run(self, start_count):
+        start, count = start_count
+
+        def step(index, carry):
+            field = [self.table_ref[start + index * FIELDS + k] for k in range(7)]
+            self.wait(field[5])
+            pl.when(field[0] == MULTIPLY)(functools.partial(self.multiply, field))
+            if self.levels is not None:
+                if self.levels[0] is not None:
+                    pl.when(field[0] == FINISH)(functools.partial(self.finish, field))
+                pl.when(field[0] == LEVEL)(functools.partial(self.add_level, field))
+            return carry
+
+        lax.fori_loop(0, count, step, 0)
+
+    def wait_rest(self, start_count):
+        start, count = start_count
+        self.wait(self.table_ref[start + count * FIELDS + 5])
+
+
+def copy_all(pairs, sem):
+    copies = [pltpu.make_async_copy(source, to, sem.at[k]) for k, (source, to) in enumerate(pairs)]
+    for copy in copies:
+        copy.start()
+    return copies
+
+
+def square_kernel(first, steps, left_count, slots, own, table_ref, place_ref, *refs):
+    refs = list(refs)
+    row_refs = [refs.pop(0) for _ in range(left_count)]
+    sources = {"own": [refs.pop(0) for _ in range(3)]} if own else {}
+    for slot in slots:
+        if slot > OWN1:
+            sources[slot] = (refs.pop(0), refs.pop(0))
+    old_ref = None if first else refs.pop(0)
+    new_ref, block_ref, block_sem, left_ref, left_sem, total_ref, total_sem, new_sem = refs
+    half = left_ref.shape[1]
+    worker = Worker(table_ref, place_ref[0], half, block_ref, block_sem, left_ref, left_sem, total_ref, total_sem)
+    worker.load_rows(row_refs)
+    for position, slot in enumerate(slots):
+        worker.load_block(position, slot, sources)
+        if position == 0 and not first:
+            for k in range(4):
+                worker.load_total(k, old_ref.at[k])
+    if first:
+        total_ref[...] = jnp.zeros_like(total_ref)
+    worker.run(steps)
+    worker.wait_rest(steps)
+    for copy in copy_all([(total_ref.at[k], new_ref.at[k]) for k in range(4)], new_sem):
+        copy.wait()
+
+
+def early_kernel(steps, more, slots_at, open_at, table_ref, place_ref, *refs):
+    refs = list(refs)
+    row_refs = [refs.pop(0) for _ in range(4)]
+    sources = {"own": [refs.pop(0) for _ in range(3)]}
+    for slot in range(X1, Z3 + 1):
+        sources[slot] = (refs.pop(0), refs.pop(0))
+    old_ref, level_rows_ref, level_ref, open_ref, cube_ref, diag_ref = (refs.pop(0) for _ in range(6))
+    block_ref, block_sem, left_ref, left_sem, total_ref, total_sem, out_sem = refs
+    half = left_ref.shape[1]
+    worker = Worker(table_ref, place_ref[0], half, block_ref, block_sem, left_ref, left_sem, total_ref, total_sem)
+    worker.levels = (level_rows_ref, level_ref, diag_ref)
+    worker.load_rows(row_refs)
+    worker.load_block(0, X3, sources)
+    for k in range(4):
+        worker.load_total(k, old_ref.at[k])
+    worker.load_block(1, Z3, sources)
+    worker.run(steps)
+    worker.wait_rest(steps)
+    done = [
+        (total_ref.at[table_ref[open_at + k]], open_ref.at[k]) for k in range(2)
+    ]
+    copies = copy_all(done, out_sem)
+    worker.blocks, worker.lefts, worker.totals = [], [], []
+    for k in range(4):
+        worker.load_block(2 + k, table_ref[slots_at + k], sources)
+    diag_ref[...] = jnp.zeros_like(diag_ref)
+    total_ref[4:6] = jnp.zeros_like(total_ref[4:6])
+    worker.run(more)
+    worker.wait_rest(more)
+    copies += copy_all([(total_ref.at[4 + k], cube_ref.at[k]) for k in range(2)], out_sem.at[pl.ds(2, 2)])
+    for copy in copies:
+        copy.wait()
+
+
+def late_kernel(steps, more, slots_at, table_ref, place_ref, *refs):
+    refs = list(refs)
+    row_refs = [refs.pop(0) for _ in range(4)]
+    sources = {"own": [refs.pop(0) for _ in range(3)]}
+    for slot in range(X1, Z4 + 1):
+        sources[slot] = (refs.pop(0), refs.pop(0))
+    open_ref, cubes_ref, old_diag_ref, level_rows_ref, level_ref, made_ref, cube_ref, diag_ref = (
+        refs.pop(0) for _ in range(8)
+    )
+    block_ref, block_sem, left_ref, left_sem, total_ref, total_sem, out_sem = refs
+    half = left_ref.shape[1]
+    core = place_ref[0]
+    worker = Worker(table_ref, core, half, block_ref, block_sem, left_ref, left_sem, total_ref, total_sem)
+    worker.levels = (level_rows_ref, level_ref, diag_ref)
+    worker.load_rows(row_refs)
+    worker.load_block(0, X4, sources)
+    worker.load_block(1, Z4, sources)
+    for k in range(2):
+        worker.load_total(k, open_ref.at[k])
+    diag_ref[...] = old_diag_ref[...]
+    worker.run(steps)
+    worker.wait_rest(steps)
+    copies = copy_all([(left_ref.at[4 + k], made_ref.at[k]) for k in range(2)], out_sem)
+    worker.blocks, worker.lefts, worker.totals = [], [], []
+    for k in range(2):
+        worker.load_block(2 + k, table_ref[slots_at + k], sources)
+    worker.load_total(2, cubes_ref.at[1 - core])
+    worker.run(more)
+    worker.wait_rest(more)
+    cube_ref[...] = total_ref[2].astype(cube_ref.dtype)
+    for copy in copies:
+        copy.wait()
+
+
+def own_kernel(steps, slots_at, table_ref, place_ref, *refs):
+    refs = list(refs)
+    sources = {"own": [refs.pop(0) for _ in range(3)]}
+    for slot in range(X1, Z4 + 1):
+        sources[slot] = (refs.pop(0), refs.pop(0))
+    made_ref, cubes_ref, level_ref, cube_ref = (refs.pop(0) for _ in range(4))
+    block_ref, block_sem, left_ref, left_sem, total_ref, total_sem = refs
+    half = left_ref.shape[1]
+    core = place_ref[0]
+    worker = Worker(table_ref, core, half, block_ref, block_sem, left_ref, left_sem, total_ref, total_sem)
+    worker.levels = (None, level_ref, None)
+    for k in range(2):
+        worker.load_left(k, made_ref.at[k])
+        worker.load_block(k, table_ref[slots_at + k], sources)
+        if k == 0:
+            worker.load_total(0, cubes_ref.at[core])
+    worker.run(steps)
+    worker.wait_rest(steps)
+    cube_ref[...] = total_ref[0]
+
+
+HERE = pl.BlockSpec(memory_space=pl.ANY)
+SCALARS = pl.BlockSpec(memory_space=pltpu.SMEM)
+VMEM = pl.BlockSpec(memory_space=pltpu.VMEM)
+VMEM_BYTES = 60 * 2**20
+
+
+def work_scratch(half, width, blocks, lefts, totals, outs):
+    return [
+        pltpu.VMEM((blocks, 2 * half, width), jnp.bfloat16),
+        pltpu.SemaphoreType.DMA((blocks, 2)),
+        pltpu.VMEM((lefts, half, width), jnp.bfloat16),
+        pltpu.SemaphoreType.DMA((lefts,)),
+        pltpu.VMEM((totals, half, width), jnp.float32),
+        pltpu.SemaphoreType.DMA((totals,)),
+    ] + ([pltpu.SemaphoreType.DMA((outs,))] if outs else [])
+
+
+def call_kernel(name, kernel, scalars, operands, in_vmem, out_shape, out_specs, scratch):
+    return pl.pallas_call(
+        kernel,
+        out_shape=out_shape,
+        in_specs=[SCALARS] * len(scalars) + [HERE] * len(operands) + [VMEM] * len(in_vmem),
+        out_specs=out_specs,
+        scratch_shapes=scratch,
+        compiler_params=pltpu.CompilerParams(vmem_limit_bytes=VMEM_BYTES),
+        name=name,
+    )(*scalars, *operands, *in_vmem)
+
+
+def pick_kernel(whole_rows, count, choice_ref, *refs):
+    sources, refs = refs[:count], refs[count:]
+    outs, held_ref, in_sem, out_sem = refs[:-3], refs[-3], refs[-2], refs[-1]
+    parts = in_sem.shape[1]
+    size = held_ref.shape[1] // parts
+    for part in range(parts):
+        for k in range(len(outs)):
+            to = held_ref.at[k, pl.ds(part * size, size)]
+            for number, source in enumerate(sources):
+                @pl.when(choice_ref[k] == number)
+                def _():
+                    first = part * size
+                    if number == 0 and whole_rows:
+                        first = pl.multiple_of(choice_ref[len(outs)] + first, size)
+                    pltpu.make_async_copy(source.at[pl.ds(first, size)], to, in_sem.at[k, part]).start()
+    for part in range(parts):
+        for k, out_ref in enumerate(outs):
+            rows = pl.ds(part * size, size)
+            pltpu.make_async_copy(held_ref.at[k, rows], held_ref.at[k, rows], in_sem.at[k, part]).wait()
+            pltpu.make_async_copy(held_ref.at[k, rows], out_ref.at[rows], out_sem.at[k, part]).start()
+    for part in range(parts):
+        for k, out_ref in enumerate(outs):
+            rows = pl.ds(part * size, size)
+            pltpu.make_async_copy(held_ref.at[k, rows], out_ref.at[rows], out_sem.at[k, part]).wait()
+
+
+def pick(choices, sources, whole_rows=0, first=None):
+    shape, dtype = sources[-1].shape, sources[-1].dtype
+    numbers = jnp.stack(list(choices) + ([first] if whole_rows else [])).astype(jnp.int32)
+    parts = 4
+    return pl.pallas_call(
+        functools.partial(pick_kernel, whole_rows, len(sources)),
+        out_shape=[jax.ShapeDtypeStruct(shape, dtype)] * len(choices),
+        in_specs=[SCALARS] + [HERE] * len(sources),
+        out_specs=[HERE] * len(choices),
+        scratch_shapes=[
+            pltpu.VMEM((len(choices),) + shape, dtype),
+            pltpu.SemaphoreType.DMA((len(choices), parts)),
+            pltpu.SemaphoreType.DMA((len(choices), parts)),
+        ],
+        compiler_params=pltpu.CompilerParams(vmem_limit_bytes=VMEM_BYTES),
+        name="pick",
+    )(numbers, *sources)
+
+
+def pairs_kernel(spots_ref, points_ref, out_ref, high_ref, low_ref, wide_ref):
+    count, total = points_ref.shape[0], spots_ref.shape[1]
+    tiles = 4
+    for k in range(4):
+        wide_ref[k] = jnp.broadcast_to(points_ref[:, k : k + 1], (count, 128))
+
+    def one(index, carry):
+        lanes = [pl.ds(pl.multiple_of((index * tiles + m) * 128, 128), 128) for m in range(tiles)]
+        spots = [[jnp.broadcast_to(spots_ref[k : k + 1, at], (16, 128)) for k in range(3)] for at in lanes]
+
+        def step(group, sums):
+            rows = pl.ds(pl.multiple_of(group * 16, 16), 16)
+            px, py, pz, charge = (wide_ref[k, rows, :] for k in range(4))
+            sums = list(sums)
+            for m, at in enumerate(lanes):
+                dx, dy, dz = spots[m][0] - px, spots[m][1] - py, spots[m][2] - pz
+                inv = lax.rsqrt(dx * dx + dy * dy + dz * dz + 1.0)
+                sums[m] = sums[m] + charge * inv
+                weight = inv * (inv * inv)
+                high = weight.astype(jnp.bfloat16)
+                high_ref[rows, at] = high
+                low_ref[rows, at] = (weight - high.astype(jnp.float32)).astype(jnp.bfloat16)
+            return tuple(sums)
+
+        zeros = tuple(jnp.zeros((16, 128), jnp.float32) for _ in range(tiles))
+        sums = lax.fori_loop(0, count // 16, step, zeros, unroll=2)
+        for m, at in enumerate(lanes):
+            out_ref[:, at] = jnp.sum(sums[m], 0, keepdims=True)
+        return carry
+
+    lax.fori_loop(0, total // (128 * tiles), one, 0)
+
+
+def pair_terms(centers, points):
+    total, count = centers.shape[1], points.shape[0]
+    part = jax.ShapeDtypeStruct((count, total), jnp.bfloat16)
+    return pl.pallas_call(
+        pairs_kernel,
+        out_shape=(jax.ShapeDtypeStruct((1, total), jnp.float32), part, part),
+        scratch_shapes=[pltpu.VMEM((4, count, 128), jnp.float32)],
+        compiler_params=pltpu.CompilerParams(vmem_limit_bytes=VMEM_BYTES),
+        name="pairs",
+    )(centers, points)
+
+
+MIDDLE = 10.0
+
+
+def pull_kernel(spots_ref, occ_ref, high_ref, low_ref, coords_ref, charge_ref, out_ref, total_ref):
+    index = pl.program_id(0)
+    occ = occ_ref[...]
+    weights = [occ] + [occ * (spots_ref[k : k + 1, :] - MIDDLE) for k in range(3)]
+    width = occ.shape[1]
+    stacked = jnp.concatenate(weights + [jnp.zeros((4, width), jnp.float32)], 0)
+    high = stacked.astype(jnp.bfloat16)
+    low = (stacked - high.astype(jnp.float32)).astype(jnp.bfloat16)
+    blank = jnp.zeros((128 - 16, width), jnp.bfloat16)
+    both = jnp.concatenate([high, low, blank], 0)
+    first = jnp.concatenate([high, jnp.zeros_like(low), blank], 0)
+    dims = (((1,), (1,)), ((), ()))
+    part = lax.dot_general(high_ref[...], both, dims, preferred_element_type=jnp.float32)
+    part = part + lax.dot_general(low_ref[...], first, dims, preferred_element_type=jnp.float32)
+
+    @pl.when(index == 0)
+    def _():
+        total_ref[...] = part
+
+    @pl.when(index > 0)
+    def _():
+        total_ref[...] += part
+
+    @pl.when(index == pl.num_programs(0) - 1)
+    def _():
+        sums = total_ref[...].T
+        sums = sums[0:8] + sums[8:16]
+        for k in range(3):
+            pull = (coords_ref[k : k + 1, :] - MIDDLE) * sums[0:1] - sums[k + 1 : k + 2]
+            out_ref[k : k + 1, :] = -charge_ref[...] * pull
+
+
+def pull_terms(centers, occupation, high, low, mm_coords, mm_charges):
+    total, count = centers.shape[1], mm_coords.shape[1]
+    width = 1024
+    return pl.pallas_call(
+        pull_kernel,
+        grid=(total // width,),
+        out_shape=jax.ShapeDtypeStruct((3, count), jnp.float32),
+        in_specs=[
+            pl.BlockSpec((3, width), lambda i: (0, i)),
+            pl.BlockSpec((1, width), lambda i: (0, i)),
+            pl.BlockSpec((count, width), lambda i: (0, i)),
+            pl.BlockSpec((count, width), lambda i: (0, i)),
+            pl.BlockSpec((3, count), lambda i: (0, 0)),
+            pl.BlockSpec((1, count), lambda i: (0, 0)),
+        ],
+        out_specs=pl.BlockSpec((3, count), lambda i: (0, 0)),
+        scratch_shapes=[pltpu.VMEM((count, 128), jnp.float32)],
+        name="pull",
+    )(centers, occupation, high, low, mm_coords, mm_charges[None])
+
+
+def density_kernel(steps, place_ref, gain_ref, ham_ref, near_ref, far_ref, level_ref, out_ref):
+    index = pl.program_id(0)
+    core, row, col = place_ref[0], place_ref[1], place_ref[2]
+    gain = gain_ref[0]
+    height, width = out_ref.shape
+    chunk = 16
+    linear, cubic = -1.5 * gain, 2.0 * (gain * gain * gain)
+
+    def pass_rows(cube_ref, with_diag):
+        def one(k, carry):
+            rows = pl.ds(pl.multiple_of(k * chunk, chunk), chunk)
+            value = linear * ham_ref[rows, :].astype(jnp.float32) + cubic * cube_ref[rows, :].astype(jnp.float32)
+            if with_diag:
+                own = lax.broadcasted_iota(jnp.int32, (chunk, width), 0) + (index * height + k * chunk)
+                on_diag = own == lax.broadcasted_iota(jnp.int32, (chunk, width), 1)
+                value = value + jnp.where(on_diag, 0.5 + linear * level_ref[...], 0.0)
+            out_ref[rows, :] = value
+            return carry
+
+        lax.fori_loop(0, height // chunk, one, 0, unroll=2)
+
+    in_near = lax.div(index, jnp.int32(steps)) == core
+    holds_diag = row == 2 * col + core
+    for cube_ref, here in ((near_ref, in_near), (far_ref, jnp.logical_not(in_near))):
+        for with_diag, diag_here in ((True, holds_diag), (False, jnp.logical_not(holds_diag))):
+            pl.when(jnp.logical_and(here, diag_here))(functools.partial(pass_rows, cube_ref, with_diag))
+
+
+def density_block(place, gain, ham, near, far, level_cols):
+    height, width = ham.shape
+    chunk = 320
+    steps = near.shape[0] // chunk
+    part = pl.BlockSpec((chunk, width), lambda i: (lax.rem(i, steps), 0))
+    return pl.pallas_call(
+        functools.partial(density_kernel, steps),
+        grid=(height // chunk,),
+        out_shape=jax.ShapeDtypeStruct((height, width), jnp.float32),
+        in_specs=[SCALARS, SCALARS, pl.BlockSpec((chunk, width), lambda i: (i, 0)), part, part]
+        + [pl.BlockSpec((1, width), lambda i: (0, 0))],
+        out_specs=pl.BlockSpec((chunk, width), lambda i: (i, 0)),
+        name="density",
+    )(place, gain, ham, near, far, level_cols)
+
+
+def gossip_shards(sizes, h_core, centers, mm_coords, mm_charges):
+    height, width = h_core.shape
+    half = height // 2
+    total, count = centers.shape[1], mm_coords.shape[1]
+    row, col, core = (lax.axis_index(name) for name in ("sec", "col", "rep"))
+    row_start = row * height
+    col_start = (2 * col + core) * width
+    rows, steps, slots_at, open_at = device_tables()
+    table = lax.dynamic_index_in_dim(jnp.asarray(rows, jnp.int32), 4 * row + 2 * col + core, 0, keepdims=False)
+    place = jnp.stack([core, row, col]).astype(jnp.int32)
+
+    def of_row(values):
+        return lax.dynamic_index_in_dim(jnp.asarray(values, jnp.int32), row, 0, keepdims=False)
+
+    def over_rep(value):
+        return lax.ppermute(value, "rep", [(0, 1), (1, 0)])
+
+    def over_col(value):
+        return lax.ppermute(value, "col", [(0, 1), (1, 0)])
+
+    def over_sec(value, step):
+        moves = [(2 * start + x, 2 * to + x) for x in range(2) for start, to in Z_MOVES[step][x]]
+        return lax.ppermute(value, ("sec", "col"), moves)
+
+    def swap_all(values):
+        return [(value, over_rep(value)) for value in values]
+
+    def flat(groups):
+        return [value for group in groups for value in group]
+
+    def after(arrived, work):
+        return lax.optimization_barrier((arrived, work))
+
+    def own_source(slot):
+        return (slot != core).astype(jnp.int32)
+
+    far = lax.dynamic_slice_in_dim(h_core, (1 - core) * half, half, 0)
+    got = over_rep(far)
+    x_first, z_first = of_row(X_SENDS[0]), of_row(Z_SENDS[0])
+    sends = pick(
+        (own_source(x_first), own_source(z_first), own_source(1 - x_first), jnp.int32(0)),
+        (h_core, got), half, core * half,
+    )
+    x1 = over_col(sends[0])
+    z1 = over_sec(sends[1], 0)
+    x_second, near = sends[2], sends[3]
+    other = over_rep(near)
+    points = jnp.concatenate([mm_coords, mm_charges[None]], 0).T
+    terms, high, low = pair_terms(centers, points)
+    rows_glob = row_start + lax.broadcasted_iota(jnp.int32, (height, width), 0)
+    cols_glob = col_start + lax.broadcasted_iota(jnp.int32, (height, width), 1)
+    on_diag = rows_glob == cols_glob
+    wide = h_core.astype(jnp.float32)
+    own_diag = jnp.sum(jnp.where(on_diag, wide, 0.0), 0)
+    own_off = jnp.sum(jnp.where(on_diag, 0.0, wide * wide))
+    diag = lax.dynamic_update_slice_in_dim(jnp.zeros((total,), jnp.float32), own_diag, col_start, 0)
+    packed = jnp.concatenate([terms[0], diag, jnp.full((128,), own_off)])
+    packed = packed + over_rep(packed)
+    (x1, z1), (packed, high, low, x_second, other, table) = after(
+        (x1, z1), (packed, high, low, x_second, other, table)
+    )
+    z_second = of_row(Z_SENDS[1])
+    source = jnp.where(z_second == X1, 2, own_source(z_second))
+    z2 = over_sec(pick((source,), (near, got, x1))[0], 1)
+    x2 = over_col(x_second)
+    own_parts = (h_core, got, other)
+    pairs = dict(zip((X1, Z1), swap_all((x1, z1))))
+    shape = (half, width)
+
+    def grow_square(stage, lefts, slots, old):
+        operands = list(lefts) + list(own_parts) + flat(pairs[slot] for slot in slots) + ([] if old is None else [old])
+        kernel = functools.partial(square_kernel, old is None, steps[stage], len(lefts), (OWN0, OWN1) + slots, True)
+        return call_kernel(
+            f"square_{stage}", kernel, (table, place), operands, (),
+            jax.ShapeDtypeStruct((4,) + shape, jnp.float32), HERE,
+            work_scratch(half, width, 2 + len(slots), 4, 4, 4),
+        )
+
+    lefts = [near, got, x1]
+    square = grow_square(0, lefts, (X1, Z1), None)
+    col_packed = over_col(packed)
+    (x2, z2, col_packed), (square, packed) = after((x2, z2, col_packed), (square, packed))
+    x3 = over_col(z2)
+    z3 = over_sec(x2, 2)
+    pairs.update(zip((X2, Z2), swap_all((x2, z2))))
+    lefts.append(x2)
+    square = grow_square(1, lefts, (X1, Z1, X2, Z2), square)
+    packed = packed + col_packed
+    others = [lax.ppermute(packed, "sec", [(i, (i + hop) % 4) for i in range(4)]) for hop in (1, 2, 3)]
+    (x3, z3, others), (square, packed) = after((x3, z3, others), (square, packed))
+    source = (of_row(X_SENDS[3]) == Z3).astype(jnp.int32)
+    last_send = pick((source,), (z1, z3))[0]
+    x4 = over_col(last_send)
+    z4 = over_sec(last_send, 3)
+    pairs.update(zip((X3, Z3), swap_all((x3, z3))))
+    sums = packed + others[0] + others[1] + others[2]
+    potential, diag, off_total = sums[:total], sums[total : 2 * total], sums[2 * total]
+    diag_vals = potential + diag
+    mean_level = jnp.sum(diag_vals) / total
+    above = diag_vals - mean_level
+    level = potential - mean_level
+    spread = jnp.sqrt((off_total + jnp.sum(above * above)) / total + 1e-05)
+    gain = 1.0 / (3.0 * spread)
+    level_rows = lax.dynamic_slice_in_dim(level, row_start + core * half, half, 0)[:, None]
+    level_cols = lax.dynamic_slice_in_dim(level, col_start, width, 0)[None]
+    open_square, cubes, cube_diag = call_kernel(
+        "early_cube", functools.partial(early_kernel, steps[2], steps[3], slots_at[0], open_at), (table, place),
+        lefts + list(own_parts) + flat(pairs[slot] for slot in range(X1, Z3 + 1)) + [square],
+        (level_rows, level[None]),
+        (
+            jax.ShapeDtypeStruct((2,) + shape, jnp.float32),
+            jax.ShapeDtypeStruct((2,) + shape, jnp.float32),
+            jax.ShapeDtypeStruct((half, 1), jnp.float32),
+        ),
+        (HERE, HERE, VMEM), work_scratch(half, width, 6, 6, 6, 4),
+    )
+    (x4, z4), (open_square, cubes, cube_diag, above, level_rows, level, level_cols, gain) = after(
+        (x4, z4), (open_square, cubes, cube_diag, above, level_rows, level, level_cols, gain)
+    )
+    pairs.update(zip((X4, Z4), swap_all((x4, z4))))
+    blocks = list(own_parts) + flat(pairs[slot] for slot in range(X1, Z4 + 1))
+    made, sibling, cube_diag = call_kernel(
+        "late_cube", functools.partial(late_kernel, steps[4], steps[5], slots_at[1]), (table, place),
+        lefts + blocks + [open_square, cubes], (cube_diag, level_rows, level[None]),
+        (
+            jax.ShapeDtypeStruct((2,) + shape, jnp.bfloat16),
+            jax.ShapeDtypeStruct(shape, jnp.bfloat16),
+            jax.ShapeDtypeStruct((half, 1), jnp.float32),
+        ),
+        (HERE, VMEM, VMEM), work_scratch(half, width, 4, 6, 3, 2),
+    )
+    sibling = over_rep(sibling)
+    cube_diag = lax.dynamic_update_slice_in_dim(
+        jnp.zeros((total,), jnp.float32), cube_diag[:, 0], row_start + core * half, 0
+    )
+    cube_diag = butterfly_sum(cube_diag, sizes, ("rep", "sec"))
+    mine = call_kernel(
+        "own_cube", functools.partial(own_kernel, steps[6], slots_at[2]), (table, place),
+        blocks + [made, cubes], (level[None],), jax.ShapeDtypeStruct(shape, jnp.float32), VMEM,
+        work_scratch(half, width, 2, 2, 1, 0),
+    )
+    density = density_block(place, gain[None], h_core, mine, sibling, level_cols)
+    occupation = 0.5 - 1.5 * gain * above + 2.0 * gain**3 * cube_diag
+    forces = pull_terms(centers, occupation[None], high, low, mm_coords, mm_charges)
+    return (density, forces)
+
+
 def solution(mesh):
     in_specs = (
         P(("groups", "sec"), ("col", "rep")),
@@ -155,5 +916,7 @@
         P(("groups", "sec", "col", "rep")),
     )
     out_specs = (P(("groups", "sec"), ("col", "rep")), P(None, ("groups", "sec", "col", "rep")))
-    body = functools.partial(shards, dict(mesh.shape))
+    sizes = dict(mesh.shape)
+    small = (sizes["sec"], sizes["col"], sizes["rep"]) == (4, 2, 2)
+    body = functools.partial(gossip_shards if small else gather_shards, sizes)
     return jax.shard_map(body, mesh=mesh, in_specs=in_specs, out_specs=out_specs, check_vma=False)

time: 471 us -> 271 us (0.58)
  waiting for transfers between devices: 335 us -> 42.7 us
  Pallas kernels: 39.7 us -> 169 us
  matrix products: 50.7 us -> 0 us
  starting transfers between devices: 10.1 us -> 25.9 us
  local copies, waits for them, and re-layouts: 5.52 us -> 17 us
  between operations: 15.9 us -> 6.89 us
  other arithmetic: 13.3 us -> 7.74 us
    all_gather x3 -> x0, waiting for transfers between devices: 308 us -> none  [the longest x1 182 us: shards(): col_panel = lax.all_gather(off, 'sec', axis=0, tiled=True)]
    pallas_call x2 -> x11, Pallas kernels: 39.7 us -> 169 us  [the longest x5 130 us: call_kernel(): pl.pallas_call(kernel, out_shape=out_shape, in_specs=[SCALARS] * len(scal...]
    dot_general x2 -> x0, matrix products: 50.7 us -> none  [fold_with(): return jnp.dot(left, piece, preferred_element_type=jnp.float32)]
    ppermute x0 -> x24, waiting for transfers between devices: none -> 39.4 us  [the longest x5 22 us: over_col(): return lax.ppermute(value, 'col', [(0, 1), (1, 0)])]
    ppermute x8 -> x3, waiting for transfers between devices: 26.5 us -> 3.28 us  [butterfly_sum(): lax.ppermute(value, axis, [(i, i ^ hop) for i in range(size)])]
    ppermute x0 -> x24, starting transfers between devices: none -> 19.2 us  [the longest x3 5.54 us: gossip_shards(): lax.ppermute(packed, 'sec', [(i, (i + hop) % 4) for i in range(4)])]
    dynamic_slice x1 -> x8, local copies, waits for them, and re-layouts: 0.71 us -> 6.52 us  [the longest x1 2.71 us: gossip_shards(): far = lax.dynamic_slice_in_dim(h_core, (1 - core) * half, half, 0)]
    ppermute x8 -> x3, starting transfers between devices: 9.98 us -> 6.77 us  [butterfly_sum(): lax.ppermute(value, axis, [(i, i ^ hop) for i in range(size)])]
  transfers between devices with their start and end apart: 11 -> 27, of which waited for: 11 -> 10; matrix products, arithmetic and copies ran while one was open for 3% -> 6% of each run, Pallas kernels for 8% -> 46%
where the time goes in v2:
time: 271 us; the launch traced here: 270 us
  Pallas kernels  169 us (62%)
  waiting for transfers between devices  42.7 us (16%)
  starting transfers between devices  25.9 us (10%)
  local copies, waits for them, and re-layouts  17 us (6%)
  other arithmetic  7.74 us (3%)
  between operations  6.89 us (3%)
    pallas_call x5, Pallas kernels, call_kernel(): pl.pallas_call(kernel, out_shape=out_shape, in_specs=[SCALARS] * len(scal...  130 us
    ppermute x5, waiting for transfers between devices, over_col(): return lax.ppermute(value, 'col', [(0, 1), (1, 0)])  22 us
    pallas_call x1, Pallas kernels, pair_terms(): pl.pallas_call(pairs_kernel, out_shape=(jax.ShapeDtypeStruct((1, total),...  12.7 us
    pallas_call x3, Pallas kernels, pick(): pl.pallas_call(functools.partial(pick_kernel, whole_rows, len(sources)),...  11 us
    pallas_call x1, Pallas kernels, density_block(): pl.pallas_call(functools.partial(density_kernel, steps), grid=(height //...  8.53 us
    ppermute x3, waiting for transfers between devices, gossip_shards(): lax.ppermute(packed, 'sec', [(i, (i + hop) % 4) for i in range(4)])  8.39 us
    pallas_call x1, Pallas kernels, pull_terms(): pl.pallas_call(pull_kernel, grid=(total // width,), out_shape=jax.ShapeDt...  7.63 us
    ppermute x3, starting transfers between devices, butterfly_sum(): lax.ppermute(value, axis, [(i, i ^ hop) for i in range(size)])  6.77 us
  transfers between devices with their start and end apart: 27, of which 10 were waited for; matrix products, arithmetic and copies ran while one was open for 6% of the time, Pallas kernels for 46%

profile of v2, /device:TPU:0, one launch (start us, length us, event | category | flops | bytes accessed | tf_op | source)
XLA Modules:
  0.0 269.7 jit_solution(403201810320737928)
XLA Ops:
  0.7 2.7 %constant_dynamic-slice_fusion = bf16[640,1280]{1,0:T(8,128)(2,1)} fusion(bf16[1280,1280]{1,0:T(8,128)(2,1)} %ham_ref.1, s32[]{:T(128)S(6)} %select_n.35), kind=kLoop, calls=%fused_computation.19 | loop fusion | bytes 3276804 | tf_op jit(solution)/shard_map/dynamic_slice | solution.py:800
  3.4 0.5 collective-permute-start
  3.8 0.6 dynamic_slice.27
  5.7 0.6 dynamic_slice.28
  6.9 0.6 stack.51.choice_ref
  7.5 6.6 %pick.3 = (bf16[640,1280]{1,0:T(8,128)(2,1)}, bf16[640,1280]{1,0:T(8,128)(2,1)}, bf16[640,1280]{1,0:T(8,128)(2,1)}, bf16[640,1280]{1,0:T(8,128)(2,1)}) custom-call(s32[5]{0:T(128)} %stack.51.choice_ref, bf16[1280,1280]{1,0:T(8,128)(2,1)} %ham_ref.1, bf16[640,1280]{1,0:T(8,128)(2,1)} %collective-permute-done.refs_1_.refs_4_.refs_5_), custom_call_target="tpu_custom_call" | custom-call | tf_op jit(solution)/shard_map/pick/pallas_call | solution.py:604
  14.1 0.2 collective-permute-start.4
  14.3 2.8 %collective-permute-start.1 = (bf16[640,1280]{1,0:T(8,128)(2,1)}, bf16[640,1280]{1,0:T(8,128)(2,1)}, u32[]{:S(2)}, u32[]{:S(2)}) collective-permute-start(bf16[640,1280]{1,0:T(8,128)(2,1)} %get-tuple-element.45), channel_id=1, source_target_pairs={{0,2},{2,0},{1,3},{3,1},{4,6},{6,4},{5,7},{7,5},{8,10},{10,8},{9,1... | collective-permute-start | bytes 4915208 | tf_op jit(solution)/shard_map/ppermute | solution.py:782
  17.1 1.6 collective-permute-start.2
  18.7 0.9 copy.17
  19.6 12.7 %pairs.1 = (f32[1,5120]{1,0:T(1,128)}, bf16[512,5120]{1,0:T(8,128)(2,1)}, bf16[512,5120]{1,0:T(8,128)(2,1)}) custom-call(f32[3,5120]{1,0:T(4,128)} %spots_ref.3, f32[512,4]{1,0:T(8,128)} %bitcast.19), custom_call_target="tpu_custom_call" | custom-call | tf_op jit(solution)/shard_map/pairs/pallas_call | solution.py:655
  32.4 3.8 %fusion = (f32[1280]{0:T(1024)S(1)}, f32[]{:T(128)}) fusion(bf16[1280,1280]{1,0:T(8,128)(2,1)S(1)} %copy-done, s32[1280]{0:T(1024)S(1)} %get-tuple-element.93, s32[1280]{0:T(1024)S(1)} %get-tuple-element.94), kind=kLoop, calls=%fused_computation.3 | loop fusion | flops 11467519 | bytes 3292164 | tf_op jit(solution)/shard_map/reduce_sum | solution.py:817
  36.4 0.6 broadcast_in_dim.34
  37.2 0.6 dynamic_slice.31
  39.1 1.3 dynamic-slice_reduce_fusion.table_ref
  40.4 13.2 %collective-permute-done.1.refs_2_.refs_6_.refs_7_.refs_3_ = bf16[640,1280]{1,0:T(8,128)(2,1)} collective-permute-done((bf16[640,1280]{1,0:T(8,128)(2,1)}, bf16[640,1280]{1,0:T(8,128)(2,1)}, u32[]{:S(2)}, u32[]{:S(2)}) %collective-permute-start.1) | collective-permute-done | bytes 1638432 | tf_op jit(solution)/shard_map/ppermute | solution.py:782
  53.6 3.3 %collective-permute-done.2.refs_8_.refs_9_.refs_0_.refs_5_ = bf16[640,1280]{1,0:T(8,128)(2,1)} collective-permute-done((bf16[640,1280]{1,0:T(8,128)(2,1)}, bf16[640,1280]{1,0:T(8,128)(2,1)}, u32[]{:S(2)}, u32[]{:S(2)}) %collective-permute-start.2) | collective-permute-done | bytes 1638432 | tf_op jit(solution)/shard_map/ppermute | solution.py:786
  56.9 0.5 collective-permute-start.9
  57.4 2.2 pick.4
  59.6 1.8 collective-permute-start.6
  61.4 2.0 collective-permute-start.7
  63.5 0.6 pad_add_fusion.place_ref
  64.1 1.2 copy-done.2
  65.3 25.9 %square_0.1.refs_15_ = f32[4,640,1280]{2,1,0:T(8,128)} custom-call(s32[346]{0:T(512)} %dynamic-slice_reduce_fusion.table_ref, s32[3]{0:T(128)} %pad_add_fusion.place_ref, bf16[640,1280]{1,0:T(8,128)(2,1)} %get-tuple-element.51.refs_0_, bf16[640,1280]{1,0:T(8,128)(2,1)} %collective-permute-done.refs_1_.refs_4_.refs_5_, ...), custom_call_target="tpu_custom_call" | custom-call | tf_op jit(solution)/shard_map/square_0/pallas_call | solution.py:563
  91.2 8.8 %collective-permute-done.7 = f32[10368]{0:T(1024)S(1)} collective-permute-done((f32[10368]{0:T(1024)S(1)}, f32[10368]{0:T(1024)S(1)}, u32[]{:S(2)}, u32[]{:S(2)}) %collective-permute-start.7) | collective-permute-done | bytes 41504 | tf_op jit(solution)/shard_map/ppermute | solution.py:782
  100.1 0.5 collective-permute-start.16
  100.6 0.3 collective-permute-start.10
  100.9 0.3 collective-permute-start.11
  101.2 2.9 %collective-permute-start.12 = (f32[10368]{0:T(1024)S(1)}, f32[10368]{0:T(1024)S(1)}, u32[]{:S(2)}, u32[]{:S(2)}) collective-permute-start(f32[10368]{0:T(1024)S(1)} %add.98), channel_id=1, source_target_pairs={{0,4},{4,8},{8,12},{12,0},{1,5},{5,9},{9,13},{13,1},{2,6},{6,10},{... | collective-permute-start | bytes 124424 | tf_op jit(solution)/shard_map/ppermute | solution.py:852
  104.1 1.1 collective-permute-done.15.refs_12_.refs_8_
  105.2 1.2 copy-done.4
  106.4 1.2 collective-permute-start.13
  107.5 1.5 collective-permute-start.14
  109.0 0.6 dynamic_slice.26
  109.6 25.2 %square_1.1.refs_19_ = f32[4,640,1280]{2,1,0:T(8,128)} custom-call(s32[346]{0:T(512)} %dynamic-slice_reduce_fusion.table_ref, s32[3]{0:T(128)} %pad_add_fusion.place_ref, bf16[640,1280]{1,0:T(8,128)(2,1)} %get-tuple-element.51.refs_0_, bf16[640,1280]{1,0:T(8,128)(2,1)} %collective-permute-done.refs_1_.refs_4_.refs_5_, ...), custom_call_target="tpu_custom_call" | custom-call | tf_op jit(solution)/shard_map/square_1/pallas_call | solution.py:563
  134.8 7.4 %collective-permute-done.12 = f32[10368]{0:T(1024)S(1)} collective-permute-done((f32[10368]{0:T(1024)S(1)}, f32[10368]{0:T(1024)S(1)}, u32[]{:S(2)}, u32[]{:S(2)}) %collective-permute-start.12) | collective-permute-done | bytes 41504 | tf_op jit(solution)/shard_map/ppermute | solution.py:852
  142.3 0.9 collective-permute-done.13
  143.3 0.5 collective-permute-start.20
  144.5 2.3 pick.5
  146.8 1.7 collective-permute-start.18
  148.5 0.5 slice.14
  149.1 0.7 fusion.2
  150.4 0.7 multiply_reduce_fusion
  152.6 0.9 copy.18.refs_20_
  153.5 0.6 broadcast_in_dim.37.level_ref
  154.2 37.0 %early_cube.1 = (f32[2,640,1280]{2,1,0:T(8,128)}, f32[2,640,1280]{2,1,0:T(8,128)}, f32[640,1]{1,0:T(8,128)}) custom-call(s32[346]{0:T(512)} %dynamic-slice_reduce_fusion.table_ref, s32[3]{0:T(128)} %pad_add_fusion.place_ref, bf16[640,1280]{1,0:T(8,128)(2,1)} %get-tuple-element.51.refs_0_, bf16[640,1280]{1,0:T(8,128)(2,1)} %collective-permute-done.refs_1_.refs_4_.refs_5_, ...), custom_call_target="tpu_custom_call" | custom-call | tf_op jit(solution)/shard_map/early_cube/pallas_call | solution.py:563
  191.3 0.5 collective-permute-start.22
  191.8 0.9 copy.19.refs_26_
  192.7 2.3 collective-permute-done.21.refs_20_.refs_16_
  195.0 2.3 collective-permute-done.22.refs_22_.refs_18_
  197.3 1.1 copy-done.6
  198.5 29.5 %late_cube.1 = (bf16[2,640,1280]{2,1,0:T(8,128)(2,1)}, bf16[640,1280]{1,0:T(8,128)(2,1)}, f32[640,1]{1,0:T(8,128)}) custom-call(s32[346]{0:T(512)} %dynamic-slice_reduce_fusion.table_ref, s32[3]{0:T(128)} %pad_add_fusion.place_ref, bf16[640,1280]{1,0:T(8,128)(2,1)} %get-tuple-element.51.refs_0_, ...), custom_call_target="tpu_custom_call" | custom-call | tf_op jit(solution)/shard_map/late_cube/pallas_call | solution.py:563
  228.0 1.1 reduce.1
  229.2 0.3 dynamic_update_slice.9
  229.5 0.5 collective-permute-start.24
  230.0 1.5 collective-permute-done.24
  231.7 3.6 %collective-permute-start.25 = (f32[5120]{0:T(1024)S(1)}, f32[5120]{0:T(1024)S(1)}, u32[]{:S(2)}, u32[]{:S(2)}) collective-permute-start(f32[5120]{0:T(1024)S(1)} %add_dynamic-update-slice_fusion), channel_id=1, source_target_pairs={{0,4},{4,0},{8,12},{12,8},{1,5},{5,1},{9,13},{13,9},{2,6},{6,2},{1... | collective-permute-start | bytes 61448 | tf_op jit(solution)/shard_map/ppermute | solution.py:97
  235.4 1.8 collective-permute-done.25
  237.1 2.6 collective-permute-start.26
  239.7 11.9 %own_cube.1.near_ref = f32[640,1280]{1,0:T(8,128)} custom-call(s32[346]{0:T(512)} %dynamic-slice_reduce_fusion.table_ref, s32[3]{0:T(128)} %pad_add_fusion.place_ref, bf16[1280,1280]{1,0:T(8,128)(2,1)} %ham_ref.1, bf16[640,1280]{1,0:T(8,128)(2,1)} %collective-permute-done.refs_1_.refs_4_.refs_5_, ...), custom_call_target="tpu_custom_call" | custom-call | tf_op jit(solution)/shard_map/own_cube/pallas_call | solution.py:563
  251.7 0.6 multiply_add_fusion
  252.3 7.6 %pull.1 = f32[3,512]{1,0:T(4,128)} custom-call(f32[3,5120]{1,0:T(4,128)} %spots_ref.3, f32[1,5120]{1,0:T(1,128)} %bitcast.23, bf16[512,5120]{1,0:T(8,128)(2,1)} %get-tuple-element.86.high_ref, bf16[512,5120]{1,0:T(8,128)(2,1)} %get-tuple-element.87.low_ref, f32[3,512]{1,0:T(4,128)} %coords_ref.1, f32[1,512]{1,0:T(1,128)} %bitcast.26), custom_call_target="tpu_custom_call" | custom-call | tf_op jit(solution)/shard_map/pull/pallas_call | solution.py:702
  259.9 1.3 copy-done.7
  261.2 8.5 %density.1 = f32[1280,1280]{1,0:T(8,128)} custom-call(s32[3]{0:T(128)} %pad_add_fusion.place_ref, f32[1]{0:T(128)} %bitcast.16.gain_ref, bf16[1280,1280]{1,0:T(8,128)(2,1)} %ham_ref.1, f32[640,1280]{1,0:T(8,128)} %own_cube.1.near_ref, bf16[640,1280]{1,0:T(8,128)(2,1)} %copy-done.7, f32[1,1280]{1,0:T(1,128)} %broadcast_in_dim.37.level_ref), custom_call_target="tpu_custom_call" | custom-call | tf_op jit(solution)/shard_map/density/pallas_call | solution.py:753
  (67 shorter events, 1.1 us)
Async XLA Ops:
  0.6 3.2 %copy-start.15 = (s32[4]{0:T(128)S(1)}, s32[4]{0:T(128)}, u32[]{:S(2)}) copy-start(s32[4]{0:T(128)} %constant.75.clone) | copy-start | bytes 52
  0.6 5.1 %copy-start.14 = (s32[4]{0:T(128)S(1)}, s32[4]{0:T(128)}, u32[]{:S(2)}) copy-start(s32[4]{0:T(128)} %constant.76.clone) | copy-start | bytes 52
  3.4 4.1 %collective-permute-start = (bf16[640,1280]{1,0:T(8,128)(2,1)}, bf16[640,1280]{1,0:T(8,128)(2,1)}, u32[]{:S(2)}, u32[]{:S(2)}) collective-permute-start(bf16[640,1280]{1,0:T(8,128)(2,1)} %constant_dynamic-slice_fusion), channel_id=1, source_target_pairs={{0,1},{1,0},{2,3},{3,2},{4,5},{5,4},{6,7},{7,6},{8,9},{9,8},{10,11... | collective-permute-start | bytes 4915208 | tf_op jit(solution)/shard_map/ppermute | solution.py:779
  7.5 11.3 %copy-start.10 = (f32[3,512]{1,0:T(4,128)S(1)}, f32[3,512]{1,0:T(4,128)}, u32[]{:S(2)}) copy-start(f32[3,512]{1,0:T(4,128)} %coords_ref.1) | copy-start | bytes 18436
  7.5 11.3 %copy-start.11 = (f32[512]{0:T(512)S(1)}, f32[512]{0:T(512)}, u32[]{:S(2)}) copy-start(f32[512]{0:T(512)} %param.12) | copy-start | bytes 6148
  7.5 24.9 %copy-start = (bf16[1280,1280]{1,0:T(8,128)(2,1)S(1)}, bf16[1280,1280]{1,0:T(8,128)(2,1)}, u32[]{:S(2)}) copy-start(bf16[1280,1280]{1,0:T(8,128)(2,1)} %ham_ref.1) | copy-start | bytes 9830404
  14.1 26.3 %collective-permute-start.4 = (bf16[640,1280]{1,0:T(8,128)(2,1)}, bf16[640,1280]{1,0:T(8,128)(2,1)}, u32[]{:S(2)}, u32[]{:S(2)}) collective-permute-start(bf16[640,1280]{1,0:T(8,128)(2,1)} %get-tuple-element.51.refs_0_), channel_id=1, source_target_pairs={{0,1},{1,0},{2,3},{3,2},{4,5},{5,4},{6,7},{7,6},{8,9},{9,8},{10,11... | collective-permute-start | bytes 4915208 | tf_op jit(solution)/shard_map/ppermute | solution.py:779
  14.3 39.3 %collective-permute-start.1 = (bf16[640,1280]{1,0:T(8,128)(2,1)}, bf16[640,1280]{1,0:T(8,128)(2,1)}, u32[]{:S(2)}, u32[]{:S(2)}) collective-permute-start(bf16[640,1280]{1,0:T(8,128)(2,1)} %get-tuple-element.45), channel_id=1, source_target_pairs={{0,2},{2,0},{1,3},{3,1},{4,6},{6,4},{5,7},{7,5},{8,10},{10,8},{9,1... | collective-permute-start | bytes 4915208 | tf_op jit(solution)/shard_map/ppermute | solution.py:782
  17.1 39.8 %collective-permute-start.2 = (bf16[640,1280]{1,0:T(8,128)(2,1)}, bf16[640,1280]{1,0:T(8,128)(2,1)}, u32[]{:S(2)}, u32[]{:S(2)}) collective-permute-start(bf16[640,1280]{1,0:T(8,128)(2,1)} %get-tuple-element.46), channel_id=1, source_target_pairs={{0,4},{4,8},{8,12},{12,0},{2,14},{14,10},{10,6},{6,2},{1,5},{5,9},... | collective-permute-start | bytes 4915208 | tf_op jit(solution)/shard_map/ppermute | solution.py:786
  32.3 4.7 %copy-start.9 = (f32[1,5120]{1,0:T(1,128)S(1)}, f32[1,5120]{1,0:T(1,128)}, u32[]{:S(2)}) copy-start(f32[1,5120]{1,0:T(1,128)} %get-tuple-element.47) | copy-start | bytes 61444
  32.3 4.8 %copy-start.13 = (s32[4]{0:T(128)S(1)}, s32[4]{0:T(128)}, u32[]{:S(2)}) copy-start(s32[4]{0:T(128)} %constant.77.clone) | copy-start | bytes 52
  37.1 3.3 %collective-permute-start.3 = (f32[10368]{0:T(1024)S(1)}, f32[10368]{0:T(1024)S(1)}, u32[]{:S(2)}, u32[]{:S(2)}) collective-permute-start(f32[10368]{0:T(1024)S(1)} %pad_maximum_fusion), channel_id=1, source_target_pairs={{0,1},{1,0},{2,3},{3,2},{4,5},{5,4},{6,7},{7,6},{8,9},{9,8},{10,11... | collective-permute-start | bytes 124424 | tf_op jit(solution)/shard_map/ppermute | solution.py:779
  56.9 7.2 %collective-permute-start.8 = (bf16[640,1280]{1,0:T(8,128)(2,1)}, bf16[640,1280]{1,0:T(8,128)(2,1)S(1)}, u32[]{:S(2)}, u32[]{:S(2)}) collective-permute-start(bf16[640,1280]{1,0:T(8,128)(2,1)} %collective-permute-done.1.refs_2_.refs_6_.refs_7_.refs_3_), channel_id=1, source_target_pairs={{0,1},{1,0},{2,3},{3,2},{4,5},{5,4},{6,7},{7,6},{8,9},{9,8},{10,11... | collective-permute-start | bytes 4915208 | tf_op jit(solution)/shard_map/ppermute | solution.py:779
  56.9 7.2 %collective-permute-start.9 = (bf16[640,1280]{1,0:T(8,128)(2,1)}, bf16[640,1280]{1,0:T(8,128)(2,1)}, u32[]{:S(2)}, u32[]{:S(2)}) collective-permute-start(bf16[640,1280]{1,0:T(8,128)(2,1)} %collective-permute-done.2.refs_8_.refs_9_.refs_0_.refs_5_), channel_id=1, source_target_pairs={{0,1},{1,0},{2,3},{3,2},{4,5},{5,4},{6,7},{7,6},{8,9},{9,8},{10,11... | collective-permute-start | bytes 4915208 | tf_op jit(solution)/shard_map/ppermute | solution.py:779
  59.6 40.4 %collective-permute-start.6 = (bf16[640,1280]{1,0:T(8,128)(2,1)}, bf16[640,1280]{1,0:T(8,128)(2,1)}, u32[]{:S(2)}, u32[]{:S(2)}) collective-permute-start(bf16[640,1280]{1,0:T(8,128)(2,1)} %pick.4), channel_id=1, source_target_pairs={{0,12},{12,8},{8,4},{4,0},{2,6},{6,10},{10,14},{14,2},{1,13},{13,9... | collective-permute-start | bytes 4915208 | tf_op jit(solution)/shard_map/ppermute | solution.py:786
  61.4 38.6 %collective-permute-start.5 = (bf16[640,1280]{1,0:T(8,128)(2,1)}, bf16[640,1280]{1,0:T(8,128)(2,1)S(1)}, u32[]{:S(2)}, u32[]{:S(2)}) collective-permute-start(bf16[640,1280]{1,0:T(8,128)(2,1)} %get-tuple-element.53), channel_id=1, source_target_pairs={{0,2},{2,0},{1,3},{3,1},{4,6},{6,4},{5,7},{7,5},{8,10},{10,8},{9,1... | collective-permute-start | bytes 4915208 | tf_op jit(solution)/shard_map/ppermute | solution.py:782
  61.4 38.6 %collective-permute-start.7 = (f32[10368]{0:T(1024)S(1)}, f32[10368]{0:T(1024)S(1)}, u32[]{:S(2)}, u32[]{:S(2)}) collective-permute-start(f32[10368]{0:T(1024)S(1)} %fusion.3), channel_id=1, source_target_pairs={{0,2},{2,0},{1,3},{3,1},{4,6},{6,4},{5,7},{7,5},{8,10},{10,8},{9,1... | collective-permute-start | bytes 124424 | tf_op jit(solution)/shard_map/ppermute | solution.py:782
  64.1 45.0 %copy-start.12 = (s32[4]{0:T(128)S(1)}, s32[4]{0:T(128)}, u32[]{:S(2)}) copy-start(s32[4]{0:T(128)} %constant.78.clone) | copy-start | bytes 52
  64.1 1.2 copy-start.2
  100.0 9.6 %copy-start.1 = (bf16[640,1280]{1,0:T(8,128)(2,1)}, bf16[640,1280]{1,0:T(8,128)(2,1)S(1)}, u32[]{:S(2)}) copy-start(bf16[640,1280]{1,0:T(8,128)(2,1)S(1)} %collective-permute-done.5.refs_3_.refs_11_.refs_7_) | copy-start | bytes 4915204
  100.1 5.1 %collective-permute-start.15 = (bf16[640,1280]{1,0:T(8,128)(2,1)S(1)}, bf16[640,1280]{1,0:T(8,128)(2,1)S(1)}, u32[]{:S(2)}, u32[]{:S(2)}) collective-permute-start(bf16[640,1280]{1,0:T(8,128)(2,1)S(1)} %collective-permute-done.5.refs_3_.refs_11_.refs_7_), channel_id=1, source_target_pairs={{0,1},{1,0},{2,3},{3,2},{4,5},{5,4},{6,7},{7,6},{8,9},{9,8},{10,11... | collective-permute-start | bytes 4915208 | tf_op jit(solution)/shard_map/ppermute | solution.py:779
  100.1 7.4 %collective-permute-start.16 = (bf16[640,1280]{1,0:T(8,128)(2,1)}, bf16[640,1280]{1,0:T(8,128)(2,1)}, u32[]{:S(2)}, u32[]{:S(2)}) collective-permute-start(bf16[640,1280]{1,0:T(8,128)(2,1)} %collective-permute-done.6.refs_13_.refs_9_), channel_id=1, source_target_pairs={{0,1},{1,0},{2,3},{3,2},{4,5},{5,4},{6,7},{7,6},{8,9},{9,8},{10,11... | collective-permute-start | bytes 4915208 | tf_op jit(solution)/shard_map/ppermute | solution.py:779
  100.6 42.6 %collective-permute-start.10 = (bf16[640,1280]{1,0:T(8,128)(2,1)}, bf16[640,1280]{1,0:T(8,128)(2,1)}, u32[]{:S(2)}, u32[]{:S(2)}) collective-permute-start(bf16[640,1280]{1,0:T(8,128)(2,1)} %collective-permute-done.6.refs_13_.refs_9_), channel_id=1, source_target_pairs={{0,2},{2,0},{1,3},{3,1},{4,6},{6,4},{5,7},{7,5},{8,10},{10,8},{9,1... | collective-permute-start | bytes 4915208 | tf_op jit(solution)/shard_map/ppermute | solution.py:782
  100.9 42.3 %collective-permute-start.11 = (bf16[640,1280]{1,0:T(8,128)(2,1)S(1)}, bf16[640,1280]{1,0:T(8,128)(2,1)S(1)}, u32[]{:S(2)}, u32[]{:S(2)}) collective-permute-start(bf16[640,1280]{1,0:T(8,128)(2,1)S(1)} %collective-permute-done.5.refs_3_.refs_11_.refs_7_), channel_id=1, source_target_pairs={{0,4},{4,8},{8,12},{12,0},{2,14},{14,10},{10,6},{6,2},{1,5},{5,9},... | collective-permute-start | bytes 4915208 | tf_op jit(solution)/shard_map/ppermute | solution.py:786
  101.2 41.1 %collective-permute-start.12 = (f32[10368]{0:T(1024)S(1)}, f32[10368]{0:T(1024)S(1)}, u32[]{:S(2)}, u32[]{:S(2)}) collective-permute-start(f32[10368]{0:T(1024)S(1)} %add.98), channel_id=1, source_target_pairs={{0,4},{4,8},{8,12},{12,0},{1,5},{5,9},{9,13},{13,1},{2,6},{6,10},{... | collective-permute-start | bytes 124424 | tf_op jit(solution)/shard_map/ppermute | solution.py:852
  105.2 1.2 copy-start.4
  106.4 36.9 %collective-permute-start.13 = (f32[10368]{0:T(1024)S(1)}, f32[10368]{0:T(1024)S(1)}, u32[]{:S(2)}, u32[]{:S(2)}) collective-permute-start(f32[10368]{0:T(1024)S(1)} %add.98), channel_id=1, source_target_pairs={{0,8},{4,12},{8,0},{12,4},{1,9},{5,13},{9,1},{13,5},{2,10},{6,14},... | collective-permute-start | bytes 124424 | tf_op jit(solution)/shard_map/ppermute | solution.py:852
  107.5 35.7 %collective-permute-start.14 = (f32[10368]{0:T(1024)S(1)}, f32[10368]{0:T(1024)S(1)}, u32[]{:S(2)}, u32[]{:S(2)}) collective-permute-start(f32[10368]{0:T(1024)S(1)} %add.98), channel_id=1, source_target_pairs={{0,12},{4,0},{8,4},{12,8},{1,13},{5,1},{9,5},{13,9},{2,14},{6,2},{... | collective-permute-start | bytes 124424 | tf_op jit(solution)/shard_map/ppermute | solution.py:852
  143.2 1.2 copy-start.3
  143.3 10.9 %collective-permute-start.19 = (bf16[640,1280]{1,0:T(8,128)(2,1)}, bf16[640,1280]{1,0:T(8,128)(2,1)}, u32[]{:S(2)}, u32[]{:S(2)}) collective-permute-start(bf16[640,1280]{1,0:T(8,128)(2,1)} %collective-permute-done.10.refs_15_.refs_11_), channel_id=1, source_target_pairs={{0,1},{1,0},{2,3},{3,2},{4,5},{5,4},{6,7},{7,6},{8,9},{9,8},{10,11... | collective-permute-start | bytes 4915208 | tf_op jit(solution)/shard_map/ppermute | solution.py:779
  143.3 10.9 %collective-permute-start.20 = (bf16[640,1280]{1,0:T(8,128)(2,1)S(1)}, bf16[640,1280]{1,0:T(8,128)(2,1)}, u32[]{:S(2)}, u32[]{:S(2)}) collective-permute-start(bf16[640,1280]{1,0:T(8,128)(2,1)S(1)} %collective-permute-done.11.refs_1_.refs_17_.refs_13_), channel_id=1, source_target_pairs={{0,1},{1,0},{2,3},{3,2},{4,5},{5,4},{6,7},{7,6},{8,9},{9,8},{10,11... | collective-permute-start | bytes 4915208 | tf_op jit(solution)/shard_map/ppermute | solution.py:779
  146.8 44.4 %collective-permute-start.17 = (bf16[640,1280]{1,0:T(8,128)(2,1)}, bf16[640,1280]{1,0:T(8,128)(2,1)}, u32[]{:S(2)}, u32[]{:S(2)}) collective-permute-start(bf16[640,1280]{1,0:T(8,128)(2,1)} %pick.5), channel_id=1, source_target_pairs={{0,2},{2,0},{1,3},{3,1},{4,6},{6,4},{5,7},{7,5},{8,10},{10,8},{9,1... | collective-permute-start | bytes 4915208 | tf_op jit(solution)/shard_map/ppermute | solution.py:782
  146.8 44.4 %collective-permute-start.18 = (bf16[640,1280]{1,0:T(8,128)(2,1)}, bf16[640,1280]{1,0:T(8,128)(2,1)}, u32[]{:S(2)}, u32[]{:S(2)}) collective-permute-start(bf16[640,1280]{1,0:T(8,128)(2,1)} %pick.5), channel_id=1, source_target_pairs={{0,4},{4,8},{8,12},{12,0},{2,14},{14,10},{10,6},{6,2},{1,5},{5,9},... | collective-permute-start | bytes 4915208 | tf_op jit(solution)/shard_map/ppermute | solution.py:786
  151.1 3.1 %copy-start.8 = (f32[5120]{0:T(1024)}, f32[5120]{0:T(1024)S(1)}, u32[]{:S(2)}) copy-start(f32[5120]{0:T(1024)S(1)} %get-tuple-element.80) | copy-start | bytes 61444
  191.2 3.8 %collective-permute-start.21 = (bf16[640,1280]{1,0:T(8,128)(2,1)}, bf16[640,1280]{1,0:T(8,128)(2,1)S(1)}, u32[]{:S(2)}, u32[]{:S(2)}) collective-permute-start(bf16[640,1280]{1,0:T(8,128)(2,1)} %collective-permute-done.17.refs_19_.refs_15_), channel_id=1, source_target_pairs={{0,1},{1,0},{2,3},{3,2},{4,5},{5,4},{6,7},{7,6},{8,9},{9,8},{10,11... | collective-permute-start | bytes 4915208 | tf_op jit(solution)/shard_map/ppermute | solution.py:779
  191.3 6.0 %collective-permute-start.22 = (bf16[640,1280]{1,0:T(8,128)(2,1)}, bf16[640,1280]{1,0:T(8,128)(2,1)S(1)}, u32[]{:S(2)}, u32[]{:S(2)}) collective-permute-start(bf16[640,1280]{1,0:T(8,128)(2,1)} %collective-permute-done.18.refs_21_.refs_17_), channel_id=1, source_target_pairs={{0,1},{1,0},{2,3},{3,2},{4,5},{5,4},{6,7},{7,6},{8,9},{9,8},{10,11... | collective-permute-start | bytes 4915208 | tf_op jit(solution)/shard_map/ppermute | solution.py:779
  195.0 2.3 copy-start.5
  197.3 1.1 copy-start.6
  228.0 32.0 %collective-permute-start.23 = (bf16[640,1280]{1,0:T(8,128)(2,1)}, bf16[640,1280]{1,0:T(8,128)(2,1)S(1)}, u32[]{:S(2)}, u32[]{:S(2)}) collective-permute-start(bf16[640,1280]{1,0:T(8,128)(2,1)} %get-tuple-element.82), channel_id=1, source_target_pairs={{0,1},{1,0},{2,3},{3,2},{4,5},{5,4},{6,7},{7,6},{8,9},{9,8},{10,11... | collective-permute-start | bytes 4915208 | tf_op jit(solution)/shard_map/ppermute | solution.py:779
  229.5 2.1 collective-permute-start.24
  231.7 5.4 %collective-permute-start.25 = (f32[5120]{0:T(1024)S(1)}, f32[5120]{0:T(1024)S(1)}, u32[]{:S(2)}, u32[]{:S(2)}) collective-permute-start(f32[5120]{0:T(1024)S(1)} %add_dynamic-update-slice_fusion), channel_id=1, source_target_pairs={{0,4},{4,0},{8,12},{12,8},{1,5},{5,1},{9,13},{13,9},{2,6},{6,2},{1... | collective-permute-start | bytes 61448 | tf_op jit(solution)/shard_map/ppermute | solution.py:97
  237.1 14.5 %collective-permute-start.26 = (f32[5120]{0:T(1024)S(1)}, f32[5120]{0:T(1024)S(1)}, u32[]{:S(2)}, u32[]{:S(2)}) collective-permute-start(f32[5120]{0:T(1024)S(1)} %add.108), channel_id=1, source_target_pairs={{0,8},{4,12},{8,0},{12,4},{1,9},{5,13},{9,1},{13,5},{2,10},{6,14},... | collective-permute-start | bytes 61448 | tf_op jit(solution)/shard_map/ppermute | solution.py:97
  259.9 1.3 copy-start.7

commit v3 on v2

v3 whole, which is shorter than its diff:
```python
import functools

import jax
import jax.numpy as jnp
from jax import lax
from jax.experimental import pallas as pl
from jax.experimental.pallas import tpu as pltpu
from jax.sharding import PartitionSpec as P

PART = ("sec", "col", "rep")


def potential_kernel(spots_ref, points_ref, out_ref):
    count = points_ref.shape[0]
    width = spots_ref.shape[1]
    sx, sy, sz = (spots_ref[k : k + 1, :] for k in range(3))

    def step(index, accum):
        rows = points_ref[pl.ds(pl.multiple_of(index * 8, 8), 8), :]
        dx = sx - rows[:, 0:1]
        dy = sy - rows[:, 1:2]
        dz = sz - rows[:, 2:3]
        dist = dx * dx + dy * dy + dz * dz + 1.0
        return accum + rows[:, 3:4] * lax.rsqrt(dist)

    total = lax.fori_loop(0, count // 8, step, jnp.zeros((8, width), jnp.float32), unroll=4)
    out_ref[...] = jnp.sum(total, 0, keepdims=True)


def potential_terms(centers, mm_coords, mm_charges):
    total = centers.shape[1]
    count = mm_coords.shape[1]
    width = 1024 if total % 1024 == 0 else total
    points = jnp.concatenate([mm_coords, mm_charges[None]], 0).T
    return pl.pallas_call(
        potential_kernel,
        grid=(total // width,),
        out_shape=jax.ShapeDtypeStruct((1, total), jnp.float32),
        in_specs=[
            pl.BlockSpec((3, width), lambda i: (0, i)),
            pl.BlockSpec((count, 4), lambda i: (0, 0)),
        ],
        out_specs=pl.BlockSpec((1, width), lambda i: (0, i)),
        name="potential",
    )(centers, points)


def force_kernel(spots_ref, occ_ref, points_ref, out_ref):
    total = spots_ref.shape[1]
    rows = points_ref[...]
    px, py, pz, charge = (rows[:, k : k + 1] for k in range(4))
    count = rows.shape[0]

    def step(index, accum):
        lanes = pl.ds(pl.multiple_of(index * 128, 128), 128)
        dx = px - spots_ref[0:1, lanes]
        dy = py - spots_ref[1:2, lanes]
        dz = pz - spots_ref[2:3, lanes]
        inv = lax.rsqrt(dx * dx + dy * dy + dz * dz + 1.0)
        weight = occ_ref[:, lanes] * inv * (inv * inv)
        return (accum[0] + dx * weight, accum[1] + dy * weight, accum[2] + dz * weight)

    zero = jnp.zeros((count, 128), jnp.float32)
    sums = lax.fori_loop(0, total // 128, step, (zero, zero, zero), unroll=4)
    for k in range(3):
        out_ref[:, k : k + 1] = -charge * jnp.sum(sums[k], 1, keepdims=True)


def force_terms(centers, occupation, mm_coords, mm_charges):
    total = centers.shape[1]
    count = mm_coords.shape[1]
    width = 32
    points = jnp.concatenate([mm_coords, mm_charges[None]], 0).T
    summed = pl.pallas_call(
        force_kernel,
        grid=(count // width,),
        out_shape=jax.ShapeDtypeStruct((count, 4), jnp.float32),
        in_specs=[
            pl.BlockSpec((3, total), lambda i: (0, 0)),
            pl.BlockSpec((1, total), lambda i: (0, 0)),
            pl.BlockSpec((width, 4), lambda i: (i, 0)),
        ],
        out_specs=pl.BlockSpec((width, 4), lambda i: (i, 0)),
        name="forces",
    )(centers, occupation, points)
    return summed[:, :3].T


def butterfly_sum(value, sizes, axes=("rep", "col", "sec")):
    for axis in axes:
        size = sizes[axis]
        if size & (size - 1):
            value = lax.psum(value, axis)
            continue
        hop = 1
        while hop < size:
            value = value + lax.ppermute(value, axis, [(i, i ^ hop) for i in range(size)])
            hop *= 2
    return value


def fold_with(left, piece):
    return jnp.dot(left, piece, preferred_element_type=jnp.float32)


def gather_shards(sizes, h_core, centers, mm_coords, mm_charges):
    row_count, col_count = h_core.shape
    total = centers.shape[1]
    row_start = lax.axis_index("sec") * row_count
    col_start = lax.axis_index(("col", "rep")) * col_count
    rows_glob = row_start + lax.broadcasted_iota(jnp.int32, (row_count, col_count), 0)
    cols_glob = col_start + lax.broadcasted_iota(jnp.int32, (row_count, col_count), 1)
    on_diag = rows_glob == cols_glob
    off = jnp.where(on_diag, jnp.zeros((), h_core.dtype), h_core)
    row_panel = lax.all_gather(off, ("col", "rep"), axis=1, tiled=True)
    col_panel = lax.all_gather(off, "sec", axis=0, tiled=True)

    wide = h_core.astype(jnp.float32)
    own_diag = jnp.sum(jnp.where(on_diag, wide, 0.0), 0)
    own_off = jnp.sum(jnp.where(on_diag, 0.0, wide * wide))
    terms = potential_terms(centers, mm_coords, mm_charges)[0]
    own_cols = lax.dynamic_slice_in_dim(terms, col_start, col_count, 0) + own_diag
    terms = lax.dynamic_update_slice_in_dim(terms, own_cols, col_start, 0)
    sums = butterfly_sum(jnp.concatenate([terms, jnp.full((128,), own_off)]), sizes)
    diag_vals, off_total = sums[:total], sums[total]
    mean_level = jnp.sum(diag_vals) / total
    level = diag_vals - mean_level
    spread = jnp.sqrt((off_total + jnp.sum(level * level)) / total + 1e-05)
    gain = 1.0 / (3.0 * spread)

    level_rows = lax.dynamic_slice_in_dim(level, row_start, row_count, 0)[:, None]
    level_cols = lax.dynamic_slice_in_dim(level, col_start, col_count, 0)[None, :]
    off_wide = off.astype(jnp.float32)
    square = fold_with(row_panel, col_panel)
    square = square + off_wide * (level_rows + level_cols) + jnp.where(on_diag, level_rows * level_rows, 0.0)
    shifted = off_wide + jnp.where(on_diag, level_rows, 0.0)
    square_b = square.astype(jnp.bfloat16)
    square_panel = lax.all_gather(square_b, ("col", "rep"), axis=1, tiled=True)
    own_cube = jnp.sum(square * shifted, 0)
    cube_diag = lax.dynamic_update_slice_in_dim(jnp.zeros((total,), jnp.float32), own_cube, col_start, 0)
    cube_diag = butterfly_sum(cube_diag, sizes)
    occupation = 0.5 - 1.5 * gain * level + 2.0 * gain**3 * cube_diag
    forces = force_terms(centers, occupation[None], mm_coords, mm_charges)

    cube = fold_with(square_panel, col_panel) + square_b.astype(jnp.float32) * level_cols
    density = jnp.where(on_diag, 0.5, 0.0) - 1.5 * gain * shifted + 2.0 * gain**3 * cube
    return (density, forces)


ROUND = ((0, 1), (1, 2), (2, 3), (3, 0))
BACK = ((0, 3), (3, 2), (2, 1), (1, 0))
Z_MOVES = ((ROUND, BACK), (BACK, ROUND), (ROUND, BACK), (ROUND, BACK))
OWN0, OWN1, X1, Z1, X2, Z2, X3, Z3, X4, Z4 = range(10)
X_SENDS = ((OWN1, OWN0, OWN1, OWN0), (OWN0, OWN1, OWN0, OWN1), (Z2,) * 4, (Z3, Z1, Z1, Z3))
Z_SENDS = ((OWN0, OWN1, OWN0, OWN1), (OWN1, X1, X1, OWN0), (X2,) * 4, (Z3, Z1, Z1, Z3))
SLOT_STAGE = (0, 0, 0, 0, 1, 1, 2, 2, 3, 3)
LEFT_SLOTS = (OWN0, OWN1, X1, X2)
LEFT_STAGE = (0, 0, 0, 1)
FIELDS = 10
NOTHING, MULTIPLY, FINISH, LEVEL, SEND, ZERO = range(6)
BLOCK_BIT, LEFT_BIT = 0, 8


def block_places():
    chips = [(z, x) for z in range(4) for x in range(2)]
    held = {(z, x): [(z, 2 * x), (z, 2 * x + 1)] for z, x in chips}
    for step in range(4):
        arrived = {}
        for z, x in chips:
            before = next(start for start, to in Z_MOVES[step][x] if to == z)
            arrived[(z, x)] = [held[(z, 1 - x)][X_SENDS[step][z]], held[(before, x)][Z_SENDS[step][before]]]
        for chip in chips:
            held[chip] = held[chip] + arrived[chip]
    return [held[chip] for chip in chips]


def rows_of(products, length, lefts, ahead):
    seen, firsts = set(), []
    for kind, left, block, flip, total, column in products:
        bits = []
        if kind in (MULTIPLY, FINISH, LEVEL):
            loaded_left = block if kind == FINISH else left
            if loaded_left in lefts:
                bits.append(LEFT_BIT + loaded_left)
        if kind == MULTIPLY:
            bits.append(BLOCK_BIT + block)
        firsts.append([bit for bit in dict.fromkeys(bits) if bit not in seen])
        seen.update(bits)
    mask = lambda bits: sum(1 << bit for bit in bits)
    waves = [k for k, first in enumerate(firsts) if first]
    starts = [[] for _ in products]
    for number, k in enumerate(waves):
        at = 0 if number <= ahead else waves[number - ahead]
        starts[at] += firsts[k]
    rows = []
    for k, (kind, left, block, flip, total, column) in enumerate(products):
        rows.append([kind, left, block, flip, total, mask(firsts[k]), column, mask(starts[k]), 0, 0])
    return rows + [[NOTHING] + [0] * (FIELDS - 1)] * (length - len(rows))


def device_lists():
    devices = []
    for chip, slots in enumerate(block_places()):
        assert len({tuple(sorted(place)) for place in slots}) == 10
        row, col = divmod(chip, 2)
        assert all(slots[s][0] == row for s in LEFT_SLOTS)
        lefts = [slots[s][1] for s in LEFT_SLOTS]
        stages = [[], [], [], []]
        for slot, (first, second) in enumerate(slots):
            for inner, outer, flip in [(first, second, 0), (second, first, 1)][: 1 if first == second else 2]:
                left = lefts.index(inner)
                stage = max(LEFT_STAGE[left], SLOT_STAGE[slot])
                base = (0, 0, X3, X4)[stage]
                key = max(slot, LEFT_SLOTS[left])
                stages[stage].append((key, (MULTIPLY, left, slot - base, flip, outer, 0)))
        stages = [[product for _, product in sorted(stage)] for stage in stages]
        first, touched = [], set()
        for product in stages[0]:
            if product[4] not in touched:
                first.append((ZERO, 0, 0, 0, product[4], 0))
            touched.add(product[4])
            first.append(product)
        first += [(ZERO, 0, 0, 0, total, 0) for total in range(4) if total not in touched]
        open_columns = sorted({product[4] for product in stages[3]})
        done_columns = [column for column in range(4) if column not in open_columns]
        assert len(open_columns) == 2

        def find(inner, outer):
            if (inner, outer) in slots:
                return slots.index((inner, outer)), 0
            return slots.index((outer, inner)), 1

        for core in range(2):
            early, early_slots = list(stages[2]), []
            early += [(ZERO, 0, 0, 0, 4 + which, 0) for which in range(2)]
            for k, column in enumerate(done_columns):
                early.append((FINISH, 4 + k, lefts.index(column), int(column == row), column, column))
            for which in range(2):
                for k, column in enumerate(done_columns):
                    slot, flip = find(column, 2 * col + which)
                    early.append((MULTIPLY, 4 + k, 2 + len(early_slots), flip, 4 + which, 0))
                    early_slots.append(slot)
                    if column == 2 * col + which:
                        early.append((LEVEL, 4 + k, 0, 0, 4 + which, column))
            late, late_slots = [], []
            for product in stages[3]:
                left = open_columns.index(lefts[product[1]])
                late.append((MULTIPLY, left) + product[2:])
            for k, column in enumerate(open_columns):
                late.append((FINISH, 2 + k, k, int(column == row), column, column))
            for k, which in enumerate((1 - core, core)):
                for m, column in enumerate(open_columns):
                    slot, flip = find(column, 2 * col + which)
                    late.append((MULTIPLY, 2 + m, 2 + len(late_slots), flip, 4 + which, 0))
                    late_slots.append(slot)
                    if column == 2 * col + which:
                        late.append((LEVEL, 2 + m, 0, 0, 4 + which, column))
                if k == 0:
                    late.append((SEND, 0, 0, 0, 4 + which, 0))
            own_rows = lambda slot: int(slot != core)
            second = Z_SENDS[1][row]
            info = [
                core, row, col, core * 640,
                own_rows(X_SENDS[0][row]), own_rows(Z_SENDS[0][row]), own_rows(X_SENDS[1][row]), 0,
                2 if second == X1 else own_rows(second), int(X_SENDS[3][row] == Z3),
            ] + [lefts.index(column) for column in open_columns] + open_columns
            devices.append(
                dict(
                    kernels=[first, stages[1], early, late],
                    slots=[early_slots, late_slots],
                    info=info,
                )
            )
    return devices


CORE, ROW, COL, FIRST_ROW, SEND_X1, SEND_Z1, SEND_X2, NEAR, SEND_Z2, SEND_LAST, OPEN_LEFT, OPEN = (*range(11), 12)


def device_tables(half):
    devices = device_lists()
    steps, rows = [], [[] for _ in devices]
    for kernel, (lefts, ahead) in enumerate((((0, 1, 2), 2), (range(4), 2), (range(4), 2), ((0, 1), 1))):
        length = max(len(device["kernels"][kernel]) for device in devices)
        steps.append((len(rows[0]), length))
        for row, device in zip(rows, devices):
            for fields in rows_of(device["kernels"][kernel], length, lefts, ahead):
                row += fields
    slots = []
    for kernel in range(2):
        slots.append(len(rows[0]))
        for row, device in zip(rows, devices):
            row += device["slots"][kernel]
    for device in devices:
        device["info"][FIRST_ROW] = device["info"][CORE] * half
    return [device["info"] for device in devices], rows, steps, slots


def bit_set(mask, bit):
    return jnp.bitwise_and(mask, jnp.int32(1 << bit)) != 0


class Worker:
    def __init__(self, table_ref, core, half, block_ref, block_sem, left_ref, left_sem, total_ref):
        self.table_ref, self.core, self.half = table_ref, core, half
        self.block_ref, self.block_sem = block_ref, block_sem
        self.left_ref, self.left_sem = left_ref, left_sem
        self.total_ref = total_ref
        self.near = pl.ds(pl.multiple_of(core * half, half), half)
        self.far = pl.ds(pl.multiple_of((1 - core) * half, half), half)
        self.blocks, self.lefts, self.send = {}, {}, None
        self.levels = None

    def load_halves(self, position, near_ref, far_ref):
        pltpu.make_async_copy(near_ref, self.block_ref.at[position, self.near], self.block_sem.at[position, 0]).start()
        pltpu.make_async_copy(far_ref, self.block_ref.at[position, self.far], self.block_sem.at[position, 1]).start()

    def load_block(self, position, slot, sources):
        self.blocks[position] = functools.partial(self.start_block, position, slot, sources)

    def start_block(self, position, slot, sources):
        fixed = isinstance(slot, int)
        if "own" in sources and (not fixed or slot <= OWN1):
            for at, ref in zip((self.core, 1 - self.core), sources["own"]):
                @pl.when(slot == at)
                def _():
                    self.load_halves(position, ref.at[self.near], ref.at[self.far])

        if not fixed:
            for number, halves in sources.items():
                if number != "own":
                    pl.when(slot == number)(functools.partial(self.load_halves, position, *halves))
        elif slot > OWN1:
            self.load_halves(position, *sources[slot])

    def left_places(self, refs):
        own = [(self.core, refs[0].at[self.near]), (1 - self.core, refs[1].at[self.near])]
        return own + list(enumerate(refs))[2:]

    def load_left(self, index, number, refs):
        self.lefts[index] = functools.partial(self.start_left, index, number, refs)

    def start_left(self, index, number, refs):
        for at, ref in self.left_places(refs):
            if isinstance(at, int) and isinstance(number, int):
                if at == number:
                    self.copy_left(index, ref)
            else:
                pl.when(at == number)(functools.partial(self.copy_left, index, ref))

    def copy_left(self, index, ref):
        pltpu.make_async_copy(ref, self.left_ref.at[index], self.left_sem.at[index]).start()

    def load_rows(self, refs):
        for k in range(len(refs)):
            self.load_left(k, k, refs)

    def start(self, mask):
        for base, loads in ((LEFT_BIT, self.lefts), (BLOCK_BIT, self.blocks)):
            for index, load in loads.items():
                pl.when(bit_set(mask, base + index))(load)

    def wait(self, mask):
        half_block = self.block_ref.at[0, pl.ds(0, self.half)]
        for position in self.blocks:
            @pl.when(bit_set(mask, BLOCK_BIT + position))
            def _():
                for part in range(2):
                    pltpu.make_async_copy(half_block, half_block, self.block_sem.at[position, part]).wait()
        for index in self.lefts:
            @pl.when(bit_set(mask, LEFT_BIT + index))
            def _():
                pltpu.make_async_copy(self.left_ref.at[0], self.left_ref.at[0], self.left_sem.at[index]).wait()

    def multiply(self, field):
        total, left, block = self.total_ref.at[field[4]], self.left_ref.at[field[1]], self.block_ref.at[field[2]]

        @pl.when(field[3] == 0)
        def _():
            total[...] += jnp.dot(left[...], block[...], preferred_element_type=jnp.float32)

        @pl.when(field[3] == 1)
        def _():
            total[...] += lax.dot_general(
                left[...], block[...], (((1,), (1,)), ((), ())), preferred_element_type=jnp.float32
            )

    def tiles(self, cols_ref, column):
        width = self.block_ref.shape[2]
        base = column * width
        return [
            jnp.broadcast_to(cols_ref[:, pl.ds(pl.multiple_of(base + m * 128, 128), 128)], (16, 128))
            for m in range(width // 128)
        ]

    def finish(self, field):
        rows_ref, cols_ref, diag_ref = self.levels
        half = self.half
        total, left, made = self.total_ref.at[field[4]], self.left_ref.at[field[2]], self.left_ref.at[field[1]]
        cols = self.tiles(cols_ref, field[6])

        def one(index, carry):
            rows = pl.ds(pl.multiple_of(index * 16, 16), 16)
            level = rows_ref[rows, :]
            share = jnp.zeros((16, 128), jnp.float32)
            for m, col in enumerate(cols):
                at = slice(m * 128, (m + 1) * 128)
                ham = left[rows, at].astype(jnp.float32)
                square = total[rows, at] + ham * (level + col)
                made[rows, at] = square.astype(jnp.bfloat16)
                share = share + square * ham
            diag_ref[rows, :] += share
            return carry

        lax.fori_loop(0, half // 16, one, 0, unroll=2)

        @pl.when(field[3] == 1)
        def _():
            eye = lax.broadcasted_iota(jnp.int32, (128, 128), 0) == lax.broadcasted_iota(jnp.int32, (128, 128), 1)

            def fix(index, carry):
                rows = pl.ds(pl.multiple_of(index * 128, 128), 128)
                at = pl.ds(pl.multiple_of(self.core * half + index * 128, 128), 128)
                col = cols_ref[:, pl.ds(pl.multiple_of(field[6] * (2 * half) + self.core * half + index * 128, 128), 128)]
                level = rows_ref[rows, :]
                ham = left[rows, at].astype(jnp.float32)
                square = total[rows, at] + ham * (level + col)
                full = square + jnp.where(eye, level * level, 0.0)
                made[rows, at] = full.astype(jnp.bfloat16)
                diag_ref[rows, :] += jnp.where(eye, full * (ham + level) - square * ham, 0.0)
                return carry

            lax.fori_loop(0, half // 128, fix, 0)

    def add_level(self, field):
        cols = self.tiles(self.levels[1], field[6])
        total, left = self.total_ref.at[field[4]], self.left_ref.at[field[1]]

        def one(index, carry):
            rows = pl.ds(pl.multiple_of(index * 16, 16), 16)
            for m, col in enumerate(cols):
                at = slice(m * 128, (m + 1) * 128)
                total[rows, at] += left[rows, at].astype(jnp.float32) * col
            return carry

        lax.fori_loop(0, self.half // 16, one, 0, unroll=2)

    def clear(self, field):
        self.total_ref[field[4]] = jnp.zeros_like(self.total_ref[0])

    def run(self, start_count):
        start, count = start_count
        works = [(MULTIPLY, self.multiply), (ZERO, self.clear)]
        if self.levels is not None:
            works += [(FINISH, self.finish), (LEVEL, self.add_level)]
        if self.send is not None:
            works.append((SEND, self.send))

        def step(index, carry):
            field = [self.table_ref[start + index * FIELDS + k] for k in range(8)]
            pl.when(field[7] != 0)(functools.partial(self.start, field[7]))
            pl.when(field[5] != 0)(functools.partial(self.wait, field[5]))
            for kind, work in works:
                pl.when(field[0] == kind)(functools.partial(work, field))
            return carry

        lax.fori_loop(0, count, step, 0)


def square_kernel(first, steps, left_count, slots, table_ref, info_ref, *refs):
    refs = list(refs)
    row_refs = [refs.pop(0) for _ in range(left_count)]
    sources = {"own": [refs.pop(0) for _ in range(2)]}
    for slot in slots:
        if slot > OWN1:
            sources[slot] = (refs.pop(0), refs.pop(0))
    refs = refs[0 if first else 2 :]
    total_ref, token_ref, block_ref, block_sem, left_ref, left_sem = refs
    half = left_ref.shape[1]
    worker = Worker(table_ref, info_ref[CORE], half, block_ref, block_sem, left_ref, left_sem, total_ref)
    worker.load_rows(row_refs)
    for position, slot in enumerate(slots):
        worker.load_block(position, slot, sources)
    worker.run(steps)
    token_ref[...] = jnp.zeros_like(token_ref)


def early_kernel(steps, slots_at, table_ref, info_ref, *refs):
    refs = list(refs)
    row_refs = [refs.pop(0) for _ in range(4)]
    sources = {"own": [refs.pop(0) for _ in range(2)]}
    for slot in range(X1, Z3 + 1):
        sources[slot] = (refs.pop(0), refs.pop(0))
    _, _, level_rows_ref, level_ref, total_ref, diag_ref = (refs.pop(0) for _ in range(6))
    block_ref, block_sem, left_ref, left_sem = refs
    half = left_ref.shape[1]
    worker = Worker(table_ref, info_ref[CORE], half, block_ref, block_sem, left_ref, left_sem, total_ref)
    worker.levels = (level_rows_ref, level_ref, diag_ref)
    worker.load_rows(row_refs)
    worker.load_block(0, X3, sources)
    worker.load_block(1, Z3, sources)
    for k in range(4):
        worker.load_block(2 + k, table_ref[slots_at + k], sources)
    diag_ref[...] = jnp.zeros_like(diag_ref)
    worker.run(steps)


def late_kernel(steps, slots_at, table_ref, info_ref, gain_ref, *refs):
    refs = list(refs)
    row_refs = [refs.pop(0) for _ in range(4)]
    sources = {"own": [refs.pop(0) for _ in range(2)]}
    for slot in range(X1, Z4 + 1):
        sources[slot] = (refs.pop(0), refs.pop(0))
    _, old_diag_ref, level_rows_ref, level_ref, total_ref, cube_ref, density_ref, diag_ref = (
        refs.pop(0) for _ in range(8)
    )
    block_ref, block_sem, left_ref, left_sem, out_sem, sent_ref, ham_ref, ham_sem = refs
    half, width = left_ref.shape[1:]
    core, row, col = info_ref[CORE], info_ref[ROW], info_ref[COL]
    worker = Worker(table_ref, core, half, block_ref, block_sem, left_ref, left_sem, total_ref)
    worker.levels = (level_rows_ref, level_ref, diag_ref)
    worker.load_block(0, X4, sources)
    worker.load_block(1, Z4, sources)
    for k in range(2):
        worker.load_left(k, info_ref[OPEN_LEFT + k], row_refs)
    for k in range(4):
        worker.load_block(2 + k, table_ref[slots_at + k], sources)
    ham_copy = pltpu.make_async_copy(row_refs[0].at[worker.near], ham_ref, ham_sem)
    sent_copy = pltpu.make_async_copy(sent_ref, cube_ref, out_sem.at[0])
    density_copy = pltpu.make_async_copy(total_ref.at[4 + core], density_ref.at[worker.near], out_sem.at[1])

    def send(field):
        sent_ref[...] = total_ref[field[4]].astype(sent_ref.dtype)
        sent_copy.start()
        ham_copy.start()

    worker.send = send
    diag_ref[...] = old_diag_ref[...]
    worker.run(steps)
    ham_copy.wait()
    gain = gain_ref[0]
    linear, cubic = -1.5 * gain, 2.0 * (gain * gain * gain)

    def one(index, carry):
        rows = pl.ds(pl.multiple_of(index * 16, 16), 16)
        for m in range(width // 128):
            at = slice(m * 128, (m + 1) * 128)
            cube = total_ref[4 + core, rows, at]
            total_ref[4 + core, rows, at] = linear * ham_ref[rows, at].astype(jnp.float32) + cubic * cube
        return carry

    lax.fori_loop(0, half // 16, one, 0, unroll=2)

    @pl.when(row == 2 * col + core)
    def _():
        eye = lax.broadcasted_iota(jnp.int32, (128, 128), 0) == lax.broadcasted_iota(jnp.int32, (128, 128), 1)

        def fix(index, carry):
            rows = pl.ds(pl.multiple_of(index * 128, 128), 128)
            at = pl.ds(pl.multiple_of(core * half + index * 128, 128), 128)
            total_ref[4 + core, rows, at] += jnp.where(eye, 0.5 + linear * level_rows_ref[rows, :], 0.0)
            return carry

        lax.fori_loop(0, half // 128, fix, 0)

    density_copy.start()
    sent_copy.wait()
    density_copy.wait()


HERE = pl.BlockSpec(memory_space=pltpu.HBM)
SCALARS = pl.BlockSpec(memory_space=pltpu.SMEM)
VMEM = pl.BlockSpec(memory_space=pltpu.VMEM)
VMEM_BYTES = 38 * 2**20


def in_hbm(values):
    return [pltpu.with_memory_space_constraint(value, pltpu.HBM) for value in values]


def work_scratch(half, width, blocks, lefts):
    return [
        pltpu.VMEM((blocks, 2 * half, width), jnp.bfloat16),
        pltpu.SemaphoreType.DMA((blocks, 2)),
        pltpu.VMEM((lefts, half, width), jnp.bfloat16),
        pltpu.SemaphoreType.DMA((lefts,)),
    ]


def call_kernel(name, kernel, shape, scalars, operands, totals, in_vmem, out_shape, out_specs, scratch):
    first = len(scalars) + len(operands)
    held = [] if totals is None else [pltpu.with_memory_space_constraint(totals, pltpu.VMEM)]
    return pl.pallas_call(
        kernel,
        out_shape=(pltpu.VMEM((6,) + shape, jnp.float32),) + tuple(out_shape),
        in_specs=[SCALARS] * len(scalars) + [HERE] * len(operands) + [VMEM] * (len(held) + len(in_vmem)),
        out_specs=(VMEM,) + tuple(out_specs),
        scratch_shapes=scratch,
        input_output_aliases={first: 0} if held else {},
        compiler_params=pltpu.CompilerParams(vmem_limit_bytes=VMEM_BYTES),
        name=name,
    )(*scalars, *in_hbm(operands), *held, *in_vmem)


def pick_kernel(choices, whole, count, info_ref, *refs):
    sources, refs = refs[:count], refs[count:]
    outs, held_ref, in_sem, out_sem = refs[:-3], refs[-3], refs[-2], refs[-1]
    parts = in_sem.shape[1]
    size = held_ref.shape[1] // parts
    for part in range(parts):
        for k, choice in enumerate(choices):
            to = held_ref.at[k, pl.ds(part * size, size)]
            for number, source in enumerate(sources):
                @pl.when(info_ref[choice] == number)
                def _():
                    first = part * size
                    if number < whole:
                        first = pl.multiple_of(info_ref[FIRST_ROW] + first, size)
                    pltpu.make_async_copy(source.at[pl.ds(first, size)], to, in_sem.at[k, part]).start()
    for part in range(parts):
        for k, out_ref in enumerate(outs):
            rows = pl.ds(part * size, size)
            pltpu.make_async_copy(held_ref.at[k, rows], held_ref.at[k, rows], in_sem.at[k, part]).wait()
            pltpu.make_async_copy(held_ref.at[k, rows], out_ref.at[rows], out_sem.at[k, part]).start()
    for part in range(parts):
        for k, out_ref in enumerate(outs):
            rows = pl.ds(part * size, size)
            pltpu.make_async_copy(held_ref.at[k, rows], out_ref.at[rows], out_sem.at[k, part]).wait()


def pick(info, choices, sources, whole, shape):
    dtype = sources[0].dtype
    parts = 4
    return pl.pallas_call(
        functools.partial(pick_kernel, choices, whole, len(sources)),
        out_shape=[jax.ShapeDtypeStruct(shape, dtype)] * len(choices),
        in_specs=[SCALARS] + [HERE] * len(sources),
        out_specs=[HERE] * len(choices),
        scratch_shapes=[
            pltpu.VMEM((len(choices),) + shape, dtype),
            pltpu.SemaphoreType.DMA((len(choices), parts)),
            pltpu.SemaphoreType.DMA((len(choices), parts)),
        ],
        compiler_params=pltpu.CompilerParams(vmem_limit_bytes=VMEM_BYTES),
        name="pick",
    )(info, *in_hbm(sources))


def pairs_kernel(spots_ref, points_ref, out_ref, high_ref, low_ref, wide_ref):
    count, width = points_ref.shape[0], spots_ref.shape[1]
    tiles = width // 128

    @pl.when(pl.program_id(0) == 0)
    def _():
        for k in range(4):
            wide_ref[k] = jnp.broadcast_to(points_ref[:, k : k + 1], (count, 128))

    lanes = [slice(m * 128, (m + 1) * 128) for m in range(tiles)]
    spots = [[jnp.broadcast_to(spots_ref[k : k + 1, at], (16, 128)) for k in range(3)] for at in lanes]

    def step(group, sums):
        rows = pl.ds(pl.multiple_of(group * 16, 16), 16)
        px, py, pz, charge = (wide_ref[k, rows, :] for k in range(4))
        sums = list(sums)
        for m, at in enumerate(lanes):
            dx, dy, dz = spots[m][0] - px, spots[m][1] - py, spots[m][2] - pz
            inv = lax.rsqrt(dx * dx + dy * dy + dz * dz + 1.0)
            sums[m] = sums[m] + charge * inv
            weight = inv * (inv * inv)
            high = weight.astype(jnp.bfloat16)
            high_ref[rows, at] = high
            low_ref[rows, at] = (weight - high.astype(jnp.float32)).astype(jnp.bfloat16)
        return tuple(sums)

    zeros = tuple(jnp.zeros((16, 128), jnp.float32) for _ in range(tiles))
    sums = lax.fori_loop(0, count // 16, step, zeros, unroll=2)
    for m, at in enumerate(lanes):
        out_ref[:, at] = jnp.sum(sums[m], 0, keepdims=True)


def pair_terms(centers, points):
    total, count = centers.shape[1], points.shape[0]
    width = 512
    part = jax.ShapeDtypeStruct((count, total), jnp.bfloat16)
    return pl.pallas_call(
        pairs_kernel,
        grid=(total // width,),
        out_shape=(jax.ShapeDtypeStruct((1, total), jnp.float32), part, part),
        in_specs=[pl.BlockSpec((3, width), lambda i: (0, i)), pl.BlockSpec((count, 4), lambda i: (0, 0))],
        out_specs=[pl.BlockSpec((1, width), lambda i: (0, i))] + [pl.BlockSpec((count, width), lambda i: (0, i))] * 2,
        scratch_shapes=[pltpu.VMEM((4, count, 128), jnp.float32)],
        compiler_params=pltpu.CompilerParams(vmem_limit_bytes=VMEM_BYTES),
        name="pairs",
    )(centers, points)


MIDDLE = 10.0


def pull_kernel(spots_ref, occ_ref, high_ref, low_ref, coords_ref, charge_ref, out_ref, total_ref):
    index = pl.program_id(0)
    occ = occ_ref[...]
    weights = [occ] + [occ * (spots_ref[k : k + 1, :] - MIDDLE) for k in range(3)]
    width = occ.shape[1]
    stacked = jnp.concatenate(weights + [jnp.zeros((4, width), jnp.float32)], 0)
    high = stacked.astype(jnp.bfloat16)
    low = (stacked - high.astype(jnp.float32)).astype(jnp.bfloat16)
    blank = jnp.zeros((128 - 16, width), jnp.bfloat16)
    both = jnp.concatenate([high, low, blank], 0)
    first = jnp.concatenate([high, jnp.zeros_like(low), blank], 0)
    dims = (((1,), (1,)), ((), ()))
    part = lax.dot_general(high_ref[...], both, dims, preferred_element_type=jnp.float32)
    part = part + lax.dot_general(low_ref[...], first, dims, preferred_element_type=jnp.float32)

    @pl.when(index == 0)
    def _():
        total_ref[...] = part

    @pl.when(index > 0)
    def _():
        total_ref[...] += part

    @pl.when(index == pl.num_programs(0) - 1)
    def _():
        sums = total_ref[...].T
        sums = sums[0:8] + sums[8:16]
        for k in range(3):
            pull = (coords_ref[k : k + 1, :] - MIDDLE) * sums[0:1] - sums[k + 1 : k + 2]
            out_ref[k : k + 1, :] = -charge_ref[...] * pull


def pull_terms(centers, occupation, high, low, mm_coords, mm_charges):
    total, count = centers.shape[1], mm_coords.shape[1]
    width = 1024
    return pl.pallas_call(
        pull_kernel,
        grid=(total // width,),
        out_shape=jax.ShapeDtypeStruct((3, count), jnp.float32),
        in_specs=[
            pl.BlockSpec((3, width), lambda i: (0, i)),
            pl.BlockSpec((1, width), lambda i: (0, i)),
            pl.BlockSpec((count, width), lambda i: (0, i)),
            pl.BlockSpec((count, width), lambda i: (0, i)),
            pl.BlockSpec((3, count), lambda i: (0, 0)),
            pl.BlockSpec((1, count), lambda i: (0, 0)),
        ],
        out_specs=pl.BlockSpec((3, count), lambda i: (0, 0)),
        scratch_shapes=[pltpu.VMEM((count, 128), jnp.float32)],
        name="pull",
    )(centers, occupation, high, low, mm_coords, mm_charges[None])


def density_kernel(steps, info_ref, gain_ref, ham_ref, far_ref, level_ref, _, out_ref):
    index = pl.program_id(0)
    core, row, col = info_ref[CORE], info_ref[ROW], info_ref[COL]
    gain = gain_ref[0]
    height, width = out_ref.shape
    linear, cubic = -1.5 * gain, 2.0 * (gain * gain * gain)
    first = ((1 - core) * steps + index) * height

    def one(k, carry):
        rows = pl.ds(pl.multiple_of(k * 16, 16), 16)
        for m in range(width // 128):
            at = slice(m * 128, (m + 1) * 128)
            cube = far_ref[rows, at].astype(jnp.float32)
            out_ref[rows, at] = linear * ham_ref[rows, at].astype(jnp.float32) + cubic * cube
        return carry

    lax.fori_loop(0, height // 16, one, 0, unroll=2)

    @pl.when(row == 2 * col + core)
    def _():
        eye = lax.broadcasted_iota(jnp.int32, (128, 128), 0) == lax.broadcasted_iota(jnp.int32, (128, 128), 1)

        def fix(k, carry):
            rows = pl.ds(pl.multiple_of(k * 128, 128), 128)
            at = pl.ds(pl.multiple_of(first + k * 128, 128), 128)
            out_ref[rows, at] += jnp.where(eye, 0.5 + linear * level_ref[:, at], 0.0)
            return carry

        lax.fori_loop(0, height // 128, fix, 0)


def density_rest(info, gain, ham, far, level_cols, density):
    height, width = ham.shape
    steps = 1
    chunk = far.shape[0] // steps
    return pl.pallas_call(
        functools.partial(density_kernel, steps),
        grid_spec=pltpu.PrefetchScalarGridSpec(
            num_scalar_prefetch=1,
            grid=(steps,),
            in_specs=[
                SCALARS,
                pl.BlockSpec((chunk, width), lambda i, info: ((1 - info[CORE]) * steps + i, 0)),
                pl.BlockSpec((chunk, width), lambda i, info: (i, 0)),
                pl.BlockSpec((1, width), lambda i, info: (0, 0)),
                HERE,
            ],
            out_specs=pl.BlockSpec((chunk, width), lambda i, info: ((1 - info[CORE]) * steps + i, 0)),
        ),
        out_shape=jax.ShapeDtypeStruct((height, width), jnp.float32),
        input_output_aliases={5: 0},
        compiler_params=pltpu.CompilerParams(vmem_limit_bytes=VMEM_BYTES),
        name="density",
    )(info, gain, ham, far, level_cols, density)


def gossip_shards(sizes, h_core, centers, mm_coords, mm_charges):
    height, width = h_core.shape
    half = height // 2
    total, count = centers.shape[1], mm_coords.shape[1]
    row, col, core = (lax.axis_index(name) for name in ("sec", "col", "rep"))
    row_start = row * height
    col_start = (2 * col + core) * width
    infos, rows, steps, slots_at = device_tables(half)
    device = 4 * row + 2 * col + core
    info, table = (
        lax.dynamic_index_in_dim(jnp.asarray(values, jnp.int32), device, 0, keepdims=False) for values in (infos, rows)
    )

    def over_rep(value):
        return lax.ppermute(value, "rep", [(0, 1), (1, 0)])

    def over_col(value):
        return lax.ppermute(value, "col", [(0, 1), (1, 0)])

    def over_sec(value, step):
        moves = [(2 * start + x, 2 * to + x) for x in range(2) for start, to in Z_MOVES[step][x]]
        return lax.ppermute(value, ("sec", "col"), moves)

    def swap_all(values):
        return [(value, over_rep(value)) for value in values]

    def flat(groups):
        return [value for group in groups for value in group]

    def after(arrived, work):
        return lax.optimization_barrier((arrived, work))

    shape = (half, width)
    own_parts = (h_core, over_rep(h_core))
    sends = pick(info, (SEND_X1, SEND_Z1), own_parts, 2, shape)
    x1 = over_col(sends[0])
    z1 = over_sec(sends[1], 0)
    points = jnp.concatenate([mm_coords, mm_charges[None]], 0).T
    terms, high, low = pair_terms(centers, points)
    rows_glob = row_start + lax.broadcasted_iota(jnp.int32, (height, width), 0)
    cols_glob = col_start + lax.broadcasted_iota(jnp.int32, (height, width), 1)
    on_diag = rows_glob == cols_glob
    wide = h_core.astype(jnp.float32)
    own_diag = jnp.sum(jnp.where(on_diag, wide, 0.0), 0)
    own_off = jnp.sum(jnp.where(on_diag, 0.0, wide * wide))
    diag = lax.dynamic_update_slice_in_dim(jnp.zeros((total,), jnp.float32), own_diag, col_start, 0)
    packed = jnp.concatenate([terms[0], diag, jnp.full((128,), own_off)])
    packed = packed + over_rep(packed)
    (x1, z1), (packed, high, low, table) = after((x1, z1), (packed, high, low, table))
    sends = pick(info, (SEND_X2, SEND_Z2), own_parts + (x1,), 2, shape)
    x2 = over_col(sends[0])
    z2 = over_sec(sends[1], 1)
    pairs = dict(zip((X1, Z1), swap_all((x1, z1))))

    def grow_square(stage, lefts, slots, totals, token):
        operands = list(lefts) + list(own_parts) + flat(pairs[slot] for slot in slots)
        operands += [] if token is None else [token]
        kernel = functools.partial(square_kernel, totals is None, steps[stage], len(lefts), (OWN0, OWN1) + slots)
        return call_kernel(
            f"square_{stage}", kernel, shape, (table, info), operands, totals, (),
            (jax.ShapeDtypeStruct((8, 128), jnp.float32),), (VMEM,), work_scratch(half, width, 2 + len(slots), 4),
        )

    lefts = list(own_parts) + [x1]
    totals, token = grow_square(0, lefts, (X1, Z1), None, None)
    col_packed = over_col(packed)
    (x2, z2, col_packed), (token, packed) = after((x2, z2, col_packed), (token, packed))
    x3 = over_col(z2)
    z3 = over_sec(x2, 2)
    pairs.update(zip((X2, Z2), swap_all((x2, z2))))
    lefts.append(x2)
    totals, token = grow_square(1, lefts, (X1, Z1, X2, Z2), totals, token)
    packed = packed + col_packed
    others = [lax.ppermute(packed, "sec", [(i, (i + hop) % 4) for i in range(4)]) for hop in (1, 2, 3)]
    (x3, z3, others), (token, packed) = after((x3, z3, others), (token, packed))
    last_send = pick(info, (SEND_LAST,), (z1, z3), 0, shape)[0]
    x4 = over_col(last_send)
    z4 = over_sec(last_send, 3)
    pairs.update(zip((X3, Z3), swap_all((x3, z3))))
    sums = packed + others[0] + others[1] + others[2]
    potential, diag, off_total = sums[:total], sums[total : 2 * total], sums[2 * total]
    diag_vals = potential + diag
    mean_level = jnp.sum(diag_vals) / total
    above = diag_vals - mean_level
    level = potential - mean_level
    spread = jnp.sqrt((off_total + jnp.sum(above * above)) / total + 1e-05)
    gain = 1.0 / (3.0 * spread)
    level_rows = lax.dynamic_slice_in_dim(level, row_start + core * half, half, 0)
    level_rows = jnp.broadcast_to(level_rows[:, None], (half, 128))
    level_cols = lax.dynamic_slice_in_dim(level, col_start, width, 0)[None]
    share = jax.ShapeDtypeStruct((half, 128), jnp.float32)
    totals, cube_diag = call_kernel(
        "early_cube", functools.partial(early_kernel, steps[2], slots_at[0]), shape, (table, info),
        lefts + list(own_parts) + flat(pairs[slot] for slot in range(X1, Z3 + 1)) + [token], totals, (level_rows, level[None]),
        (share,), (VMEM,), work_scratch(half, width, 6, 6),
    )
    (x4, z4), (cube_diag, above, level_rows, level, level_cols, gain) = after(
        (x4, z4), (cube_diag, above, level_rows, level, level_cols, gain)
    )
    pairs.update(zip((X4, Z4), swap_all((x4, z4))))
    blocks = list(own_parts) + flat(pairs[slot] for slot in range(X1, Z4 + 1))
    _, sibling, density, cube_diag = call_kernel(
        "late_cube", functools.partial(late_kernel, steps[3], slots_at[1]), shape, (table, info, gain[None]),
        lefts + blocks, totals, (cube_diag, level_rows, level[None]),
        (jax.ShapeDtypeStruct(shape, jnp.bfloat16), jax.ShapeDtypeStruct((height, width), jnp.float32), share),
        (HERE, HERE, VMEM),
        work_scratch(half, width, 6, 4)
        + [
            pltpu.SemaphoreType.DMA((2,)),
            pltpu.VMEM(shape, jnp.bfloat16),
            pltpu.VMEM(shape, jnp.bfloat16),
            pltpu.SemaphoreType.DMA,
        ],
    )
    sibling = over_rep(sibling)
    cube_diag = lax.dynamic_update_slice_in_dim(
        jnp.zeros((total,), jnp.float32), jnp.sum(cube_diag, 1), row_start + core * half, 0
    )
    cube_diag = cube_diag + over_rep(cube_diag)
    others = [lax.ppermute(cube_diag, "sec", [(i, (i + hop) % 4) for i in range(4)]) for hop in (1, 2, 3)]
    density = density_rest(info, gain[None], h_core, sibling, level_cols, density)
    others, density = after(others, density)
    cube_diag = cube_diag + others[0] + others[1] + others[2]
    occupation = 0.5 - 1.5 * gain * above + 2.0 * gain**3 * cube_diag
    forces = pull_terms(centers, occupation[None], high, low, mm_coords, mm_charges)
    return (density, forces)


def solution(mesh):
    in_specs = (
        P(("groups", "sec"), ("col", "rep")),
        P(None, "groups"),
        P(None, ("groups", "sec", "col", "rep")),
        P(("groups", "sec", "col", "rep")),
    )
    out_specs = (P(("groups", "sec"), ("col", "rep")), P(None, ("groups", "sec", "col", "rep")))
    sizes = dict(mesh.shape)
    small = (sizes["sec"], sizes["col"], sizes["rep"]) == (4, 2, 2)
    body = functools.partial(gossip_shards if small else gather_shards, sizes)
    return jax.shard_map(body, mesh=mesh, in_specs=in_specs, out_specs=out_specs, check_vma=False)
```

time: 271 us -> 245 us (0.904)
  Pallas kernels: 169 us -> 122 us
  waiting for transfers between devices: 42.7 us -> 53 us
  local copies, waits for them, and re-layouts: 17 us -> 26.5 us
  starting transfers between devices: 25.9 us -> 31.3 us
  between operations: 6.89 us -> 2.81 us
    pallas_call x10 -> x9, Pallas kernels: 162 us -> 114 us  [the longest x4 91.8 us: call_kernel(): pl.pallas_call(kernel, out_shape=(pltpu.VMEM((6,) + shape, jnp.float32),)...]
    unnamed x32 -> x42, local copies, waits for them, and re-layouts: 4.83 us -> 21.5 us
    ppermute x12, waiting for transfers between devices: 5.72 us -> 13.1 us  [over_rep(): return lax.ppermute(value, 'rep', [(0, 1), (1, 0)])]
    dynamic_slice x7 -> x2, local copies, waits for them, and re-layouts: 6.43 us -> 1.34 us  [the longest x1 1.26 us: gossip_shards(): lax.dynamic_index_in_dim(jnp.asarray(values, jnp.int32), device, 0, keepd...]
    ppermute x3, waiting for transfers between devices: 8.39 us -> 12.6 us  [gossip_shards(): lax.ppermute(packed, 'sec', [(i, (i + hop) % 4) for i in range(4)])]
    ppermute x3, waiting for transfers between devices: 3.28 us -> 0.01 us  [gossip_shards(): lax.ppermute(cube_diag, 'sec', [(i, (i + hop) % 4) for i in range(4)])]
  transfers between devices with their start and end apart: 27 -> 27, of which waited for: 10 -> 11; matrix products, arithmetic and copies ran while one was open for 6% -> 5% of each run, Pallas kernels for 46% -> 34%
where the time goes in v3:
time: 245 us; the launch traced here: 244 us
  Pallas kernels  122 us (50%)
  waiting for transfers between devices  53 us (22%)
  starting transfers between devices  31.3 us (13%)
  local copies, waits for them, and re-layouts  26.5 us (11%)
  other arithmetic  8.47 us (3%)
  between operations  2.81 us (1%)
    pallas_call x4, Pallas kernels, call_kernel(): pl.pallas_call(kernel, out_shape=(pltpu.VMEM((6,) + shape, jnp.float32),)...  91.8 us
    ppermute x5, waiting for transfers between devices, over_col(): return lax.ppermute(value, 'col', [(0, 1), (1, 0)])  23.6 us
    unnamed x42, local copies, waits for them, and re-layouts  21.5 us
    ppermute x12, waiting for transfers between devices, over_rep(): return lax.ppermute(value, 'rep', [(0, 1), (1, 0)])  13.1 us
    ppermute x3, waiting for transfers between devices, gossip_shards(): lax.ppermute(packed, 'sec', [(i, (i + hop) % 4) for i in range(4)])  12.6 us
    pallas_call x3, Pallas kernels, pick(): pl.pallas_call(functools.partial(pick_kernel, choices, whole, len(sources...  9.49 us
    pallas_call x1, Pallas kernels, pair_terms(): pl.pallas_call(pairs_kernel, grid=(total // width,), out_shape=(jax.Shape...  8.73 us
    ppermute x3, starting transfers between devices, gossip_shards(): lax.ppermute(cube_diag, 'sec', [(i, (i + hop) % 4) for i in range(4)])  8.71 us
  transfers between devices with their start and end apart: 27, of which 11 were waited for; matrix products, arithmetic and copies ran while one was open for 5% of the time, Pallas kernels for 34%

profile of v3, /device:TPU:0, one launch (start us, length us, event | category | flops | bytes accessed | tf_op | source)
XLA Modules:
  0.0 244.1 jit_solution(14359315916485845261)
XLA Ops:
  0.6 0.5 collective-permute-start
  1.1 0.7 dynamic-slice_bitcast_fusion.info_ref
  1.8 5.1 %collective-permute-done.refs_1_.refs_4_.refs_5_ = bf16[1280,1280]{1,0:T(8,128)(2,1)} collective-permute-done((bf16[1280,1280]{1,0:T(8,128)(2,1)}, bf16[1280,1280]{1,0:T(8,128)(2,1)}, u32[]{:S(2)}, u32[]{:S(2)}) %collective-permute-start) | collective-permute-done | bytes 3276832 | tf_op jit(solution)/shard_map/ppermute | solution.py:823
  7.0 3.7 %pick.3 = (bf16[640,1280]{1,0:T(8,128)(2,1)}, bf16[640,1280]{1,0:T(8,128)(2,1)}) custom-call(s32[14]{0:T(128)S(1)} %dynamic-slice_bitcast_fusion.info_ref, bf16[1280,1280]{1,0:T(8,128)(2,1)} %ham_ref.1, bf16[1280,1280]{1,0:T(8,128)(2,1)} %collective-permute-done.refs_1_.refs_4_.refs_5_), custom_call_target="tpu_custom_call" | custom-call | tf_op jit(solution)/shard_map/pick/pallas_call | solution.py:634
  10.6 2.9 %collective-permute-start.1 = (bf16[640,1280]{1,0:T(8,128)(2,1)}, bf16[640,1280]{1,0:T(8,128)(2,1)}, u32[]{:S(2)}, u32[]{:S(2)}) collective-permute-start(bf16[640,1280]{1,0:T(8,128)(2,1)} %get-tuple-element.48), channel_id=1, source_target_pairs={{0,2},{2,0},{1,3},{3,1},{4,6},{6,4},{5,7},{7,5},{8,10},{10,8},{9,1... | collective-permute-start | bytes 4915208 | tf_op jit(solution)/shard_map/ppermute | solution.py:826
  13.6 1.6 collective-permute-start.2
  15.2 0.1 copy.14
  15.3 0.9 copy-done.6
  16.2 8.7 %pairs.1 = (f32[1,5120]{1,0:T(1,128)S(1)}, bf16[512,5120]{1,0:T(8,128)(2,1)S(1)}, bf16[512,5120]{1,0:T(8,128)(2,1)S(1)}) custom-call(f32[3,5120]{1,0:T(4,128)S(1)} %copy-done.6, f32[512,4]{1,0:T(8,128)S(1)} %bitcast.11), custom_call_target="tpu_custom_call" | custom-call | tf_op jit(solution)/shard_map/pairs/pallas_call | solution.py:685
  25.0 2.3 copy-done.4
  27.3 2.4 copy-done.5
  29.7 3.8 %fusion = (f32[1280]{0:T(1024)S(1)}, f32[]{:T(128)}) fusion(bf16[1280,1280]{1,0:T(8,128)(2,1)S(1)} %copy-done, s32[1280]{0:T(1024)S(1)} %get-tuple-element.99, s32[1280]{0:T(1024)S(1)} %get-tuple-element.100), kind=kLoop, calls=%fused_computation.3 | loop fusion | flops 11467519 | bytes 3292164 | tf_op jit(solution)/shard_map/reduce_sum | solution.py:852
  33.5 0.3 dynamic_update_slice.8
  33.8 0.6 broadcast_in_dim.37
  34.5 0.7 pad_maximum_fusion
  35.2 1.3 constant_dynamic-slice_fusion
  36.5 0.7 fusion.3
  37.2 12.8 %collective-permute-done.1.refs_2_.refs_5_.refs_6_ = bf16[640,1280]{1,0:T(8,128)(2,1)} collective-permute-done((bf16[640,1280]{1,0:T(8,128)(2,1)}, bf16[640,1280]{1,0:T(8,128)(2,1)}, u32[]{:S(2)}, u32[]{:S(2)}) %collective-permute-start.1) | collective-permute-done | bytes 1638432 | tf_op jit(solution)/shard_map/ppermute | solution.py:826
  50.0 3.3 %collective-permute-done.2.refs_7_.refs_8_.refs_0_ = bf16[640,1280]{1,0:T(8,128)(2,1)} collective-permute-done((bf16[640,1280]{1,0:T(8,128)(2,1)}, bf16[640,1280]{1,0:T(8,128)(2,1)}, u32[]{:S(2)}, u32[]{:S(2)}) %collective-permute-start.2) | collective-permute-done | bytes 1638432 | tf_op jit(solution)/shard_map/ppermute | solution.py:830
  53.3 0.5 collective-permute-start.8
  53.8 3.4 %pick.4 = (bf16[640,1280]{1,0:T(8,128)(2,1)S(1)}, bf16[640,1280]{1,0:T(8,128)(2,1)S(1)}) custom-call(s32[14]{0:T(128)S(1)} %dynamic-slice_bitcast_fusion.info_ref, bf16[1280,1280]{1,0:T(8,128)(2,1)} %ham_ref.1, bf16[1280,1280]{1,0:T(8,128)(2,1)} %collective-permute-done.refs_1_.refs_4_.refs_5_, bf16[640,1280]{1,0:T(8,128)(2,1)} %collective-permute-done.1.refs_2_.refs_5_.refs_6_), custom_call_target="tpu_custom_call" | custom-call | tf_op jit(solution)/shard_map/pick/pallas_call | solution.py:634
  57.3 4.1 %collective-permute-start.5 = (bf16[640,1280]{1,0:T(8,128)(2,1)S(1)}, bf16[640,1280]{1,0:T(8,128)(2,1)}, u32[]{:S(2)}, u32[]{:S(2)}) collective-permute-start(bf16[640,1280]{1,0:T(8,128)(2,1)S(1)} %get-tuple-element.57), channel_id=1, source_target_pairs={{0,12},{12,8},{8,4},{4,0},{2,6},{6,10},{10,14},{14,2},{1,13},{13,9... | collective-permute-start | bytes 4915208 | tf_op jit(solution)/shard_map/ppermute | solution.py:830
  61.4 1.2 copy-done.12
  62.5 22.6 %square_0.1 = (f32[6,640,1280]{2,1,0:T(8,128)S(1)}, f32[8,128]{1,0:T(8,128)}) custom-call(s32[428]{0:T(512)} %bitcast.17, s32[14]{0:T(128)} %copy-done.8, bf16[1280,1280]{1,0:T(8,128)(2,1)} %ham_ref.1, bf16[1280,1280]{1,0:T(8,128)(2,1)} %collective-permute-done.refs_1_.refs_4_.refs_5_, bf16[640,1280]{1,0:T(8,128)(2,1)} %collective-permute-done.1.refs_2_.refs_5_.refs_6_, ...), custom_call_target="tpu_custom_call" | custom-call | tf_op jit(solution)/shard_map/square_0/pallas_call | solution.py:593
  85.1 10.8 %collective-permute-done.6 = f32[10368]{0:T(1024)S(1)} collective-permute-done((f32[10368]{0:T(1024)S(1)}, f32[10368]{0:T(1024)S(1)}, u32[]{:S(2)}, u32[]{:S(2)}) %collective-permute-start.6) | collective-permute-done | bytes 41504 | tf_op jit(solution)/shard_map/ppermute | solution.py:826
  95.9 0.3 collective-permute-done.5.refs_12_
  96.3 0.5 collective-permute-start.15
  96.8 3.8 %collective-permute-start.9 = (bf16[640,1280]{1,0:T(8,128)(2,1)}, bf16[640,1280]{1,0:T(8,128)(2,1)}, u32[]{:S(2)}, u32[]{:S(2)}) collective-permute-start(bf16[640,1280]{1,0:T(8,128)(2,1)} %collective-permute-done.5.refs_12_), channel_id=1, source_target_pairs={{0,2},{2,0},{1,3},{3,1},{4,6},{6,4},{5,7},{7,5},{8,10},{10,8},{9,1... | collective-permute-start | bytes 4915208 | tf_op jit(solution)/shard_map/ppermute | solution.py:826
  100.6 0.6 collective-permute-start.11
  101.2 0.9 collective-permute-done.14.refs_11_
  102.1 1.4 collective-permute-start.12
  103.5 3.2 %collective-permute-start.13 = (f32[10368]{0:T(1024)S(1)}, f32[10368]{0:T(1024)S(1)}, u32[]{:S(2)}, u32[]{:S(2)}) collective-permute-start(f32[10368]{0:T(1024)S(1)} %add.91), channel_id=1, source_target_pairs={{0,12},{4,0},{8,4},{12,8},{1,13},{5,1},{9,5},{13,9},{2,14},{6,2},{... | collective-permute-start | bytes 124424 | tf_op jit(solution)/shard_map/ppermute | solution.py:882
  106.7 14.2 %square_1.1 = (f32[6,640,1280]{2,1,0:T(8,128)S(1)}, f32[8,128]{1,0:T(8,128)}) custom-call(s32[428]{0:T(512)} %bitcast.18, s32[14]{0:T(128)} %copy-done.8, bf16[1280,1280]{1,0:T(8,128)(2,1)} %ham_ref.1, bf16[1280,1280]{1,0:T(8,128)(2,1)} %collective-permute-done.refs_1_.refs_4_.refs_5_, ...), custom_call_target="tpu_custom_call", output_to_operand_aliasing={{0}: (17, {})} | custom-call | tf_op jit(solution)/shard_map/square_1/pallas_call | solution.py:593
  120.9 6.6 %copy-done.2 = f32[6,640,1280]{2,1,0:T(8,128)} copy-done((f32[6,640,1280]{2,1,0:T(8,128)}, f32[6,640,1280]{2,1,0:T(8,128)S(1)}, u32[]{:S(2)}) %copy-start.2) | copy-done | bytes 19660824
  127.6 11.3 %collective-permute-done.11 = f32[10368]{0:T(1024)S(1)} collective-permute-done((f32[10368]{0:T(1024)S(1)}, f32[10368]{0:T(1024)S(1)}, u32[]{:S(2)}, u32[]{:S(2)}) %collective-permute-start.11) | collective-permute-done | bytes 41504 | tf_op jit(solution)/shard_map/ppermute | solution.py:882
  138.9 1.3 collective-permute-done.12
  140.2 0.5 collective-permute-start.19
  140.7 2.5 %pick.5 = bf16[640,1280]{1,0:T(8,128)(2,1)S(1)} custom-call(s32[14]{0:T(128)S(1)} %copy-done.9, bf16[640,1280]{1,0:T(8,128)(2,1)} %collective-permute-done.2.refs_7_.refs_8_.refs_0_, bf16[640,1280]{1,0:T(8,128)(2,1)} %collective-permute-done.10.refs_1_.refs_16_), custom_call_target="tpu_custom_call" | custom-call | tf_op jit(solution)/shard_map/pick/pallas_call | solution.py:634
  143.3 1.6 collective-permute-start.17
  144.9 0.5 slice.14
  145.4 0.6 fusion.2
  146.6 0.6 multiply_reduce_fusion
  148.5 0.1 dynamic_slice.17
  148.6 0.1 dynamic_slice.16
  148.8 1.0 broadcast_in_dim.38.refs_20_.refs_24_
  149.8 0.2 copy-done.15
  150.0 6.6 %copy-done.3 = f32[6,640,1280]{2,1,0:T(8,128)S(1)} copy-done((f32[6,640,1280]{2,1,0:T(8,128)S(1)}, f32[6,640,1280]{2,1,0:T(8,128)}, u32[]{:S(2)}) %copy-start.3) | copy-done | bytes 19660824
  156.6 27.6 %early_cube.1 = (f32[6,640,1280]{2,1,0:T(8,128)S(1)}, f32[640,128]{1,0:T(8,128)}) custom-call(s32[428]{0:T(512)} %bitcast.19, s32[14]{0:T(128)} %copy-done.8, bf16[1280,1280]{1,0:T(8,128)(2,1)} %ham_ref.1, bf16[1280,1280]{1,0:T(8,128)(2,1)} %collective-permute-done.refs_1_.refs_4_.refs_5_, ...), custom_call_target="tpu_custom_call", output_to_operand_aliasing={{0}: (21, {})} | custom-call | tf_op jit(solution)/shard_map/early_cube/pallas_call | solution.py:593
  184.2 0.5 collective-permute-start.21
  184.7 3.2 %collective-permute-done.20.refs_19_ = bf16[640,1280]{1,0:T(8,128)(2,1)S(1)} collective-permute-done((bf16[640,1280]{1,0:T(8,128)(2,1)}, bf16[640,1280]{1,0:T(8,128)(2,1)S(1)}, u32[]{:S(2)}, u32[]{:S(2)}) %collective-permute-start.20) | collective-permute-done | bytes 1638432 | tf_op jit(solution)/shard_map/ppermute | solution.py:823
  187.9 2.3 collective-permute-done.21.refs_21_
  190.3 1.2 copy-done.17
  191.5 27.5 %late_cube.1 = (f32[6,640,1280]{2,1,0:T(8,128)S(1)}, bf16[640,1280]{1,0:T(8,128)(2,1)}, f32[1280,1280]{1,0:T(8,128)}, f32[640,128]{1,0:T(8,128)}) custom-call(s32[428]{0:T(512)} %bitcast.20, s32[14]{0:T(128)} %copy-done.8, f32[1]{0:T(128)} %bitcast.7.gain_ref, bf16[1280,1280]{1,0:T(8,128)(2,1)} %ham_ref.1, ...), custom_call_target="tpu_custom_call", output_to_operand_aliasing={{0}: (25, {})} | custom-call | tf_op jit(solution)/shard_map/late_cube/pallas_call | solution.py:593
  219.0 1.1 reduce_sum.49
  220.2 0.3 dynamic_update_slice.9
  220.5 0.5 collective-permute-start.22
  221.0 1.5 collective-permute-done.22
  222.6 0.2 add_dynamic-update-slice_fusion
  222.7 3.4 %collective-permute-start.23 = (f32[5120]{0:T(1024)S(1)}, f32[5120]{0:T(1024)S(1)}, u32[]{:S(2)}, u32[]{:S(2)}) collective-permute-start(f32[5120]{0:T(1024)S(1)} %add_dynamic-update-slice_fusion), channel_id=1, source_target_pairs={{0,4},{4,8},{8,12},{12,0},{1,5},{5,9},{9,13},{13,1},{2,6},{6,10},{... | collective-permute-start | bytes 61448 | tf_op jit(solution)/shard_map/ppermute | solution.py:928
  226.1 2.4 %collective-permute-start.24 = (f32[5120]{0:T(1024)S(1)}, f32[5120]{0:T(1024)S(1)}, u32[]{:S(2)}, u32[]{:S(2)}) collective-permute-start(f32[5120]{0:T(1024)S(1)} %add_dynamic-update-slice_fusion), channel_id=1, source_target_pairs={{0,8},{4,12},{8,0},{12,4},{1,9},{5,13},{9,1},{13,5},{2,10},{6,14},... | collective-permute-start | bytes 61448 | tf_op jit(solution)/shard_map/ppermute | solution.py:928
  228.6 2.9 %collective-permute-start.25 = (f32[5120]{0:T(1024)S(1)}, f32[5120]{0:T(1024)S(1)}, u32[]{:S(2)}, u32[]{:S(2)}) collective-permute-start(f32[5120]{0:T(1024)S(1)} %add_dynamic-update-slice_fusion), channel_id=1, source_target_pairs={{0,12},{4,0},{8,4},{12,8},{1,13},{5,1},{9,5},{13,9},{2,14},{6,2},{... | collective-permute-start | bytes 61448 | tf_op jit(solution)/shard_map/ppermute | solution.py:928
  231.4 4.5 %density.1 = f32[1280,1280]{1,0:T(8,128)} custom-call(s32[14]{0:T(128)S(1)} %copy-done.10, f32[1]{0:T(128)} %bitcast.7.gain_ref, bf16[1280,1280]{1,0:T(8,128)(2,1)S(1)} %copy-done.1, bf16[640,1280]{1,0:T(8,128)(2,1)} %collective-permute-done.26.far_ref, f32[1,1280]{1,0:T(1,128)S(1)} %broadcast_in_dim.40.level_ref, ...), custom_call_target="tpu_custom_call", output_to_operand_aliasing={{}: (5, {})} | custom-call | tf_op jit(solution)/shard_map/density/pallas_call | solution.py:788
  235.9 0.6 multiply_add_fusion
  236.5 7.6 %pull.1 = f32[3,512]{1,0:T(4,128)} custom-call(f32[3,5120]{1,0:T(4,128)} %spots_ref.3, f32[1,5120]{1,0:T(1,128)} %bitcast.16, bf16[512,5120]{1,0:T(8,128)(2,1)} %copy-done.4, bf16[512,5120]{1,0:T(8,128)(2,1)} %copy-done.5, f32[3,512]{1,0:T(4,128)} %coords_ref.1, f32[1,512]{1,0:T(1,128)} %bitcast.21), custom_call_target="tpu_custom_call" | custom-call | tf_op jit(solution)/shard_map/pull/pallas_call | solution.py:735
  (67 shorter events, 0.5 us)
Async XLA Ops:
  0.6 6.3 %collective-permute-start = (bf16[1280,1280]{1,0:T(8,128)(2,1)}, bf16[1280,1280]{1,0:T(8,128)(2,1)}, u32[]{:S(2)}, u32[]{:S(2)}) collective-permute-start(bf16[1280,1280]{1,0:T(8,128)(2,1)} %ham_ref.1), channel_id=1, source_target_pairs={{0,1},{1,0},{2,3},{3,2},{4,5},{5,4},{6,7},{7,6},{8,9},{9,8},{10,11... | collective-permute-start | bytes 9830408 | tf_op jit(solution)/shard_map/ppermute | solution.py:823
  1.8 52.0 %copy-start.8 = (s32[14]{0:T(128)}, s32[14]{0:T(128)S(1)}, u32[]{:S(2)}) copy-start(s32[14]{0:T(128)S(1)} %dynamic-slice_bitcast_fusion.info_ref) | copy-start | bytes 172
  1.8 13.3 %copy-start.19 = (f32[3,512]{1,0:T(4,128)S(1)}, f32[3,512]{1,0:T(4,128)}, u32[]{:S(2)}) copy-start(f32[3,512]{1,0:T(4,128)} %coords_ref.1) | copy-start | bytes 18436
  1.8 13.3 %copy-start.20 = (f32[512]{0:T(512)S(1)}, f32[512]{0:T(512)}, u32[]{:S(2)}) copy-start(f32[512]{0:T(512)} %param.9) | copy-start | bytes 6148
  7.0 22.7 %copy-start = (bf16[1280,1280]{1,0:T(8,128)(2,1)S(1)}, bf16[1280,1280]{1,0:T(8,128)(2,1)}, u32[]{:S(2)}) copy-start(bf16[1280,1280]{1,0:T(8,128)(2,1)} %ham_ref.1) | copy-start | bytes 9830404
  10.6 39.3 %collective-permute-start.1 = (bf16[640,1280]{1,0:T(8,128)(2,1)}, bf16[640,1280]{1,0:T(8,128)(2,1)}, u32[]{:S(2)}, u32[]{:S(2)}) collective-permute-start(bf16[640,1280]{1,0:T(8,128)(2,1)} %get-tuple-element.48), channel_id=1, source_target_pairs={{0,2},{2,0},{1,3},{3,1},{4,6},{6,4},{5,7},{7,5},{8,10},{10,8},{9,1... | collective-permute-start | bytes 4915208 | tf_op jit(solution)/shard_map/ppermute | solution.py:826
  13.6 39.7 %collective-permute-start.2 = (bf16[640,1280]{1,0:T(8,128)(2,1)}, bf16[640,1280]{1,0:T(8,128)(2,1)}, u32[]{:S(2)}, u32[]{:S(2)}) collective-permute-start(bf16[640,1280]{1,0:T(8,128)(2,1)} %get-tuple-element.49), channel_id=1, source_target_pairs={{0,4},{4,8},{8,12},{12,0},{2,14},{14,10},{10,6},{6,2},{1,5},{5,9},... | collective-permute-start | bytes 4915208 | tf_op jit(solution)/shard_map/ppermute | solution.py:830
  15.3 0.9 copy-start.6
  25.0 2.3 copy-start.4
  27.3 2.4 copy-start.5
  29.7 3.8 %copy-start.7 = (f32[1,5120]{1,0:T(1,128)}, f32[1,5120]{1,0:T(1,128)S(1)}, u32[]{:S(2)}) copy-start(f32[1,5120]{1,0:T(1,128)S(1)} %get-tuple-element.50) | copy-start | bytes 61444
  35.2 1.3 collective-permute-start.3
  53.3 8.0 %collective-permute-start.7 = (bf16[640,1280]{1,0:T(8,128)(2,1)}, bf16[640,1280]{1,0:T(8,128)(2,1)S(1)}, u32[]{:S(2)}, u32[]{:S(2)}) collective-permute-start(bf16[640,1280]{1,0:T(8,128)(2,1)} %collective-permute-done.1.refs_2_.refs_5_.refs_6_), channel_id=1, source_target_pairs={{0,1},{1,0},{2,3},{3,2},{4,5},{5,4},{6,7},{7,6},{8,9},{9,8},{10,11... | collective-permute-start | bytes 4915208 | tf_op jit(solution)/shard_map/ppermute | solution.py:823
  53.3 8.0 %collective-permute-start.8 = (bf16[640,1280]{1,0:T(8,128)(2,1)}, bf16[640,1280]{1,0:T(8,128)(2,1)}, u32[]{:S(2)}, u32[]{:S(2)}) collective-permute-start(bf16[640,1280]{1,0:T(8,128)(2,1)} %collective-permute-done.2.refs_7_.refs_8_.refs_0_), channel_id=1, source_target_pairs={{0,1},{1,0},{2,3},{3,2},{4,5},{5,4},{6,7},{7,6},{8,9},{9,8},{10,11... | collective-permute-start | bytes 4915208 | tf_op jit(solution)/shard_map/ppermute | solution.py:823
  57.2 38.7 %collective-permute-start.4 = (bf16[640,1280]{1,0:T(8,128)(2,1)S(1)}, bf16[640,1280]{1,0:T(8,128)(2,1)S(1)}, u32[]{:S(2)}, u32[]{:S(2)}) collective-permute-start(bf16[640,1280]{1,0:T(8,128)(2,1)S(1)} %get-tuple-element.56), channel_id=1, source_target_pairs={{0,2},{2,0},{1,3},{3,1},{4,6},{6,4},{5,7},{7,5},{8,10},{10,8},{9,1... | collective-permute-start | bytes 4915208 | tf_op jit(solution)/shard_map/ppermute | solution.py:826
  57.3 39.0 %collective-permute-start.5 = (bf16[640,1280]{1,0:T(8,128)(2,1)S(1)}, bf16[640,1280]{1,0:T(8,128)(2,1)}, u32[]{:S(2)}, u32[]{:S(2)}) collective-permute-start(bf16[640,1280]{1,0:T(8,128)(2,1)S(1)} %get-tuple-element.57), channel_id=1, source_target_pairs={{0,12},{12,8},{8,4},{4,0},{2,6},{6,10},{10,14},{14,2},{1,13},{13,9... | collective-permute-start | bytes 4915208 | tf_op jit(solution)/shard_map/ppermute | solution.py:830
  61.3 34.6 %collective-permute-start.6 = (f32[10368]{0:T(1024)S(1)}, f32[10368]{0:T(1024)S(1)}, u32[]{:S(2)}, u32[]{:S(2)}) collective-permute-start(f32[10368]{0:T(1024)S(1)} %fusion.3), channel_id=1, source_target_pairs={{0,2},{2,0},{1,3},{3,1},{4,6},{6,4},{5,7},{7,5},{8,10},{10,8},{9,1... | collective-permute-start | bytes 124424 | tf_op jit(solution)/shard_map/ppermute | solution.py:826
  61.3 1.2 copy-start.12
  95.9 10.8 %copy-start.11 = (bf16[640,1280]{1,0:T(8,128)(2,1)}, bf16[640,1280]{1,0:T(8,128)(2,1)S(1)}, u32[]{:S(2)}) copy-start(bf16[640,1280]{1,0:T(8,128)(2,1)S(1)} %collective-permute-done.4.refs_3_.refs_10_) | copy-start | bytes 4915204
  96.3 5.8 %collective-permute-start.14 = (bf16[640,1280]{1,0:T(8,128)(2,1)S(1)}, bf16[640,1280]{1,0:T(8,128)(2,1)S(1)}, u32[]{:S(2)}, u32[]{:S(2)}) collective-permute-start(bf16[640,1280]{1,0:T(8,128)(2,1)S(1)} %collective-permute-done.4.refs_3_.refs_10_), channel_id=1, source_target_pairs={{0,1},{1,0},{2,3},{3,2},{4,5},{5,4},{6,7},{7,6},{8,9},{9,8},{10,11... | collective-permute-start | bytes 4915208 | tf_op jit(solution)/shard_map/ppermute | solution.py:823
  96.3 7.2 %collective-permute-start.15 = (bf16[640,1280]{1,0:T(8,128)(2,1)}, bf16[640,1280]{1,0:T(8,128)(2,1)S(1)}, u32[]{:S(2)}, u32[]{:S(2)}) collective-permute-start(bf16[640,1280]{1,0:T(8,128)(2,1)} %collective-permute-done.5.refs_12_), channel_id=1, source_target_pairs={{0,1},{1,0},{2,3},{3,2},{4,5},{5,4},{6,7},{7,6},{8,9},{9,8},{10,11... | collective-permute-start | bytes 4915208 | tf_op jit(solution)/shard_map/ppermute | solution.py:823
  96.8 43.4 %collective-permute-start.10 = (bf16[640,1280]{1,0:T(8,128)(2,1)S(1)}, bf16[640,1280]{1,0:T(8,128)(2,1)}, u32[]{:S(2)}, u32[]{:S(2)}) collective-permute-start(bf16[640,1280]{1,0:T(8,128)(2,1)S(1)} %collective-permute-done.4.refs_3_.refs_10_), channel_id=1, source_target_pairs={{0,4},{4,8},{8,12},{12,0},{2,14},{14,10},{10,6},{6,2},{1,5},{5,9},... | collective-permute-start | bytes 4915208 | tf_op jit(solution)/shard_map/ppermute | solution.py:830
  96.8 43.4 %collective-permute-start.9 = (bf16[640,1280]{1,0:T(8,128)(2,1)}, bf16[640,1280]{1,0:T(8,128)(2,1)}, u32[]{:S(2)}, u32[]{:S(2)}) collective-permute-start(bf16[640,1280]{1,0:T(8,128)(2,1)} %collective-permute-done.5.refs_12_), channel_id=1, source_target_pairs={{0,2},{2,0},{1,3},{3,1},{4,6},{6,4},{5,7},{7,5},{8,10},{10,8},{9,1... | collective-permute-start | bytes 4915208 | tf_op jit(solution)/shard_map/ppermute | solution.py:826
  100.6 38.3 %collective-permute-start.11 = (f32[10368]{0:T(1024)S(1)}, f32[10368]{0:T(1024)S(1)}, u32[]{:S(2)}, u32[]{:S(2)}) collective-permute-start(f32[10368]{0:T(1024)S(1)} %add.91), channel_id=1, source_target_pairs={{0,4},{4,8},{8,12},{12,0},{1,5},{5,9},{9,13},{13,1},{2,6},{6,10},{... | collective-permute-start | bytes 124424 | tf_op jit(solution)/shard_map/ppermute | solution.py:882
  102.1 4.6 %copy-start.13 = (bf16[640,1280]{1,0:T(8,128)(2,1)}, bf16[640,1280]{1,0:T(8,128)(2,1)S(1)}, u32[]{:S(2)}) copy-start(bf16[640,1280]{1,0:T(8,128)(2,1)S(1)} %collective-permute-done.14.refs_11_) | copy-start | bytes 4915204
  102.1 38.1 %collective-permute-start.12 = (f32[10368]{0:T(1024)S(1)}, f32[10368]{0:T(1024)S(1)}, u32[]{:S(2)}, u32[]{:S(2)}) collective-permute-start(f32[10368]{0:T(1024)S(1)} %add.91), channel_id=1, source_target_pairs={{0,8},{4,12},{8,0},{12,4},{1,9},{5,13},{9,1},{13,5},{2,10},{6,14},... | collective-permute-start | bytes 124424 | tf_op jit(solution)/shard_map/ppermute | solution.py:882
  103.5 3.2 %copy-start.14 = (bf16[640,1280]{1,0:T(8,128)(2,1)}, bf16[640,1280]{1,0:T(8,128)(2,1)S(1)}, u32[]{:S(2)}) copy-start(bf16[640,1280]{1,0:T(8,128)(2,1)S(1)} %collective-permute-done.15.refs_13_) | copy-start | bytes 4915204
  103.5 36.7 %collective-permute-start.13 = (f32[10368]{0:T(1024)S(1)}, f32[10368]{0:T(1024)S(1)}, u32[]{:S(2)}, u32[]{:S(2)}) collective-permute-start(f32[10368]{0:T(1024)S(1)} %add.91), channel_id=1, source_target_pairs={{0,12},{4,0},{8,4},{12,8},{1,13},{5,1},{9,5},{13,9},{2,14},{6,2},{... | collective-permute-start | bytes 124424 | tf_op jit(solution)/shard_map/ppermute | solution.py:882
  106.7 34.0 %copy-start.9 = (s32[14]{0:T(128)S(1)}, s32[14]{0:T(128)}, u32[]{:S(2)}) copy-start(s32[14]{0:T(128)} %copy-done.8) | copy-start | bytes 172
  120.9 6.7 %copy-start.2 = (f32[6,640,1280]{2,1,0:T(8,128)}, f32[6,640,1280]{2,1,0:T(8,128)S(1)}, u32[]{:S(2)}) copy-start(f32[6,640,1280]{2,1,0:T(8,128)S(1)} %get-tuple-element.70.refs_19_) | copy-start | bytes 58982404
  140.2 8.6 %collective-permute-start.18 = (bf16[640,1280]{1,0:T(8,128)(2,1)}, bf16[640,1280]{1,0:T(8,128)(2,1)S(1)}, u32[]{:S(2)}, u32[]{:S(2)}) collective-permute-start(bf16[640,1280]{1,0:T(8,128)(2,1)} %collective-permute-done.9.refs_14_), channel_id=1, source_target_pairs={{0,1},{1,0},{2,3},{3,2},{4,5},{5,4},{6,7},{7,6},{8,9},{9,8},{10,11... | collective-permute-start | bytes 4915208 | tf_op jit(solution)/shard_map/ppermute | solution.py:823
  140.2 8.5 %collective-permute-start.19 = (bf16[640,1280]{1,0:T(8,128)(2,1)}, bf16[640,1280]{1,0:T(8,128)(2,1)}, u32[]{:S(2)}, u32[]{:S(2)}) collective-permute-start(bf16[640,1280]{1,0:T(8,128)(2,1)} %collective-permute-done.10.refs_1_.refs_16_), channel_id=1, source_target_pairs={{0,1},{1,0},{2,3},{3,2},{4,5},{5,4},{6,7},{7,6},{8,9},{9,8},{10,11... | collective-permute-start | bytes 4915208 | tf_op jit(solution)/shard_map/ppermute | solution.py:823
  143.2 40.9 %collective-permute-start.16 = (bf16[640,1280]{1,0:T(8,128)(2,1)S(1)}, bf16[640,1280]{1,0:T(8,128)(2,1)}, u32[]{:S(2)}, u32[]{:S(2)}) collective-permute-start(bf16[640,1280]{1,0:T(8,128)(2,1)S(1)} %pick.5), channel_id=1, source_target_pairs={{0,2},{2,0},{1,3},{3,1},{4,6},{6,4},{5,7},{7,5},{8,10},{10,8},{9,1... | collective-permute-start | bytes 4915208 | tf_op jit(solution)/shard_map/ppermute | solution.py:826
  143.3 40.9 %collective-permute-start.17 = (bf16[640,1280]{1,0:T(8,128)(2,1)S(1)}, bf16[640,1280]{1,0:T(8,128)(2,1)}, u32[]{:S(2)}, u32[]{:S(2)}) collective-permute-start(bf16[640,1280]{1,0:T(8,128)(2,1)S(1)} %pick.5), channel_id=1, source_target_pairs={{0,4},{4,8},{8,12},{12,0},{2,14},{14,10},{10,6},{6,2},{1,5},{5,9},... | collective-permute-start | bytes 4915208 | tf_op jit(solution)/shard_map/ppermute | solution.py:830
  147.2 2.5 %copy-start.18 = (f32[5120]{0:T(1024)}, f32[5120]{0:T(1024)S(1)}, u32[]{:S(2)}) copy-start(f32[5120]{0:T(1024)S(1)} %get-tuple-element.82) | copy-start | bytes 61444
  148.7 1.3 copy-start.15
  150.0 6.6 %copy-start.3 = (f32[6,640,1280]{2,1,0:T(8,128)S(1)}, f32[6,640,1280]{2,1,0:T(8,128)}, u32[]{:S(2)}) copy-start(f32[6,640,1280]{2,1,0:T(8,128)} %copy-done.2) | copy-start | bytes 58982404
  184.2 3.8 %collective-permute-start.20 = (bf16[640,1280]{1,0:T(8,128)(2,1)}, bf16[640,1280]{1,0:T(8,128)(2,1)S(1)}, u32[]{:S(2)}, u32[]{:S(2)}) collective-permute-start(bf16[640,1280]{1,0:T(8,128)(2,1)} %collective-permute-done.16.refs_18_), channel_id=1, source_target_pairs={{0,1},{1,0},{2,3},{3,2},{4,5},{5,4},{6,7},{7,6},{8,9},{9,8},{10,11... | collective-permute-start | bytes 4915208 | tf_op jit(solution)/shard_map/ppermute | solution.py:823
  184.2 6.0 %collective-permute-start.21 = (bf16[640,1280]{1,0:T(8,128)(2,1)}, bf16[640,1280]{1,0:T(8,128)(2,1)S(1)}, u32[]{:S(2)}, u32[]{:S(2)}) collective-permute-start(bf16[640,1280]{1,0:T(8,128)(2,1)} %collective-permute-done.17.refs_20_), channel_id=1, source_target_pairs={{0,1},{1,0},{2,3},{3,2},{4,5},{5,4},{6,7},{7,6},{8,9},{9,8},{10,11... | collective-permute-start | bytes 4915208 | tf_op jit(solution)/shard_map/ppermute | solution.py:823
  187.9 2.3 copy-start.16
  190.3 1.2 copy-start.17
  191.5 40.0 %copy-start.1 = (bf16[1280,1280]{1,0:T(8,128)(2,1)S(1)}, bf16[1280,1280]{1,0:T(8,128)(2,1)}, u32[]{:S(2)}) copy-start(bf16[1280,1280]{1,0:T(8,128)(2,1)} %ham_ref.1) | copy-start | bytes 9830404
  191.5 40.0 %copy-start.10 = (s32[14]{0:T(128)S(1)}, s32[14]{0:T(128)}, u32[]{:S(2)}) copy-start(s32[14]{0:T(128)} %copy-done.8) | copy-start | bytes 172
  219.0 12.5 %collective-permute-start.26 = (bf16[640,1280]{1,0:T(8,128)(2,1)}, bf16[640,1280]{1,0:T(8,128)(2,1)}, u32[]{:S(2)}, u32[]{:S(2)}) collective-permute-start(bf16[640,1280]{1,0:T(8,128)(2,1)} %get-tuple-element.84), channel_id=1, source_target_pairs={{0,1},{1,0},{2,3},{3,2},{4,5},{5,4},{6,7},{7,6},{8,9},{9,8},{10,11... | collective-permute-start | bytes 4915208 | tf_op jit(solution)/shard_map/ppermute | solution.py:823
  220.5 2.1 collective-permute-start.22
  222.7 13.2 %collective-permute-start.23 = (f32[5120]{0:T(1024)S(1)}, f32[5120]{0:T(1024)S(1)}, u32[]{:S(2)}, u32[]{:S(2)}) collective-permute-start(f32[5120]{0:T(1024)S(1)} %add_dynamic-update-slice_fusion), channel_id=1, source_target_pairs={{0,4},{4,8},{8,12},{12,0},{1,5},{5,9},{9,13},{13,1},{2,6},{6,10},{... | collective-permute-start | bytes 61448 | tf_op jit(solution)/shard_map/ppermute | solution.py:928
  226.1 9.8 %collective-permute-start.24 = (f32[5120]{0:T(1024)S(1)}, f32[5120]{0:T(1024)S(1)}, u32[]{:S(2)}, u32[]{:S(2)}) collective-permute-start(f32[5120]{0:T(1024)S(1)} %add_dynamic-update-slice_fusion), channel_id=1, source_target_pairs={{0,8},{4,12},{8,0},{12,4},{1,9},{5,13},{9,1},{13,5},{2,10},{6,14},... | collective-permute-start | bytes 61448 | tf_op jit(solution)/shard_map/ppermute | solution.py:928
  228.6 7.4 %collective-permute-start.25 = (f32[5120]{0:T(1024)S(1)}, f32[5120]{0:T(1024)S(1)}, u32[]{:S(2)}, u32[]{:S(2)}) collective-permute-start(f32[5120]{0:T(1024)S(1)} %add_dynamic-update-slice_fusion), channel_id=1, source_target_pairs={{0,12},{4,0},{8,4},{12,8},{1,13},{5,1},{9,5},{13,9},{2,14},{6,2},{... | collective-permute-start | bytes 61448 | tf_op jit(solution)/shard_map/ppermute | solution.py:928

commit v4 on v3

--- a/solution.py
+++ b/solution.py
@@ -258,11 +258,12 @@
                 if k == 0:
                     late.append((SEND, 0, 0, 0, 4 + which, 0))
             own_rows = lambda slot: int(slot != core)
-            second = Z_SENDS[1][row]
+            straight = core == X_SENDS[0][row]
+            second, last = Z_SENDS[1][row], X_SENDS[3][row]
             info = [
                 core, row, col, core * 640,
-                own_rows(X_SENDS[0][row]), own_rows(Z_SENDS[0][row]), own_rows(X_SENDS[1][row]), 0,
-                2 if second == X1 else own_rows(second), int(X_SENDS[3][row] == Z3),
+                own_rows(X_SENDS[1][row]), (2 if straight else 3) if second == X1 else own_rows(second),
+                0 if last == Z3 else (1 if straight else 2), int(straight),
             ] + [lefts.index(column) for column in open_columns] + open_columns
             devices.append(
                 dict(
@@ -274,7 +275,7 @@
     return devices
 
 
-CORE, ROW, COL, FIRST_ROW, SEND_X1, SEND_Z1, SEND_X2, NEAR, SEND_Z2, SEND_LAST, OPEN_LEFT, OPEN = (*range(11), 12)
+CORE, ROW, COL, FIRST_ROW, SEND_X2, SEND_Z2, SEND_LAST, STRAIGHT, OPEN_LEFT, OPEN = (*range(9), 10)
 
 
 def device_tables(half):
@@ -319,40 +320,57 @@
         self.blocks[position] = functools.partial(self.start_block, position, slot, sources)
 
     def start_block(self, position, slot, sources):
-        fixed = isinstance(slot, int)
-        if "own" in sources and (not fixed or slot <= OWN1):
-            for at, ref in zip((self.core, 1 - self.core), sources["own"]):
-                @pl.when(slot == at)
-                def _():
-                    self.load_halves(position, ref.at[self.near], ref.at[self.far])
-
-        if not fixed:
-            for number, halves in sources.items():
-                if number != "own":
-                    pl.when(slot == number)(functools.partial(self.load_halves, position, *halves))
-        elif slot > OWN1:
-            self.load_halves(position, *sources[slot])
-
-    def left_places(self, refs):
-        own = [(self.core, refs[0].at[self.near]), (1 - self.core, refs[1].at[self.near])]
-        return own + list(enumerate(refs))[2:]
+        for number, choices in sources.items():
+            if isinstance(slot, int) and slot != number:
+                continue
+            for condition, near_ref, far_ref in choices:
+                condition = slot == number if condition is None else jnp.logical_and(slot == number, condition)
+                load = functools.partial(self.load_halves, position, near_ref, far_ref)
+                if isinstance(condition, bool):
+                    load()
+                else:
+                    pl.when(condition)(load)
+
+    def own_sources(self, whole_ref, got_ref, other_ref):
+        own = (whole_ref.at[self.near], whole_ref.at[self.far])
+        return {
+            slot: [(self.core == slot, *own), (self.core != slot, got_ref, other_ref)] for slot in (OWN0, OWN1)
+        }
+
+    def first_sources(self, straight, first, second, sibling_first, sibling_second):
+        crossed = jnp.logical_not(straight)
+        return {
+            X1: [(straight, first, sibling_second), (crossed, second, sibling_first)],
+            Z1: [(straight, sibling_first, second), (crossed, sibling_second, first)],
+        }
 
     def load_left(self, index, number, refs):
         self.lefts[index] = functools.partial(self.start_left, index, number, refs)
 
+    def left_places(self, refs):
+        whole_ref, got_ref, straight, first, second = refs[:5]
+        places = [(self.core, None, whole_ref.at[self.near]), (1 - self.core, None, got_ref)]
+        places += [(2, straight, first), (2, jnp.logical_not(straight), second)]
+        return places + [(3, None, ref) for ref in refs[5:]]
+
     def start_left(self, index, number, refs):
-        for at, ref in self.left_places(refs):
-            if isinstance(at, int) and isinstance(number, int):
-                if at == number:
-                    self.copy_left(index, ref)
+        for at, condition, ref in self.left_places(refs):
+            if isinstance(at, int) and isinstance(number, int) and at != number:
+                continue
+            here = at == number
+            if condition is not None:
+                here = jnp.logical_and(here, condition)
+            copy = functools.partial(self.copy_left, index, ref)
+            if isinstance(here, bool):
+                copy()
             else:
-                pl.when(at == number)(functools.partial(self.copy_left, index, ref))
+                pl.when(here)(copy)
 
     def copy_left(self, index, ref):
         pltpu.make_async_copy(ref, self.left_ref.at[index], self.left_sem.at[index]).start()
 
     def load_rows(self, refs):
-        for k in range(len(refs)):
+        for k in range(len(refs) - 2):
             self.load_left(k, k, refs)
 
     def start(self, mask):
@@ -386,12 +404,8 @@
             )
 
     def tiles(self, cols_ref, column):
-        width = self.block_ref.shape[2]
-        base = column * width
-        return [
-            jnp.broadcast_to(cols_ref[:, pl.ds(pl.multiple_of(base + m * 128, 128), 128)], (16, 128))
-            for m in range(width // 128)
-        ]
+        lines = self.block_ref.shape[2] // 128
+        return [jnp.broadcast_to(cols_ref[pl.ds(column * lines + m, 1), :], (16, 128)) for m in range(lines)]
 
     def finish(self, field):
         rows_ref, cols_ref, diag_ref = self.levels
@@ -421,7 +435,7 @@
             def fix(index, carry):
                 rows = pl.ds(pl.multiple_of(index * 128, 128), 128)
                 at = pl.ds(pl.multiple_of(self.core * half + index * 128, 128), 128)
-                col = cols_ref[:, pl.ds(pl.multiple_of(field[6] * (2 * half) + self.core * half + index * 128, 128), 128)]
+                col = cols_ref[pl.ds((2 * field[6] + self.core) * (half // 128) + index, 1), :]
                 level = rows_ref[rows, :]
                 ham = left[rows, at].astype(jnp.float32)
                 square = total[rows, at] + ham * (level + col)
@@ -467,18 +481,28 @@
         lax.fori_loop(0, count, step, 0)
 
 
+def take_inputs(refs, last):
+    count = 7 + 2 * max(last - Z1, 0)
+    return list(refs[:count]), list(refs[count:])
+
+
+def use_inputs(worker, info_ref, inputs):
+    own, first, rest = inputs[:3], inputs[3:7], inputs[7:]
+    straight = info_ref[STRAIGHT] == 1
+    sources = {**worker.own_sources(*own), **worker.first_sources(straight, *first)}
+    for k in range(len(rest) // 2):
+        sources[X2 + k] = [(None, rest[2 * k], rest[2 * k + 1])]
+    return [own[0], own[1], straight, first[0], first[1]] + rest[:1], sources
+
+
 def square_kernel(first, steps, left_count, slots, table_ref, info_ref, *refs):
-    refs = list(refs)
-    row_refs = [refs.pop(0) for _ in range(left_count)]
-    sources = {"own": [refs.pop(0) for _ in range(2)]}
-    for slot in slots:
-        if slot > OWN1:
-            sources[slot] = (refs.pop(0), refs.pop(0))
+    inputs, refs = take_inputs(refs, slots[-1])
     refs = refs[0 if first else 2 :]
     total_ref, token_ref, block_ref, block_sem, left_ref, left_sem = refs
     half = left_ref.shape[1]
     worker = Worker(table_ref, info_ref[CORE], half, block_ref, block_sem, left_ref, left_sem, total_ref)
-    worker.load_rows(row_refs)
+    row_refs, sources = use_inputs(worker, info_ref, inputs)
+    worker.load_rows(row_refs[: left_count + 2])
     for position, slot in enumerate(slots):
         worker.load_block(position, slot, sources)
     worker.run(steps)
@@ -486,16 +510,13 @@
 
 
 def early_kernel(steps, slots_at, table_ref, info_ref, *refs):
-    refs = list(refs)
-    row_refs = [refs.pop(0) for _ in range(4)]
-    sources = {"own": [refs.pop(0) for _ in range(2)]}
-    for slot in range(X1, Z3 + 1):
-        sources[slot] = (refs.pop(0), refs.pop(0))
+    inputs, refs = take_inputs(refs, Z3)
     _, _, level_rows_ref, level_ref, total_ref, diag_ref = (refs.pop(0) for _ in range(6))
     block_ref, block_sem, left_ref, left_sem = refs
     half = left_ref.shape[1]
     worker = Worker(table_ref, info_ref[CORE], half, block_ref, block_sem, left_ref, left_sem, total_ref)
     worker.levels = (level_rows_ref, level_ref, diag_ref)
+    row_refs, sources = use_inputs(worker, info_ref, inputs)
     worker.load_rows(row_refs)
     worker.load_block(0, X3, sources)
     worker.load_block(1, Z3, sources)
@@ -506,19 +527,16 @@
 
 
 def late_kernel(steps, slots_at, table_ref, info_ref, gain_ref, *refs):
-    refs = list(refs)
-    row_refs = [refs.pop(0) for _ in range(4)]
-    sources = {"own": [refs.pop(0) for _ in range(2)]}
-    for slot in range(X1, Z4 + 1):
-        sources[slot] = (refs.pop(0), refs.pop(0))
-    _, old_diag_ref, level_rows_ref, level_ref, total_ref, cube_ref, density_ref, diag_ref = (
+    inputs, refs = take_inputs(refs, Z4)
+    _, old_diag_ref, level_rows_ref, level_ref, total_ref, cube_ref, density_ref, cube_diag_ref = (
         refs.pop(0) for _ in range(8)
     )
-    block_ref, block_sem, left_ref, left_sem, out_sem, sent_ref, ham_ref, ham_sem = refs
+    block_ref, block_sem, left_ref, left_sem, out_sem, sent_ref, ham_ref, ham_sem, diag_ref = refs
     half, width = left_ref.shape[1:]
     core, row, col = info_ref[CORE], info_ref[ROW], info_ref[COL]
     worker = Worker(table_ref, core, half, block_ref, block_sem, left_ref, left_sem, total_ref)
     worker.levels = (level_rows_ref, level_ref, diag_ref)
+    row_refs, sources = use_inputs(worker, info_ref, inputs)
     worker.load_block(0, X4, sources)
     worker.load_block(1, Z4, sources)
     for k in range(2):
@@ -564,6 +582,11 @@
         lax.fori_loop(0, half // 128, fix, 0)
 
     density_copy.start()
+    lines = half // 128
+    cube_diag_ref[...] = jnp.zeros_like(cube_diag_ref)
+    for k in range(lines):
+        share = jnp.sum(diag_ref[pl.ds(k * 128, 128), :].T, 0, keepdims=True)
+        cube_diag_ref[pl.ds((2 * row + core) * lines + k, 1), :] = share
     sent_copy.wait()
     density_copy.wait()
 
@@ -641,12 +664,12 @@
             pltpu.SemaphoreType.DMA((len(choices), parts)),
             pltpu.SemaphoreType.DMA((len(choices), parts)),
         ],
-        compiler_params=pltpu.CompilerParams(vmem_limit_bytes=VMEM_BYTES),
+        compiler_params=pltpu.CompilerParams(vmem_limit_bytes=8 * 2**20),
         name="pick",
     )(info, *in_hbm(sources))
 
 
-def pairs_kernel(spots_ref, points_ref, out_ref, high_ref, low_ref, wide_ref):
+def pairs_kernel(spots_ref, points_ref, out_ref, weight_ref, wide_ref):
     count, width = points_ref.shape[0], spots_ref.shape[1]
     tiles = width // 128
 
@@ -666,10 +689,7 @@
             dx, dy, dz = spots[m][0] - px, spots[m][1] - py, spots[m][2] - pz
             inv = lax.rsqrt(dx * dx + dy * dy + dz * dz + 1.0)
             sums[m] = sums[m] + charge * inv
-            weight = inv * (inv * inv)
-            high = weight.astype(jnp.bfloat16)
-            high_ref[rows, at] = high
-            low_ref[rows, at] = (weight - high.astype(jnp.float32)).astype(jnp.bfloat16)
+            weight_ref[rows, at] = (inv * (inv * inv)).astype(jnp.bfloat16)
         return tuple(sums)
 
     zeros = tuple(jnp.zeros((16, 128), jnp.float32) for _ in range(tiles))
@@ -685,32 +705,67 @@
     return pl.pallas_call(
         pairs_kernel,
         grid=(total // width,),
-        out_shape=(jax.ShapeDtypeStruct((1, total), jnp.float32), part, part),
+        out_shape=(jax.ShapeDtypeStruct((1, total), jnp.float32), part),
         in_specs=[pl.BlockSpec((3, width), lambda i: (0, i)), pl.BlockSpec((count, 4), lambda i: (0, 0))],
-        out_specs=[pl.BlockSpec((1, width), lambda i: (0, i))] + [pl.BlockSpec((count, width), lambda i: (0, i))] * 2,
+        out_specs=[pl.BlockSpec((1, width), lambda i: (0, i))] + [pl.BlockSpec((count, width), lambda i: (0, i))],
         scratch_shapes=[pltpu.VMEM((4, count, 128), jnp.float32)],
         compiler_params=pltpu.CompilerParams(vmem_limit_bytes=VMEM_BYTES),
         name="pairs",
     )(centers, points)
 
 
+def levels_kernel(info_ref, own_ref, first_ref, second_ref, third_ref, gain_ref, level_ref, above_ref, rows_ref):
+    lines = level_ref.shape[0]
+    sums = own_ref[...] + first_ref[...] + second_ref[...] + third_ref[...]
+    potential, diag = sums[0:lines], sums[lines : 2 * lines] + sums[0:lines]
+    total = float(lines * 128)
+    mean = jnp.sum(diag) / total
+    above = diag - mean
+    squares = (jnp.sum(sums[2 * lines : 2 * lines + 1]) / 128.0 + jnp.sum(above * above)) / total
+    spread = jnp.sqrt(jnp.full((8, 128), squares + 1e-05, jnp.float32))
+    gain_ref[0] = jnp.max(1.0 / (3.0 * spread))
+    level_ref[...] = potential - mean
+    above_ref[...] = above
+    half = rows_ref.shape[0]
+    first = (2 * info_ref[ROW] + info_ref[CORE]) * (half // 128)
+    for k in range(half // 128):
+        line = level_ref[pl.ds(first + k, 1), :]
+        rows_ref[pl.ds(k * 128, 128), :] = jnp.broadcast_to(line, (128, 128)).T
+
+
+def level_terms(info, parts, lines, half):
+    line = jax.ShapeDtypeStruct((lines, 128), jnp.float32)
+    return pl.pallas_call(
+        levels_kernel,
+        out_shape=(jax.ShapeDtypeStruct((1,), jnp.float32), line, line, jax.ShapeDtypeStruct((half, 128), jnp.float32)),
+        in_specs=[SCALARS] + [VMEM] * 4,
+        out_specs=(SCALARS, VMEM, VMEM, VMEM),
+        compiler_params=pltpu.CompilerParams(vmem_limit_bytes=4 * 2**20),
+        name="levels",
+    )(info, *parts)
+
+
 MIDDLE = 10.0
 
 
-def pull_kernel(spots_ref, occ_ref, high_ref, low_ref, coords_ref, charge_ref, out_ref, total_ref):
+def pull_kernel(gain_ref, spots_ref, above_ref, near_ref, far_ref, weight_ref, coords_ref, charge_ref, out_ref, total_ref):
     index = pl.program_id(0)
-    occ = occ_ref[...]
+    gain = gain_ref[0]
+    width = spots_ref.shape[1]
+    pieces = []
+    for m in range(width // 128):
+        line = pl.ds(index * (width // 128) + m, 1)
+        cube = near_ref[line, :] + far_ref[line, :]
+        pieces.append(0.5 - 1.5 * gain * above_ref[line, :] + 2.0 * (gain * gain * gain) * cube)
+    occ = jnp.concatenate(pieces, 1)
     weights = [occ] + [occ * (spots_ref[k : k + 1, :] - MIDDLE) for k in range(3)]
-    width = occ.shape[1]
     stacked = jnp.concatenate(weights + [jnp.zeros((4, width), jnp.float32)], 0)
     high = stacked.astype(jnp.bfloat16)
     low = (stacked - high.astype(jnp.float32)).astype(jnp.bfloat16)
     blank = jnp.zeros((128 - 16, width), jnp.bfloat16)
     both = jnp.concatenate([high, low, blank], 0)
-    first = jnp.concatenate([high, jnp.zeros_like(low), blank], 0)
     dims = (((1,), (1,)), ((), ()))
-    part = lax.dot_general(high_ref[...], both, dims, preferred_element_type=jnp.float32)
-    part = part + lax.dot_general(low_ref[...], first, dims, preferred_element_type=jnp.float32)
+    part = lax.dot_general(weight_ref[...], both, dims, preferred_element_type=jnp.float32)
 
     @pl.when(index == 0)
     def _():
@@ -729,17 +784,19 @@
             out_ref[k : k + 1, :] = -charge_ref[...] * pull
 
 
-def pull_terms(centers, occupation, high, low, mm_coords, mm_charges):
+def pull_terms(gain, centers, above, near, far, weights, mm_coords, mm_charges):
     total, count = centers.shape[1], mm_coords.shape[1]
-    width = 1024
+    width = 1280
     return pl.pallas_call(
         pull_kernel,
         grid=(total // width,),
         out_shape=jax.ShapeDtypeStruct((3, count), jnp.float32),
         in_specs=[
+            SCALARS,
             pl.BlockSpec((3, width), lambda i: (0, i)),
-            pl.BlockSpec((1, width), lambda i: (0, i)),
-            pl.BlockSpec((count, width), lambda i: (0, i)),
+            pl.BlockSpec(above.shape, lambda i: (0, 0)),
+            pl.BlockSpec(above.shape, lambda i: (0, 0)),
+            pl.BlockSpec(above.shape, lambda i: (0, 0)),
             pl.BlockSpec((count, width), lambda i: (0, i)),
             pl.BlockSpec((3, count), lambda i: (0, 0)),
             pl.BlockSpec((1, count), lambda i: (0, 0)),
@@ -747,7 +804,7 @@
         out_specs=pl.BlockSpec((3, count), lambda i: (0, 0)),
         scratch_shapes=[pltpu.VMEM((count, 128), jnp.float32)],
         name="pull",
-    )(centers, occupation, high, low, mm_coords, mm_charges[None])
+    )(gain, centers, above, near, far, weights, mm_coords, mm_charges[None])
 
 
 def density_kernel(steps, info_ref, gain_ref, ham_ref, far_ref, level_ref, _, out_ref):
@@ -775,13 +832,14 @@
         def fix(k, carry):
             rows = pl.ds(pl.multiple_of(k * 128, 128), 128)
             at = pl.ds(pl.multiple_of(first + k * 128, 128), 128)
-            out_ref[rows, at] += jnp.where(eye, 0.5 + linear * level_ref[:, at], 0.0)
+            line = pl.ds((2 * col + core) * (width // 128) + first // 128 + k, 1)
+            out_ref[rows, at] += jnp.where(eye, 0.5 + linear * level_ref[line, :], 0.0)
             return carry
 
         lax.fori_loop(0, height // 128, fix, 0)
 
 
-def density_rest(info, gain, ham, far, level_cols, density):
+def density_rest(info, gain, ham, far, level, density):
     height, width = ham.shape
     steps = 1
     chunk = far.shape[0] // steps
@@ -794,7 +852,7 @@
                 SCALARS,
                 pl.BlockSpec((chunk, width), lambda i, info: ((1 - info[CORE]) * steps + i, 0)),
                 pl.BlockSpec((chunk, width), lambda i, info: (i, 0)),
-                pl.BlockSpec((1, width), lambda i, info: (0, 0)),
+                pl.BlockSpec(level.shape, lambda i, info: (0, 0)),
                 HERE,
             ],
             out_specs=pl.BlockSpec((chunk, width), lambda i, info: ((1 - info[CORE]) * steps + i, 0)),
@@ -803,7 +861,7 @@
         input_output_aliases={5: 0},
         compiler_params=pltpu.CompilerParams(vmem_limit_bytes=VMEM_BYTES),
         name="density",
-    )(info, gain, ham, far, level_cols, density)
+    )(info, gain, ham, far, level, density)
 
 
 def gossip_shards(sizes, h_core, centers, mm_coords, mm_charges):
@@ -829,6 +887,16 @@
         moves = [(2 * start + x, 2 * to + x) for x in range(2) for start, to in Z_MOVES[step][x]]
         return lax.ppermute(value, ("sec", "col"), moves)
 
+    def over_both(value, own):
+        moves = []
+        for z, x, c in ((z, x, c) for z in range(4) for x in range(2) for c in range(2)):
+            if (c if own else 1 - c) == X_SENDS[0][z]:
+                to = (z, 1 - x, c)
+            else:
+                to = (dict(Z_MOVES[0][x])[z], x, 1 - c)
+            moves.append((4 * z + 2 * x + c, 4 * to[0] + 2 * to[1] + to[2]))
+        return lax.ppermute(value, ("sec", "col", "rep"), moves)
+
     def swap_all(values):
         return [(value, over_rep(value)) for value in values]
 
@@ -839,12 +907,13 @@
         return lax.optimization_barrier((arrived, work))
 
     shape = (half, width)
-    own_parts = (h_core, over_rep(h_core))
-    sends = pick(info, (SEND_X1, SEND_Z1), own_parts, 2, shape)
-    x1 = over_col(sends[0])
-    z1 = over_sec(sends[1], 0)
+    near = lax.dynamic_slice_in_dim(h_core, core * half, half, 0)
+    far = lax.dynamic_slice_in_dim(h_core, (1 - core) * half, half, 0)
+    got = over_rep(far)
+    firsts = (over_both(near, True), over_both(got, False))
+    other = over_rep(near)
     points = jnp.concatenate([mm_coords, mm_charges[None]], 0).T
-    terms, high, low = pair_terms(centers, points)
+    terms, weights = pair_terms(centers, points)
     rows_glob = row_start + lax.broadcasted_iota(jnp.int32, (height, width), 0)
     cols_glob = col_start + lax.broadcasted_iota(jnp.int32, (height, width), 1)
     on_diag = rows_glob == cols_glob
@@ -852,65 +921,53 @@
     own_diag = jnp.sum(jnp.where(on_diag, wide, 0.0), 0)
     own_off = jnp.sum(jnp.where(on_diag, 0.0, wide * wide))
     diag = lax.dynamic_update_slice_in_dim(jnp.zeros((total,), jnp.float32), own_diag, col_start, 0)
-    packed = jnp.concatenate([terms[0], diag, jnp.full((128,), own_off)])
+    packed = jnp.concatenate([terms[0], diag, jnp.full((8 * 128,), own_off)]).reshape(-1, 128)
     packed = packed + over_rep(packed)
-    (x1, z1), (packed, high, low, table) = after((x1, z1), (packed, high, low, table))
-    sends = pick(info, (SEND_X2, SEND_Z2), own_parts + (x1,), 2, shape)
+    firsts, (packed, weights, table, other) = after(firsts, (packed, weights, table, other))
+    own_parts = [h_core, got, other]
+    sends = pick(info, (SEND_X2, SEND_Z2), (h_core, got) + tuple(firsts), 1, shape)
+    firsts, sends = lax.optimization_barrier((list(firsts), sends))
     x2 = over_col(sends[0])
     z2 = over_sec(sends[1], 1)
-    pairs = dict(zip((X1, Z1), swap_all((x1, z1))))
-
-    def grow_square(stage, lefts, slots, totals, token):
-        operands = list(lefts) + list(own_parts) + flat(pairs[slot] for slot in slots)
-        operands += [] if token is None else [token]
-        kernel = functools.partial(square_kernel, totals is None, steps[stage], len(lefts), (OWN0, OWN1) + slots)
+    operands = own_parts + firsts + [over_rep(first) for first in firsts]
+
+    def grow_square(stage, left_count, slots, totals, token):
+        kernel = functools.partial(square_kernel, totals is None, steps[stage], left_count, slots)
         return call_kernel(
-            f"square_{stage}", kernel, shape, (table, info), operands, totals, (),
-            (jax.ShapeDtypeStruct((8, 128), jnp.float32),), (VMEM,), work_scratch(half, width, 2 + len(slots), 4),
+            f"square_{stage}", kernel, shape, (table, info), operands + ([] if token is None else [token]), totals, (),
+            (jax.ShapeDtypeStruct((8, 128), jnp.float32),), (VMEM,), work_scratch(half, width, len(slots), 4),
         )
 
-    lefts = list(own_parts) + [x1]
-    totals, token = grow_square(0, lefts, (X1, Z1), None, None)
+    totals, token = grow_square(0, 3, (OWN0, OWN1, X1, Z1), None, None)
     col_packed = over_col(packed)
     (x2, z2, col_packed), (token, packed) = after((x2, z2, col_packed), (token, packed))
     x3 = over_col(z2)
     z3 = over_sec(x2, 2)
-    pairs.update(zip((X2, Z2), swap_all((x2, z2))))
-    lefts.append(x2)
-    totals, token = grow_square(1, lefts, (X1, Z1, X2, Z2), totals, token)
+    operands = operands + flat(swap_all((x2, z2)))
+    totals, token = grow_square(1, 4, (OWN0, OWN1, X1, Z1, X2, Z2), totals, token)
     packed = packed + col_packed
     others = [lax.ppermute(packed, "sec", [(i, (i + hop) % 4) for i in range(4)]) for hop in (1, 2, 3)]
     (x3, z3, others), (token, packed) = after((x3, z3, others), (token, packed))
-    last_send = pick(info, (SEND_LAST,), (z1, z3), 0, shape)[0]
+    last_send = pick(info, (SEND_LAST,), [z3] + operands[5:7], 0, shape)[0]
     x4 = over_col(last_send)
     z4 = over_sec(last_send, 3)
-    pairs.update(zip((X3, Z3), swap_all((x3, z3))))
-    sums = packed + others[0] + others[1] + others[2]
-    potential, diag, off_total = sums[:total], sums[total : 2 * total], sums[2 * total]
-    diag_vals = potential + diag
-    mean_level = jnp.sum(diag_vals) / total
-    above = diag_vals - mean_level
-    level = potential - mean_level
-    spread = jnp.sqrt((off_total + jnp.sum(above * above)) / total + 1e-05)
-    gain = 1.0 / (3.0 * spread)
-    level_rows = lax.dynamic_slice_in_dim(level, row_start + core * half, half, 0)
-    level_rows = jnp.broadcast_to(level_rows[:, None], (half, 128))
-    level_cols = lax.dynamic_slice_in_dim(level, col_start, width, 0)[None]
+    operands = operands + flat(swap_all((x3, z3)))
+    gain, level, above, level_rows = level_terms(info, [packed] + list(others), total // 128, half)
+    lines = jax.ShapeDtypeStruct((total // 128, 128), jnp.float32)
     share = jax.ShapeDtypeStruct((half, 128), jnp.float32)
     totals, cube_diag = call_kernel(
         "early_cube", functools.partial(early_kernel, steps[2], slots_at[0]), shape, (table, info),
-        lefts + list(own_parts) + flat(pairs[slot] for slot in range(X1, Z3 + 1)) + [token], totals, (level_rows, level[None]),
+        operands + [token], totals, (level_rows, level),
         (share,), (VMEM,), work_scratch(half, width, 6, 6),
     )
-    (x4, z4), (cube_diag, above, level_rows, level, level_cols, gain) = after(
-        (x4, z4), (cube_diag, above, level_rows, level, level_cols, gain)
+    (x4, z4), (cube_diag, above, level_rows, level, gain) = after(
+        (x4, z4), (cube_diag, above, level_rows, level, gain)
     )
-    pairs.update(zip((X4, Z4), swap_all((x4, z4))))
-    blocks = list(own_parts) + flat(pairs[slot] for slot in range(X1, Z4 + 1))
+    operands = operands + flat(swap_all((x4, z4)))
     _, sibling, density, cube_diag = call_kernel(
-        "late_cube", functools.partial(late_kernel, steps[3], slots_at[1]), shape, (table, info, gain[None]),
-        lefts + blocks, totals, (cube_diag, level_rows, level[None]),
-        (jax.ShapeDtypeStruct(shape, jnp.bfloat16), jax.ShapeDtypeStruct((height, width), jnp.float32), share),
+        "late_cube", functools.partial(late_kernel, steps[3], slots_at[1]), shape, (table, info, gain),
+        operands, totals, (cube_diag, level_rows, level),
+        (jax.ShapeDtypeStruct(shape, jnp.bfloat16), jax.ShapeDtypeStruct((height, width), jnp.float32), lines),
         (HERE, HERE, VMEM),
         work_scratch(half, width, 6, 4)
         + [
@@ -918,19 +975,16 @@
             pltpu.VMEM(shape, jnp.bfloat16),
             pltpu.VMEM(shape, jnp.bfloat16),
             pltpu.SemaphoreType.DMA,
+            pltpu.VMEM((half, 128), jnp.float32),
         ],
     )
     sibling = over_rep(sibling)
-    cube_diag = lax.dynamic_update_slice_in_dim(
-        jnp.zeros((total,), jnp.float32), jnp.sum(cube_diag, 1), row_start + core * half, 0
-    )
     cube_diag = cube_diag + over_rep(cube_diag)
-    others = [lax.ppermute(cube_diag, "sec", [(i, (i + hop) % 4) for i in range(4)]) for hop in (1, 2, 3)]
-    density = density_rest(info, gain[None], h_core, sibling, level_cols, density)
-    others, density = after(others, density)
-    cube_diag = cube_diag + others[0] + others[1] + others[2]
-    occupation = 0.5 - 1.5 * gain * above + 2.0 * gain**3 * cube_diag
-    forces = pull_terms(centers, occupation[None], high, low, mm_coords, mm_charges)
+    cube_diag = cube_diag + lax.ppermute(cube_diag, "sec", [(i, i ^ 1) for i in range(4)])
+    from_far = lax.ppermute(cube_diag, "sec", [(i, i ^ 2) for i in range(4)])
+    density = density_rest(info, gain, h_core, sibling, level, density)
+    from_far, density = after(from_far, density)
+    forces = pull_terms(gain, centers, above, cube_diag, from_far, weights, mm_coords, mm_charges)
     return (density, forces)
 
 

time: 245 us -> 235 us (0.959)
  waiting for transfers between devices: 53 us -> 62.7 us
  local copies, waits for them, and re-layouts: 26.5 us -> 18.2 us
  Pallas kernels: 122 us -> 116 us
    ppermute x3 -> x4, waiting for transfers between devices: 0.01 us -> 15.6 us  [the longest x2 11.6 us: over_both(): return lax.ppermute(value, ('sec', 'col', 'rep'), moves)]
    ppermute x5 -> x4, waiting for transfers between devices: 23.6 us -> 8.63 us  [over_col(): return lax.ppermute(value, 'col', [(0, 1), (1, 0)])]
    unnamed x42 -> x50, local copies, waits for them, and re-layouts: 21.5 us -> 11.7 us
    ppermute x3, waiting for transfers between devices: 12.6 us -> 22.2 us  [gossip_shards(): lax.ppermute(packed, 'sec', [(i, (i + hop) % 4) for i in range(4)])]
    pallas_call x3 -> x2, Pallas kernels: 9.49 us -> 5.81 us  [pick(): pl.pallas_call(functools.partial(pick_kernel, choices, whole, len(sources...]
    dynamic_slice x2 -> x1, local copies, waits for them, and re-layouts: 0.16 us -> 3.45 us  [gossip_shards(): far = lax.dynamic_slice_in_dim(h_core, (1 - core) * half, half, 0)]
    ppermute x4 -> x3, starting transfers between devices: 7.26 us -> 4.84 us  [over_sec(): return lax.ppermute(value, ('sec', 'col'), moves)]
    ppermute x3 -> x4, starting transfers between devices: 8.71 us -> 6.77 us  [the longest x2 6.04 us: over_both(): return lax.ppermute(value, ('sec', 'col', 'rep'), moves)]
  transfers between devices with their start and end apart: 27 -> 27, of which waited for: 11 -> 15; matrix products, arithmetic and copies ran while one was open for 5% -> 4% of each run, Pallas kernels for 34% -> 34%
where the time goes in v4:
time: 235 us; the launch traced here: 234 us
  Pallas kernels  116 us (49%)
  waiting for transfers between devices  62.7 us (27%)
  starting transfers between devices  30.3 us (13%)
  local copies, waits for them, and re-layouts  18.2 us (8%)
  other arithmetic  6.05 us (3%)
    pallas_call x4, Pallas kernels, call_kernel(): pl.pallas_call(kernel, out_shape=(pltpu.VMEM((6,) + shape, jnp.float32),)...  92 us
    ppermute x3, waiting for transfers between devices, gossip_shards(): lax.ppermute(packed, 'sec', [(i, (i + hop) % 4) for i in range(4)])  22.2 us
    unnamed x50, local copies, waits for them, and re-layouts  11.7 us
    ppermute x13, waiting for transfers between devices, over_rep(): return lax.ppermute(value, 'rep', [(0, 1), (1, 0)])  11.6 us
    ppermute x2, waiting for transfers between devices, over_both(): return lax.ppermute(value, ('sec', 'col', 'rep'), moves)  11.6 us
    ppermute x4, waiting for transfers between devices, over_col(): return lax.ppermute(value, 'col', [(0, 1), (1, 0)])  8.63 us
    pallas_call x1, Pallas kernels, pair_terms(): pl.pallas_call(pairs_kernel, grid=(total // width,), out_shape=(jax.Shape...  7.48 us
    ppermute x4, starting transfers between devices, over_col(): return lax.ppermute(value, 'col', [(0, 1), (1, 0)])  7.19 us
  transfers between devices with their start and end apart: 27, of which 15 were waited for; matrix products, arithmetic and copies ran while one was open for 4% of the time, Pallas kernels for 34%

profile of v4, /device:TPU:0, one launch (start us, length us, event | category | flops | bytes accessed | tf_op | source)
XLA Modules:
  0.0 234.2 jit_solution(11052876965211661936)
XLA Ops:
  0.7 3.5 %constant_dynamic-slice_fusion.2 = (bf16[640,1280]{1,0:T(8,128)(2,1)S(1)}, bf16[640,1280]{1,0:T(8,128)(2,1)}) fusion(bf16[1280,1280]{1,0:T(8,128)(2,1)} %ham_ref.1, s32[]{:T(128)S(6)} %select_n.24, s32[]{:T(128)S(6)} %select_n.23), kind=kLoop, calls=%fused_computation.11 | loop fusion | bytes 6553608 | tf_op jit(solution)/shard_map/dynamic_slice | solution.py:911
  4.1 0.5 collective-permute-start.1
  4.6 2.6 %collective-permute-start = (bf16[640,1280]{1,0:T(8,128)(2,1)}, bf16[640,1280]{1,0:T(8,128)(2,1)}, u32[]{:S(2)}, u32[]{:S(2)}) collective-permute-start(bf16[640,1280]{1,0:T(8,128)(2,1)} %get-tuple-element.101), channel_id=1, source_target_pairs={{0,5},{1,3},{2,15},{3,1},{4,6},{5,8},{6,4},{7,2},{8,13},{9,11},{10... | collective-permute-start | bytes 4915208 | tf_op jit(solution)/shard_map/ppermute | solution.py:898
  7.3 2.3 collective-permute-done.1.refs_1_
  9.6 3.4 %collective-permute-start.2 = (bf16[640,1280]{1,0:T(8,128)(2,1)}, bf16[640,1280]{1,0:T(8,128)(2,1)}, u32[]{:S(2)}, u32[]{:S(2)}) collective-permute-start(bf16[640,1280]{1,0:T(8,128)(2,1)} %collective-permute-done.1.refs_1_), channel_id=1, source_target_pairs={{0,2},{1,4},{2,0},{3,14},{4,9},{5,7},{6,3},{7,5},{8,10},{9,12},{10... | collective-permute-start | bytes 4915208 | tf_op jit(solution)/shard_map/ppermute | solution.py:898
  13.0 0.1 copy.14
  13.2 0.9 copy-done.4
  14.1 7.5 %pairs.1 = (f32[1,5120]{1,0:T(1,128)S(1)}, bf16[512,5120]{1,0:T(8,128)(2,1)S(1)}) custom-call(f32[3,5120]{1,0:T(4,128)S(1)} %copy-done.4, f32[512,4]{1,0:T(8,128)S(1)} %bitcast.10), custom_call_target="tpu_custom_call" | custom-call | tf_op jit(solution)/shard_map/pairs/pallas_call | solution.py:705
  21.6 2.3 copy-done.2
  23.9 3.8 %fusion = (f32[1280]{0:T(1024)S(1)}, f32[]{:T(128)}) fusion(bf16[1280,1280]{1,0:T(8,128)(2,1)S(1)} %copy-done, s32[1280]{0:T(1024)S(1)} %get-tuple-element.102, s32[1280]{0:T(1024)S(1)} %get-tuple-element.103), kind=kLoop, calls=%fused_computation.3 | loop fusion | flops 11467519 | bytes 3292164 | tf_op jit(solution)/shard_map/reduce_sum | solution.py:921
  27.7 0.3 dynamic_update_slice.3
  28.0 0.6 broadcast_in_dim.19
  28.7 0.7 maximum_bitcast_fusion
  29.4 0.2 collective-permute-start.3
  29.6 1.3 constant_dynamic-slice_fusion.1
  30.8 0.7 fusion.2.info_ref
  31.5 0.7 fusion.3
  32.3 7.5 %collective-permute-done.refs_2_.refs_3_ = bf16[640,1280]{1,0:T(8,128)(2,1)} collective-permute-done((bf16[640,1280]{1,0:T(8,128)(2,1)}, bf16[640,1280]{1,0:T(8,128)(2,1)}, u32[]{:S(2)}, u32[]{:S(2)}) %collective-permute-start) | collective-permute-done | bytes 1638432 | tf_op jit(solution)/shard_map/ppermute | solution.py:898
  39.8 4.1 %collective-permute-done.2.refs_3_.refs_4_ = bf16[640,1280]{1,0:T(8,128)(2,1)} collective-permute-done((bf16[640,1280]{1,0:T(8,128)(2,1)}, bf16[640,1280]{1,0:T(8,128)(2,1)}, u32[]{:S(2)}, u32[]{:S(2)}) %collective-permute-start.2) | collective-permute-done | bytes 1638432 | tf_op jit(solution)/shard_map/ppermute | solution.py:898
  43.9 3.4 %pick.2 = (bf16[640,1280]{1,0:T(8,128)(2,1)S(1)}, bf16[640,1280]{1,0:T(8,128)(2,1)S(1)}) custom-call(s32[12]{0:T(128)S(1)} %fusion.2.info_ref, bf16[1280,1280]{1,0:T(8,128)(2,1)} %ham_ref.1, bf16[640,1280]{1,0:T(8,128)(2,1)} %collective-permute-done.1.refs_1_, bf16[640,1280]{1,0:T(8,128)(2,1)} %collective-permute-done.refs_2_.refs_3_, ...), custom_call_target="tpu_custom_call" | custom-call | tf_op jit(solution)/shard_map/pick/pallas_call | solution.py:657
  47.2 2.0 collective-permute-start.8
  49.3 1.6 collective-permute-start.5
  50.9 4.6 %collective-permute-start.6 = (bf16[640,1280]{1,0:T(8,128)(2,1)S(1)}, bf16[640,1280]{1,0:T(8,128)(2,1)}, u32[]{:S(2)}, u32[]{:S(2)}) collective-permute-start(bf16[640,1280]{1,0:T(8,128)(2,1)S(1)} %get-tuple-element.58), channel_id=1, source_target_pairs={{0,12},{12,8},{8,4},{4,0},{2,6},{6,10},{10,14},{14,2},{1,13},{13,9... | collective-permute-start | bytes 4915208 | tf_op jit(solution)/shard_map/ppermute | solution.py:888
  55.6 1.2 copy-done.12
  56.7 1.2 copy-done.13
  57.9 22.4 %square_0.1 = (f32[6,640,1280]{2,1,0:T(8,128)S(1)}, f32[8,128]{1,0:T(8,128)}) custom-call(s32[428]{0:T(512)} %bitcast.13, s32[12]{0:T(128)} %copy-done.8, bf16[1280,1280]{1,0:T(8,128)(2,1)} %ham_ref.1, bf16[640,1280]{1,0:T(8,128)(2,1)} %collective-permute-done.1.refs_1_, bf16[640,1280]{1,0:T(8,128)(2,1)} %collective-permute-done.4.refs_2_, ...), custom_call_target="tpu_custom_call" | custom-call | tf_op jit(solution)/shard_map/square_0/pallas_call | solution.py:616
  80.3 8.1 %collective-permute-done.7 = f32[88,128]{1,0:T(8,128)S(1)} collective-permute-done((f32[88,128]{1,0:T(8,128)S(1)}, f32[88,128]{1,0:T(8,128)S(1)}, u32[]{:S(2)}, u32[]{:S(2)}) %collective-permute-start.7) | collective-permute-done | bytes 45088 | tf_op jit(solution)/shard_map/ppermute | solution.py:884
  88.4 2.1 collective-permute-done.6.refs_9_
  90.6 0.5 collective-permute-start.15
  91.1 1.1 collective-permute-start.10
  92.2 3.8 %collective-permute-start.14 = (f32[88,128]{1,0:T(8,128)S(1)}, f32[88,128]{1,0:T(8,128)S(1)}, u32[]{:S(2)}, u32[]{:S(2)}) collective-permute-start(f32[88,128]{1,0:T(8,128)S(1)} %add.62.own_ref), channel_id=1, source_target_pairs={{0,12},{4,0},{8,4},{12,8},{1,13},{5,1},{9,5},{13,9},{2,14},{6,2},{... | collective-permute-start | bytes 135176 | tf_op jit(solution)/shard_map/ppermute | solution.py:949
  96.1 0.5 collective-permute-done.15.refs_8_
  96.6 2.6 %collective-permute-start.12 = (f32[88,128]{1,0:T(8,128)S(1)}, f32[88,128]{1,0:T(8,128)S(1)}, u32[]{:S(2)}, u32[]{:S(2)}) collective-permute-start(f32[88,128]{1,0:T(8,128)S(1)} %add.62.own_ref), channel_id=1, source_target_pairs={{0,4},{4,8},{8,12},{12,0},{1,5},{5,9},{9,13},{13,1},{2,6},{6,10},{... | collective-permute-start | bytes 135176 | tf_op jit(solution)/shard_map/ppermute | solution.py:949
  99.2 14.0 %square_1.1 = (f32[6,640,1280]{2,1,0:T(8,128)S(1)}, f32[8,128]{1,0:T(8,128)}) custom-call(s32[428]{0:T(512)} %bitcast.14, s32[12]{0:T(128)} %copy-done.8, bf16[1280,1280]{1,0:T(8,128)(2,1)} %ham_ref.1, bf16[640,1280]{1,0:T(8,128)(2,1)} %collective-permute-done.1.refs_1_, ...), custom_call_target="tpu_custom_call", output_to_operand_aliasing={{0}: (14, {})} | custom-call | tf_op jit(solution)/shard_map/square_1/pallas_call | solution.py:616
  113.3 16.3 %collective-permute-done.14.third_ref = f32[88,128]{1,0:T(8,128)S(1)} collective-permute-done((f32[88,128]{1,0:T(8,128)S(1)}, f32[88,128]{1,0:T(8,128)S(1)}, u32[]{:S(2)}, u32[]{:S(2)}) %collective-permute-start.14) | collective-permute-done | bytes 45088 | tf_op jit(solution)/shard_map/ppermute | solution.py:949
  129.6 5.9 %collective-permute-done.13.second_ref = f32[88,128]{1,0:T(8,128)S(1)} collective-permute-done((f32[88,128]{1,0:T(8,128)S(1)}, f32[88,128]{1,0:T(8,128)S(1)}, u32[]{:S(2)}, u32[]{:S(2)}) %collective-permute-start.13) | collective-permute-done | bytes 45088 | tf_op jit(solution)/shard_map/ppermute | solution.py:949
  135.6 0.5 collective-permute-start.20
  136.1 0.7 copy-done.14
  136.8 2.4 %pick.3 = bf16[640,1280]{1,0:T(8,128)(2,1)S(1)} custom-call(s32[12]{0:T(128)S(1)} %copy-done.9, bf16[640,1280]{1,0:T(8,128)(2,1)} %copy-done.14, bf16[640,1280]{1,0:T(8,128)(2,1)} %copy-done.12, bf16[640,1280]{1,0:T(8,128)(2,1)} %copy-done.13), custom_call_target="tpu_custom_call" | custom-call | tf_op jit(solution)/shard_map/pick/pallas_call | solution.py:657
  139.2 0.2 collective-permute-start.18
  139.5 4.4 %collective-permute-start.17 = (bf16[640,1280]{1,0:T(8,128)(2,1)S(1)}, bf16[640,1280]{1,0:T(8,128)(2,1)}, u32[]{:S(2)}, u32[]{:S(2)}) collective-permute-start(bf16[640,1280]{1,0:T(8,128)(2,1)S(1)} %pick.3), channel_id=1, source_target_pairs={{0,2},{2,0},{1,3},{3,1},{4,6},{6,4},{5,7},{7,5},{8,10},{10,8},{9,1... | collective-permute-start | bytes 4915208 | tf_op jit(solution)/shard_map/ppermute | solution.py:884
  143.9 1.4 levels.1
  145.3 0.7 copy-done.3
  146.0 0.6 copy-done.5
  146.6 0.6 copy-done.11
  147.2 1.2 copy-done.18
  148.4 0.5 copy-done.17
  149.0 27.6 %early_cube.1 = (f32[6,640,1280]{2,1,0:T(8,128)S(1)}, f32[640,128]{1,0:T(8,128)}) custom-call(s32[428]{0:T(512)} %bitcast.15, s32[12]{0:T(128)} %copy-done.8, bf16[1280,1280]{1,0:T(8,128)(2,1)} %ham_ref.1, bf16[640,1280]{1,0:T(8,128)(2,1)} %collective-permute-done.1.refs_1_, ...), custom_call_target="tpu_custom_call", output_to_operand_aliasing={{0}: (18, {})} | custom-call | tf_op jit(solution)/shard_map/early_cube/pallas_call | solution.py:616
  176.6 2.5 %collective-permute-done.18.refs_17_ = bf16[640,1280]{1,0:T(8,128)(2,1)} collective-permute-done((bf16[640,1280]{1,0:T(8,128)(2,1)S(1)}, bf16[640,1280]{1,0:T(8,128)(2,1)}, u32[]{:S(2)}, u32[]{:S(2)}) %collective-permute-start.18) | collective-permute-done | bytes 1638432 | tf_op jit(solution)/shard_map/ppermute | solution.py:888
  179.1 0.5 collective-permute-done.17.refs_15_
  179.6 0.5 collective-permute-start.22
  180.1 3.2 %collective-permute-done.21.refs_16_ = bf16[640,1280]{1,0:T(8,128)(2,1)S(1)} collective-permute-done((bf16[640,1280]{1,0:T(8,128)(2,1)}, bf16[640,1280]{1,0:T(8,128)(2,1)S(1)}, u32[]{:S(2)}, u32[]{:S(2)}) %collective-permute-start.21) | collective-permute-done | bytes 1638432 | tf_op jit(solution)/shard_map/ppermute | solution.py:881
  183.3 2.3 collective-permute-done.22.refs_18_
  185.7 1.2 copy-done.20
  186.9 28.0 %late_cube.1 = (f32[6,640,1280]{2,1,0:T(8,128)S(1)}, bf16[640,1280]{1,0:T(8,128)(2,1)}, f32[1280,1280]{1,0:T(8,128)}, f32[40,128]{1,0:T(8,128)}) custom-call(s32[428]{0:T(512)} %bitcast.16, s32[12]{0:T(128)} %copy-done.8, f32[1]{0:T(128)} %get-tuple-element.84.gain_ref, bf16[1280,1280]{1,0:T(8,128)(2,1)} %ham_ref.1, ...), custom_call_target="tpu_custom_call", output_to_operand_aliasing={{0}: (22, {})} | custom-call | tf_op jit(solution)/shard_map/late_cube/pallas_call | solution.py:616
  214.9 0.5 collective-permute-start.23
  215.4 3.2 %collective-permute-done.23 = f32[40,128]{1,0:T(8,128)S(1)} collective-permute-done((f32[40,128]{1,0:T(8,128)}, f32[40,128]{1,0:T(8,128)S(1)}, u32[]{:S(2)}, u32[]{:S(2)}) %collective-permute-start.23) | collective-permute-done | bytes 20512 | tf_op jit(solution)/shard_map/ppermute | solution.py:881
  218.7 0.7 add.63
  219.4 3.8 %collective-permute-done.24 = f32[40,128]{1,0:T(8,128)S(1)} collective-permute-done((f32[40,128]{1,0:T(8,128)S(1)}, f32[40,128]{1,0:T(8,128)S(1)}, u32[]{:S(2)}, u32[]{:S(2)}) %collective-permute-start.24) | collective-permute-done | bytes 20512 | tf_op jit(solution)/shard_map/ppermute | solution.py:983
  223.2 0.7 collective-permute-start.25
  224.0 3.7 %density.1 = f32[1280,1280]{1,0:T(8,128)} custom-call(s32[12]{0:T(128)S(1)} %copy-done.10, f32[1]{0:T(128)} %get-tuple-element.84.gain_ref, bf16[1280,1280]{1,0:T(8,128)(2,1)S(1)} %copy-done.1, bf16[640,1280]{1,0:T(8,128)(2,1)S(1)} %collective-permute-done.26.far_ref, f32[40,128]{1,0:T(8,128)S(1)} %copy-done.6, ...), custom_call_target="tpu_custom_call", output_to_operand_aliasing={{}: (5, {})} | custom-call | tf_op jit(solution)/shard_map/density/pallas_call | solution.py:846
  227.7 0.2 collective-permute-done.25.far_ref
  227.9 0.6 copy-done.23
  228.5 5.7 %pull.1 = f32[3,512]{1,0:T(4,128)} custom-call(f32[1]{0:T(128)} %get-tuple-element.84.gain_ref, f32[3,5120]{1,0:T(4,128)} %spots_ref.3, f32[40,128]{1,0:T(8,128)} %copy-done.11, f32[40,128]{1,0:T(8,128)} %copy-done.21, f32[40,128]{1,0:T(8,128)} %copy-done.23, bf16[512,5120]{1,0:T(8,128)(2,1)} %copy-done.2, f32[3,512]{1,0:T(4,128)} %coords_ref.1, ...), custom_call_target="tpu_custom_call" | custom-call | tf_op jit(solution)/shard_map/pull/pallas_call | solution.py:790
  (65 shorter events, 0.5 us)
Async XLA Ops:
  0.6 12.4 %copy-start.22 = (f32[3,512]{1,0:T(4,128)S(1)}, f32[3,512]{1,0:T(4,128)}, u32[]{:S(2)}) copy-start(f32[3,512]{1,0:T(4,128)} %coords_ref.1) | copy-start | bytes 18436
  0.6 12.4 %copy-start.24 = (f32[512]{0:T(512)S(1)}, f32[512]{0:T(512)}, u32[]{:S(2)}) copy-start(f32[512]{0:T(512)} %param.9) | copy-start | bytes 6148
  0.7 23.2 %copy-start = (bf16[1280,1280]{1,0:T(8,128)(2,1)S(1)}, bf16[1280,1280]{1,0:T(8,128)(2,1)}, u32[]{:S(2)}) copy-start(bf16[1280,1280]{1,0:T(8,128)(2,1)} %ham_ref.1) | copy-start | bytes 9830404
  4.1 5.5 %collective-permute-start.1 = (bf16[640,1280]{1,0:T(8,128)(2,1)S(1)}, bf16[640,1280]{1,0:T(8,128)(2,1)}, u32[]{:S(2)}, u32[]{:S(2)}) collective-permute-start(bf16[640,1280]{1,0:T(8,128)(2,1)S(1)} %get-tuple-element.100), channel_id=1, source_target_pairs={{0,1},{1,0},{2,3},{3,2},{4,5},{5,4},{6,7},{7,6},{8,9},{9,8},{10,11... | collective-permute-start | bytes 4915208 | tf_op jit(solution)/shard_map/ppermute | solution.py:881
  4.6 27.7 %collective-permute-start.4 = (bf16[640,1280]{1,0:T(8,128)(2,1)}, bf16[640,1280]{1,0:T(8,128)(2,1)}, u32[]{:S(2)}, u32[]{:S(2)}) collective-permute-start(bf16[640,1280]{1,0:T(8,128)(2,1)} %get-tuple-element.101), channel_id=1, source_target_pairs={{0,1},{1,0},{2,3},{3,2},{4,5},{5,4},{6,7},{7,6},{8,9},{9,8},{10,11... | collective-permute-start | bytes 4915208 | tf_op jit(solution)/shard_map/ppermute | solution.py:881
  4.6 35.1 %collective-permute-start = (bf16[640,1280]{1,0:T(8,128)(2,1)}, bf16[640,1280]{1,0:T(8,128)(2,1)}, u32[]{:S(2)}, u32[]{:S(2)}) collective-permute-start(bf16[640,1280]{1,0:T(8,128)(2,1)} %get-tuple-element.101), channel_id=1, source_target_pairs={{0,5},{1,3},{2,15},{3,1},{4,6},{5,8},{6,4},{7,2},{8,13},{9,11},{10... | collective-permute-start | bytes 4915208 | tf_op jit(solution)/shard_map/ppermute | solution.py:898
  9.6 34.3 %collective-permute-start.2 = (bf16[640,1280]{1,0:T(8,128)(2,1)}, bf16[640,1280]{1,0:T(8,128)(2,1)}, u32[]{:S(2)}, u32[]{:S(2)}) collective-permute-start(bf16[640,1280]{1,0:T(8,128)(2,1)} %collective-permute-done.1.refs_1_), channel_id=1, source_target_pairs={{0,2},{1,4},{2,0},{3,14},{4,9},{5,7},{6,3},{7,5},{8,10},{9,12},{10... | collective-permute-start | bytes 4915208 | tf_op jit(solution)/shard_map/ppermute | solution.py:898
  13.2 0.9 copy-start.4
  21.6 2.3 copy-start.2
  23.9 3.8 %copy-start.7 = (f32[1,5120]{1,0:T(1,128)}, f32[1,5120]{1,0:T(1,128)S(1)}, u32[]{:S(2)}) copy-start(f32[1,5120]{1,0:T(1,128)S(1)} %get-tuple-element.50) | copy-start | bytes 61444
  29.4 2.2 collective-permute-start.3
  31.5 15.7 %copy-start.8 = (s32[12]{0:T(128)}, s32[12]{0:T(128)S(1)}, u32[]{:S(2)}) copy-start(s32[12]{0:T(128)S(1)} %fusion.2.info_ref) | copy-start | bytes 148
  47.2 8.3 %collective-permute-start.8 = (bf16[640,1280]{1,0:T(8,128)(2,1)}, bf16[640,1280]{1,0:T(8,128)(2,1)S(1)}, u32[]{:S(2)}, u32[]{:S(2)}) collective-permute-start(bf16[640,1280]{1,0:T(8,128)(2,1)} %collective-permute-done.refs_2_.refs_3_), channel_id=1, source_target_pairs={{0,1},{1,0},{2,3},{3,2},{4,5},{5,4},{6,7},{7,6},{8,9},{9,8},{10,11... | collective-permute-start | bytes 4915208 | tf_op jit(solution)/shard_map/ppermute | solution.py:881
  49.2 6.3 %collective-permute-start.9 = (bf16[640,1280]{1,0:T(8,128)(2,1)}, bf16[640,1280]{1,0:T(8,128)(2,1)S(1)}, u32[]{:S(2)}, u32[]{:S(2)}) collective-permute-start(bf16[640,1280]{1,0:T(8,128)(2,1)} %collective-permute-done.2.refs_3_.refs_4_), channel_id=1, source_target_pairs={{0,1},{1,0},{2,3},{3,2},{4,5},{5,4},{6,7},{7,6},{8,9},{9,8},{10,11... | collective-permute-start | bytes 4915208 | tf_op jit(solution)/shard_map/ppermute | solution.py:881
  49.3 39.1 %collective-permute-start.5 = (bf16[640,1280]{1,0:T(8,128)(2,1)S(1)}, bf16[640,1280]{1,0:T(8,128)(2,1)}, u32[]{:S(2)}, u32[]{:S(2)}) collective-permute-start(bf16[640,1280]{1,0:T(8,128)(2,1)S(1)} %get-tuple-element.57), channel_id=1, source_target_pairs={{0,2},{2,0},{1,3},{3,1},{4,6},{6,4},{5,7},{7,5},{8,10},{10,8},{9,1... | collective-permute-start | bytes 4915208 | tf_op jit(solution)/shard_map/ppermute | solution.py:884
  50.9 39.6 %collective-permute-start.6 = (bf16[640,1280]{1,0:T(8,128)(2,1)S(1)}, bf16[640,1280]{1,0:T(8,128)(2,1)}, u32[]{:S(2)}, u32[]{:S(2)}) collective-permute-start(bf16[640,1280]{1,0:T(8,128)(2,1)S(1)} %get-tuple-element.58), channel_id=1, source_target_pairs={{0,12},{12,8},{8,4},{4,0},{2,6},{6,10},{10,14},{14,2},{1,13},{13,9... | collective-permute-start | bytes 4915208 | tf_op jit(solution)/shard_map/ppermute | solution.py:888
  55.5 32.9 %collective-permute-start.7 = (f32[88,128]{1,0:T(8,128)S(1)}, f32[88,128]{1,0:T(8,128)S(1)}, u32[]{:S(2)}, u32[]{:S(2)}) collective-permute-start(f32[88,128]{1,0:T(8,128)S(1)} %fusion.3), channel_id=1, source_target_pairs={{0,2},{2,0},{1,3},{3,1},{4,6},{6,4},{5,7},{7,5},{8,10},{10,8},{9,1... | collective-permute-start | bytes 135176 | tf_op jit(solution)/shard_map/ppermute | solution.py:884
  55.5 1.2 copy-start.12
  56.7 1.2 copy-start.13
  90.6 5.5 %collective-permute-start.16 = (bf16[640,1280]{1,0:T(8,128)(2,1)}, bf16[640,1280]{1,0:T(8,128)(2,1)S(1)}, u32[]{:S(2)}, u32[]{:S(2)}) collective-permute-start(bf16[640,1280]{1,0:T(8,128)(2,1)} %collective-permute-done.6.refs_9_), channel_id=1, source_target_pairs={{0,1},{1,0},{2,3},{3,2},{4,5},{5,4},{6,7},{7,6},{8,9},{9,8},{10,11... | collective-permute-start | bytes 4915208 | tf_op jit(solution)/shard_map/ppermute | solution.py:881
  90.6 6.1 %collective-permute-start.15 = (bf16[640,1280]{1,0:T(8,128)(2,1)}, bf16[640,1280]{1,0:T(8,128)(2,1)S(1)}, u32[]{:S(2)}, u32[]{:S(2)}) collective-permute-start(bf16[640,1280]{1,0:T(8,128)(2,1)} %collective-permute-done.5.refs_7_), channel_id=1, source_target_pairs={{0,1},{1,0},{2,3},{3,2},{4,5},{5,4},{6,7},{7,6},{8,9},{9,8},{10,11... | collective-permute-start | bytes 4915208 | tf_op jit(solution)/shard_map/ppermute | solution.py:881
  91.1 44.4 %collective-permute-start.10 = (bf16[640,1280]{1,0:T(8,128)(2,1)}, bf16[640,1280]{1,0:T(8,128)(2,1)}, u32[]{:S(2)}, u32[]{:S(2)}) collective-permute-start(bf16[640,1280]{1,0:T(8,128)(2,1)} %collective-permute-done.6.refs_9_), channel_id=1, source_target_pairs={{0,2},{2,0},{1,3},{3,1},{4,6},{6,4},{5,7},{7,5},{8,10},{10,8},{9,1... | collective-permute-start | bytes 4915208 | tf_op jit(solution)/shard_map/ppermute | solution.py:884
  92.2 43.3 %collective-permute-start.11 = (bf16[640,1280]{1,0:T(8,128)(2,1)}, bf16[640,1280]{1,0:T(8,128)(2,1)S(1)}, u32[]{:S(2)}, u32[]{:S(2)}) collective-permute-start(bf16[640,1280]{1,0:T(8,128)(2,1)} %collective-permute-done.5.refs_7_), channel_id=1, source_target_pairs={{0,4},{4,8},{8,12},{12,0},{2,14},{14,10},{10,6},{6,2},{1,5},{5,9},... | collective-permute-start | bytes 4915208 | tf_op jit(solution)/shard_map/ppermute | solution.py:888
  92.2 37.4 %collective-permute-start.14 = (f32[88,128]{1,0:T(8,128)S(1)}, f32[88,128]{1,0:T(8,128)S(1)}, u32[]{:S(2)}, u32[]{:S(2)}) collective-permute-start(f32[88,128]{1,0:T(8,128)S(1)} %add.62.own_ref), channel_id=1, source_target_pairs={{0,12},{4,0},{8,4},{12,8},{1,13},{5,1},{9,5},{13,9},{2,14},{6,2},{... | collective-permute-start | bytes 135176 | tf_op jit(solution)/shard_map/ppermute | solution.py:949
  96.0 3.2 %copy-start.15 = (bf16[640,1280]{1,0:T(8,128)(2,1)}, bf16[640,1280]{1,0:T(8,128)(2,1)S(1)}, u32[]{:S(2)}) copy-start(bf16[640,1280]{1,0:T(8,128)(2,1)S(1)} %collective-permute-done.16.refs_10_) | copy-start | bytes 4915204
  96.0 39.5 %collective-permute-start.13 = (f32[88,128]{1,0:T(8,128)S(1)}, f32[88,128]{1,0:T(8,128)S(1)}, u32[]{:S(2)}, u32[]{:S(2)}) collective-permute-start(f32[88,128]{1,0:T(8,128)S(1)} %add.62.own_ref), channel_id=1, source_target_pairs={{0,8},{4,12},{8,0},{12,4},{1,9},{5,13},{9,1},{13,5},{2,10},{6,14},... | collective-permute-start | bytes 135176 | tf_op jit(solution)/shard_map/ppermute | solution.py:949
  96.6 2.6 %copy-start.16 = (bf16[640,1280]{1,0:T(8,128)(2,1)}, bf16[640,1280]{1,0:T(8,128)(2,1)S(1)}, u32[]{:S(2)}) copy-start(bf16[640,1280]{1,0:T(8,128)(2,1)S(1)} %collective-permute-done.15.refs_8_) | copy-start | bytes 4915204
  96.6 38.9 %collective-permute-start.12 = (f32[88,128]{1,0:T(8,128)S(1)}, f32[88,128]{1,0:T(8,128)S(1)}, u32[]{:S(2)}, u32[]{:S(2)}) collective-permute-start(f32[88,128]{1,0:T(8,128)S(1)} %add.62.own_ref), channel_id=1, source_target_pairs={{0,4},{4,8},{8,12},{12,0},{1,5},{5,9},{9,13},{13,1},{2,6},{6,10},{... | collective-permute-start | bytes 135176 | tf_op jit(solution)/shard_map/ppermute | solution.py:949
  99.2 37.5 %copy-start.9 = (s32[12]{0:T(128)S(1)}, s32[12]{0:T(128)}, u32[]{:S(2)}) copy-start(s32[12]{0:T(128)} %copy-done.8) | copy-start | bytes 148
  135.5 1.3 copy-start.14
  135.5 11.7 %collective-permute-start.19 = (bf16[640,1280]{1,0:T(8,128)(2,1)}, bf16[640,1280]{1,0:T(8,128)(2,1)S(1)}, u32[]{:S(2)}, u32[]{:S(2)}) collective-permute-start(bf16[640,1280]{1,0:T(8,128)(2,1)} %collective-permute-done.10.refs_11_), channel_id=1, source_target_pairs={{0,1},{1,0},{2,3},{3,2},{4,5},{5,4},{6,7},{7,6},{8,9},{9,8},{10,11... | collective-permute-start | bytes 4915208 | tf_op jit(solution)/shard_map/ppermute | solution.py:881
  135.6 11.6 %collective-permute-start.20 = (bf16[640,1280]{1,0:T(8,128)(2,1)S(1)}, bf16[640,1280]{1,0:T(8,128)(2,1)S(1)}, u32[]{:S(2)}, u32[]{:S(2)}) collective-permute-start(bf16[640,1280]{1,0:T(8,128)(2,1)S(1)} %collective-permute-done.11.refs_0_.refs_13_), channel_id=1, source_target_pairs={{0,1},{1,0},{2,3},{3,2},{4,5},{5,4},{6,7},{7,6},{8,9},{9,8},{10,11... | collective-permute-start | bytes 4915208 | tf_op jit(solution)/shard_map/ppermute | solution.py:881
  139.2 39.9 %collective-permute-start.18 = (bf16[640,1280]{1,0:T(8,128)(2,1)S(1)}, bf16[640,1280]{1,0:T(8,128)(2,1)}, u32[]{:S(2)}, u32[]{:S(2)}) collective-permute-start(bf16[640,1280]{1,0:T(8,128)(2,1)S(1)} %pick.3), channel_id=1, source_target_pairs={{0,4},{4,8},{8,12},{12,0},{2,14},{14,10},{10,6},{6,2},{1,5},{5,9},... | collective-permute-start | bytes 4915208 | tf_op jit(solution)/shard_map/ppermute | solution.py:888
  139.5 40.1 %collective-permute-start.17 = (bf16[640,1280]{1,0:T(8,128)(2,1)S(1)}, bf16[640,1280]{1,0:T(8,128)(2,1)}, u32[]{:S(2)}, u32[]{:S(2)}) collective-permute-start(bf16[640,1280]{1,0:T(8,128)(2,1)S(1)} %pick.3), channel_id=1, source_target_pairs={{0,2},{2,0},{1,3},{3,1},{4,6},{6,4},{5,7},{7,5},{8,10},{10,8},{9,1... | collective-permute-start | bytes 4915208 | tf_op jit(solution)/shard_map/ppermute | solution.py:884
  145.3 0.7 copy-start.3
  146.0 0.6 copy-start.5
  146.6 0.6 copy-start.11
  147.2 1.7 copy-start.17
  147.2 1.2 copy-start.18
  179.6 3.7 %collective-permute-start.21 = (bf16[640,1280]{1,0:T(8,128)(2,1)}, bf16[640,1280]{1,0:T(8,128)(2,1)S(1)}, u32[]{:S(2)}, u32[]{:S(2)}) collective-permute-start(bf16[640,1280]{1,0:T(8,128)(2,1)} %collective-permute-done.17.refs_15_), channel_id=1, source_target_pairs={{0,1},{1,0},{2,3},{3,2},{4,5},{5,4},{6,7},{7,6},{8,9},{9,8},{10,11... | collective-permute-start | bytes 4915208 | tf_op jit(solution)/shard_map/ppermute | solution.py:881
  179.6 6.1 %collective-permute-start.22 = (bf16[640,1280]{1,0:T(8,128)(2,1)}, bf16[640,1280]{1,0:T(8,128)(2,1)S(1)}, u32[]{:S(2)}, u32[]{:S(2)}) collective-permute-start(bf16[640,1280]{1,0:T(8,128)(2,1)} %collective-permute-done.18.refs_17_), channel_id=1, source_target_pairs={{0,1},{1,0},{2,3},{3,2},{4,5},{5,4},{6,7},{7,6},{8,9},{9,8},{10,11... | collective-permute-start | bytes 4915208 | tf_op jit(solution)/shard_map/ppermute | solution.py:881
  183.3 2.3 %copy-start.19 = (bf16[640,1280]{1,0:T(8,128)(2,1)}, bf16[640,1280]{1,0:T(8,128)(2,1)S(1)}, u32[]{:S(2)}) copy-start(bf16[640,1280]{1,0:T(8,128)(2,1)S(1)} %collective-permute-done.21.refs_16_) | copy-start | bytes 4915204
  185.7 1.2 copy-start.20
  186.8 37.1 %copy-start.1 = (bf16[1280,1280]{1,0:T(8,128)(2,1)S(1)}, bf16[1280,1280]{1,0:T(8,128)(2,1)}, u32[]{:S(2)}) copy-start(bf16[1280,1280]{1,0:T(8,128)(2,1)} %ham_ref.1) | copy-start | bytes 9830404
  186.8 37.1 %copy-start.6 = (f32[40,128]{1,0:T(8,128)S(1)}, f32[40,128]{1,0:T(8,128)}, u32[]{:S(2)}) copy-start(f32[40,128]{1,0:T(8,128)} %copy-done.5) | copy-start | bytes 61444
  186.8 37.1 %copy-start.10 = (s32[12]{0:T(128)S(1)}, s32[12]{0:T(128)}, u32[]{:S(2)}) copy-start(s32[12]{0:T(128)} %copy-done.8) | copy-start | bytes 148
  214.9 9.1 %collective-permute-start.26 = (bf16[640,1280]{1,0:T(8,128)(2,1)}, bf16[640,1280]{1,0:T(8,128)(2,1)S(1)}, u32[]{:S(2)}, u32[]{:S(2)}) collective-permute-start(bf16[640,1280]{1,0:T(8,128)(2,1)} %get-tuple-element.92), channel_id=1, source_target_pairs={{0,1},{1,0},{2,3},{3,2},{4,5},{5,4},{6,7},{7,6},{8,9},{9,8},{10,11... | collective-permute-start | bytes 4915208 | tf_op jit(solution)/shard_map/ppermute | solution.py:881
  214.9 3.7 %collective-permute-start.23 = (f32[40,128]{1,0:T(8,128)}, f32[40,128]{1,0:T(8,128)S(1)}, u32[]{:S(2)}, u32[]{:S(2)}) collective-permute-start(f32[40,128]{1,0:T(8,128)} %get-tuple-element.91), channel_id=1, source_target_pairs={{0,1},{1,0},{2,3},{3,2},{4,5},{5,4},{6,7},{7,6},{8,9},{9,8},{10,11... | collective-permute-start | bytes 61448 | tf_op jit(solution)/shard_map/ppermute | solution.py:881
  219.4 3.8 %collective-permute-start.24 = (f32[40,128]{1,0:T(8,128)S(1)}, f32[40,128]{1,0:T(8,128)S(1)}, u32[]{:S(2)}, u32[]{:S(2)}) collective-permute-start(f32[40,128]{1,0:T(8,128)S(1)} %add.63), channel_id=1, source_target_pairs={{0,4},{4,0},{8,12},{12,8},{1,5},{5,1},{9,13},{13,9},{2,6},{6,2},{1... | collective-permute-start | bytes 61448 | tf_op jit(solution)/shard_map/ppermute | solution.py:983
  223.2 4.5 %copy-start.21 = (f32[40,128]{1,0:T(8,128)}, f32[40,128]{1,0:T(8,128)S(1)}, u32[]{:S(2)}) copy-start(f32[40,128]{1,0:T(8,128)S(1)} %add.64.near_ref) | copy-start | bytes 61444
  223.2 4.7 %collective-permute-start.25 = (f32[40,128]{1,0:T(8,128)S(1)}, f32[40,128]{1,0:T(8,128)S(1)}, u32[]{:S(2)}, u32[]{:S(2)}) collective-permute-start(f32[40,128]{1,0:T(8,128)S(1)} %add.64.near_ref), channel_id=1, source_target_pairs={{0,8},{4,12},{8,0},{12,4},{1,9},{5,13},{9,1},{13,5},{2,10},{6,14},... | collective-permute-start | bytes 61448 | tf_op jit(solution)/shard_map/ppermute | solution.py:984
  227.9 0.6 copy-start.23

commit v5 on v4

--- a/solution.py
+++ b/solution.py
@@ -545,7 +545,13 @@
         worker.load_block(2 + k, table_ref[slots_at + k], sources)
     ham_copy = pltpu.make_async_copy(row_refs[0].at[worker.near], ham_ref, ham_sem)
     sent_copy = pltpu.make_async_copy(sent_ref, cube_ref, out_sem.at[0])
-    density_copy = pltpu.make_async_copy(total_ref.at[4 + core], density_ref.at[worker.near], out_sem.at[1])
+    parts = 5
+    rows_each = half // parts
+
+    def density_copy(part):
+        rows = pl.ds(pl.multiple_of(part * rows_each, rows_each), rows_each)
+        to = pl.ds(pl.multiple_of(core * half + part * rows_each, rows_each), rows_each)
+        return pltpu.make_async_copy(total_ref.at[4 + core, rows], density_ref.at[to], out_sem.at[1])
 
     def send(field):
         sent_ref[...] = total_ref[field[4]].astype(sent_ref.dtype)
@@ -559,36 +565,37 @@
     gain = gain_ref[0]
     linear, cubic = -1.5 * gain, 2.0 * (gain * gain * gain)
 
-    def one(index, carry):
-        rows = pl.ds(pl.multiple_of(index * 16, 16), 16)
-        for m in range(width // 128):
-            at = slice(m * 128, (m + 1) * 128)
-            cube = total_ref[4 + core, rows, at]
-            total_ref[4 + core, rows, at] = linear * ham_ref[rows, at].astype(jnp.float32) + cubic * cube
+    eye = lax.broadcasted_iota(jnp.int32, (128, 128), 0) == lax.broadcasted_iota(jnp.int32, (128, 128), 1)
+
+    def one_part(part, carry):
+        def one(index, carry):
+            rows = pl.ds(pl.multiple_of(part * rows_each + index * 16, 16), 16)
+            for m in range(width // 128):
+                at = slice(m * 128, (m + 1) * 128)
+                cube = total_ref[4 + core, rows, at]
+                total_ref[4 + core, rows, at] = linear * ham_ref[rows, at].astype(jnp.float32) + cubic * cube
+            return carry
+
+        lax.fori_loop(0, rows_each // 16, one, 0, unroll=2)
+
+        @pl.when(row == 2 * col + core)
+        def _():
+            rows = pl.ds(pl.multiple_of(part * rows_each, rows_each), rows_each)
+            at = pl.ds(pl.multiple_of(core * half + part * rows_each, rows_each), rows_each)
+            total_ref[4 + core, rows, at] += jnp.where(eye, 0.5 + linear * level_rows_ref[rows, :], 0.0)
+
+        density_copy(part).start()
         return carry
 
-    lax.fori_loop(0, half // 16, one, 0, unroll=2)
-
-    @pl.when(row == 2 * col + core)
-    def _():
-        eye = lax.broadcasted_iota(jnp.int32, (128, 128), 0) == lax.broadcasted_iota(jnp.int32, (128, 128), 1)
-
-        def fix(index, carry):
-            rows = pl.ds(pl.multiple_of(index * 128, 128), 128)
-            at = pl.ds(pl.multiple_of(core * half + index * 128, 128), 128)
-            total_ref[4 + core, rows, at] += jnp.where(eye, 0.5 + linear * level_rows_ref[rows, :], 0.0)
-            return carry
-
-        lax.fori_loop(0, half // 128, fix, 0)
-
-    density_copy.start()
+    lax.fori_loop(0, parts, one_part, 0)
     lines = half // 128
     cube_diag_ref[...] = jnp.zeros_like(cube_diag_ref)
     for k in range(lines):
         share = jnp.sum(diag_ref[pl.ds(k * 128, 128), :].T, 0, keepdims=True)
         cube_diag_ref[pl.ds((2 * row + core) * lines + k, 1), :] = share
     sent_copy.wait()
-    density_copy.wait()
+    for part in range(parts):
+        density_copy(part).wait()
 
 
 HERE = pl.BlockSpec(memory_space=pltpu.HBM)
@@ -626,13 +633,12 @@
 
 
 def pick_kernel(choices, whole, count, info_ref, *refs):
-    sources, refs = refs[:count], refs[count:]
-    outs, held_ref, in_sem, out_sem = refs[:-3], refs[-3], refs[-2], refs[-1]
+    sources, outs, in_sem = refs[:count], refs[count:-1], refs[-1]
     parts = in_sem.shape[1]
-    size = held_ref.shape[1] // parts
+    size = outs[0].shape[0] // parts
     for part in range(parts):
         for k, choice in enumerate(choices):
-            to = held_ref.at[k, pl.ds(part * size, size)]
+            to = outs[k].at[pl.ds(part * size, size)]
             for number, source in enumerate(sources):
                 @pl.when(info_ref[choice] == number)
                 def _():
@@ -642,28 +648,18 @@
                     pltpu.make_async_copy(source.at[pl.ds(first, size)], to, in_sem.at[k, part]).start()
     for part in range(parts):
         for k, out_ref in enumerate(outs):
-            rows = pl.ds(part * size, size)
-            pltpu.make_async_copy(held_ref.at[k, rows], held_ref.at[k, rows], in_sem.at[k, part]).wait()
-            pltpu.make_async_copy(held_ref.at[k, rows], out_ref.at[rows], out_sem.at[k, part]).start()
-    for part in range(parts):
-        for k, out_ref in enumerate(outs):
-            rows = pl.ds(part * size, size)
-            pltpu.make_async_copy(held_ref.at[k, rows], out_ref.at[rows], out_sem.at[k, part]).wait()
+            to = out_ref.at[pl.ds(part * size, size)]
+            pltpu.make_async_copy(to, to, in_sem.at[k, part]).wait()
 
 
 def pick(info, choices, sources, whole, shape):
-    dtype = sources[0].dtype
     parts = 4
     return pl.pallas_call(
         functools.partial(pick_kernel, choices, whole, len(sources)),
-        out_shape=[jax.ShapeDtypeStruct(shape, dtype)] * len(choices),
+        out_shape=[pltpu.VMEM(shape, sources[0].dtype)] * len(choices),
         in_specs=[SCALARS] + [HERE] * len(sources),
-        out_specs=[HERE] * len(choices),
-        scratch_shapes=[
-            pltpu.VMEM((len(choices),) + shape, dtype),
-            pltpu.SemaphoreType.DMA((len(choices), parts)),
-            pltpu.SemaphoreType.DMA((len(choices), parts)),
-        ],
+        out_specs=[VMEM] * len(choices),
+        scratch_shapes=[pltpu.SemaphoreType.DMA((len(choices), parts))],
         compiler_params=pltpu.CompilerParams(vmem_limit_bytes=8 * 2**20),
         name="pick",
     )(info, *in_hbm(sources))
@@ -714,9 +710,9 @@
     )(centers, points)
 
 
-def levels_kernel(info_ref, own_ref, first_ref, second_ref, third_ref, gain_ref, level_ref, above_ref, rows_ref):
+def levels_kernel(info_ref, near_ref, far_ref, gain_ref, level_ref, above_ref, rows_ref):
     lines = level_ref.shape[0]
-    sums = own_ref[...] + first_ref[...] + second_ref[...] + third_ref[...]
+    sums = near_ref[...] + far_ref[...]
     potential, diag = sums[0:lines], sums[lines : 2 * lines] + sums[0:lines]
     total = float(lines * 128)
     mean = jnp.sum(diag) / total
@@ -738,7 +734,7 @@
     return pl.pallas_call(
         levels_kernel,
         out_shape=(jax.ShapeDtypeStruct((1,), jnp.float32), line, line, jax.ShapeDtypeStruct((half, 128), jnp.float32)),
-        in_specs=[SCALARS] + [VMEM] * 4,
+        in_specs=[SCALARS] + [VMEM] * 2,
         out_specs=(SCALARS, VMEM, VMEM, VMEM),
         compiler_params=pltpu.CompilerParams(vmem_limit_bytes=4 * 2**20),
         name="levels",
@@ -749,62 +745,51 @@
 
 
 def pull_kernel(gain_ref, spots_ref, above_ref, near_ref, far_ref, weight_ref, coords_ref, charge_ref, out_ref, total_ref):
-    index = pl.program_id(0)
     gain = gain_ref[0]
-    width = spots_ref.shape[1]
-    pieces = []
-    for m in range(width // 128):
-        line = pl.ds(index * (width // 128) + m, 1)
-        cube = near_ref[line, :] + far_ref[line, :]
-        pieces.append(0.5 - 1.5 * gain * above_ref[line, :] + 2.0 * (gain * gain * gain) * cube)
-    occ = jnp.concatenate(pieces, 1)
-    weights = [occ] + [occ * (spots_ref[k : k + 1, :] - MIDDLE) for k in range(3)]
-    stacked = jnp.concatenate(weights + [jnp.zeros((4, width), jnp.float32)], 0)
-    high = stacked.astype(jnp.bfloat16)
-    low = (stacked - high.astype(jnp.float32)).astype(jnp.bfloat16)
-    blank = jnp.zeros((128 - 16, width), jnp.bfloat16)
-    both = jnp.concatenate([high, low, blank], 0)
-    dims = (((1,), (1,)), ((), ()))
-    part = lax.dot_general(weight_ref[...], both, dims, preferred_element_type=jnp.float32)
-
-    @pl.when(index == 0)
-    def _():
-        total_ref[...] = part
-
-    @pl.when(index > 0)
-    def _():
-        total_ref[...] += part
-
-    @pl.when(index == pl.num_programs(0) - 1)
-    def _():
-        sums = total_ref[...].T
-        sums = sums[0:8] + sums[8:16]
-        for k in range(3):
-            pull = (coords_ref[k : k + 1, :] - MIDDLE) * sums[0:1] - sums[k + 1 : k + 2]
-            out_ref[k : k + 1, :] = -charge_ref[...] * pull
+    lines = 10
+    width = lines * 128
+
+    def one(index, carry):
+        lanes = pl.ds(pl.multiple_of(index * width, width), width)
+        pieces = []
+        for m in range(lines):
+            line = pl.ds(index * lines + m, 1)
+            cube = near_ref[line, :] + far_ref[line, :]
+            pieces.append(0.5 - 1.5 * gain * above_ref[line, :] + 2.0 * (gain * gain * gain) * cube)
+        occ = jnp.concatenate(pieces, 1)
+        weights = [occ] + [occ * (spots_ref[k : k + 1, lanes] - MIDDLE) for k in range(3)]
+        stacked = jnp.concatenate(weights + [jnp.zeros((4, width), jnp.float32)], 0)
+        high = stacked.astype(jnp.bfloat16)
+        low = (stacked - high.astype(jnp.float32)).astype(jnp.bfloat16)
+        both = jnp.concatenate([high, low, jnp.zeros((128 - 16, width), jnp.bfloat16)], 0)
+        total_ref[...] += lax.dot_general(
+            weight_ref[:, lanes], both, (((1,), (1,)), ((), ())), preferred_element_type=jnp.float32
+        )
+        return carry
+
+    total_ref[...] = jnp.zeros_like(total_ref)
+    lax.fori_loop(0, spots_ref.shape[1] // width, one, 0)
+    sums = total_ref[...].T
+    sums = sums[0:8] + sums[8:16]
+    for k in range(3):
+        pull = (coords_ref[k : k + 1, :] - MIDDLE) * sums[0:1] - sums[k + 1 : k + 2]
+        out_ref[k : k + 1, :] = -charge_ref[...] * pull
 
 
 def pull_terms(gain, centers, above, near, far, weights, mm_coords, mm_charges):
-    total, count = centers.shape[1], mm_coords.shape[1]
-    width = 1280
+    count = mm_coords.shape[1]
     return pl.pallas_call(
         pull_kernel,
-        grid=(total // width,),
         out_shape=jax.ShapeDtypeStruct((3, count), jnp.float32),
-        in_specs=[
-            SCALARS,
-            pl.BlockSpec((3, width), lambda i: (0, i)),
-            pl.BlockSpec(above.shape, lambda i: (0, 0)),
-            pl.BlockSpec(above.shape, lambda i: (0, 0)),
-            pl.BlockSpec(above.shape, lambda i: (0, 0)),
-            pl.BlockSpec((count, width), lambda i: (0, i)),
-            pl.BlockSpec((3, count), lambda i: (0, 0)),
-            pl.BlockSpec((1, count), lambda i: (0, 0)),
-        ],
-        out_specs=pl.BlockSpec((3, count), lambda i: (0, 0)),
+        in_specs=[SCALARS] + [VMEM] * 7,
+        out_specs=VMEM,
         scratch_shapes=[pltpu.VMEM((count, 128), jnp.float32)],
+        compiler_params=pltpu.CompilerParams(vmem_limit_bytes=16 * 2**20),
         name="pull",
-    )(gain, centers, above, near, far, weights, mm_coords, mm_charges[None])
+    )(
+        gain, centers, above, near, far, pltpu.with_memory_space_constraint(weights, pltpu.VMEM), mm_coords,
+        mm_charges[None],
+    )
 
 
 def density_kernel(steps, info_ref, gain_ref, ham_ref, far_ref, level_ref, _, out_ref):
@@ -923,12 +908,15 @@
     diag = lax.dynamic_update_slice_in_dim(jnp.zeros((total,), jnp.float32), own_diag, col_start, 0)
     packed = jnp.concatenate([terms[0], diag, jnp.full((8 * 128,), own_off)]).reshape(-1, 128)
     packed = packed + over_rep(packed)
-    firsts, (packed, weights, table, other) = after(firsts, (packed, weights, table, other))
+    from_col = over_col(packed)
+    (firsts, from_col), (packed, weights, table, other) = after((firsts, from_col), (packed, weights, table, other))
     own_parts = [h_core, got, other]
     sends = pick(info, (SEND_X2, SEND_Z2), (h_core, got) + tuple(firsts), 1, shape)
     firsts, sends = lax.optimization_barrier((list(firsts), sends))
     x2 = over_col(sends[0])
     z2 = over_sec(sends[1], 1)
+    packed = packed + from_col
+    from_near = lax.ppermute(packed, "sec", [(i, i ^ 1) for i in range(4)])
     operands = own_parts + firsts + [over_rep(first) for first in firsts]
 
     def grow_square(stage, left_count, slots, totals, token):
@@ -939,20 +927,20 @@
         )
 
     totals, token = grow_square(0, 3, (OWN0, OWN1, X1, Z1), None, None)
-    col_packed = over_col(packed)
-    (x2, z2, col_packed), (token, packed) = after((x2, z2, col_packed), (token, packed))
+    (x2, z2, from_near), (token, packed) = after((x2, z2, from_near), (token, packed))
     x3 = over_col(z2)
     z3 = over_sec(x2, 2)
     operands = operands + flat(swap_all((x2, z2)))
     totals, token = grow_square(1, 4, (OWN0, OWN1, X1, Z1, X2, Z2), totals, token)
-    packed = packed + col_packed
-    others = [lax.ppermute(packed, "sec", [(i, (i + hop) % 4) for i in range(4)]) for hop in (1, 2, 3)]
-    (x3, z3, others), (token, packed) = after((x3, z3, others), (token, packed))
+    packed = packed + from_near
+    from_far = lax.ppermute(packed, "sec", [(i, i ^ 2) for i in range(4)])
+    (x3, z3, from_far), (token, packed) = after((x3, z3, from_far), (token, packed))
     last_send = pick(info, (SEND_LAST,), [z3] + operands[5:7], 0, shape)[0]
+    (x3, z3), last_send = after((x3, z3), last_send)
     x4 = over_col(last_send)
     z4 = over_sec(last_send, 3)
     operands = operands + flat(swap_all((x3, z3)))
-    gain, level, above, level_rows = level_terms(info, [packed] + list(others), total // 128, half)
+    gain, level, above, level_rows = level_terms(info, [packed, from_far], total // 128, half)
     lines = jax.ShapeDtypeStruct((total // 128, 128), jnp.float32)
     share = jax.ShapeDtypeStruct((half, 128), jnp.float32)
     totals, cube_diag = call_kernel(

time: 235 us -> 232 us (0.987)
  Pallas kernels: 116 us -> 112 us
  local copies, waits for them, and re-layouts: 18.2 us -> 21.9 us
    ppermute x2, waiting for transfers between devices: 11.6 us -> 0.01 us  [over_both(): return lax.ppermute(value, ('sec', 'col', 'rep'), moves)]
    ppermute x3 -> x2, waiting for transfers between devices: 22.2 us -> 32.4 us  [the longest x1 21.2 us: gossip_shards(): from_far = lax.ppermute(packed, 'sec', [(i, i ^ 2) for i in range(4)])]
    ppermute x3 -> x2, starting transfers between devices: 6.52 us -> 1.98 us  [the longest x1 1.98 us: gossip_shards(): from_far = lax.ppermute(packed, 'sec', [(i, i ^ 2) for i in range(4)])]
    ppermute x4, starting transfers between devices: 7.19 us -> 10.5 us  [over_col(): return lax.ppermute(value, 'col', [(0, 1), (1, 0)])]
    unnamed x50 -> x48, local copies, waits for them, and re-layouts: 11.7 us -> 14.7 us
    pallas_call x1, Pallas kernels: 5.72 us -> 3.35 us  [pull_terms(): pl.pallas_call(pull_kernel, out_shape=jax.ShapeDtypeStruct((3, count), jn...]
  transfers between devices with their start and end apart: 27 -> 26, of which waited for: 15 -> 12; matrix products, arithmetic and copies ran while one was open for 4% -> 4% of each run, Pallas kernels for 34% -> 33%
where the time goes in v5:
time: 232 us; the launch traced here: 231 us
  Pallas kernels  112 us (48%)
  waiting for transfers between devices  60.7 us (26%)
  starting transfers between devices  29.1 us (13%)
  local copies, waits for them, and re-layouts  21.9 us (9%)
  other arithmetic  6.65 us (3%)
    pallas_call x4, Pallas kernels, call_kernel(): pl.pallas_call(kernel, out_shape=(pltpu.VMEM((6,) + shape, jnp.float32),)...  91.6 us
    ppermute x1, waiting for transfers between devices, gossip_shards(): from_far = lax.ppermute(packed, 'sec', [(i, i ^ 2) for i in range(4)])  21.2 us
    unnamed x48, local copies, waits for them, and re-layouts  14.7 us
    ppermute x13, waiting for transfers between devices, over_rep(): return lax.ppermute(value, 'rep', [(0, 1), (1, 0)])  12.2 us
    ppermute x1, waiting for transfers between devices, gossip_shards(): from_near = lax.ppermute(packed, 'sec', [(i, i ^ 1) for i in range(4)])  11.1 us
    ppermute x4, starting transfers between devices, over_col(): return lax.ppermute(value, 'col', [(0, 1), (1, 0)])  10.5 us
    ppermute x4, waiting for transfers between devices, over_col(): return lax.ppermute(value, 'col', [(0, 1), (1, 0)])  8.6 us
    pallas_call x1, Pallas kernels, pair_terms(): pl.pallas_call(pairs_kernel, grid=(total // width,), out_shape=(jax.Shape...  7.48 us
  transfers between devices with their start and end apart: 26, of which 12 were waited for; matrix products, arithmetic and copies ran while one was open for 4% of the time, Pallas kernels for 33%

profile of v5, /device:TPU:0, one launch (start us, length us, event | category | flops | bytes accessed | tf_op | source)
XLA Modules:
  0.0 231.2 jit_solution(7112225973011488503)
XLA Ops:
  0.7 3.5 %constant_dynamic-slice_fusion.2 = (bf16[640,1280]{1,0:T(8,128)(2,1)S(1)}, bf16[640,1280]{1,0:T(8,128)(2,1)}) fusion(bf16[1280,1280]{1,0:T(8,128)(2,1)} %ham_ref.1, s32[]{:T(128)S(6)} %select_n.24, s32[]{:T(128)S(6)} %select_n.23), kind=kLoop, calls=%fused_computation.11 | loop fusion | bytes 6553608 | tf_op jit(solution)/shard_map/dynamic_slice | solution.py:896
  4.1 0.5 collective-permute-start.1
  4.6 2.6 %collective-permute-start = (bf16[640,1280]{1,0:T(8,128)(2,1)}, bf16[640,1280]{1,0:T(8,128)(2,1)}, u32[]{:S(2)}, u32[]{:S(2)}) collective-permute-start(bf16[640,1280]{1,0:T(8,128)(2,1)} %get-tuple-element.105), channel_id=1, source_target_pairs={{0,5},{1,3},{2,15},{3,1},{4,6},{5,8},{6,4},{7,2},{8,13},{9,11},{10... | collective-permute-start | bytes 4915208 | tf_op jit(solution)/shard_map/ppermute | solution.py:883
  7.3 2.3 %collective-permute-done.1.refs_1_ = bf16[640,1280]{1,0:T(8,128)(2,1)} collective-permute-done((bf16[640,1280]{1,0:T(8,128)(2,1)S(1)}, bf16[640,1280]{1,0:T(8,128)(2,1)}, u32[]{:S(2)}, u32[]{:S(2)}) %collective-permute-start.1) | collective-permute-done | bytes 1638432 | tf_op jit(solution)/shard_map/ppermute | solution.py:866
  9.6 3.4 %collective-permute-start.2 = (bf16[640,1280]{1,0:T(8,128)(2,1)}, bf16[640,1280]{1,0:T(8,128)(2,1)}, u32[]{:S(2)}, u32[]{:S(2)}) collective-permute-start(bf16[640,1280]{1,0:T(8,128)(2,1)} %collective-permute-done.1.refs_1_), channel_id=1, source_target_pairs={{0,2},{1,4},{2,0},{3,14},{4,9},{5,7},{6,3},{7,5},{8,10},{9,12},{10... | collective-permute-start | bytes 4915208 | tf_op jit(solution)/shard_map/ppermute | solution.py:883
  13.0 0.6 pad_maximum_fusion
  13.6 0.8 copy.14
  14.5 0.9 copy-done.5
  15.4 7.5 %pairs.1 = (f32[1,5120]{1,0:T(1,128)S(1)}, bf16[512,5120]{1,0:T(8,128)(2,1)S(1)}) custom-call(f32[3,5120]{1,0:T(4,128)S(1)} %copy-done.5, f32[512,4]{1,0:T(8,128)S(1)} %bitcast.10), custom_call_target="tpu_custom_call" | custom-call | tf_op jit(solution)/shard_map/pairs/pallas_call | solution.py:701
  22.9 2.3 %copy-done.2 = bf16[512,5120]{1,0:T(8,128)(2,1)} copy-done((bf16[512,5120]{1,0:T(8,128)(2,1)}, bf16[512,5120]{1,0:T(8,128)(2,1)S(1)}, u32[]{:S(2)}) %copy-start.2) | copy-done | bytes 5242904
  25.2 3.8 %fusion = (f32[1280]{0:T(1024)S(1)}, f32[]{:T(128)}) fusion(bf16[1280,1280]{1,0:T(8,128)(2,1)S(1)} %copy-done, s32[1280]{0:T(1024)S(1)} %get-tuple-element.106, s32[1280]{0:T(1024)S(1)} %get-tuple-element.107), kind=kLoop, calls=%fused_computation.3 | loop fusion | flops 11467519 | bytes 3292164 | tf_op jit(solution)/shard_map/reduce_sum | solution.py:906
  29.0 0.3 dynamic_update_slice.3
  29.3 0.6 broadcast_in_dim.19
  29.9 0.7 maximum_bitcast_fusion
  30.7 0.2 collective-permute-start.3
  30.9 1.3 constant_dynamic-slice_fusion.1
  32.2 0.7 fusion.3
  32.9 3.5 %collective-permute-start.4 = (f32[88,128]{1,0:T(8,128)S(1)}, f32[88,128]{1,0:T(8,128)S(1)}, u32[]{:S(2)}, u32[]{:S(2)}) collective-permute-start(f32[88,128]{1,0:T(8,128)S(1)} %fusion.3), channel_id=1, source_target_pairs={{0,2},{2,0},{1,3},{3,1},{4,6},{6,4},{5,7},{7,5},{8,10},{10,8},{9,1... | collective-permute-start | bytes 135176 | tf_op jit(solution)/shard_map/ppermute | solution.py:869
  36.4 0.7 fusion.2.info_ref
  37.1 7.6 %collective-permute-done.4 = f32[88,128]{1,0:T(8,128)S(1)} collective-permute-done((f32[88,128]{1,0:T(8,128)S(1)}, f32[88,128]{1,0:T(8,128)S(1)}, u32[]{:S(2)}, u32[]{:S(2)}) %collective-permute-start.4) | collective-permute-done | bytes 45088 | tf_op jit(solution)/shard_map/ppermute | solution.py:869
  44.7 2.5 %pick.2 = (bf16[640,1280]{1,0:T(8,128)(2,1)S(1)}, bf16[640,1280]{1,0:T(8,128)(2,1)S(1)}) custom-call(s32[12]{0:T(128)S(1)} %fusion.2.info_ref, bf16[1280,1280]{1,0:T(8,128)(2,1)} %ham_ref.1, bf16[640,1280]{1,0:T(8,128)(2,1)} %collective-permute-done.1.refs_1_, bf16[640,1280]{1,0:T(8,128)(2,1)} %collective-permute-done.refs_2_.refs_3_, ...), custom_call_target="tpu_custom_call" | custom-call | tf_op jit(solution)/shard_map/pick/pallas_call | solution.py:657
  47.2 1.1 collective-permute-start.9
  48.4 0.1 collective-permute-start.10
  48.4 1.6 collective-permute-start.6
  50.1 4.6 %collective-permute-start.7 = (bf16[640,1280]{1,0:T(8,128)(2,1)S(1)}, bf16[640,1280]{1,0:T(8,128)(2,1)}, u32[]{:S(2)}, u32[]{:S(2)}) collective-permute-start(bf16[640,1280]{1,0:T(8,128)(2,1)S(1)} %get-tuple-element.60), channel_id=1, source_target_pairs={{0,12},{12,8},{8,4},{4,0},{2,6},{6,10},{10,14},{14,2},{1,13},{13,9... | collective-permute-start | bytes 4915208 | tf_op jit(solution)/shard_map/ppermute | solution.py:873
  54.7 1.2 copy-done.15
  55.9 1.2 copy-done.16
  57.0 22.5 %square_0.1 = (f32[6,640,1280]{2,1,0:T(8,128)S(1)}, f32[8,128]{1,0:T(8,128)}) custom-call(s32[428]{0:T(512)} %bitcast.15, s32[12]{0:T(128)} %copy-done.11, bf16[1280,1280]{1,0:T(8,128)(2,1)} %ham_ref.1, bf16[640,1280]{1,0:T(8,128)(2,1)} %collective-permute-done.1.refs_1_, bf16[640,1280]{1,0:T(8,128)(2,1)} %collective-permute-done.5.refs_2_, ...), custom_call_target="tpu_custom_call" | custom-call | tf_op jit(solution)/shard_map/square_0/pallas_call | solution.py:623
  79.5 11.1 %collective-permute-done.8 = f32[88,128]{1,0:T(8,128)S(1)} collective-permute-done((f32[88,128]{1,0:T(8,128)S(1)}, f32[88,128]{1,0:T(8,128)S(1)}, u32[]{:S(2)}, u32[]{:S(2)}) %collective-permute-start.8) | collective-permute-done | bytes 45088 | tf_op jit(solution)/shard_map/ppermute | solution.py:919
  90.6 0.5 collective-permute-start.14
  91.2 0.6 collective-permute-start.11
  91.8 1.8 collective-permute-start.12
  93.6 2.0 collective-permute-start.13
  95.6 1.1 collective-permute-done.14.refs_8_
  96.7 0.1 copy-done.18
  96.8 1.1 copy-done.19
  97.9 14.0 %square_1.1 = (f32[6,640,1280]{2,1,0:T(8,128)S(1)}, f32[8,128]{1,0:T(8,128)}) custom-call(s32[428]{0:T(512)} %bitcast.16, s32[12]{0:T(128)} %copy-done.11, bf16[1280,1280]{1,0:T(8,128)(2,1)} %ham_ref.1, bf16[640,1280]{1,0:T(8,128)(2,1)} %collective-permute-done.1.refs_1_, ...), custom_call_target="tpu_custom_call", output_to_operand_aliasing={{0}: (14, {})} | custom-call | tf_op jit(solution)/shard_map/square_1/pallas_call | solution.py:623
  111.9 21.2 %collective-permute-done.13.far_ref = f32[88,128]{1,0:T(8,128)S(1)} collective-permute-done((f32[88,128]{1,0:T(8,128)S(1)}, f32[88,128]{1,0:T(8,128)S(1)}, u32[]{:S(2)}, u32[]{:S(2)}) %collective-permute-start.13) | collective-permute-done | bytes 45088 | tf_op jit(solution)/shard_map/ppermute | solution.py:936
  133.2 1.3 copy-done.17
  134.4 2.0 pick.3
  136.4 0.1 collective-permute-start.18
  136.5 0.5 collective-permute-start.19
  137.0 4.8 %collective-permute-start.16 = (bf16[640,1280]{1,0:T(8,128)(2,1)S(1)}, bf16[640,1280]{1,0:T(8,128)(2,1)}, u32[]{:S(2)}, u32[]{:S(2)}) collective-permute-start(bf16[640,1280]{1,0:T(8,128)(2,1)S(1)} %pick.3), channel_id=1, source_target_pairs={{0,2},{2,0},{1,3},{3,1},{4,6},{6,4},{5,7},{7,5},{8,10},{10,8},{9,1... | collective-permute-start | bytes 4915208 | tf_op jit(solution)/shard_map/ppermute | solution.py:869
  141.8 1.4 levels.1
  143.1 0.7 copy-done.4
  143.9 0.6 copy-done.7
  144.5 1.2 copy-done.20
  145.7 0.5 copy-done.21
  146.2 27.6 %early_cube.1 = (f32[6,640,1280]{2,1,0:T(8,128)S(1)}, f32[640,128]{1,0:T(8,128)}) custom-call(s32[428]{0:T(512)} %bitcast.17, s32[12]{0:T(128)} %copy-done.11, bf16[1280,1280]{1,0:T(8,128)(2,1)} %ham_ref.1, bf16[640,1280]{1,0:T(8,128)(2,1)} %collective-permute-done.1.refs_1_, ...), custom_call_target="tpu_custom_call", output_to_operand_aliasing={{0}: (18, {})} | custom-call | tf_op jit(solution)/shard_map/early_cube/pallas_call | solution.py:623
  173.8 2.9 %collective-permute-done.17.refs_17_ = bf16[640,1280]{1,0:T(8,128)(2,1)} collective-permute-done((bf16[640,1280]{1,0:T(8,128)(2,1)S(1)}, bf16[640,1280]{1,0:T(8,128)(2,1)}, u32[]{:S(2)}, u32[]{:S(2)}) %collective-permute-start.17) | collective-permute-done | bytes 1638432 | tf_op jit(solution)/shard_map/ppermute | solution.py:873
  176.6 1.0 collective-permute-done.16.refs_15_
  177.6 0.5 collective-permute-start.21
  178.1 3.2 %collective-permute-done.20.refs_16_ = bf16[640,1280]{1,0:T(8,128)(2,1)S(1)} collective-permute-done((bf16[640,1280]{1,0:T(8,128)(2,1)}, bf16[640,1280]{1,0:T(8,128)(2,1)S(1)}, u32[]{:S(2)}, u32[]{:S(2)}) %collective-permute-start.20) | collective-permute-done | bytes 1638432 | tf_op jit(solution)/shard_map/ppermute | solution.py:866
  181.3 2.3 %collective-permute-done.21.refs_18_ = bf16[640,1280]{1,0:T(8,128)(2,1)S(1)} collective-permute-done((bf16[640,1280]{1,0:T(8,128)(2,1)}, bf16[640,1280]{1,0:T(8,128)(2,1)S(1)}, u32[]{:S(2)}, u32[]{:S(2)}) %collective-permute-start.21) | collective-permute-done | bytes 1638432 | tf_op jit(solution)/shard_map/ppermute | solution.py:866
  183.7 1.2 copy-done.23
  184.9 27.5 %late_cube.1 = (f32[6,640,1280]{2,1,0:T(8,128)S(1)}, bf16[640,1280]{1,0:T(8,128)(2,1)}, f32[1280,1280]{1,0:T(8,128)}, f32[40,128]{1,0:T(8,128)}) custom-call(s32[428]{0:T(512)} %bitcast.18, s32[12]{0:T(128)} %copy-done.11, f32[1]{0:T(128)} %get-tuple-element.88.gain_ref, bf16[1280,1280]{1,0:T(8,128)(2,1)} %ham_ref.1, ...), custom_call_target="tpu_custom_call", output_to_operand_aliasing={{0}: (22, {})} | custom-call | tf_op jit(solution)/shard_map/late_cube/pallas_call | solution.py:623
  212.4 0.5 collective-permute-start.22
  212.9 3.2 %collective-permute-done.22 = f32[40,128]{1,0:T(8,128)S(1)} collective-permute-done((f32[40,128]{1,0:T(8,128)}, f32[40,128]{1,0:T(8,128)S(1)}, u32[]{:S(2)}, u32[]{:S(2)}) %collective-permute-start.22) | collective-permute-done | bytes 20512 | tf_op jit(solution)/shard_map/ppermute | solution.py:866
  216.2 0.7 add.67
  216.9 3.8 %collective-permute-done.23 = f32[40,128]{1,0:T(8,128)S(1)} collective-permute-done((f32[40,128]{1,0:T(8,128)S(1)}, f32[40,128]{1,0:T(8,128)S(1)}, u32[]{:S(2)}, u32[]{:S(2)}) %collective-permute-start.23) | collective-permute-done | bytes 20512 | tf_op jit(solution)/shard_map/ppermute | solution.py:971
  220.8 3.7 %density.1 = f32[1280,1280]{1,0:T(8,128)} custom-call(s32[12]{0:T(128)S(1)} %copy-done.13, f32[1]{0:T(128)} %get-tuple-element.88.gain_ref, bf16[1280,1280]{1,0:T(8,128)(2,1)S(1)} %copy-done.1, bf16[640,1280]{1,0:T(8,128)(2,1)S(1)} %collective-permute-done.25.far_ref, f32[40,128]{1,0:T(8,128)S(1)} %copy-done.8, ...), custom_call_target="tpu_custom_call", output_to_operand_aliasing={{}: (5, {})} | custom-call | tf_op jit(solution)/shard_map/density/pallas_call | solution.py:831
  224.5 0.8 collective-permute-done.24.far_ref
  225.4 2.5 %copy-done.3 = bf16[512,5120]{1,0:T(8,128)(2,1)S(1)} copy-done((bf16[512,5120]{1,0:T(8,128)(2,1)S(1)}, bf16[512,5120]{1,0:T(8,128)(2,1)}, u32[]{:S(2)}) %copy-start.3) | copy-done | bytes 5242904
  227.9 3.3 %pull.1 = f32[3,512]{1,0:T(4,128)} custom-call(f32[1]{0:T(128)} %get-tuple-element.88.gain_ref, f32[3,5120]{1,0:T(4,128)S(1)} %copy-done.6, f32[40,128]{1,0:T(8,128)S(1)} %get-tuple-element.99.above_ref, f32[40,128]{1,0:T(8,128)S(1)} %add.68.near_ref, f32[40,128]{1,0:T(8,128)S(1)} %collective-permute-done.24.far_ref, bf16[512,5120]{1,0:T(8,128)(2,1)S(1)} %copy-done.3, ...), custom_call_target="tpu_custom_call" | custom-call | tf_op jit(solution)/shard_map/pull/pallas_call | solution.py:781
  (62 shorter events, 0.3 us)
Async XLA Ops:
  0.6 12.4 %copy-start.10 = (f32[3,512]{1,0:T(4,128)S(1)}, f32[3,512]{1,0:T(4,128)}, u32[]{:S(2)}) copy-start(f32[3,512]{1,0:T(4,128)} %coords_ref.1) | copy-start | bytes 18436
  0.6 12.4 %copy-start.14 = (f32[512]{0:T(512)S(1)}, f32[512]{0:T(512)}, u32[]{:S(2)}) copy-start(f32[512]{0:T(512)} %param.9) | copy-start | bytes 6148
  0.7 24.5 %copy-start = (bf16[1280,1280]{1,0:T(8,128)(2,1)S(1)}, bf16[1280,1280]{1,0:T(8,128)(2,1)}, u32[]{:S(2)}) copy-start(bf16[1280,1280]{1,0:T(8,128)(2,1)} %ham_ref.1) | copy-start | bytes 9830404
  4.1 5.5 %collective-permute-start.1 = (bf16[640,1280]{1,0:T(8,128)(2,1)S(1)}, bf16[640,1280]{1,0:T(8,128)(2,1)}, u32[]{:S(2)}, u32[]{:S(2)}) collective-permute-start(bf16[640,1280]{1,0:T(8,128)(2,1)S(1)} %get-tuple-element.104), channel_id=1, source_target_pairs={{0,1},{1,0},{2,3},{3,2},{4,5},{5,4},{6,7},{7,6},{8,9},{9,8},{10,11... | collective-permute-start | bytes 4915208 | tf_op jit(solution)/shard_map/ppermute | solution.py:866
  4.6 40.1 %collective-permute-start.5 = (bf16[640,1280]{1,0:T(8,128)(2,1)}, bf16[640,1280]{1,0:T(8,128)(2,1)}, u32[]{:S(2)}, u32[]{:S(2)}) collective-permute-start(bf16[640,1280]{1,0:T(8,128)(2,1)} %get-tuple-element.105), channel_id=1, source_target_pairs={{0,1},{1,0},{2,3},{3,2},{4,5},{5,4},{6,7},{7,6},{8,9},{9,8},{10,11... | collective-permute-start | bytes 4915208 | tf_op jit(solution)/shard_map/ppermute | solution.py:866
  4.6 40.1 %collective-permute-start = (bf16[640,1280]{1,0:T(8,128)(2,1)}, bf16[640,1280]{1,0:T(8,128)(2,1)}, u32[]{:S(2)}, u32[]{:S(2)}) collective-permute-start(bf16[640,1280]{1,0:T(8,128)(2,1)} %get-tuple-element.105), channel_id=1, source_target_pairs={{0,5},{1,3},{2,15},{3,1},{4,6},{5,8},{6,4},{7,2},{8,13},{9,11},{10... | collective-permute-start | bytes 4915208 | tf_op jit(solution)/shard_map/ppermute | solution.py:883
  9.6 35.1 %collective-permute-start.2 = (bf16[640,1280]{1,0:T(8,128)(2,1)}, bf16[640,1280]{1,0:T(8,128)(2,1)}, u32[]{:S(2)}, u32[]{:S(2)}) collective-permute-start(bf16[640,1280]{1,0:T(8,128)(2,1)} %collective-permute-done.1.refs_1_), channel_id=1, source_target_pairs={{0,2},{1,4},{2,0},{3,14},{4,9},{5,7},{6,3},{7,5},{8,10},{9,12},{10... | collective-permute-start | bytes 4915208 | tf_op jit(solution)/shard_map/ppermute | solution.py:883
  14.5 0.9 copy-start.5
  22.8 2.3 %copy-start.2 = (bf16[512,5120]{1,0:T(8,128)(2,1)}, bf16[512,5120]{1,0:T(8,128)(2,1)S(1)}, u32[]{:S(2)}) copy-start(bf16[512,5120]{1,0:T(8,128)(2,1)S(1)} %get-tuple-element.101.weight_ref) | copy-start | bytes 15728644
  25.2 3.8 %copy-start.9 = (f32[1,5120]{1,0:T(1,128)}, f32[1,5120]{1,0:T(1,128)S(1)}, u32[]{:S(2)}) copy-start(f32[1,5120]{1,0:T(1,128)S(1)} %get-tuple-element.52) | copy-start | bytes 61444
  30.7 1.5 collective-permute-start.3
  32.9 11.8 %collective-permute-start.4 = (f32[88,128]{1,0:T(8,128)S(1)}, f32[88,128]{1,0:T(8,128)S(1)}, u32[]{:S(2)}, u32[]{:S(2)}) collective-permute-start(f32[88,128]{1,0:T(8,128)S(1)} %fusion.3), channel_id=1, source_target_pairs={{0,2},{2,0},{1,3},{3,1},{4,6},{6,4},{5,7},{7,5},{8,10},{10,8},{9,1... | collective-permute-start | bytes 135176 | tf_op jit(solution)/shard_map/ppermute | solution.py:869
  37.1 10.1 %copy-start.11 = (s32[12]{0:T(128)}, s32[12]{0:T(128)S(1)}, u32[]{:S(2)}) copy-start(s32[12]{0:T(128)S(1)} %fusion.2.info_ref) | copy-start | bytes 148
  47.2 7.4 %collective-permute-start.9 = (bf16[640,1280]{1,0:T(8,128)(2,1)}, bf16[640,1280]{1,0:T(8,128)(2,1)S(1)}, u32[]{:S(2)}, u32[]{:S(2)}) collective-permute-start(bf16[640,1280]{1,0:T(8,128)(2,1)} %collective-permute-done.refs_2_.refs_3_), channel_id=1, source_target_pairs={{0,1},{1,0},{2,3},{3,2},{4,5},{5,4},{6,7},{7,6},{8,9},{9,8},{10,11... | collective-permute-start | bytes 4915208 | tf_op jit(solution)/shard_map/ppermute | solution.py:866
  48.4 6.3 %collective-permute-start.10 = (bf16[640,1280]{1,0:T(8,128)(2,1)}, bf16[640,1280]{1,0:T(8,128)(2,1)S(1)}, u32[]{:S(2)}, u32[]{:S(2)}) collective-permute-start(bf16[640,1280]{1,0:T(8,128)(2,1)} %collective-permute-done.2.refs_3_.refs_4_), channel_id=1, source_target_pairs={{0,1},{1,0},{2,3},{3,2},{4,5},{5,4},{6,7},{7,6},{8,9},{9,8},{10,11... | collective-permute-start | bytes 4915208 | tf_op jit(solution)/shard_map/ppermute | solution.py:866
  48.4 42.2 %collective-permute-start.6 = (bf16[640,1280]{1,0:T(8,128)(2,1)S(1)}, bf16[640,1280]{1,0:T(8,128)(2,1)}, u32[]{:S(2)}, u32[]{:S(2)}) collective-permute-start(bf16[640,1280]{1,0:T(8,128)(2,1)S(1)} %get-tuple-element.59), channel_id=1, source_target_pairs={{0,2},{2,0},{1,3},{3,1},{4,6},{6,4},{5,7},{7,5},{8,10},{10,8},{9,1... | collective-permute-start | bytes 4915208 | tf_op jit(solution)/shard_map/ppermute | solution.py:869
  50.1 40.6 %collective-permute-start.7 = (bf16[640,1280]{1,0:T(8,128)(2,1)S(1)}, bf16[640,1280]{1,0:T(8,128)(2,1)}, u32[]{:S(2)}, u32[]{:S(2)}) collective-permute-start(bf16[640,1280]{1,0:T(8,128)(2,1)S(1)} %get-tuple-element.60), channel_id=1, source_target_pairs={{0,12},{12,8},{8,4},{4,0},{2,6},{6,10},{10,14},{14,2},{1,13},{13,9... | collective-permute-start | bytes 4915208 | tf_op jit(solution)/shard_map/ppermute | solution.py:873
  54.7 36.0 %collective-permute-start.8 = (f32[88,128]{1,0:T(8,128)S(1)}, f32[88,128]{1,0:T(8,128)S(1)}, u32[]{:S(2)}, u32[]{:S(2)}) collective-permute-start(f32[88,128]{1,0:T(8,128)S(1)} %add.65), channel_id=1, source_target_pairs={{0,4},{4,0},{8,12},{12,8},{1,5},{5,1},{9,13},{13,9},{2,6},{6,2},{1... | collective-permute-start | bytes 135176 | tf_op jit(solution)/shard_map/ppermute | solution.py:919
  54.7 1.2 copy-start.15
  55.9 1.2 copy-start.16
  90.6 5.0 %collective-permute-start.15 = (bf16[640,1280]{1,0:T(8,128)(2,1)}, bf16[640,1280]{1,0:T(8,128)(2,1)S(1)}, u32[]{:S(2)}, u32[]{:S(2)}) collective-permute-start(bf16[640,1280]{1,0:T(8,128)(2,1)} %collective-permute-done.7.refs_9_), channel_id=1, source_target_pairs={{0,1},{1,0},{2,3},{3,2},{4,5},{5,4},{6,7},{7,6},{8,9},{9,8},{10,11... | collective-permute-start | bytes 4915208 | tf_op jit(solution)/shard_map/ppermute | solution.py:866
  90.6 6.1 %collective-permute-start.14 = (bf16[640,1280]{1,0:T(8,128)(2,1)}, bf16[640,1280]{1,0:T(8,128)(2,1)S(1)}, u32[]{:S(2)}, u32[]{:S(2)}) collective-permute-start(bf16[640,1280]{1,0:T(8,128)(2,1)} %collective-permute-done.6.refs_7_), channel_id=1, source_target_pairs={{0,1},{1,0},{2,3},{3,2},{4,5},{5,4},{6,7},{7,6},{8,9},{9,8},{10,11... | collective-permute-start | bytes 4915208 | tf_op jit(solution)/shard_map/ppermute | solution.py:866
  91.2 42.0 %collective-permute-start.11 = (bf16[640,1280]{1,0:T(8,128)(2,1)}, bf16[640,1280]{1,0:T(8,128)(2,1)}, u32[]{:S(2)}, u32[]{:S(2)}) collective-permute-start(bf16[640,1280]{1,0:T(8,128)(2,1)} %collective-permute-done.7.refs_9_), channel_id=1, source_target_pairs={{0,2},{2,0},{1,3},{3,1},{4,6},{6,4},{5,7},{7,5},{8,10},{10,8},{9,1... | collective-permute-start | bytes 4915208 | tf_op jit(solution)/shard_map/ppermute | solution.py:869
  91.8 41.4 %collective-permute-start.12 = (bf16[640,1280]{1,0:T(8,128)(2,1)}, bf16[640,1280]{1,0:T(8,128)(2,1)S(1)}, u32[]{:S(2)}, u32[]{:S(2)}) collective-permute-start(bf16[640,1280]{1,0:T(8,128)(2,1)} %collective-permute-done.6.refs_7_), channel_id=1, source_target_pairs={{0,4},{4,8},{8,12},{12,0},{2,14},{14,10},{10,6},{6,2},{1,5},{5,9},... | collective-permute-start | bytes 4915208 | tf_op jit(solution)/shard_map/ppermute | solution.py:873
  93.6 39.5 %collective-permute-start.13 = (f32[88,128]{1,0:T(8,128)S(1)}, f32[88,128]{1,0:T(8,128)S(1)}, u32[]{:S(2)}, u32[]{:S(2)}) collective-permute-start(f32[88,128]{1,0:T(8,128)S(1)} %add.66.near_ref), channel_id=1, source_target_pairs={{0,8},{4,12},{8,0},{12,4},{1,9},{5,13},{9,1},{13,5},{2,10},{6,14},... | collective-permute-start | bytes 135176 | tf_op jit(solution)/shard_map/ppermute | solution.py:936
  95.6 1.2 copy-start.18
  96.7 1.2 copy-start.19
  97.9 36.5 %copy-start.12 = (s32[12]{0:T(128)S(1)}, s32[12]{0:T(128)}, u32[]{:S(2)}) copy-start(s32[12]{0:T(128)} %copy-done.11) | copy-start | bytes 148
  133.2 1.3 copy-start.17
  136.4 8.1 %collective-permute-start.18 = (bf16[640,1280]{1,0:T(8,128)(2,1)}, bf16[640,1280]{1,0:T(8,128)(2,1)S(1)}, u32[]{:S(2)}, u32[]{:S(2)}) collective-permute-start(bf16[640,1280]{1,0:T(8,128)(2,1)} %collective-permute-done.11.refs_11_), channel_id=1, source_target_pairs={{0,1},{1,0},{2,3},{3,2},{4,5},{5,4},{6,7},{7,6},{8,9},{9,8},{10,11... | collective-permute-start | bytes 4915208 | tf_op jit(solution)/shard_map/ppermute | solution.py:866
  136.5 8.0 %collective-permute-start.19 = (bf16[640,1280]{1,0:T(8,128)(2,1)}, bf16[640,1280]{1,0:T(8,128)(2,1)S(1)}, u32[]{:S(2)}, u32[]{:S(2)}) collective-permute-start(bf16[640,1280]{1,0:T(8,128)(2,1)} %copy-done.17), channel_id=1, source_target_pairs={{0,1},{1,0},{2,3},{3,2},{4,5},{5,4},{6,7},{7,6},{8,9},{9,8},{10,11... | collective-permute-start | bytes 4915208 | tf_op jit(solution)/shard_map/ppermute | solution.py:866
  137.0 39.7 %collective-permute-start.17 = (bf16[640,1280]{1,0:T(8,128)(2,1)S(1)}, bf16[640,1280]{1,0:T(8,128)(2,1)}, u32[]{:S(2)}, u32[]{:S(2)}) collective-permute-start(bf16[640,1280]{1,0:T(8,128)(2,1)S(1)} %pick.3), channel_id=1, source_target_pairs={{0,4},{4,8},{8,12},{12,0},{2,14},{14,10},{10,6},{6,2},{1,5},{5,9},... | collective-permute-start | bytes 4915208 | tf_op jit(solution)/shard_map/ppermute | solution.py:873
  137.0 40.7 %collective-permute-start.16 = (bf16[640,1280]{1,0:T(8,128)(2,1)S(1)}, bf16[640,1280]{1,0:T(8,128)(2,1)}, u32[]{:S(2)}, u32[]{:S(2)}) collective-permute-start(bf16[640,1280]{1,0:T(8,128)(2,1)S(1)} %pick.3), channel_id=1, source_target_pairs={{0,2},{2,0},{1,3},{3,1},{4,6},{6,4},{5,7},{7,5},{8,10},{10,8},{9,1... | collective-permute-start | bytes 4915208 | tf_op jit(solution)/shard_map/ppermute | solution.py:869
  143.1 0.7 copy-start.4
  143.9 0.6 copy-start.7
  144.5 1.3 copy-start.20
  144.5 1.7 copy-start.21
  177.6 3.7 %collective-permute-start.20 = (bf16[640,1280]{1,0:T(8,128)(2,1)}, bf16[640,1280]{1,0:T(8,128)(2,1)S(1)}, u32[]{:S(2)}, u32[]{:S(2)}) collective-permute-start(bf16[640,1280]{1,0:T(8,128)(2,1)} %collective-permute-done.16.refs_15_), channel_id=1, source_target_pairs={{0,1},{1,0},{2,3},{3,2},{4,5},{5,4},{6,7},{7,6},{8,9},{9,8},{10,11... | collective-permute-start | bytes 4915208 | tf_op jit(solution)/shard_map/ppermute | solution.py:866
  177.6 6.1 %collective-permute-start.21 = (bf16[640,1280]{1,0:T(8,128)(2,1)}, bf16[640,1280]{1,0:T(8,128)(2,1)S(1)}, u32[]{:S(2)}, u32[]{:S(2)}) collective-permute-start(bf16[640,1280]{1,0:T(8,128)(2,1)} %collective-permute-done.17.refs_17_), channel_id=1, source_target_pairs={{0,1},{1,0},{2,3},{3,2},{4,5},{5,4},{6,7},{7,6},{8,9},{9,8},{10,11... | collective-permute-start | bytes 4915208 | tf_op jit(solution)/shard_map/ppermute | solution.py:866
  181.3 2.3 %copy-start.22 = (bf16[640,1280]{1,0:T(8,128)(2,1)}, bf16[640,1280]{1,0:T(8,128)(2,1)S(1)}, u32[]{:S(2)}) copy-start(bf16[640,1280]{1,0:T(8,128)(2,1)S(1)} %collective-permute-done.20.refs_16_) | copy-start | bytes 4915204
  183.7 1.2 copy-start.23
  184.9 35.9 %copy-start.1 = (bf16[1280,1280]{1,0:T(8,128)(2,1)S(1)}, bf16[1280,1280]{1,0:T(8,128)(2,1)}, u32[]{:S(2)}) copy-start(bf16[1280,1280]{1,0:T(8,128)(2,1)} %ham_ref.1) | copy-start | bytes 9830404
  184.9 35.9 %copy-start.8 = (f32[40,128]{1,0:T(8,128)S(1)}, f32[40,128]{1,0:T(8,128)}, u32[]{:S(2)}) copy-start(f32[40,128]{1,0:T(8,128)} %copy-done.7) | copy-start | bytes 61444
  184.9 35.9 %copy-start.13 = (s32[12]{0:T(128)S(1)}, s32[12]{0:T(128)}, u32[]{:S(2)}) copy-start(s32[12]{0:T(128)} %copy-done.11) | copy-start | bytes 148
  212.4 8.4 %collective-permute-start.25 = (bf16[640,1280]{1,0:T(8,128)(2,1)}, bf16[640,1280]{1,0:T(8,128)(2,1)S(1)}, u32[]{:S(2)}, u32[]{:S(2)}) collective-permute-start(bf16[640,1280]{1,0:T(8,128)(2,1)} %get-tuple-element.96), channel_id=1, source_target_pairs={{0,1},{1,0},{2,3},{3,2},{4,5},{5,4},{6,7},{7,6},{8,9},{9,8},{10,11... | collective-permute-start | bytes 4915208 | tf_op jit(solution)/shard_map/ppermute | solution.py:866
  212.4 3.7 %collective-permute-start.22 = (f32[40,128]{1,0:T(8,128)}, f32[40,128]{1,0:T(8,128)S(1)}, u32[]{:S(2)}, u32[]{:S(2)}) collective-permute-start(f32[40,128]{1,0:T(8,128)} %get-tuple-element.95), channel_id=1, source_target_pairs={{0,1},{1,0},{2,3},{3,2},{4,5},{5,4},{6,7},{7,6},{8,9},{9,8},{10,11... | collective-permute-start | bytes 61448 | tf_op jit(solution)/shard_map/ppermute | solution.py:866
  216.9 3.8 %collective-permute-start.23 = (f32[40,128]{1,0:T(8,128)S(1)}, f32[40,128]{1,0:T(8,128)S(1)}, u32[]{:S(2)}, u32[]{:S(2)}) collective-permute-start(f32[40,128]{1,0:T(8,128)S(1)} %add.67), channel_id=1, source_target_pairs={{0,4},{4,0},{8,12},{12,8},{1,5},{5,1},{9,13},{13,9},{2,6},{6,2},{1... | collective-permute-start | bytes 61448 | tf_op jit(solution)/shard_map/ppermute | solution.py:971
  220.7 4.7 %collective-permute-start.24 = (f32[40,128]{1,0:T(8,128)S(1)}, f32[40,128]{1,0:T(8,128)S(1)}, u32[]{:S(2)}, u32[]{:S(2)}) collective-permute-start(f32[40,128]{1,0:T(8,128)S(1)} %add.68.near_ref), channel_id=1, source_target_pairs={{0,8},{4,12},{8,0},{12,4},{1,9},{5,13},{9,1},{13,5},{2,10},{6,14},... | collective-permute-start | bytes 61448 | tf_op jit(solution)/shard_map/ppermute | solution.py:972
  220.8 4.6 %copy-start.6 = (f32[3,5120]{1,0:T(4,128)S(1)}, f32[3,5120]{1,0:T(4,128)}, u32[]{:S(2)}) copy-start(f32[3,5120]{1,0:T(4,128)} %spots_ref.3) | copy-start | bytes 184324
  225.4 2.5 %copy-start.3 = (bf16[512,5120]{1,0:T(8,128)(2,1)S(1)}, bf16[512,5120]{1,0:T(8,128)(2,1)}, u32[]{:S(2)}) copy-start(bf16[512,5120]{1,0:T(8,128)(2,1)} %copy-done.2) | copy-start | bytes 15728644

commit v6 on v5

--- a/solution.py
+++ b/solution.py
@@ -792,13 +792,13 @@
     )
 
 
-def density_kernel(steps, info_ref, gain_ref, ham_ref, far_ref, level_ref, _, out_ref):
+def density_kernel(start, steps, info_ref, gain_ref, ham_ref, far_ref, level_ref, _, out_ref):
     index = pl.program_id(0)
     core, row, col = info_ref[CORE], info_ref[ROW], info_ref[COL]
     gain = gain_ref[0]
     height, width = out_ref.shape
     linear, cubic = -1.5 * gain, 2.0 * (gain * gain * gain)
-    first = ((1 - core) * steps + index) * height
+    first = ((1 - core) * steps + start + index) * height
 
     def one(k, carry):
         rows = pl.ds(pl.multiple_of(k * 16, 16), 16)
@@ -824,23 +824,23 @@
         lax.fori_loop(0, height // 128, fix, 0)
 
 
-def density_rest(info, gain, ham, far, level, density):
+def density_rest(info, gain, ham, far, level, density, start, stop):
     height, width = ham.shape
-    steps = 1
-    chunk = far.shape[0] // steps
+    chunk = 128
+    steps = far.shape[0] // chunk
     return pl.pallas_call(
-        functools.partial(density_kernel, steps),
+        functools.partial(density_kernel, start, steps),
         grid_spec=pltpu.PrefetchScalarGridSpec(
             num_scalar_prefetch=1,
-            grid=(steps,),
+            grid=(stop - start,),
             in_specs=[
                 SCALARS,
-                pl.BlockSpec((chunk, width), lambda i, info: ((1 - info[CORE]) * steps + i, 0)),
-                pl.BlockSpec((chunk, width), lambda i, info: (i, 0)),
+                pl.BlockSpec((chunk, width), lambda i, info: ((1 - info[CORE]) * steps + start + i, 0)),
+                pl.BlockSpec((chunk, width), lambda i, info: (start + i, 0)),
                 pl.BlockSpec(level.shape, lambda i, info: (0, 0)),
                 HERE,
             ],
-            out_specs=pl.BlockSpec((chunk, width), lambda i, info: ((1 - info[CORE]) * steps + i, 0)),
+            out_specs=pl.BlockSpec((chunk, width), lambda i, info: ((1 - info[CORE]) * steps + start + i, 0)),
         ),
         out_shape=jax.ShapeDtypeStruct((height, width), jnp.float32),
         input_output_aliases={5: 0},
@@ -913,8 +913,8 @@
     own_parts = [h_core, got, other]
     sends = pick(info, (SEND_X2, SEND_Z2), (h_core, got) + tuple(firsts), 1, shape)
     firsts, sends = lax.optimization_barrier((list(firsts), sends))
+    z2 = over_sec(sends[1], 1)
     x2 = over_col(sends[0])
-    z2 = over_sec(sends[1], 1)
     packed = packed + from_col
     from_near = lax.ppermute(packed, "sec", [(i, i ^ 1) for i in range(4)])
     operands = own_parts + firsts + [over_rep(first) for first in firsts]
@@ -928,8 +928,8 @@
 
     totals, token = grow_square(0, 3, (OWN0, OWN1, X1, Z1), None, None)
     (x2, z2, from_near), (token, packed) = after((x2, z2, from_near), (token, packed))
+    z3 = over_sec(x2, 2)
     x3 = over_col(z2)
-    z3 = over_sec(x2, 2)
     operands = operands + flat(swap_all((x2, z2)))
     totals, token = grow_square(1, 4, (OWN0, OWN1, X1, Z1, X2, Z2), totals, token)
     packed = packed + from_near
@@ -937,8 +937,8 @@
     (x3, z3, from_far), (token, packed) = after((x3, z3, from_far), (token, packed))
     last_send = pick(info, (SEND_LAST,), [z3] + operands[5:7], 0, shape)[0]
     (x3, z3), last_send = after((x3, z3), last_send)
+    z4 = over_sec(last_send, 3)
     x4 = over_col(last_send)
-    z4 = over_sec(last_send, 3)
     operands = operands + flat(swap_all((x3, z3)))
     gain, level, above, level_rows = level_terms(info, [packed, from_far], total // 128, half)
     lines = jax.ShapeDtypeStruct((total // 128, 128), jnp.float32)
@@ -968,9 +968,12 @@
     )
     sibling = over_rep(sibling)
     cube_diag = cube_diag + over_rep(cube_diag)
-    cube_diag = cube_diag + lax.ppermute(cube_diag, "sec", [(i, i ^ 1) for i in range(4)])
+    from_near = lax.ppermute(cube_diag, "sec", [(i, i ^ 1) for i in range(4)])
+    density = density_rest(info, gain, h_core, sibling, level, density, 0, 3)
+    from_near, density = after(from_near, density)
+    cube_diag = cube_diag + from_near
     from_far = lax.ppermute(cube_diag, "sec", [(i, i ^ 2) for i in range(4)])
-    density = density_rest(info, gain, h_core, sibling, level, density)
+    density = density_rest(info, gain, h_core, sibling, level, density, 3, 5)
     from_far, density = after(from_far, density)
     forces = pull_terms(gain, centers, above, cube_diag, from_far, weights, mm_coords, mm_charges)
     return (density, forces)

time: 232 us -> 230 us (level)
  waiting for transfers between devices: 60.7 us -> 57 us
  local copies, waits for them, and re-layouts: 21.9 us -> 19.4 us
    ppermute x1, waiting for transfers between devices: 3.78 us -> 0.32 us  [gossip_shards(): from_near = lax.ppermute(cube_diag, 'sec', [(i, i ^ 1) for i in range(4)])]
    unnamed x48 -> x50, local copies, waits for them, and re-layouts: 14.7 us -> 12.3 us
    pallas_call x1 -> x2, Pallas kernels: 3.75 us -> 5.9 us  [density_rest(): pl.pallas_call(functools.partial(density_kernel, start, steps), grid_spec...]
  transfers between devices with their start and end apart: 26 -> 26, of which waited for: 12 -> 12; matrix products, arithmetic and copies ran while one was open for 4% -> 5% of each run, Pallas kernels for 33% -> 34%
where the time goes in v6:
time: 230 us; the launch traced here: 229 us
  Pallas kernels  114 us (50%)
  waiting for transfers between devices  57 us (25%)
  starting transfers between devices  30.9 us (13%)
  local copies, waits for them, and re-layouts  19.4 us (8%)
  other arithmetic  6.66 us (3%)
    pallas_call x4, Pallas kernels, call_kernel(): pl.pallas_call(kernel, out_shape=(pltpu.VMEM((6,) + shape, jnp.float32),)...  91.5 us
    ppermute x1, waiting for transfers between devices, gossip_shards(): from_far = lax.ppermute(packed, 'sec', [(i, i ^ 2) for i in range(4)])  21.2 us
    unnamed x50, local copies, waits for them, and re-layouts  12.3 us
    ppermute x13, waiting for transfers between devices, over_rep(): return lax.ppermute(value, 'rep', [(0, 1), (1, 0)])  12.2 us
    ppermute x1, waiting for transfers between devices, gossip_shards(): from_near = lax.ppermute(packed, 'sec', [(i, i ^ 1) for i in range(4)])  11.2 us
    ppermute x4, starting transfers between devices, over_col(): return lax.ppermute(value, 'col', [(0, 1), (1, 0)])  10.5 us
    ppermute x4, waiting for transfers between devices, over_col(): return lax.ppermute(value, 'col', [(0, 1), (1, 0)])  8.66 us
    pallas_call x1, Pallas kernels, pair_terms(): pl.pallas_call(pairs_kernel, grid=(total // width,), out_shape=(jax.Shape...  7.48 us
  transfers between devices with their start and end apart: 26, of which 12 were waited for; matrix products, arithmetic and copies ran while one was open for 5% of the time, Pallas kernels for 34%

profile of v6, /device:TPU:0, one launch (start us, length us, event | category | flops | bytes accessed | tf_op | source)
XLA Modules:
  0.0 229.0 jit_solution(7381531853016990349)
XLA Ops:
  0.7 3.5 %constant_dynamic-slice_fusion.2 = (bf16[640,1280]{1,0:T(8,128)(2,1)S(1)}, bf16[640,1280]{1,0:T(8,128)(2,1)}) fusion(bf16[1280,1280]{1,0:T(8,128)(2,1)} %ham_ref.3, s32[]{:T(128)S(6)} %select_n.24, s32[]{:T(128)S(6)} %select_n.23), kind=kLoop, calls=%fused_computation.11 | loop fusion | bytes 6553608 | tf_op jit(solution)/shard_map/dynamic_slice | solution.py:896
  4.1 0.5 collective-permute-start.1
  4.6 2.6 %collective-permute-start = (bf16[640,1280]{1,0:T(8,128)(2,1)}, bf16[640,1280]{1,0:T(8,128)(2,1)}, u32[]{:S(2)}, u32[]{:S(2)}) collective-permute-start(bf16[640,1280]{1,0:T(8,128)(2,1)} %get-tuple-element.109), channel_id=1, source_target_pairs={{0,5},{1,3},{2,15},{3,1},{4,6},{5,8},{6,4},{7,2},{8,13},{9,11},{10... | collective-permute-start | bytes 4915208 | tf_op jit(solution)/shard_map/ppermute | solution.py:883
  7.3 2.3 %collective-permute-done.1.refs_1_ = bf16[640,1280]{1,0:T(8,128)(2,1)} collective-permute-done((bf16[640,1280]{1,0:T(8,128)(2,1)S(1)}, bf16[640,1280]{1,0:T(8,128)(2,1)}, u32[]{:S(2)}, u32[]{:S(2)}) %collective-permute-start.1) | collective-permute-done | bytes 1638432 | tf_op jit(solution)/shard_map/ppermute | solution.py:866
  9.6 3.4 %collective-permute-start.2 = (bf16[640,1280]{1,0:T(8,128)(2,1)}, bf16[640,1280]{1,0:T(8,128)(2,1)}, u32[]{:S(2)}, u32[]{:S(2)}) collective-permute-start(bf16[640,1280]{1,0:T(8,128)(2,1)} %collective-permute-done.1.refs_1_), channel_id=1, source_target_pairs={{0,2},{1,4},{2,0},{3,14},{4,9},{5,7},{6,3},{7,5},{8,10},{9,12},{10... | collective-permute-start | bytes 4915208 | tf_op jit(solution)/shard_map/ppermute | solution.py:883
  13.0 0.6 pad_maximum_fusion
  13.6 0.8 copy.15
  14.5 0.9 copy-done.6
  15.4 7.5 %pairs.1 = (f32[1,5120]{1,0:T(1,128)S(1)}, bf16[512,5120]{1,0:T(8,128)(2,1)S(1)}) custom-call(f32[3,5120]{1,0:T(4,128)S(1)} %copy-done.6, f32[512,4]{1,0:T(8,128)S(1)} %bitcast.12), custom_call_target="tpu_custom_call" | custom-call | tf_op jit(solution)/shard_map/pairs/pallas_call | solution.py:701
  22.9 2.3 %copy-done.2 = bf16[512,5120]{1,0:T(8,128)(2,1)} copy-done((bf16[512,5120]{1,0:T(8,128)(2,1)}, bf16[512,5120]{1,0:T(8,128)(2,1)S(1)}, u32[]{:S(2)}) %copy-start.2) | copy-done | bytes 5242904
  25.2 3.8 %fusion = (f32[1280]{0:T(1024)S(1)}, f32[]{:T(128)}) fusion(bf16[1280,1280]{1,0:T(8,128)(2,1)S(1)} %copy-done, s32[1280]{0:T(1024)S(1)} %get-tuple-element.110, s32[1280]{0:T(1024)S(1)} %get-tuple-element.111), kind=kLoop, calls=%fused_computation.3 | loop fusion | flops 11467519 | bytes 3292164 | tf_op jit(solution)/shard_map/reduce_sum | solution.py:906
  29.0 0.3 dynamic_update_slice.3
  29.3 0.6 broadcast_in_dim.19
  29.9 0.7 maximum_bitcast_fusion
  30.7 0.2 collective-permute-start.3
  30.9 1.3 constant_dynamic-slice_fusion.1
  32.1 0.7 fusion.3
  32.9 3.5 %collective-permute-start.4 = (f32[88,128]{1,0:T(8,128)S(1)}, f32[88,128]{1,0:T(8,128)S(1)}, u32[]{:S(2)}, u32[]{:S(2)}) collective-permute-start(f32[88,128]{1,0:T(8,128)S(1)} %fusion.3), channel_id=1, source_target_pairs={{0,2},{2,0},{1,3},{3,1},{4,6},{6,4},{5,7},{7,5},{8,10},{10,8},{9,1... | collective-permute-start | bytes 135176 | tf_op jit(solution)/shard_map/ppermute | solution.py:869
  36.3 0.7 fusion.2.info_ref
  37.0 7.7 %collective-permute-done.4 = f32[88,128]{1,0:T(8,128)S(1)} collective-permute-done((f32[88,128]{1,0:T(8,128)S(1)}, f32[88,128]{1,0:T(8,128)S(1)}, u32[]{:S(2)}, u32[]{:S(2)}) %collective-permute-start.4) | collective-permute-done | bytes 45088 | tf_op jit(solution)/shard_map/ppermute | solution.py:869
  44.7 2.5 %pick.2 = (bf16[640,1280]{1,0:T(8,128)(2,1)S(1)}, bf16[640,1280]{1,0:T(8,128)(2,1)S(1)}) custom-call(s32[12]{0:T(128)S(1)} %fusion.2.info_ref, bf16[1280,1280]{1,0:T(8,128)(2,1)} %ham_ref.3, bf16[640,1280]{1,0:T(8,128)(2,1)} %collective-permute-done.1.refs_1_, bf16[640,1280]{1,0:T(8,128)(2,1)} %collective-permute-done.refs_2_.refs_3_, ...), custom_call_target="tpu_custom_call" | custom-call | tf_op jit(solution)/shard_map/pick/pallas_call | solution.py:657
  47.2 1.1 collective-permute-start.9
  48.4 1.6 collective-permute-start.6
  50.1 4.6 %collective-permute-start.7 = (bf16[640,1280]{1,0:T(8,128)(2,1)S(1)}, bf16[640,1280]{1,0:T(8,128)(2,1)}, u32[]{:S(2)}, u32[]{:S(2)}) collective-permute-start(bf16[640,1280]{1,0:T(8,128)(2,1)S(1)} %get-tuple-element.62), channel_id=1, source_target_pairs={{0,12},{12,8},{8,4},{4,0},{2,6},{6,10},{10,14},{14,2},{1,13},{13,9... | collective-permute-start | bytes 4915208 | tf_op jit(solution)/shard_map/ppermute | solution.py:873
  54.7 1.2 copy-done.14
  55.9 1.2 copy-done.15
  57.0 22.4 %square_0.1 = (f32[6,640,1280]{2,1,0:T(8,128)S(1)}, f32[8,128]{1,0:T(8,128)}) custom-call(s32[428]{0:T(512)} %bitcast.17, s32[12]{0:T(128)} %copy-done.9, bf16[1280,1280]{1,0:T(8,128)(2,1)} %ham_ref.3, bf16[640,1280]{1,0:T(8,128)(2,1)} %collective-permute-done.1.refs_1_, bf16[640,1280]{1,0:T(8,128)(2,1)} %collective-permute-done.5.refs_2_, ...), custom_call_target="tpu_custom_call" | custom-call | tf_op jit(solution)/shard_map/square_0/pallas_call | solution.py:623
  79.5 11.2 %collective-permute-done.8 = f32[88,128]{1,0:T(8,128)S(1)} collective-permute-done((f32[88,128]{1,0:T(8,128)S(1)}, f32[88,128]{1,0:T(8,128)S(1)}, u32[]{:S(2)}, u32[]{:S(2)}) %collective-permute-start.8) | collective-permute-done | bytes 45088 | tf_op jit(solution)/shard_map/ppermute | solution.py:919
  90.6 0.5 collective-permute-start.14
  91.2 0.6 collective-permute-start.11
  91.8 1.8 collective-permute-start.12
  93.6 2.0 collective-permute-start.13
  95.6 1.1 collective-permute-done.14.refs_8_
  96.7 0.1 copy-done.17
  96.8 1.1 copy-done.18
  97.9 14.0 %square_1.1 = (f32[6,640,1280]{2,1,0:T(8,128)S(1)}, f32[8,128]{1,0:T(8,128)}) custom-call(s32[428]{0:T(512)} %bitcast.18, s32[12]{0:T(128)} %copy-done.9, bf16[1280,1280]{1,0:T(8,128)(2,1)} %ham_ref.3, bf16[640,1280]{1,0:T(8,128)(2,1)} %collective-permute-done.1.refs_1_, ...), custom_call_target="tpu_custom_call", output_to_operand_aliasing={{0}: (14, {})} | custom-call | tf_op jit(solution)/shard_map/square_1/pallas_call | solution.py:623
  111.9 21.2 %collective-permute-done.13.far_ref = f32[88,128]{1,0:T(8,128)S(1)} collective-permute-done((f32[88,128]{1,0:T(8,128)S(1)}, f32[88,128]{1,0:T(8,128)S(1)}, u32[]{:S(2)}, u32[]{:S(2)}) %collective-permute-start.13) | collective-permute-done | bytes 45088 | tf_op jit(solution)/shard_map/ppermute | solution.py:936
  133.2 1.3 copy-done.16
  134.4 2.0 pick.3
  136.4 0.1 collective-permute-start.18
  136.5 0.5 collective-permute-start.19
  137.0 4.8 %collective-permute-start.16 = (bf16[640,1280]{1,0:T(8,128)(2,1)S(1)}, bf16[640,1280]{1,0:T(8,128)(2,1)}, u32[]{:S(2)}, u32[]{:S(2)}) collective-permute-start(bf16[640,1280]{1,0:T(8,128)(2,1)S(1)} %pick.3), channel_id=1, source_target_pairs={{0,2},{2,0},{1,3},{3,1},{4,6},{6,4},{5,7},{7,5},{8,10},{10,8},{9,1... | collective-permute-start | bytes 4915208 | tf_op jit(solution)/shard_map/ppermute | solution.py:869
  141.8 1.4 levels.1
  143.2 0.7 copy-done.3
  143.9 0.6 copy-done.4
  144.5 1.2 copy-done.19
  145.8 0.5 copy-done.20
  146.2 27.6 %early_cube.1 = (f32[6,640,1280]{2,1,0:T(8,128)S(1)}, f32[640,128]{1,0:T(8,128)}) custom-call(s32[428]{0:T(512)} %bitcast.19, s32[12]{0:T(128)} %copy-done.9, bf16[1280,1280]{1,0:T(8,128)(2,1)} %ham_ref.3, bf16[640,1280]{1,0:T(8,128)(2,1)} %collective-permute-done.1.refs_1_, ...), custom_call_target="tpu_custom_call", output_to_operand_aliasing={{0}: (18, {})} | custom-call | tf_op jit(solution)/shard_map/early_cube/pallas_call | solution.py:623
  173.8 2.9 %collective-permute-done.17.refs_17_ = bf16[640,1280]{1,0:T(8,128)(2,1)} collective-permute-done((bf16[640,1280]{1,0:T(8,128)(2,1)S(1)}, bf16[640,1280]{1,0:T(8,128)(2,1)}, u32[]{:S(2)}, u32[]{:S(2)}) %collective-permute-start.17) | collective-permute-done | bytes 1638432 | tf_op jit(solution)/shard_map/ppermute | solution.py:873
  176.7 1.0 collective-permute-done.16.refs_15_
  177.7 0.5 collective-permute-start.21
  178.2 3.2 %collective-permute-done.20.refs_16_ = bf16[640,1280]{1,0:T(8,128)(2,1)S(1)} collective-permute-done((bf16[640,1280]{1,0:T(8,128)(2,1)}, bf16[640,1280]{1,0:T(8,128)(2,1)S(1)}, u32[]{:S(2)}, u32[]{:S(2)}) %collective-permute-start.20) | collective-permute-done | bytes 1638432 | tf_op jit(solution)/shard_map/ppermute | solution.py:866
  181.4 2.3 %collective-permute-done.21.refs_18_ = bf16[640,1280]{1,0:T(8,128)(2,1)S(1)} collective-permute-done((bf16[640,1280]{1,0:T(8,128)(2,1)}, bf16[640,1280]{1,0:T(8,128)(2,1)S(1)}, u32[]{:S(2)}, u32[]{:S(2)}) %collective-permute-start.21) | collective-permute-done | bytes 1638432 | tf_op jit(solution)/shard_map/ppermute | solution.py:866
  183.7 1.2 copy-done.22
  184.9 27.5 %late_cube.1 = (f32[6,640,1280]{2,1,0:T(8,128)S(1)}, bf16[640,1280]{1,0:T(8,128)(2,1)}, f32[1280,1280]{1,0:T(8,128)}, f32[40,128]{1,0:T(8,128)}) custom-call(s32[428]{0:T(512)} %bitcast.20, s32[12]{0:T(128)} %copy-done.9, f32[1]{0:T(128)} %get-tuple-element.90.gain_ref, bf16[1280,1280]{1,0:T(8,128)(2,1)} %ham_ref.3, ...), custom_call_target="tpu_custom_call", output_to_operand_aliasing={{0}: (22, {})} | custom-call | tf_op jit(solution)/shard_map/late_cube/pallas_call | solution.py:623
  212.5 0.5 collective-permute-start.22
  213.0 3.2 %collective-permute-done.22 = f32[40,128]{1,0:T(8,128)S(1)} collective-permute-done((f32[40,128]{1,0:T(8,128)}, f32[40,128]{1,0:T(8,128)S(1)}, u32[]{:S(2)}, u32[]{:S(2)}) %collective-permute-start.22) | collective-permute-done | bytes 20512 | tf_op jit(solution)/shard_map/ppermute | solution.py:866
  216.2 0.7 add.67
  217.0 3.4 %density.2._ = f32[1280,1280]{1,0:T(8,128)} custom-call(s32[12]{0:T(128)S(1)} %copy-done.11, f32[1]{0:T(128)} %get-tuple-element.90.gain_ref, bf16[1280,1280]{1,0:T(8,128)(2,1)S(1)} %copy-done.1, bf16[640,1280]{1,0:T(8,128)(2,1)S(1)} %collective-permute-done.24.far_ref, f32[40,128]{1,0:T(8,128)S(1)} %copy-done.5, ...), custom_call_target="tpu_custom_call", output_to_operand_aliasing={{}: (5, {})} | custom-call | tf_op jit(solution)/shard_map/density/pallas_call | solution.py:831
  220.4 0.3 collective-permute-done.23
  220.7 1.8 collective-permute-start.25
  222.5 2.5 %density.3 = f32[1280,1280]{1,0:T(8,128)} custom-call(s32[12]{0:T(128)S(1)} %copy-done.11, f32[1]{0:T(128)} %get-tuple-element.90.gain_ref, bf16[1280,1280]{1,0:T(8,128)(2,1)S(1)} %copy-done.1, bf16[640,1280]{1,0:T(8,128)(2,1)S(1)} %collective-permute-done.24.far_ref, f32[40,128]{1,0:T(8,128)S(1)} %copy-done.5, ...), custom_call_target="tpu_custom_call", output_to_operand_aliasing={{}: (5, {})} | custom-call | tf_op jit(solution)/shard_map/density/pallas_call | solution.py:831
  225.0 0.6 collective-permute-done.25.far_ref
  225.6 3.4 %pull.1 = f32[3,512]{1,0:T(4,128)} custom-call(f32[1]{0:T(128)} %get-tuple-element.90.gain_ref, f32[3,5120]{1,0:T(4,128)S(1)} %copy-done.7, f32[40,128]{1,0:T(8,128)S(1)} %get-tuple-element.103.above_ref, f32[40,128]{1,0:T(8,128)S(1)} %add.68.near_ref, f32[40,128]{1,0:T(8,128)S(1)} %collective-permute-done.25.far_ref, bf16[512,5120]{1,0:T(8,128)(2,1)S(1)} %bitcast.11, ...), custom_call_target="tpu_custom_call" | custom-call | tf_op jit(solution)/shard_map/pull/pallas_call | solution.py:781
  (66 shorter events, 0.4 us)
Async XLA Ops:
  0.6 12.4 %copy-start.12 = (f32[3,512]{1,0:T(4,128)S(1)}, f32[3,512]{1,0:T(4,128)}, u32[]{:S(2)}) copy-start(f32[3,512]{1,0:T(4,128)} %coords_ref.1) | copy-start | bytes 18436
  0.6 12.4 %copy-start.13 = (f32[512]{0:T(512)S(1)}, f32[512]{0:T(512)}, u32[]{:S(2)}) copy-start(f32[512]{0:T(512)} %param.9) | copy-start | bytes 6148
  0.7 24.5 %copy-start = (bf16[1280,1280]{1,0:T(8,128)(2,1)S(1)}, bf16[1280,1280]{1,0:T(8,128)(2,1)}, u32[]{:S(2)}) copy-start(bf16[1280,1280]{1,0:T(8,128)(2,1)} %ham_ref.3) | copy-start | bytes 9830404
  4.1 5.5 %collective-permute-start.1 = (bf16[640,1280]{1,0:T(8,128)(2,1)S(1)}, bf16[640,1280]{1,0:T(8,128)(2,1)}, u32[]{:S(2)}, u32[]{:S(2)}) collective-permute-start(bf16[640,1280]{1,0:T(8,128)(2,1)S(1)} %get-tuple-element.108), channel_id=1, source_target_pairs={{0,1},{1,0},{2,3},{3,2},{4,5},{5,4},{6,7},{7,6},{8,9},{9,8},{10,11... | collective-permute-start | bytes 4915208 | tf_op jit(solution)/shard_map/ppermute | solution.py:866
  4.6 40.1 %collective-permute-start.5 = (bf16[640,1280]{1,0:T(8,128)(2,1)}, bf16[640,1280]{1,0:T(8,128)(2,1)}, u32[]{:S(2)}, u32[]{:S(2)}) collective-permute-start(bf16[640,1280]{1,0:T(8,128)(2,1)} %get-tuple-element.109), channel_id=1, source_target_pairs={{0,1},{1,0},{2,3},{3,2},{4,5},{5,4},{6,7},{7,6},{8,9},{9,8},{10,11... | collective-permute-start | bytes 4915208 | tf_op jit(solution)/shard_map/ppermute | solution.py:866
  4.6 40.1 %collective-permute-start = (bf16[640,1280]{1,0:T(8,128)(2,1)}, bf16[640,1280]{1,0:T(8,128)(2,1)}, u32[]{:S(2)}, u32[]{:S(2)}) collective-permute-start(bf16[640,1280]{1,0:T(8,128)(2,1)} %get-tuple-element.109), channel_id=1, source_target_pairs={{0,5},{1,3},{2,15},{3,1},{4,6},{5,8},{6,4},{7,2},{8,13},{9,11},{10... | collective-permute-start | bytes 4915208 | tf_op jit(solution)/shard_map/ppermute | solution.py:883
  9.6 35.1 %collective-permute-start.2 = (bf16[640,1280]{1,0:T(8,128)(2,1)}, bf16[640,1280]{1,0:T(8,128)(2,1)}, u32[]{:S(2)}, u32[]{:S(2)}) collective-permute-start(bf16[640,1280]{1,0:T(8,128)(2,1)} %collective-permute-done.1.refs_1_), channel_id=1, source_target_pairs={{0,2},{1,4},{2,0},{3,14},{4,9},{5,7},{6,3},{7,5},{8,10},{9,12},{10... | collective-permute-start | bytes 4915208 | tf_op jit(solution)/shard_map/ppermute | solution.py:883
  14.5 0.9 copy-start.6
  22.8 2.3 %copy-start.2 = (bf16[512,5120]{1,0:T(8,128)(2,1)}, bf16[512,5120]{1,0:T(8,128)(2,1)S(1)}, u32[]{:S(2)}) copy-start(bf16[512,5120]{1,0:T(8,128)(2,1)S(1)} %get-tuple-element.105.weight_ref) | copy-start | bytes 15728644
  25.2 3.8 %copy-start.8 = (f32[1,5120]{1,0:T(1,128)}, f32[1,5120]{1,0:T(1,128)S(1)}, u32[]{:S(2)}) copy-start(f32[1,5120]{1,0:T(1,128)S(1)} %get-tuple-element.54) | copy-start | bytes 61444
  30.7 1.5 collective-permute-start.3
  32.9 11.9 %collective-permute-start.4 = (f32[88,128]{1,0:T(8,128)S(1)}, f32[88,128]{1,0:T(8,128)S(1)}, u32[]{:S(2)}, u32[]{:S(2)}) collective-permute-start(f32[88,128]{1,0:T(8,128)S(1)} %fusion.3), channel_id=1, source_target_pairs={{0,2},{2,0},{1,3},{3,1},{4,6},{6,4},{5,7},{7,5},{8,10},{10,8},{9,1... | collective-permute-start | bytes 135176 | tf_op jit(solution)/shard_map/ppermute | solution.py:869
  37.0 10.2 %copy-start.9 = (s32[12]{0:T(128)}, s32[12]{0:T(128)S(1)}, u32[]{:S(2)}) copy-start(s32[12]{0:T(128)S(1)} %fusion.2.info_ref) | copy-start | bytes 148
  47.2 7.4 %collective-permute-start.9 = (bf16[640,1280]{1,0:T(8,128)(2,1)}, bf16[640,1280]{1,0:T(8,128)(2,1)S(1)}, u32[]{:S(2)}, u32[]{:S(2)}) collective-permute-start(bf16[640,1280]{1,0:T(8,128)(2,1)} %collective-permute-done.refs_2_.refs_3_), channel_id=1, source_target_pairs={{0,1},{1,0},{2,3},{3,2},{4,5},{5,4},{6,7},{7,6},{8,9},{9,8},{10,11... | collective-permute-start | bytes 4915208 | tf_op jit(solution)/shard_map/ppermute | solution.py:866
  48.4 6.3 %collective-permute-start.10 = (bf16[640,1280]{1,0:T(8,128)(2,1)}, bf16[640,1280]{1,0:T(8,128)(2,1)S(1)}, u32[]{:S(2)}, u32[]{:S(2)}) collective-permute-start(bf16[640,1280]{1,0:T(8,128)(2,1)} %collective-permute-done.2.refs_3_.refs_4_), channel_id=1, source_target_pairs={{0,1},{1,0},{2,3},{3,2},{4,5},{5,4},{6,7},{7,6},{8,9},{9,8},{10,11... | collective-permute-start | bytes 4915208 | tf_op jit(solution)/shard_map/ppermute | solution.py:866
  48.4 42.2 %collective-permute-start.6 = (bf16[640,1280]{1,0:T(8,128)(2,1)S(1)}, bf16[640,1280]{1,0:T(8,128)(2,1)}, u32[]{:S(2)}, u32[]{:S(2)}) collective-permute-start(bf16[640,1280]{1,0:T(8,128)(2,1)S(1)} %get-tuple-element.61), channel_id=1, source_target_pairs={{0,2},{2,0},{1,3},{3,1},{4,6},{6,4},{5,7},{7,5},{8,10},{10,8},{9,1... | collective-permute-start | bytes 4915208 | tf_op jit(solution)/shard_map/ppermute | solution.py:869
  50.1 40.6 %collective-permute-start.7 = (bf16[640,1280]{1,0:T(8,128)(2,1)S(1)}, bf16[640,1280]{1,0:T(8,128)(2,1)}, u32[]{:S(2)}, u32[]{:S(2)}) collective-permute-start(bf16[640,1280]{1,0:T(8,128)(2,1)S(1)} %get-tuple-element.62), channel_id=1, source_target_pairs={{0,12},{12,8},{8,4},{4,0},{2,6},{6,10},{10,14},{14,2},{1,13},{13,9... | collective-permute-start | bytes 4915208 | tf_op jit(solution)/shard_map/ppermute | solution.py:873
  54.7 36.0 %collective-permute-start.8 = (f32[88,128]{1,0:T(8,128)S(1)}, f32[88,128]{1,0:T(8,128)S(1)}, u32[]{:S(2)}, u32[]{:S(2)}) collective-permute-start(f32[88,128]{1,0:T(8,128)S(1)} %add.65), channel_id=1, source_target_pairs={{0,4},{4,0},{8,12},{12,8},{1,5},{5,1},{9,13},{13,9},{2,6},{6,2},{1... | collective-permute-start | bytes 135176 | tf_op jit(solution)/shard_map/ppermute | solution.py:919
  54.7 1.2 copy-start.14
  55.9 1.2 copy-start.15
  90.6 5.0 %collective-permute-start.15 = (bf16[640,1280]{1,0:T(8,128)(2,1)}, bf16[640,1280]{1,0:T(8,128)(2,1)S(1)}, u32[]{:S(2)}, u32[]{:S(2)}) collective-permute-start(bf16[640,1280]{1,0:T(8,128)(2,1)} %collective-permute-done.7.refs_9_), channel_id=1, source_target_pairs={{0,1},{1,0},{2,3},{3,2},{4,5},{5,4},{6,7},{7,6},{8,9},{9,8},{10,11... | collective-permute-start | bytes 4915208 | tf_op jit(solution)/shard_map/ppermute | solution.py:866
  90.6 6.1 %collective-permute-start.14 = (bf16[640,1280]{1,0:T(8,128)(2,1)}, bf16[640,1280]{1,0:T(8,128)(2,1)S(1)}, u32[]{:S(2)}, u32[]{:S(2)}) collective-permute-start(bf16[640,1280]{1,0:T(8,128)(2,1)} %collective-permute-done.6.refs_7_), channel_id=1, source_target_pairs={{0,1},{1,0},{2,3},{3,2},{4,5},{5,4},{6,7},{7,6},{8,9},{9,8},{10,11... | collective-permute-start | bytes 4915208 | tf_op jit(solution)/shard_map/ppermute | solution.py:866
  91.2 42.0 %collective-permute-start.11 = (bf16[640,1280]{1,0:T(8,128)(2,1)}, bf16[640,1280]{1,0:T(8,128)(2,1)}, u32[]{:S(2)}, u32[]{:S(2)}) collective-permute-start(bf16[640,1280]{1,0:T(8,128)(2,1)} %collective-permute-done.7.refs_9_), channel_id=1, source_target_pairs={{0,2},{2,0},{1,3},{3,1},{4,6},{6,4},{5,7},{7,5},{8,10},{10,8},{9,1... | collective-permute-start | bytes 4915208 | tf_op jit(solution)/shard_map/ppermute | solution.py:869
  91.8 41.4 %collective-permute-start.12 = (bf16[640,1280]{1,0:T(8,128)(2,1)}, bf16[640,1280]{1,0:T(8,128)(2,1)S(1)}, u32[]{:S(2)}, u32[]{:S(2)}) collective-permute-start(bf16[640,1280]{1,0:T(8,128)(2,1)} %collective-permute-done.6.refs_7_), channel_id=1, source_target_pairs={{0,4},{4,8},{8,12},{12,0},{2,14},{14,10},{10,6},{6,2},{1,5},{5,9},... | collective-permute-start | bytes 4915208 | tf_op jit(solution)/shard_map/ppermute | solution.py:873
  93.6 39.5 %collective-permute-start.13 = (f32[88,128]{1,0:T(8,128)S(1)}, f32[88,128]{1,0:T(8,128)S(1)}, u32[]{:S(2)}, u32[]{:S(2)}) collective-permute-start(f32[88,128]{1,0:T(8,128)S(1)} %add.66.near_ref), channel_id=1, source_target_pairs={{0,8},{4,12},{8,0},{12,4},{1,9},{5,13},{9,1},{13,5},{2,10},{6,14},... | collective-permute-start | bytes 135176 | tf_op jit(solution)/shard_map/ppermute | solution.py:936
  95.6 1.2 copy-start.17
  96.7 1.2 copy-start.18
  97.9 36.5 %copy-start.10 = (s32[12]{0:T(128)S(1)}, s32[12]{0:T(128)}, u32[]{:S(2)}) copy-start(s32[12]{0:T(128)} %copy-done.9) | copy-start | bytes 148
  133.2 1.3 copy-start.16
  136.4 8.1 %collective-permute-start.18 = (bf16[640,1280]{1,0:T(8,128)(2,1)}, bf16[640,1280]{1,0:T(8,128)(2,1)S(1)}, u32[]{:S(2)}, u32[]{:S(2)}) collective-permute-start(bf16[640,1280]{1,0:T(8,128)(2,1)} %collective-permute-done.11.refs_11_), channel_id=1, source_target_pairs={{0,1},{1,0},{2,3},{3,2},{4,5},{5,4},{6,7},{7,6},{8,9},{9,8},{10,11... | collective-permute-start | bytes 4915208 | tf_op jit(solution)/shard_map/ppermute | solution.py:866
  136.5 8.0 %collective-permute-start.19 = (bf16[640,1280]{1,0:T(8,128)(2,1)}, bf16[640,1280]{1,0:T(8,128)(2,1)S(1)}, u32[]{:S(2)}, u32[]{:S(2)}) collective-permute-start(bf16[640,1280]{1,0:T(8,128)(2,1)} %copy-done.16), channel_id=1, source_target_pairs={{0,1},{1,0},{2,3},{3,2},{4,5},{5,4},{6,7},{7,6},{8,9},{9,8},{10,11... | collective-permute-start | bytes 4915208 | tf_op jit(solution)/shard_map/ppermute | solution.py:866
  137.0 39.7 %collective-permute-start.17 = (bf16[640,1280]{1,0:T(8,128)(2,1)S(1)}, bf16[640,1280]{1,0:T(8,128)(2,1)}, u32[]{:S(2)}, u32[]{:S(2)}) collective-permute-start(bf16[640,1280]{1,0:T(8,128)(2,1)S(1)} %pick.3), channel_id=1, source_target_pairs={{0,4},{4,8},{8,12},{12,0},{2,14},{14,10},{10,6},{6,2},{1,5},{5,9},... | collective-permute-start | bytes 4915208 | tf_op jit(solution)/shard_map/ppermute | solution.py:873
  137.0 40.7 %collective-permute-start.16 = (bf16[640,1280]{1,0:T(8,128)(2,1)S(1)}, bf16[640,1280]{1,0:T(8,128)(2,1)}, u32[]{:S(2)}, u32[]{:S(2)}) collective-permute-start(bf16[640,1280]{1,0:T(8,128)(2,1)S(1)} %pick.3), channel_id=1, source_target_pairs={{0,2},{2,0},{1,3},{3,1},{4,6},{6,4},{5,7},{7,5},{8,10},{10,8},{9,1... | collective-permute-start | bytes 4915208 | tf_op jit(solution)/shard_map/ppermute | solution.py:869
  143.1 0.7 copy-start.3
  143.9 0.6 copy-start.4
  144.5 1.3 copy-start.19
  144.5 1.7 copy-start.20
  177.7 3.7 %collective-permute-start.20 = (bf16[640,1280]{1,0:T(8,128)(2,1)}, bf16[640,1280]{1,0:T(8,128)(2,1)S(1)}, u32[]{:S(2)}, u32[]{:S(2)}) collective-permute-start(bf16[640,1280]{1,0:T(8,128)(2,1)} %collective-permute-done.16.refs_15_), channel_id=1, source_target_pairs={{0,1},{1,0},{2,3},{3,2},{4,5},{5,4},{6,7},{7,6},{8,9},{9,8},{10,11... | collective-permute-start | bytes 4915208 | tf_op jit(solution)/shard_map/ppermute | solution.py:866
  177.7 6.1 %collective-permute-start.21 = (bf16[640,1280]{1,0:T(8,128)(2,1)}, bf16[640,1280]{1,0:T(8,128)(2,1)S(1)}, u32[]{:S(2)}, u32[]{:S(2)}) collective-permute-start(bf16[640,1280]{1,0:T(8,128)(2,1)} %collective-permute-done.17.refs_17_), channel_id=1, source_target_pairs={{0,1},{1,0},{2,3},{3,2},{4,5},{5,4},{6,7},{7,6},{8,9},{9,8},{10,11... | collective-permute-start | bytes 4915208 | tf_op jit(solution)/shard_map/ppermute | solution.py:866
  181.4 2.3 %copy-start.21 = (bf16[640,1280]{1,0:T(8,128)(2,1)}, bf16[640,1280]{1,0:T(8,128)(2,1)S(1)}, u32[]{:S(2)}) copy-start(bf16[640,1280]{1,0:T(8,128)(2,1)S(1)} %collective-permute-done.20.refs_16_) | copy-start | bytes 4915204
  183.7 1.2 copy-start.22
  184.9 32.0 %copy-start.1 = (bf16[1280,1280]{1,0:T(8,128)(2,1)S(1)}, bf16[1280,1280]{1,0:T(8,128)(2,1)}, u32[]{:S(2)}) copy-start(bf16[1280,1280]{1,0:T(8,128)(2,1)} %ham_ref.3) | copy-start | bytes 9830404
  184.9 32.1 %copy-start.5 = (f32[40,128]{1,0:T(8,128)S(1)}, f32[40,128]{1,0:T(8,128)}, u32[]{:S(2)}) copy-start(f32[40,128]{1,0:T(8,128)} %copy-done.4) | copy-start | bytes 61444
  184.9 32.1 %copy-start.11 = (s32[12]{0:T(128)S(1)}, s32[12]{0:T(128)}, u32[]{:S(2)}) copy-start(s32[12]{0:T(128)} %copy-done.9) | copy-start | bytes 148
  212.4 4.5 %collective-permute-start.24 = (bf16[640,1280]{1,0:T(8,128)(2,1)}, bf16[640,1280]{1,0:T(8,128)(2,1)S(1)}, u32[]{:S(2)}, u32[]{:S(2)}) collective-permute-start(bf16[640,1280]{1,0:T(8,128)(2,1)} %get-tuple-element.98), channel_id=1, source_target_pairs={{0,1},{1,0},{2,3},{3,2},{4,5},{5,4},{6,7},{7,6},{8,9},{9,8},{10,11... | collective-permute-start | bytes 4915208 | tf_op jit(solution)/shard_map/ppermute | solution.py:866
  212.5 3.7 %collective-permute-start.22 = (f32[40,128]{1,0:T(8,128)}, f32[40,128]{1,0:T(8,128)S(1)}, u32[]{:S(2)}, u32[]{:S(2)}) collective-permute-start(f32[40,128]{1,0:T(8,128)} %get-tuple-element.97), channel_id=1, source_target_pairs={{0,1},{1,0},{2,3},{3,2},{4,5},{5,4},{6,7},{7,6},{8,9},{9,8},{10,11... | collective-permute-start | bytes 61448 | tf_op jit(solution)/shard_map/ppermute | solution.py:866
  216.9 3.8 %collective-permute-start.23 = (f32[40,128]{1,0:T(8,128)S(1)}, f32[40,128]{1,0:T(8,128)S(1)}, u32[]{:S(2)}, u32[]{:S(2)}) collective-permute-start(f32[40,128]{1,0:T(8,128)S(1)} %add.67), channel_id=1, source_target_pairs={{0,4},{4,0},{8,12},{12,8},{1,5},{5,1},{9,13},{13,9},{2,6},{6,2},{1... | collective-permute-start | bytes 61448 | tf_op jit(solution)/shard_map/ppermute | solution.py:971
  217.0 8.7 %slice-start = ((s8[5242880]{0:T(1024)(128)(4,1)}), s8[4194304]{0:T(1024)(128)(4,1)S(1)}, s32[]{:S(2)}) async-start(s8[5242880]{0:T(1024)(128)(4,1)} %bitcast.10), calls=%async_computation | async-start | bytes 8388608
  220.4 5.2 %slice-start.1 = ((s8[5242880]{0:T(1024)(128)(4,1)}), s8[1048576]{0:T(1024)(128)(4,1)S(1)}, s32[]{:S(2)}) async-start(s8[5242880]{0:T(1024)(128)(4,1)} %bitcast.10), calls=%async_computation.1 | async-start | bytes 2097152
  220.7 4.9 %copy-start.7 = (f32[3,5120]{1,0:T(4,128)S(1)}, f32[3,5120]{1,0:T(4,128)}, u32[]{:S(2)}) copy-start(f32[3,5120]{1,0:T(4,128)} %spots_ref.3) | copy-start | bytes 184324
  220.7 4.9 %collective-permute-start.25 = (f32[40,128]{1,0:T(8,128)S(1)}, f32[40,128]{1,0:T(8,128)S(1)}, u32[]{:S(2)}, u32[]{:S(2)}) collective-permute-start(f32[40,128]{1,0:T(8,128)S(1)} %add.68.near_ref), channel_id=1, source_target_pairs={{0,8},{4,12},{8,0},{12,4},{1,9},{5,13},{9,1},{13,5},{2,10},{6,14},... | collective-permute-start | bytes 61448 | tf_op jit(solution)/shard_map/ppermute | solution.py:975

commit v7 on v6

--- a/solution.py
+++ b/solution.py
@@ -652,17 +652,18 @@
             pltpu.make_async_copy(to, to, in_sem.at[k, part]).wait()
 
 
-def pick(info, choices, sources, whole, shape):
+def pick(info, choices, sources, whole, shape, fresh=0):
+    held = [pltpu.with_memory_space_constraint(value, pltpu.VMEM) for value in sources[:fresh]]
     parts = 4
     return pl.pallas_call(
         functools.partial(pick_kernel, choices, whole, len(sources)),
         out_shape=[pltpu.VMEM(shape, sources[0].dtype)] * len(choices),
-        in_specs=[SCALARS] + [HERE] * len(sources),
+        in_specs=[SCALARS] + [VMEM] * fresh + [HERE] * (len(sources) - fresh),
         out_specs=[VMEM] * len(choices),
         scratch_shapes=[pltpu.SemaphoreType.DMA((len(choices), parts))],
         compiler_params=pltpu.CompilerParams(vmem_limit_bytes=8 * 2**20),
         name="pick",
-    )(info, *in_hbm(sources))
+    )(info, *held, *in_hbm(sources[fresh:]))
 
 
 def pairs_kernel(spots_ref, points_ref, out_ref, weight_ref, wide_ref):
@@ -935,7 +936,7 @@
     packed = packed + from_near
     from_far = lax.ppermute(packed, "sec", [(i, i ^ 2) for i in range(4)])
     (x3, z3, from_far), (token, packed) = after((x3, z3, from_far), (token, packed))
-    last_send = pick(info, (SEND_LAST,), [z3] + operands[5:7], 0, shape)[0]
+    last_send = pick(info, (SEND_LAST,), [z3] + operands[5:7], 0, shape, 1)[0]
     (x3, z3), last_send = after((x3, z3), last_send)
     z4 = over_sec(last_send, 3)
     x4 = over_col(last_send)

time: 230 us -> 228 us (level)
  transfers between devices with their start and end apart: 26 -> 26, of which waited for: 12 -> 12; matrix products, arithmetic and copies ran while one was open for 5% -> 5% of each run, Pallas kernels for 34% -> 35%
where the time goes in v7:
time: 228 us; the launch traced here: 227 us
  Pallas kernels  114 us (50%)
  waiting for transfers between devices  57 us (25%)
  starting transfers between devices  30.9 us (14%)
  local copies, waits for them, and re-layouts  18.2 us (8%)
  other arithmetic  6.66 us (3%)
    pallas_call x4, Pallas kernels, call_kernel(): pl.pallas_call(kernel, out_shape=(pltpu.VMEM((6,) + shape, jnp.float32),)...  91.5 us
    ppermute x1, waiting for transfers between devices, gossip_shards(): from_far = lax.ppermute(packed, 'sec', [(i, i ^ 2) for i in range(4)])  21.2 us
    ppermute x13, waiting for transfers between devices, over_rep(): return lax.ppermute(value, 'rep', [(0, 1), (1, 0)])  12.2 us
    ppermute x1, waiting for transfers between devices, gossip_shards(): from_near = lax.ppermute(packed, 'sec', [(i, i ^ 1) for i in range(4)])  11.2 us
    unnamed x50, local copies, waits for them, and re-layouts  11.1 us
    ppermute x4, starting transfers between devices, over_col(): return lax.ppermute(value, 'col', [(0, 1), (1, 0)])  10.3 us
    ppermute x4, waiting for transfers between devices, over_col(): return lax.ppermute(value, 'col', [(0, 1), (1, 0)])  8.66 us
    pallas_call x1, Pallas kernels, pair_terms(): pl.pallas_call(pairs_kernel, grid=(total // width,), out_shape=(jax.Shape...  7.48 us
  transfers between devices with their start and end apart: 26, of which 12 were waited for; matrix products, arithmetic and copies ran while one was open for 5% of the time, Pallas kernels for 35%

profile of v7, /device:TPU:0, one launch (start us, length us, event | category | flops | bytes accessed | tf_op | source)
XLA Modules:
  0.0 227.3 jit_solution(856425512478952936)
XLA Ops:
  0.7 3.5 %constant_dynamic-slice_fusion.2 = (bf16[640,1280]{1,0:T(8,128)(2,1)S(1)}, bf16[640,1280]{1,0:T(8,128)(2,1)}) fusion(bf16[1280,1280]{1,0:T(8,128)(2,1)} %ham_ref.3, s32[]{:T(128)S(6)} %select_n.24, s32[]{:T(128)S(6)} %select_n.23), kind=kLoop, calls=%fused_computation.11 | loop fusion | bytes 6553608 | tf_op jit(solution)/shard_map/dynamic_slice | solution.py:897
  4.1 0.5 collective-permute-start.1
  4.6 2.6 %collective-permute-start = (bf16[640,1280]{1,0:T(8,128)(2,1)}, bf16[640,1280]{1,0:T(8,128)(2,1)}, u32[]{:S(2)}, u32[]{:S(2)}) collective-permute-start(bf16[640,1280]{1,0:T(8,128)(2,1)} %get-tuple-element.109), channel_id=1, source_target_pairs={{0,5},{1,3},{2,15},{3,1},{4,6},{5,8},{6,4},{7,2},{8,13},{9,11},{10... | collective-permute-start | bytes 4915208 | tf_op jit(solution)/shard_map/ppermute | solution.py:884
  7.3 2.3 %collective-permute-done.1.refs_1_ = bf16[640,1280]{1,0:T(8,128)(2,1)} collective-permute-done((bf16[640,1280]{1,0:T(8,128)(2,1)S(1)}, bf16[640,1280]{1,0:T(8,128)(2,1)}, u32[]{:S(2)}, u32[]{:S(2)}) %collective-permute-start.1) | collective-permute-done | bytes 1638432 | tf_op jit(solution)/shard_map/ppermute | solution.py:867
  9.6 3.4 %collective-permute-start.2 = (bf16[640,1280]{1,0:T(8,128)(2,1)}, bf16[640,1280]{1,0:T(8,128)(2,1)}, u32[]{:S(2)}, u32[]{:S(2)}) collective-permute-start(bf16[640,1280]{1,0:T(8,128)(2,1)} %collective-permute-done.1.refs_1_), channel_id=1, source_target_pairs={{0,2},{1,4},{2,0},{3,14},{4,9},{5,7},{6,3},{7,5},{8,10},{9,12},{10... | collective-permute-start | bytes 4915208 | tf_op jit(solution)/shard_map/ppermute | solution.py:884
  13.0 0.6 pad_maximum_fusion
  13.6 0.8 copy.15
  14.5 0.9 copy-done.7
  15.4 7.5 %pairs.1 = (f32[1,5120]{1,0:T(1,128)S(1)}, bf16[512,5120]{1,0:T(8,128)(2,1)S(1)}) custom-call(f32[3,5120]{1,0:T(4,128)S(1)} %copy-done.7, f32[512,4]{1,0:T(8,128)S(1)} %bitcast.12), custom_call_target="tpu_custom_call" | custom-call | tf_op jit(solution)/shard_map/pairs/pallas_call | solution.py:702
  22.9 2.3 %copy-done.3 = bf16[512,5120]{1,0:T(8,128)(2,1)} copy-done((bf16[512,5120]{1,0:T(8,128)(2,1)}, bf16[512,5120]{1,0:T(8,128)(2,1)S(1)}, u32[]{:S(2)}) %copy-start.3) | copy-done | bytes 5242904
  25.2 3.8 %fusion = (f32[1280]{0:T(1024)S(1)}, f32[]{:T(128)}) fusion(bf16[1280,1280]{1,0:T(8,128)(2,1)S(1)} %copy-done, s32[1280]{0:T(1024)S(1)} %get-tuple-element.110, s32[1280]{0:T(1024)S(1)} %get-tuple-element.111), kind=kLoop, calls=%fused_computation.3 | loop fusion | flops 11467519 | bytes 3292164 | tf_op jit(solution)/shard_map/reduce_sum | solution.py:907
  29.0 0.3 dynamic_update_slice.3
  29.3 0.6 broadcast_in_dim.19
  29.9 0.7 maximum_bitcast_fusion
  30.7 0.2 collective-permute-start.3
  30.9 1.3 constant_dynamic-slice_fusion.1
  32.1 0.7 fusion.3
  32.9 3.5 %collective-permute-start.4 = (f32[88,128]{1,0:T(8,128)S(1)}, f32[88,128]{1,0:T(8,128)S(1)}, u32[]{:S(2)}, u32[]{:S(2)}) collective-permute-start(f32[88,128]{1,0:T(8,128)S(1)} %fusion.3), channel_id=1, source_target_pairs={{0,2},{2,0},{1,3},{3,1},{4,6},{6,4},{5,7},{7,5},{8,10},{10,8},{9,1... | collective-permute-start | bytes 135176 | tf_op jit(solution)/shard_map/ppermute | solution.py:870
  36.3 0.7 fusion.2.info_ref
  37.0 7.7 %collective-permute-done.4 = f32[88,128]{1,0:T(8,128)S(1)} collective-permute-done((f32[88,128]{1,0:T(8,128)S(1)}, f32[88,128]{1,0:T(8,128)S(1)}, u32[]{:S(2)}, u32[]{:S(2)}) %collective-permute-start.4) | collective-permute-done | bytes 45088 | tf_op jit(solution)/shard_map/ppermute | solution.py:870
  44.7 2.5 %pick.2 = (bf16[640,1280]{1,0:T(8,128)(2,1)S(1)}, bf16[640,1280]{1,0:T(8,128)(2,1)S(1)}) custom-call(s32[12]{0:T(128)S(1)} %fusion.2.info_ref, bf16[1280,1280]{1,0:T(8,128)(2,1)} %ham_ref.3, bf16[640,1280]{1,0:T(8,128)(2,1)} %collective-permute-done.1.refs_1_, bf16[640,1280]{1,0:T(8,128)(2,1)} %collective-permute-done.refs_2_.refs_3_, ...), custom_call_target="tpu_custom_call" | custom-call | tf_op jit(solution)/shard_map/pick/pallas_call | solution.py:658
  47.2 1.1 collective-permute-start.9
  48.4 1.6 collective-permute-start.6
  50.1 4.6 %collective-permute-start.7 = (bf16[640,1280]{1,0:T(8,128)(2,1)S(1)}, bf16[640,1280]{1,0:T(8,128)(2,1)}, u32[]{:S(2)}, u32[]{:S(2)}) collective-permute-start(bf16[640,1280]{1,0:T(8,128)(2,1)S(1)} %get-tuple-element.62), channel_id=1, source_target_pairs={{0,12},{12,8},{8,4},{4,0},{2,6},{6,10},{10,14},{14,2},{1,13},{13,9... | collective-permute-start | bytes 4915208 | tf_op jit(solution)/shard_map/ppermute | solution.py:874
  54.7 1.2 copy-done.15
  55.9 1.2 copy-done.16
  57.0 22.4 %square_0.1 = (f32[6,640,1280]{2,1,0:T(8,128)S(1)}, f32[8,128]{1,0:T(8,128)}) custom-call(s32[428]{0:T(512)} %bitcast.17, s32[12]{0:T(128)} %copy-done.10, bf16[1280,1280]{1,0:T(8,128)(2,1)} %ham_ref.3, bf16[640,1280]{1,0:T(8,128)(2,1)} %collective-permute-done.1.refs_1_, bf16[640,1280]{1,0:T(8,128)(2,1)} %collective-permute-done.5.refs_2_, ...), custom_call_target="tpu_custom_call" | custom-call | tf_op jit(solution)/shard_map/square_0/pallas_call | solution.py:623
  79.5 11.2 %collective-permute-done.8 = f32[88,128]{1,0:T(8,128)S(1)} collective-permute-done((f32[88,128]{1,0:T(8,128)S(1)}, f32[88,128]{1,0:T(8,128)S(1)}, u32[]{:S(2)}, u32[]{:S(2)}) %collective-permute-start.8) | collective-permute-done | bytes 45088 | tf_op jit(solution)/shard_map/ppermute | solution.py:920
  90.6 0.5 collective-permute-start.14
  91.2 0.6 collective-permute-start.11
  91.8 1.8 collective-permute-start.12
  93.6 2.0 collective-permute-start.13
  95.6 1.1 collective-permute-done.14.refs_8_
  96.7 0.1 copy-done.17
  96.8 1.1 copy-done.18
  97.9 14.0 %square_1.1 = (f32[6,640,1280]{2,1,0:T(8,128)S(1)}, f32[8,128]{1,0:T(8,128)}) custom-call(s32[428]{0:T(512)} %bitcast.18, s32[12]{0:T(128)} %copy-done.10, bf16[1280,1280]{1,0:T(8,128)(2,1)} %ham_ref.3, bf16[640,1280]{1,0:T(8,128)(2,1)} %collective-permute-done.1.refs_1_, ...), custom_call_target="tpu_custom_call", output_to_operand_aliasing={{0}: (14, {})} | custom-call | tf_op jit(solution)/shard_map/square_1/pallas_call | solution.py:623
  111.9 21.2 %collective-permute-done.13.far_ref = f32[88,128]{1,0:T(8,128)S(1)} collective-permute-done((f32[88,128]{1,0:T(8,128)S(1)}, f32[88,128]{1,0:T(8,128)S(1)}, u32[]{:S(2)}, u32[]{:S(2)}) %collective-permute-start.13) | collective-permute-done | bytes 45088 | tf_op jit(solution)/shard_map/ppermute | solution.py:937
  133.2 1.4 pick.3
  134.6 0.1 collective-permute-start.18
  134.7 0.5 collective-permute-start.19
  135.2 0.2 collective-permute-start.17
  135.4 4.6 %collective-permute-start.16 = (bf16[640,1280]{1,0:T(8,128)(2,1)S(1)}, bf16[640,1280]{1,0:T(8,128)(2,1)}, u32[]{:S(2)}, u32[]{:S(2)}) collective-permute-start(bf16[640,1280]{1,0:T(8,128)(2,1)S(1)} %pick.3), channel_id=1, source_target_pairs={{0,2},{2,0},{1,3},{3,1},{4,6},{6,4},{5,7},{7,5},{8,10},{10,8},{9,1... | collective-permute-start | bytes 4915208 | tf_op jit(solution)/shard_map/ppermute | solution.py:870
  140.0 1.4 levels.1
  141.4 0.7 copy-done.4
  142.1 0.6 copy-done.5
  142.7 1.2 copy-done.20
  143.9 0.6 copy-done.19
  144.5 27.6 %early_cube.1 = (f32[6,640,1280]{2,1,0:T(8,128)S(1)}, f32[640,128]{1,0:T(8,128)}) custom-call(s32[428]{0:T(512)} %bitcast.19, s32[12]{0:T(128)} %copy-done.10, bf16[1280,1280]{1,0:T(8,128)(2,1)} %ham_ref.3, bf16[640,1280]{1,0:T(8,128)(2,1)} %collective-permute-done.1.refs_1_, ...), custom_call_target="tpu_custom_call", output_to_operand_aliasing={{0}: (18, {})} | custom-call | tf_op jit(solution)/shard_map/early_cube/pallas_call | solution.py:623
  172.1 2.8 %collective-permute-done.17.refs_17_ = bf16[640,1280]{1,0:T(8,128)(2,1)} collective-permute-done((bf16[640,1280]{1,0:T(8,128)(2,1)S(1)}, bf16[640,1280]{1,0:T(8,128)(2,1)}, u32[]{:S(2)}, u32[]{:S(2)}) %collective-permute-start.17) | collective-permute-done | bytes 1638432 | tf_op jit(solution)/shard_map/ppermute | solution.py:874
  174.9 1.0 collective-permute-done.16.refs_15_
  175.9 0.5 collective-permute-start.21
  176.4 3.2 %collective-permute-done.20.refs_16_ = bf16[640,1280]{1,0:T(8,128)(2,1)S(1)} collective-permute-done((bf16[640,1280]{1,0:T(8,128)(2,1)}, bf16[640,1280]{1,0:T(8,128)(2,1)S(1)}, u32[]{:S(2)}, u32[]{:S(2)}) %collective-permute-start.20) | collective-permute-done | bytes 1638432 | tf_op jit(solution)/shard_map/ppermute | solution.py:867
  179.6 2.3 %collective-permute-done.21.refs_18_ = bf16[640,1280]{1,0:T(8,128)(2,1)S(1)} collective-permute-done((bf16[640,1280]{1,0:T(8,128)(2,1)}, bf16[640,1280]{1,0:T(8,128)(2,1)S(1)}, u32[]{:S(2)}, u32[]{:S(2)}) %collective-permute-start.21) | collective-permute-done | bytes 1638432 | tf_op jit(solution)/shard_map/ppermute | solution.py:867
  181.9 1.2 copy-done.22
  183.1 27.5 %late_cube.1 = (f32[6,640,1280]{2,1,0:T(8,128)S(1)}, bf16[640,1280]{1,0:T(8,128)(2,1)}, f32[1280,1280]{1,0:T(8,128)}, f32[40,128]{1,0:T(8,128)}) custom-call(s32[428]{0:T(512)} %bitcast.20, s32[12]{0:T(128)} %copy-done.10, f32[1]{0:T(128)} %get-tuple-element.90.gain_ref, bf16[1280,1280]{1,0:T(8,128)(2,1)} %ham_ref.3, ...), custom_call_target="tpu_custom_call", output_to_operand_aliasing={{0}: (22, {})} | custom-call | tf_op jit(solution)/shard_map/late_cube/pallas_call | solution.py:623
  210.7 0.5 collective-permute-start.22
  211.2 3.2 %collective-permute-done.22 = f32[40,128]{1,0:T(8,128)S(1)} collective-permute-done((f32[40,128]{1,0:T(8,128)}, f32[40,128]{1,0:T(8,128)S(1)}, u32[]{:S(2)}, u32[]{:S(2)}) %collective-permute-start.22) | collective-permute-done | bytes 20512 | tf_op jit(solution)/shard_map/ppermute | solution.py:867
  214.4 0.7 add.67
  215.2 3.4 %density.2._ = f32[1280,1280]{1,0:T(8,128)} custom-call(s32[12]{0:T(128)S(1)} %copy-done.12, f32[1]{0:T(128)} %get-tuple-element.90.gain_ref, bf16[1280,1280]{1,0:T(8,128)(2,1)S(1)} %copy-done.1, bf16[640,1280]{1,0:T(8,128)(2,1)S(1)} %collective-permute-done.24.far_ref, f32[40,128]{1,0:T(8,128)S(1)} %copy-done.6, ...), custom_call_target="tpu_custom_call", output_to_operand_aliasing={{}: (5, {})} | custom-call | tf_op jit(solution)/shard_map/density/pallas_call | solution.py:832
  218.6 0.3 collective-permute-done.23
  219.0 1.8 collective-permute-start.25
  220.8 2.5 %density.3 = f32[1280,1280]{1,0:T(8,128)} custom-call(s32[12]{0:T(128)S(1)} %copy-done.12, f32[1]{0:T(128)} %get-tuple-element.90.gain_ref, bf16[1280,1280]{1,0:T(8,128)(2,1)S(1)} %copy-done.1, bf16[640,1280]{1,0:T(8,128)(2,1)S(1)} %collective-permute-done.24.far_ref, f32[40,128]{1,0:T(8,128)S(1)} %copy-done.6, ...), custom_call_target="tpu_custom_call", output_to_operand_aliasing={{}: (5, {})} | custom-call | tf_op jit(solution)/shard_map/density/pallas_call | solution.py:832
  223.3 0.6 collective-permute-done.25.far_ref
  223.9 3.4 %pull.1 = f32[3,512]{1,0:T(4,128)} custom-call(f32[1]{0:T(128)} %get-tuple-element.90.gain_ref, f32[3,5120]{1,0:T(4,128)S(1)} %copy-done.8, f32[40,128]{1,0:T(8,128)S(1)} %get-tuple-element.103.above_ref, f32[40,128]{1,0:T(8,128)S(1)} %add.68.near_ref, f32[40,128]{1,0:T(8,128)S(1)} %collective-permute-done.25.far_ref, bf16[512,5120]{1,0:T(8,128)(2,1)S(1)} %bitcast.11, ...), custom_call_target="tpu_custom_call" | custom-call | tf_op jit(solution)/shard_map/pull/pallas_call | solution.py:782
  (66 shorter events, 0.4 us)
Async XLA Ops:
  0.6 12.4 %copy-start.13 = (f32[3,512]{1,0:T(4,128)S(1)}, f32[3,512]{1,0:T(4,128)}, u32[]{:S(2)}) copy-start(f32[3,512]{1,0:T(4,128)} %coords_ref.1) | copy-start | bytes 18436
  0.6 12.4 %copy-start.14 = (f32[512]{0:T(512)S(1)}, f32[512]{0:T(512)}, u32[]{:S(2)}) copy-start(f32[512]{0:T(512)} %param.9) | copy-start | bytes 6148
  0.7 24.5 %copy-start = (bf16[1280,1280]{1,0:T(8,128)(2,1)S(1)}, bf16[1280,1280]{1,0:T(8,128)(2,1)}, u32[]{:S(2)}) copy-start(bf16[1280,1280]{1,0:T(8,128)(2,1)} %ham_ref.3) | copy-start | bytes 9830404
  4.1 5.5 %collective-permute-start.1 = (bf16[640,1280]{1,0:T(8,128)(2,1)S(1)}, bf16[640,1280]{1,0:T(8,128)(2,1)}, u32[]{:S(2)}, u32[]{:S(2)}) collective-permute-start(bf16[640,1280]{1,0:T(8,128)(2,1)S(1)} %get-tuple-element.108), channel_id=1, source_target_pairs={{0,1},{1,0},{2,3},{3,2},{4,5},{5,4},{6,7},{7,6},{8,9},{9,8},{10,11... | collective-permute-start | bytes 4915208 | tf_op jit(solution)/shard_map/ppermute | solution.py:867
  4.6 40.1 %collective-permute-start.5 = (bf16[640,1280]{1,0:T(8,128)(2,1)}, bf16[640,1280]{1,0:T(8,128)(2,1)}, u32[]{:S(2)}, u32[]{:S(2)}) collective-permute-start(bf16[640,1280]{1,0:T(8,128)(2,1)} %get-tuple-element.109), channel_id=1, source_target_pairs={{0,1},{1,0},{2,3},{3,2},{4,5},{5,4},{6,7},{7,6},{8,9},{9,8},{10,11... | collective-permute-start | bytes 4915208 | tf_op jit(solution)/shard_map/ppermute | solution.py:867
  4.6 40.1 %collective-permute-start = (bf16[640,1280]{1,0:T(8,128)(2,1)}, bf16[640,1280]{1,0:T(8,128)(2,1)}, u32[]{:S(2)}, u32[]{:S(2)}) collective-permute-start(bf16[640,1280]{1,0:T(8,128)(2,1)} %get-tuple-element.109), channel_id=1, source_target_pairs={{0,5},{1,3},{2,15},{3,1},{4,6},{5,8},{6,4},{7,2},{8,13},{9,11},{10... | collective-permute-start | bytes 4915208 | tf_op jit(solution)/shard_map/ppermute | solution.py:884
  9.6 35.1 %collective-permute-start.2 = (bf16[640,1280]{1,0:T(8,128)(2,1)}, bf16[640,1280]{1,0:T(8,128)(2,1)}, u32[]{:S(2)}, u32[]{:S(2)}) collective-permute-start(bf16[640,1280]{1,0:T(8,128)(2,1)} %collective-permute-done.1.refs_1_), channel_id=1, source_target_pairs={{0,2},{1,4},{2,0},{3,14},{4,9},{5,7},{6,3},{7,5},{8,10},{9,12},{10... | collective-permute-start | bytes 4915208 | tf_op jit(solution)/shard_map/ppermute | solution.py:884
  14.5 0.9 copy-start.7
  22.8 2.3 %copy-start.3 = (bf16[512,5120]{1,0:T(8,128)(2,1)}, bf16[512,5120]{1,0:T(8,128)(2,1)S(1)}, u32[]{:S(2)}) copy-start(bf16[512,5120]{1,0:T(8,128)(2,1)S(1)} %get-tuple-element.105.weight_ref) | copy-start | bytes 15728644
  25.2 3.8 %copy-start.9 = (f32[1,5120]{1,0:T(1,128)}, f32[1,5120]{1,0:T(1,128)S(1)}, u32[]{:S(2)}) copy-start(f32[1,5120]{1,0:T(1,128)S(1)} %get-tuple-element.54) | copy-start | bytes 61444
  30.7 1.5 collective-permute-start.3
  32.9 11.9 %collective-permute-start.4 = (f32[88,128]{1,0:T(8,128)S(1)}, f32[88,128]{1,0:T(8,128)S(1)}, u32[]{:S(2)}, u32[]{:S(2)}) collective-permute-start(f32[88,128]{1,0:T(8,128)S(1)} %fusion.3), channel_id=1, source_target_pairs={{0,2},{2,0},{1,3},{3,1},{4,6},{6,4},{5,7},{7,5},{8,10},{10,8},{9,1... | collective-permute-start | bytes 135176 | tf_op jit(solution)/shard_map/ppermute | solution.py:870
  37.0 10.2 %copy-start.10 = (s32[12]{0:T(128)}, s32[12]{0:T(128)S(1)}, u32[]{:S(2)}) copy-start(s32[12]{0:T(128)S(1)} %fusion.2.info_ref) | copy-start | bytes 148
  47.2 7.4 %collective-permute-start.9 = (bf16[640,1280]{1,0:T(8,128)(2,1)}, bf16[640,1280]{1,0:T(8,128)(2,1)S(1)}, u32[]{:S(2)}, u32[]{:S(2)}) collective-permute-start(bf16[640,1280]{1,0:T(8,128)(2,1)} %collective-permute-done.refs_2_.refs_3_), channel_id=1, source_target_pairs={{0,1},{1,0},{2,3},{3,2},{4,5},{5,4},{6,7},{7,6},{8,9},{9,8},{10,11... | collective-permute-start | bytes 4915208 | tf_op jit(solution)/shard_map/ppermute | solution.py:867
  48.4 6.3 %collective-permute-start.10 = (bf16[640,1280]{1,0:T(8,128)(2,1)}, bf16[640,1280]{1,0:T(8,128)(2,1)S(1)}, u32[]{:S(2)}, u32[]{:S(2)}) collective-permute-start(bf16[640,1280]{1,0:T(8,128)(2,1)} %collective-permute-done.2.refs_3_.refs_4_), channel_id=1, source_target_pairs={{0,1},{1,0},{2,3},{3,2},{4,5},{5,4},{6,7},{7,6},{8,9},{9,8},{10,11... | collective-permute-start | bytes 4915208 | tf_op jit(solution)/shard_map/ppermute | solution.py:867
  48.4 42.2 %collective-permute-start.6 = (bf16[640,1280]{1,0:T(8,128)(2,1)S(1)}, bf16[640,1280]{1,0:T(8,128)(2,1)}, u32[]{:S(2)}, u32[]{:S(2)}) collective-permute-start(bf16[640,1280]{1,0:T(8,128)(2,1)S(1)} %get-tuple-element.61), channel_id=1, source_target_pairs={{0,2},{2,0},{1,3},{3,1},{4,6},{6,4},{5,7},{7,5},{8,10},{10,8},{9,1... | collective-permute-start | bytes 4915208 | tf_op jit(solution)/shard_map/ppermute | solution.py:870
  50.1 40.6 %collective-permute-start.7 = (bf16[640,1280]{1,0:T(8,128)(2,1)S(1)}, bf16[640,1280]{1,0:T(8,128)(2,1)}, u32[]{:S(2)}, u32[]{:S(2)}) collective-permute-start(bf16[640,1280]{1,0:T(8,128)(2,1)S(1)} %get-tuple-element.62), channel_id=1, source_target_pairs={{0,12},{12,8},{8,4},{4,0},{2,6},{6,10},{10,14},{14,2},{1,13},{13,9... | collective-permute-start | bytes 4915208 | tf_op jit(solution)/shard_map/ppermute | solution.py:874
  54.7 36.0 %collective-permute-start.8 = (f32[88,128]{1,0:T(8,128)S(1)}, f32[88,128]{1,0:T(8,128)S(1)}, u32[]{:S(2)}, u32[]{:S(2)}) collective-permute-start(f32[88,128]{1,0:T(8,128)S(1)} %add.65), channel_id=1, source_target_pairs={{0,4},{4,0},{8,12},{12,8},{1,5},{5,1},{9,13},{13,9},{2,6},{6,2},{1... | collective-permute-start | bytes 135176 | tf_op jit(solution)/shard_map/ppermute | solution.py:920
  54.7 1.2 copy-start.15
  55.9 1.2 copy-start.16
  90.6 5.0 %collective-permute-start.15 = (bf16[640,1280]{1,0:T(8,128)(2,1)}, bf16[640,1280]{1,0:T(8,128)(2,1)S(1)}, u32[]{:S(2)}, u32[]{:S(2)}) collective-permute-start(bf16[640,1280]{1,0:T(8,128)(2,1)} %collective-permute-done.7.refs_9_), channel_id=1, source_target_pairs={{0,1},{1,0},{2,3},{3,2},{4,5},{5,4},{6,7},{7,6},{8,9},{9,8},{10,11... | collective-permute-start | bytes 4915208 | tf_op jit(solution)/shard_map/ppermute | solution.py:867
  90.6 6.1 %collective-permute-start.14 = (bf16[640,1280]{1,0:T(8,128)(2,1)}, bf16[640,1280]{1,0:T(8,128)(2,1)S(1)}, u32[]{:S(2)}, u32[]{:S(2)}) collective-permute-start(bf16[640,1280]{1,0:T(8,128)(2,1)} %collective-permute-done.6.refs_7_), channel_id=1, source_target_pairs={{0,1},{1,0},{2,3},{3,2},{4,5},{5,4},{6,7},{7,6},{8,9},{9,8},{10,11... | collective-permute-start | bytes 4915208 | tf_op jit(solution)/shard_map/ppermute | solution.py:867
  91.2 42.0 %collective-permute-start.11 = (bf16[640,1280]{1,0:T(8,128)(2,1)}, bf16[640,1280]{1,0:T(8,128)(2,1)}, u32[]{:S(2)}, u32[]{:S(2)}) collective-permute-start(bf16[640,1280]{1,0:T(8,128)(2,1)} %collective-permute-done.7.refs_9_), channel_id=1, source_target_pairs={{0,2},{2,0},{1,3},{3,1},{4,6},{6,4},{5,7},{7,5},{8,10},{10,8},{9,1... | collective-permute-start | bytes 4915208 | tf_op jit(solution)/shard_map/ppermute | solution.py:870
  91.8 41.4 %collective-permute-start.12 = (bf16[640,1280]{1,0:T(8,128)(2,1)}, bf16[640,1280]{1,0:T(8,128)(2,1)S(1)}, u32[]{:S(2)}, u32[]{:S(2)}) collective-permute-start(bf16[640,1280]{1,0:T(8,128)(2,1)} %collective-permute-done.6.refs_7_), channel_id=1, source_target_pairs={{0,4},{4,8},{8,12},{12,0},{2,14},{14,10},{10,6},{6,2},{1,5},{5,9},... | collective-permute-start | bytes 4915208 | tf_op jit(solution)/shard_map/ppermute | solution.py:874
  93.6 39.5 %collective-permute-start.13 = (f32[88,128]{1,0:T(8,128)S(1)}, f32[88,128]{1,0:T(8,128)S(1)}, u32[]{:S(2)}, u32[]{:S(2)}) collective-permute-start(f32[88,128]{1,0:T(8,128)S(1)} %add.66.near_ref), channel_id=1, source_target_pairs={{0,8},{4,12},{8,0},{12,4},{1,9},{5,13},{9,1},{13,5},{2,10},{6,14},... | collective-permute-start | bytes 135176 | tf_op jit(solution)/shard_map/ppermute | solution.py:937
  95.6 1.2 copy-start.17
  96.7 1.2 copy-start.18
  97.9 35.3 %copy-start.11 = (s32[12]{0:T(128)S(1)}, s32[12]{0:T(128)}, u32[]{:S(2)}) copy-start(s32[12]{0:T(128)} %copy-done.10) | copy-start | bytes 148
  133.2 1.6 copy-start.2
  134.6 8.1 %collective-permute-start.18 = (bf16[640,1280]{1,0:T(8,128)(2,1)}, bf16[640,1280]{1,0:T(8,128)(2,1)S(1)}, u32[]{:S(2)}, u32[]{:S(2)}) collective-permute-start(bf16[640,1280]{1,0:T(8,128)(2,1)} %collective-permute-done.11.refs_11_), channel_id=1, source_target_pairs={{0,1},{1,0},{2,3},{3,2},{4,5},{5,4},{6,7},{7,6},{8,9},{9,8},{10,11... | collective-permute-start | bytes 4915208 | tf_op jit(solution)/shard_map/ppermute | solution.py:867
  134.7 8.0 %collective-permute-start.19 = (bf16[640,1280]{1,0:T(8,128)(2,1)S(1)}, bf16[640,1280]{1,0:T(8,128)(2,1)S(1)}, u32[]{:S(2)}, u32[]{:S(2)}) collective-permute-start(bf16[640,1280]{1,0:T(8,128)(2,1)S(1)} %collective-permute-done.12.refs_0_.refs_13_), channel_id=1, source_target_pairs={{0,1},{1,0},{2,3},{3,2},{4,5},{5,4},{6,7},{7,6},{8,9},{9,8},{10,11... | collective-permute-start | bytes 4915208 | tf_op jit(solution)/shard_map/ppermute | solution.py:867
  135.2 39.7 %collective-permute-start.17 = (bf16[640,1280]{1,0:T(8,128)(2,1)S(1)}, bf16[640,1280]{1,0:T(8,128)(2,1)}, u32[]{:S(2)}, u32[]{:S(2)}) collective-permute-start(bf16[640,1280]{1,0:T(8,128)(2,1)S(1)} %pick.3), channel_id=1, source_target_pairs={{0,4},{4,8},{8,12},{12,0},{2,14},{14,10},{10,6},{6,2},{1,5},{5,9},... | collective-permute-start | bytes 4915208 | tf_op jit(solution)/shard_map/ppermute | solution.py:874
  135.4 40.5 %collective-permute-start.16 = (bf16[640,1280]{1,0:T(8,128)(2,1)S(1)}, bf16[640,1280]{1,0:T(8,128)(2,1)}, u32[]{:S(2)}, u32[]{:S(2)}) collective-permute-start(bf16[640,1280]{1,0:T(8,128)(2,1)S(1)} %pick.3), channel_id=1, source_target_pairs={{0,2},{2,0},{1,3},{3,1},{4,6},{6,4},{5,7},{7,5},{8,10},{10,8},{9,1... | collective-permute-start | bytes 4915208 | tf_op jit(solution)/shard_map/ppermute | solution.py:870
  141.4 0.7 copy-start.4
  142.1 0.6 copy-start.5
  142.7 1.8 copy-start.19
  142.7 1.2 copy-start.20
  175.9 3.7 %collective-permute-start.20 = (bf16[640,1280]{1,0:T(8,128)(2,1)}, bf16[640,1280]{1,0:T(8,128)(2,1)S(1)}, u32[]{:S(2)}, u32[]{:S(2)}) collective-permute-start(bf16[640,1280]{1,0:T(8,128)(2,1)} %collective-permute-done.16.refs_15_), channel_id=1, source_target_pairs={{0,1},{1,0},{2,3},{3,2},{4,5},{5,4},{6,7},{7,6},{8,9},{9,8},{10,11... | collective-permute-start | bytes 4915208 | tf_op jit(solution)/shard_map/ppermute | solution.py:867
  175.9 6.1 %collective-permute-start.21 = (bf16[640,1280]{1,0:T(8,128)(2,1)}, bf16[640,1280]{1,0:T(8,128)(2,1)S(1)}, u32[]{:S(2)}, u32[]{:S(2)}) collective-permute-start(bf16[640,1280]{1,0:T(8,128)(2,1)} %collective-permute-done.17.refs_17_), channel_id=1, source_target_pairs={{0,1},{1,0},{2,3},{3,2},{4,5},{5,4},{6,7},{7,6},{8,9},{9,8},{10,11... | collective-permute-start | bytes 4915208 | tf_op jit(solution)/shard_map/ppermute | solution.py:867
  179.6 3.5 %copy-start.21 = (bf16[640,1280]{1,0:T(8,128)(2,1)}, bf16[640,1280]{1,0:T(8,128)(2,1)S(1)}, u32[]{:S(2)}) copy-start(bf16[640,1280]{1,0:T(8,128)(2,1)S(1)} %collective-permute-done.20.refs_16_) | copy-start | bytes 4915204
  181.9 1.2 copy-start.22
  183.1 32.1 %copy-start.1 = (bf16[1280,1280]{1,0:T(8,128)(2,1)S(1)}, bf16[1280,1280]{1,0:T(8,128)(2,1)}, u32[]{:S(2)}) copy-start(bf16[1280,1280]{1,0:T(8,128)(2,1)} %ham_ref.3) | copy-start | bytes 9830404
  183.1 32.1 %copy-start.6 = (f32[40,128]{1,0:T(8,128)S(1)}, f32[40,128]{1,0:T(8,128)}, u32[]{:S(2)}) copy-start(f32[40,128]{1,0:T(8,128)} %copy-done.5) | copy-start | bytes 61444
  183.1 32.1 %copy-start.12 = (s32[12]{0:T(128)S(1)}, s32[12]{0:T(128)}, u32[]{:S(2)}) copy-start(s32[12]{0:T(128)} %copy-done.10) | copy-start | bytes 148
  210.6 4.5 %collective-permute-start.24 = (bf16[640,1280]{1,0:T(8,128)(2,1)}, bf16[640,1280]{1,0:T(8,128)(2,1)S(1)}, u32[]{:S(2)}, u32[]{:S(2)}) collective-permute-start(bf16[640,1280]{1,0:T(8,128)(2,1)} %get-tuple-element.98), channel_id=1, source_target_pairs={{0,1},{1,0},{2,3},{3,2},{4,5},{5,4},{6,7},{7,6},{8,9},{9,8},{10,11... | collective-permute-start | bytes 4915208 | tf_op jit(solution)/shard_map/ppermute | solution.py:867
  210.7 3.7 %collective-permute-start.22 = (f32[40,128]{1,0:T(8,128)}, f32[40,128]{1,0:T(8,128)S(1)}, u32[]{:S(2)}, u32[]{:S(2)}) collective-permute-start(f32[40,128]{1,0:T(8,128)} %get-tuple-element.97), channel_id=1, source_target_pairs={{0,1},{1,0},{2,3},{3,2},{4,5},{5,4},{6,7},{7,6},{8,9},{9,8},{10,11... | collective-permute-start | bytes 61448 | tf_op jit(solution)/shard_map/ppermute | solution.py:867
  215.2 3.8 %collective-permute-start.23 = (f32[40,128]{1,0:T(8,128)S(1)}, f32[40,128]{1,0:T(8,128)S(1)}, u32[]{:S(2)}, u32[]{:S(2)}) collective-permute-start(f32[40,128]{1,0:T(8,128)S(1)} %add.67), channel_id=1, source_target_pairs={{0,4},{4,0},{8,12},{12,8},{1,5},{5,1},{9,13},{13,9},{2,6},{6,2},{1... | collective-permute-start | bytes 61448 | tf_op jit(solution)/shard_map/ppermute | solution.py:972
  215.2 8.7 %slice-start = ((s8[5242880]{0:T(1024)(128)(4,1)}), s8[4194304]{0:T(1024)(128)(4,1)S(1)}, s32[]{:S(2)}) async-start(s8[5242880]{0:T(1024)(128)(4,1)} %bitcast.10), calls=%async_computation | async-start | bytes 8388608
  218.6 5.2 %slice-start.1 = ((s8[5242880]{0:T(1024)(128)(4,1)}), s8[1048576]{0:T(1024)(128)(4,1)S(1)}, s32[]{:S(2)}) async-start(s8[5242880]{0:T(1024)(128)(4,1)} %bitcast.10), calls=%async_computation.1 | async-start | bytes 2097152
  219.0 4.9 %copy-start.8 = (f32[3,5120]{1,0:T(4,128)S(1)}, f32[3,5120]{1,0:T(4,128)}, u32[]{:S(2)}) copy-start(f32[3,5120]{1,0:T(4,128)} %spots_ref.3) | copy-start | bytes 184324
  219.0 4.9 %collective-permute-start.25 = (f32[40,128]{1,0:T(8,128)S(1)}, f32[40,128]{1,0:T(8,128)S(1)}, u32[]{:S(2)}, u32[]{:S(2)}) collective-permute-start(f32[40,128]{1,0:T(8,128)S(1)} %add.68.near_ref), channel_id=1, source_target_pairs={{0,8},{4,12},{8,0},{12,4},{1,9},{5,13},{9,1},{13,5},{2,10},{6,14},... | collective-permute-start | bytes 61448 | tf_op jit(solution)/shard_map/ppermute | solution.py:976
